TPU v7x, 128 devices: a whole 4x4x4 slice. The times are simulated.
128 devices in a mesh: seq: 16 (over z, x), exp: 8 (over y, core).
Axes of the slice: x: 4, y: 4, z: 4, core: 2. Of those that a mesh axis runs over, the one named last changes fastest.
Arguments:
- hidden_in: bfloat16 [16384, 2560], P(('seq', 'exp')), may hold values from -6 to 6
- grad_out: bfloat16 [16384, 2560], P(('seq', 'exp')), may hold values from -1.5 to 1.5
- expert_ids: int32 [16384, 6], P(('seq', 'exp')), may hold values from 0 to 127, as said below
- gate_weights: float32 [16384, 6], P(('seq', 'exp')), may hold values from 0.25 to 4
- w_gate: bfloat16 [128, 2560, 768], P(('seq', 'exp')), may hold values from -0.125 to 0.125
- w_up: bfloat16 [128, 2560, 768], P(('seq', 'exp')), may hold values from -0.125 to 0.125
- w_down: bfloat16 [128, 768, 2560], P(('seq', 'exp')), may hold values from -0.21875 to 0.21875
Outputs:
- grad_in: bfloat16 [16384, 2560], P(('seq', 'exp'))
- grad_gates: bfloat16 [16384, 6], P(('seq', 'exp'))
Inputs may be any that keep to these rules, and one draw needn't show every extreme that they name: `expert_ids`: expert e lies in group e // 8. Each row names 6 different experts: entries 2j and 2j + 1 (j = 0, 1, 2) lie in one group, and the three groups of a row differ. Among the 128 rows of one device each group is named by exactly 24 rows, no expert is named more than 9 times, and in every device one expert is named exactly 9 times.
All inputs are finite; a program needn't handle non-finite values.
Results may differ from a plain program's by a relative error of at most 0.0057.
Values may be sent and summed in bfloat16 or wider, within the bound.
No kernel may reach another device: no remote copies, remote signals or barrier semaphores. Data moves between devices by JAX's collectives and lax.ppermute only.
A program may use at most 128 MiB of HBM per device.

v0:
```python
import jax
import jax.numpy as jnp
from jax import lax
from jax.experimental import pallas as pl
from jax.experimental.pallas import tpu as pltpu
from jax.sharding import PartitionSpec as P

BF = jnp.bfloat16
F32 = jnp.float32
LANES = 128


def dot(a, b):
    return jnp.dot(a, b, preferred_element_type=F32)


def dot_t(a, b):
    return lax.dot_general(a, b, (((0,), (0,)), ((), ())), preferred_element_type=F32)


def dot_nt(a, b):
    return lax.dot_general(a, b, (((1,), (1,)), ((), ())), preferred_element_type=F32)


def earlier_counts(names):
    n = names.shape[-2]
    lower = (jnp.arange(n)[:, None] > jnp.arange(n)[None, :]).astype(BF)
    counts = jnp.einsum("ij,...jm->...im", lower, names.astype(BF), preferred_element_type=F32)
    return jnp.where(names, counts, -1.0)


def barrier(*values):
    return lax.optimization_barrier(values)


def exchange(blocks, n_exp):
    out = [blocks[0]]
    for k in range(1, n_exp):
        out.append(lax.ppermute(blocks[k], "exp", [(i, i ^ k) for i in range(n_exp)]))
    return out


def whole(shape, at=(0, 0)):
    return pl.BlockSpec(shape, lambda *_: at, pipeline_mode=pl.Buffered(1))


def params(mib):
    return pltpu.CompilerParams(vmem_limit_bytes=mib * 2**20)


def cost(flops, nbytes):
    return pl.CostEstimate(flops=flops, bytes_accessed=nbytes, transcendentals=0)


def window_tables(n_seq, n_exp, cap):
    pair = 2 * n_exp * cap
    d = jnp.arange(pair)
    source = d % (n_exp * cap) // cap * 32 + d // (n_exp * cap) * cap + d % cap
    i = jnp.arange(n_seq // 2)
    at = source[None, :] + (2 * cap - 16) * i[:, None]
    wide = jnp.arange(32 * n_exp)
    to_b = (at[:, :, None] == wide[None, None, :]).astype(BF)
    to_a = (at[:, None, :] == wide[None, :, None]).astype(BF)
    return to_b, to_a


def pre_kernel(n_exp, pairs, table, *refs):
    blocks, (gate, up, out_gate, out_up, rows) = refs[:n_exp], refs[n_exp:]
    size = table.shape[1]

    @pl.when(pl.program_id(0) == 0)
    def _():
        for i in range(pairs):
            window = jnp.concatenate([b[16 * i:16 * i + 32, :] for b in blocks], axis=0)
            rows[size * i:size * (i + 1), :] = dot(table[i], window).astype(BF)

    out_gate[...] = dot(rows[...], gate[...])
    out_up[...] = dot(rows[...], up[...])


def pre_products(table, blocks, gate_mat, up_mat):
    n_exp, pairs = len(blocks), table.shape[0]
    rows, features = blocks[0].shape
    total, units = rows * n_exp, gate_mat.shape[1]
    wide = 256 if units % 256 == 0 else units
    column = pl.BlockSpec((features, wide), lambda j: (0, j))
    result = pl.BlockSpec((total, wide), lambda j: (0, j))
    return pl.pallas_call(
        lambda *refs: pre_kernel(n_exp, pairs, *refs),
        grid=(units // wide,),
        in_specs=[whole(table.shape, (0, 0, 0))] + [whole((rows, features))] * n_exp + [column, column],
        out_specs=[result, result],
        out_shape=[jax.ShapeDtypeStruct((total, units), F32)] * 2,
        scratch_shapes=[pltpu.VMEM((total, features), BF)],
        compiler_params=params(44),
        cost_estimate=cost(4 * total * features * units, 2 * total * features + 4 * features * units + 8 * total * units),
        name="pre_products",
    )(table, *blocks, gate_mat, up_mat)


def grad_kernel(lane, grad, down, pre_gate, pre_up, out_gate, out_up, out_dot):
    grad_hidden = dot_nt(grad[...], down[...])
    gate, up = pre_gate[...], pre_up[...]
    sigmoid = jax.nn.sigmoid(gate)
    active = gate * sigmoid
    hidden = (active * up).astype(BF).astype(F32)
    gate_dot = jnp.sum(hidden * grad_hidden, axis=1, keepdims=True)
    out_dot[...] = (gate_dot * lane[0:1, :]).astype(BF)
    out_gate[...] = (grad_hidden * up * sigmoid * (1.0 + gate * (1.0 - sigmoid))).astype(BF)
    out_up[...] = (grad_hidden * active).astype(BF)


def hidden_grads(lane, rows_grad, down_mat, pre_gate, pre_up):
    total, features = rows_grad.shape
    units = down_mat.shape[0]
    tall = total // 4
    row = lambda width: pl.BlockSpec((tall, width), lambda i: (i, 0))
    return pl.pallas_call(
        grad_kernel,
        grid=(4,),
        in_specs=[whole(lane.shape), row(features), whole(down_mat.shape), row(units), row(units)],
        out_specs=[row(units), row(units), row(LANES)],
        out_shape=[jax.ShapeDtypeStruct((total, units), BF)] * 2 + [jax.ShapeDtypeStruct((total, LANES), BF)],
        compiler_params=params(44),
        cost_estimate=cost(2 * total * features * units, 2 * total * features + 2 * features * units + 12 * total * units),
        name="hidden_grads",
    )(lane, rows_grad, down_mat, pre_gate, pre_up)


def back_a_kernel(n_exp, pairs, table, grad_gate, grad_up, gate, up, gate_dot, *outs):
    wide = gate.shape[0]
    half = outs[0].shape[1] - LANES
    size = table.shape[2]

    def reorder(values, start, width):
        before = None
        for i in range(pairs):
            moved = dot(table[i], values[size * i:size * (i + 1), :])
            for k in range(n_exp):
                part = moved[32 * k:32 * k + 16, :]
                if before is not None:
                    part = part + before[32 * k + 16:32 * k + 32, :]
                outs[k][16 * i:16 * i + 16, pl.ds(start, width)] = part.astype(BF)
            before = moved
        for k in range(n_exp):
            part = before[32 * k + 16:32 * k + 32, :]
            outs[k][16 * pairs:16 * pairs + 16, pl.ds(start, width)] = part.astype(BF)

    j = pl.program_id(0)
    values = dot_nt(grad_gate[...], gate[...]) + dot_nt(grad_up[...], up[...])
    reorder(values.astype(BF), pl.multiple_of(j * wide, wide), wide)

    @pl.when(j == 0)
    def _():
        reorder(gate_dot[...], half, LANES)


def returned_a(table, grad_gate, grad_up, gate_mat, up_mat, gate_dot, n_exp):
    total, units = grad_gate.shape
    half = gate_mat.shape[0] // 2
    pairs = table.shape[0]
    wide = 256 if half % 256 == 0 else half
    mat = pl.BlockSpec((wide, units), lambda j: (j, 0))
    block = (total // n_exp, half + LANES)
    return pl.pallas_call(
        lambda *refs: back_a_kernel(n_exp, pairs, *refs),
        grid=(half // wide,),
        in_specs=[whole(table.shape, (0, 0, 0)), whole(grad_gate.shape), whole(grad_up.shape), mat, mat, whole(gate_dot.shape)],
        out_specs=[whole(block)] * n_exp,
        out_shape=[jax.ShapeDtypeStruct(block, BF)] * n_exp,
        compiler_params=params(44),
        cost_estimate=cost(4 * total * half * units, 4 * half * units + 4 * total * units + 2 * total * half),
        name="returned_a",
    )(table, grad_gate, grad_up, gate_mat, up_mat, gate_dot)


def back_b_kernel(grad_gate, grad_up, gate, up, out):
    out[...] = (dot_nt(grad_gate[...], gate[...]) + dot_nt(grad_up[...], up[...])).astype(BF)


def returned_b(grad_gate, grad_up, gate_mat, up_mat):
    total, units = grad_gate.shape
    half = gate_mat.shape[0] // 2
    wide = 256 if half % 256 == 0 else half
    mat = pl.BlockSpec((wide, units), lambda j: (half // wide + j, 0))
    return pl.pallas_call(
        back_b_kernel,
        grid=(half // wide,),
        in_specs=[whole(grad_gate.shape), whole(grad_up.shape), mat, mat],
        out_specs=pl.BlockSpec((total, wide), lambda j: (0, j)),
        out_shape=jax.ShapeDtypeStruct((total, half), BF),
        compiler_params=params(44),
        cost_estimate=cost(4 * total * half * units, 4 * half * units + 4 * total * units + 2 * total * half),
        name="returned_b",
    )(grad_gate, grad_up, gate_mat, up_mat)


def sum_kernel(n_exp, slot, weight, *refs):
    blocks, (out,) = refs[:n_exp], refs[n_exp:]
    half = out.shape[1] - LANES
    rows = blocks[0].shape[0]
    place = lax.broadcasted_iota(jnp.int32, (slot.shape[0], rows), 1).astype(F32)
    sums = jnp.zeros((slot.shape[0], half), F32)
    gates = jnp.zeros((slot.shape[0], LANES), F32)
    for k in range(n_exp):
        hot = slot[:, k:k + 1] == place
        sums += dot(jnp.where(hot, weight[:, k:k + 1], 0.0).astype(BF), blocks[k][:, :half])
        gates += dot(jnp.where(hot, 1.0, 0.0).astype(BF), blocks[k][:, half:])
    out[:, :half] = sums.astype(BF)
    out[:, half:] = gates.astype(BF)


def group_sums(slot, weight, blocks):
    n_exp = len(blocks)
    n_rows, width = slot.shape[0], blocks[0].shape[1]
    return pl.pallas_call(
        lambda *refs: sum_kernel(n_exp, *refs),
        grid=(1,),
        in_specs=[whole(slot.shape), whole(weight.shape)] + [whole(blocks[0].shape)] * n_exp,
        out_specs=whole((n_rows, width)),
        out_shape=jax.ShapeDtypeStruct((n_rows, width), BF),
        compiler_params=params(32),
        cost_estimate=cost(2 * n_rows * blocks[0].shape[0] * n_exp * width, 2 * n_exp * blocks[0].size),
        name="group_sums",
    )(slot, weight, *blocks)


def named_here(top, eye, meta, local):
    flat = dot_nt(eye[...], meta)
    named = weight = jnp.zeros((local.shape[0], flat.shape[1]), F32)
    for k in range(top):
        hit = flat[k:k + 1, :] == local[:, 0:1]
        named += jnp.where(hit, 1.0, 0.0)
        weight += jnp.where(hit, flat[top + k:top + k + 1, :], 0.0)
    return named, weight


def hub_kernel(top, cap, eye, local, before, block, hub, *outs):
    *blocks, out_slot, out_weight = outs
    features = blocks[0].shape[1]
    named, out_weight[...] = named_here(top, eye, hub[:, features:], local)
    slot = jnp.where(named > 0.0, block[0:1, :] * cap + dot(named.astype(BF), before[...]), -1.0)
    out_slot[...] = slot
    place = lax.broadcasted_iota(jnp.int32, (blocks[0].shape[0], slot.shape[1]), 0).astype(F32)
    for k, out in enumerate(blocks):
        hot = jnp.where(place == slot[k:k + 1, :], 1.0, 0.0).astype(BF)
        out[...] = dot(hot, hub[:, :features]).astype(BF)


def lower_counts(total, size):
    at = jnp.arange(total)
    same = at[:, None] // size == at[None, :] // size
    return (same & (at[:, None] < at[None, :])).astype(BF), jnp.broadcast_to((at // size).astype(F32), (8, total))


def hub_blocks(hub, local, per_group, top, cap):
    n_rows, width = hub.shape
    n_exp = local.shape[0]
    before, block = lower_counts(n_rows, per_group)
    shape = (n_rows // per_group * cap, width - LANES)
    row = (n_exp, n_rows)
    eye = jnp.eye(LANES, dtype=BF)
    *blocks, slot, weight = pl.pallas_call(
        lambda *refs: hub_kernel(top, cap, *refs),
        grid=(1,),
        in_specs=[whole(x.shape) for x in (eye, local, before, block, hub)],
        out_specs=[whole(shape)] * n_exp + [whole(row)] * 2,
        out_shape=[jax.ShapeDtypeStruct(shape, BF)] * n_exp + [jax.ShapeDtypeStruct(row, F32)] * 2,
        compiler_params=params(32),
        cost_estimate=cost(2 * shape[0] * n_exp * n_rows * width, 2 * n_exp * shape[0] * shape[1]),
        name="hub_blocks",
    )(eye, local, before, block, hub)
    return blocks, slot.T, weight.T


def slots_kernel(top, rows, eye, theirs, before, start, meta, out_hot, out_slot, out_weight):
    named, out_weight[...] = named_here(top, eye, meta[...], theirs)
    size = before.shape[0]
    counts = [dot(named[:, at:at + size].astype(BF), before[...]) for at in range(0, named.shape[1], size)]
    slot = jnp.where(named > 0.0, start[0:1, :] + jnp.concatenate(counts, axis=1), -1.0)
    out_slot[...] = slot
    place = lax.broadcasted_iota(jnp.int32, (rows, slot.shape[1]), 0).astype(F32)
    for g in range(0, slot.shape[0], 2):
        pair = [jnp.where(place == slot[i:i + 1, :], 1.0, 0.0) for i in (g, g + 1)]
        out_hot[g * rows:(g + 2) * rows, :] = jnp.concatenate(pair, axis=0).astype(BF)


def column_slots(meta, theirs, member, n_tok, top, cap):
    total = meta.shape[0]
    n_seq, n_exp = theirs.shape[0], total // n_tok
    before, _ = lower_counts(n_tok, n_tok)
    start = ((jnp.arange(total) // n_tok) ^ member) * cap
    start = jnp.broadcast_to(start.astype(F32), (8, total))
    eye = jnp.eye(LANES, dtype=BF)
    shapes = (n_seq * n_exp * cap, total), (n_seq, total), (n_seq, total)
    hot, slot, weight = pl.pallas_call(
        lambda *refs: slots_kernel(top, n_exp * cap, *refs),
        grid=(1,),
        in_specs=[whole(x.shape) for x in (eye, theirs, before, start, meta)],
        out_specs=[whole(shape) for shape in shapes],
        out_shape=[jax.ShapeDtypeStruct(shape, kind) for shape, kind in zip(shapes, (BF, F32, F32))],
        compiler_params=params(32),
        cost_estimate=cost(4 * total * LANES * LANES, 2 * shapes[0][0] * total),
        name="column_slots",
    )(eye, theirs, before, start, meta)
    return hot, slot.T, weight.T


def column_kernel(n_exp, member, place, spread, slot, weight, got, *refs):
    outs, (mixed,) = refs[:n_exp], refs[n_exp:]
    n_tok = outs[0].shape[0]
    for k in range(n_exp):
        rows = pl.ds(pl.multiple_of((member[0] ^ k) * n_tok, n_tok), n_tok)
        hot = dot(slot[rows, :], spread[...]) == place[0:1, :]
        mixed[n_tok * k:n_tok * (k + 1), :] = jnp.where(hot, dot(weight[rows, :], spread[...]), 0.0).astype(BF)
    half = got.shape[1]
    wide = 256 if half % 256 == 0 else half
    for start in range(0, half, wide):
        sums = dot(mixed[...], got[:, start:start + wide]).astype(BF)
        for k in range(n_exp):
            outs[k][:, start:start + wide] = sums[n_tok * k:n_tok * (k + 1), :]


def column_sums(member, slot, weight, got, n_exp):
    n_rows, n_seq = slot.shape
    total, half = got.shape
    at = jnp.arange(total)
    place = jnp.broadcast_to((at % (total // n_seq)).astype(F32), (8, total))
    spread = (jnp.arange(n_seq)[:, None] == at[None, :] // (total // n_seq)).astype(BF)
    block = (n_rows // n_exp, half)
    return pl.pallas_call(
        lambda *refs: column_kernel(n_exp, *refs),
        grid=(1,),
        in_specs=[pl.BlockSpec(memory_space=pltpu.SMEM), whole(place.shape), whole(spread.shape), whole(slot.shape),
                  whole(weight.shape), whole(got.shape)],
        out_specs=[whole(block)] * n_exp,
        out_shape=[jax.ShapeDtypeStruct(block, BF)] * n_exp,
        scratch_shapes=[pltpu.VMEM((n_rows, total), BF)],
        compiler_params=params(32),
        cost_estimate=cost(2 * n_rows * total * half, 2 * total * half + 2 * n_rows * half),
        name="column_sums",
    )(member.reshape(1), place, spread, slot.astype(BF), weight.astype(BF), got)


def per_device(hidden_in, grad_out, expert_ids, gate_weights, w_gate, w_up, w_down):
    n_tok, features = hidden_in.shape
    top = expert_ids.shape[1]
    n_seq, n_exp = lax.axis_size("seq"), lax.axis_size("exp")
    group, member = lax.axis_index("seq"), lax.axis_index("exp")
    experts = n_seq * n_exp
    cap = 3 * top * n_tok // (2 * experts)
    per_group = top // 2 * n_tok // n_seq
    half = features // 2
    gate_mat, up_mat, down_mat = w_gate[0], w_up[0], w_down[0]
    partner = member ^ jnp.arange(n_exp)
    to_b, to_a = window_tables(n_seq, n_exp, cap)

    meta = jnp.concatenate(
        (expert_ids.astype(BF), gate_weights.astype(BF), jnp.zeros((n_tok, LANES - 2 * top), BF)), axis=1)

    column_meta = lax.all_gather(meta, "exp", axis=0, tiled=True)
    column = lax.all_gather(grad_out, "exp", axis=0, tiled=True)
    theirs = jnp.broadcast_to((jnp.arange(n_seq) * n_exp + member).astype(F32)[:, None], (n_seq, LANES))
    put_b, slot_b, weight_b = column_slots(column_meta, theirs, member, n_tok, top, cap)

    group_ids = expert_ids // n_exp
    in_group = jnp.any(group_ids[:, :, None] == jnp.arange(n_seq)[None, None, :], axis=1)
    group_rank = earlier_counts(in_group).T
    pick = (group_rank[:, None, :] == jnp.arange(per_group, dtype=F32)[None, :, None])
    pick = pick.astype(BF).reshape(n_seq * per_group, n_tok)
    send = dot(pick, jnp.concatenate((hidden_in, meta), axis=1)).astype(BF)
    hub = lax.all_to_all(send.reshape(n_seq, per_group, features + LANES), "seq", 0, 0, tiled=True)
    hub = hub.reshape(n_seq * per_group, features + LANES)

    send_b = dot(put_b, column).astype(BF)
    hub, send_b = barrier(hub, send_b)
    rows_b = n_exp * cap
    recv_b = lax.all_to_all(send_b.reshape(n_seq, rows_b, features), "seq", 0, 0, tiled=True)
    recv_b = recv_b.reshape(n_seq * rows_b, features)

    local = jnp.broadcast_to((partner + group * n_exp).astype(F32)[:, None], (n_exp, LANES))
    blocks, slot_a, weight_a = hub_blocks(hub, local, per_group, top, cap)
    rows_in = exchange(blocks, n_exp)

    pre_gate, pre_up = pre_products(to_b, rows_in, gate_mat, up_mat)
    lane = jnp.broadcast_to((jnp.arange(LANES) == group * n_exp + member).astype(F32), (8, LANES))
    grad_gate, grad_up, gate_dot = hidden_grads(lane, recv_b, down_mat, pre_gate, pre_up)

    got_a = exchange(returned_a(to_a, grad_gate, grad_up, gate_mat, up_mat, gate_dot, n_exp), n_exp)
    back_b = returned_b(grad_gate, grad_up, gate_mat, up_mat)
    got_b = lax.all_to_all(back_b.reshape(n_seq, rows_b, half), "seq", 0, 0, tiled=True)
    parts = column_sums(member, slot_b, weight_b, got_b.reshape(n_seq * rows_b, half), n_exp)
    *parts, slot_a = barrier(*parts, slot_a)
    back = group_sums(slot_a, weight_a, got_a)
    back = lax.all_to_all(back.reshape(n_seq, per_group, half + LANES), "seq", 0, 0, tiled=True)
    final_b = sum(p.astype(F32) for p in exchange(parts, n_exp))
    final_a = dot_t(pick, back.reshape(n_seq * per_group, half + LANES))

    grad_in = jnp.concatenate((final_a[:, :half], final_b), axis=1).astype(BF)
    table = final_a[:, half:]
    chosen = expert_ids[:, :, None] == jnp.arange(experts)[None, None, :]
    grad_gates = jnp.sum(jnp.where(chosen, table[:, None, :experts], 0.0), axis=2).astype(BF)
    return grad_in, grad_gates


def solution(mesh):
    rows, mats = P(("seq", "exp"), None), P(("seq", "exp"), None, None)
    return jax.shard_map(
        per_device, mesh=mesh, in_specs=(rows,) * 4 + (mats,) * 3, out_specs=(rows, rows), check_vma=False
    )
```

profile of v0, /device:TPU:1, one launch (start us, length us, event | category | flops | bytes accessed | tf_op | source)
XLA Modules:
  0.0 314.0 jit_solution(7319246473145500597)
XLA Ops:
  10.6 1.2 concatenate.12
  11.8 2.0 convolution_convert_fusion.1
  13.9 8.4 %all-to-all-start = ((bf16[16,24,2688]{2,1,0:T(8,128)(2,1)}), bf16[16,24,2688]{2,1,0:T(8,128)(2,1)S(1)}, u32[]{:S(2)}, u32[]{:S(2)}) async-start(bf16[16,24,2688]{2,1,0:T(8,128)(2,1)} %bitcast.37), calls=%async_computation | async-start | bytes 4128768 | tf_op jit(solution)/shard_map/all_to_all | solution.py:372
  22.4 14.5 %all_gather.6.refs_4_ = bf16[1024,128]{1,0:T(8,128)(2,1)S(1)} all-gather(bf16[128,128]{1,0:T(8,128)(2,1)S(1)} %pad_maximum_fusion.1), channel_id=1, replica_groups=mesh['seq'=16,'exp'=8] {'exp'}, dimensions={0}, use_global_device_ids=true | all-gather | bytes 294912 | tf_op jit(solution)/shard_map/all_gather | solution.py:361
  39.2 1.4 copy-done.17
  40.6 10.4 %all-gather.2.cloned.1.call-done = bf16[1024,2560]{1,0:T(8,128)(2,1)} async-done(((bf16[128,2560]{1,0:T(8,128)(2,1)}), bf16[1024,2560]{1,0:T(8,128)(2,1)}) %all-gather.2.cloned.1.call-update) | async-done | bytes 5242896 | tf_op jit(solution)/shard_map/all_gather | solution.py:362
  51.0 10.6 %convolution_convert_fusion = bf16[1152,2560]{1,0:T(8,128)(2,1)} fusion(bf16[1152,1024]{1,0:T(8,128)(2,1)} %copy-done.17, bf16[1024,2560]{1,0:T(8,128)(2,1)} %all-gather.2.cloned.1.call-done), kind=kOutput, calls=%fused_computation | convolution fusion | flops 6042746880 | bytes 13500416 | tf_op jit(solution)/shard_map/dot_general | solution.py:14
  61.6 6.7 %all-to-all-start.1 = ((bf16[16,72,2560]{2,1,0:T(8,128)(2,1)}), bf16[16,72,2560]{2,1,0:T(8,128)(2,1)}, u32[]{:S(2)}, u32[]{:S(2)}) async-start(bf16[16,72,2560]{2,1,0:T(8,128)(2,1)} %bitcast.38), calls=%async_computation.1 | async-start | bytes 11796480 | tf_op jit(solution)/shard_map/all_to_all | solution.py:378
  68.6 4.2 %hub_blocks.1 = (bf16[144,2560]{1,0:T(8,128)(2,1)S(1)}, bf16[144,2560]{1,0:T(8,128)(2,1)S(1)}, bf16[144,2560]{1,0:T(8,128)(2,1)S(1)}, bf16[144,2560]{1,0:T(8,128...) custom-call(bf16[128,128]{1,0:T(8,128)(2,1)S(1)} %get-tuple-element., ...), custom_call_target="tpu_custom_call" | custom-call | flops 2378170368 | bytes 5898240 | tf_op jit(solution)/shard_map/hub_blocks/pallas_call | solution.py:263
  73.9 0.9 copy-done.37
  75.6 1.4 collective-permute-start.2
  77.0 1.5 collective-permute-start.3
  78.5 1.9 collective-permute-start.4
  80.4 0.9 copy-done.22
  81.8 11.8 %collective-permute-done.1.refs_3_ = bf16[144,2560]{1,0:T(8,128)(2,1)S(1)} collective-permute-done((bf16[144,2560]{1,0:T(8,128)(2,1)S(1)}, bf16[144,2560]{1,0:T(8,128)(2,1)S(1)}, u32[]{:S(2)}, u32[]{:S(2)}) %collective-permute-start.1) | collective-permute-done | bytes 737312 | tf_op jit(solution)/shard_map/ppermute | solution.py:39
  93.6 0.9 copy-done.24
  94.5 1.5 collective-permute-start.6
  96.3 13.9 %collective-permute-done.2.refs_4_ = bf16[144,2560]{1,0:T(8,128)(2,1)S(1)} collective-permute-done((bf16[144,2560]{1,0:T(8,128)(2,1)}, bf16[144,2560]{1,0:T(8,128)(2,1)S(1)}, u32[]{:S(2)}, u32[]{:S(2)}) %collective-permute-start.2) | collective-permute-done | bytes 737312 | tf_op jit(solution)/shard_map/ppermute | solution.py:39
  110.2 0.9 copy-done.26
  111.0 14.5 %collective-permute-done.3.refs_5_ = bf16[144,2560]{1,0:T(8,128)(2,1)S(1)} collective-permute-done((bf16[144,2560]{1,0:T(8,128)(2,1)}, bf16[144,2560]{1,0:T(8,128)(2,1)S(1)}, u32[]{:S(2)}, u32[]{:S(2)}) %collective-permute-start.3) | collective-permute-done | bytes 737312 | tf_op jit(solution)/shard_map/ppermute | solution.py:39
  125.5 0.9 copy-done.28
  126.4 15.1 %collective-permute-done.4.refs_6_ = bf16[144,2560]{1,0:T(8,128)(2,1)} collective-permute-done((bf16[144,2560]{1,0:T(8,128)(2,1)}, bf16[144,2560]{1,0:T(8,128)(2,1)}, u32[]{:S(2)}, u32[]{:S(2)}) %collective-permute-start.4) | collective-permute-done | bytes 737312 | tf_op jit(solution)/shard_map/ppermute | solution.py:39
  141.4 6.9 %collective-permute-done.6.refs_8_ = bf16[144,2560]{1,0:T(8,128)(2,1)} collective-permute-done((bf16[144,2560]{1,0:T(8,128)(2,1)S(1)}, bf16[144,2560]{1,0:T(8,128)(2,1)}, u32[]{:S(2)}, u32[]{:S(2)}) %collective-permute-start.6) | collective-permute-done | bytes 737312 | tf_op jit(solution)/shard_map/ppermute | solution.py:39
  148.4 1.1 copy-done.23
  149.5 1.1 copy-done.25
  150.6 1.1 copy-done.27
  151.7 1.1 copy-done.29
  152.8 1.1 copy-done.38
  153.9 15.2 %pre_products.1 = (f32[1152,768]{1,0:T(8,128)S(1)}, f32[1152,768]{1,0:T(8,128)}) custom-call(bf16[8,144,256]{2,1,0:T(8,128)(2,1)S(1)} %fusion.1.refs_0_, bf16[144,2560]{1,0:T(8,128)(2,1)S(1)} %copy-done.38, bf16[144,2560]{1,0:T(8,128)(2,1)S(1)} %copy-done.23, bf16[144,2560]{1,0:T(8,128)(2,1)S(1)} %copy-done.25, bf16[144,2560]{1,0:T(8,128)(2,1)S(1)} %copy-done.27, ...), custom_call_target="tpu_custom_call" | custom-call | flops 9059696640 | bytes 20840448 | tf_op jit(solution)/shard_map/pre_products/pallas_call | solution.py:88
  169.1 9.6 %hidden_grads.1 = (bf16[1152,768]{1,0:T(8,128)(2,1)S(1)}, bf16[1152,768]{1,0:T(8,128)(2,1)S(1)}, bf16[1152,128]{1,0:T(8,128)(2,1)S(1)}) custom-call(f32[8,128]{1,0:T(8,128)S(1)} %broadcast_in_dim.31.lane, bf16[1152,2560]{1,0:T(8,128)(2,1)} %bitcast.8.grad, bf16[768,2560]{1,0:T(8,128)(2,1)} %bitcast.39, f32[1152,768]{1,0:T(8,128)S(1)} %get-tuple-element.60.pre_gate, ...), custom_call_target="tpu_custom_call" | custom-call | flops 4529848320 | bytes 20447232 | tf_op jit(solution)/shard_map/hidden_grads/pallas_call | solution.py:118
  178.7 7.1 %returned_b.1 = bf16[1152,1280]{1,0:T(8,128)(2,1)S(1)} custom-call(bf16[1152,768]{1,0:T(8,128)(2,1)S(1)} %get-tuple-element.62.grad_gate.refs_1_, bf16[1152,768]{1,0:T(8,128)(2,1)S(1)} %get-tuple-element.63.grad_up.refs_2_, bf16[2560,768]{1,0:T(8,128)(2,1)S(1)} %bitcast.36, bf16[2560,768]{1,0:T(8,128)(2,1)} %bitcast.41), custom_call_target="tpu_custom_call" | custom-call | flops 4529848320 | bytes 10420224 | tf_op jit(solution)/shard_map/returned_b/pallas_call | solution.py:186
  185.9 1.6 copy-done
  187.6 6.9 %all-to-all-start.2 = ((bf16[16,72,1280]{2,1,0:T(8,128)(2,1)}), bf16[16,72,1280]{2,1,0:T(8,128)(2,1)S(1)}, u32[]{:S(2)}, u32[]{:S(2)}) async-start(bf16[16,72,1280]{2,1,0:T(8,128)(2,1)} %bitcast.28), calls=%async_computation.2 | async-start | bytes 5898240 | tf_op jit(solution)/shard_map/all_to_all | solution.py:391
  194.8 1.5 copy-done.19
  196.3 1.5 copy-done.21
  197.8 1.0 copy-done.36
  198.7 11.9 %returned_a.1 = (bf16[144,1408]{1,0:T(8,128)(2,1)S(1)}, bf16[144,1408]{1,0:T(8,128)(2,1)}, bf16[144,1408]{1,0:T(8,128)(2,1)}, bf16[144,1408]{1,0:T(8,128)(2,1)},...) custom-call(bf16[8,256,144]{2,1,0:T(8,128)(2,1)S(1)} %fusion.refs_0_, ...), custom_call_target="tpu_custom_call" | custom-call | flops 4529848320 | bytes 10420224 | tf_op jit(solution)/shard_map/returned_a/pallas_call | solution.py:165
  211.1 3.2 %collective-permute-start.11 = (bf16[144,1408]{1,0:T(8,128)(2,1)S(1)}, bf16[144,1408]{1,0:T(8,128)(2,1)S(1)}, u32[]{:S(2)}, u32[]{:S(2)}) collective-permute-start(bf16[144,1408]{1,0:T(8,128)(2,1)S(1)} %get-tuple-element.81), channel_id=1, source_target_pairs={{0,5},{1,4},{2,7},{3,6},{4,1},{5,0},{6,3},{7,2},{8,13},{9,12},{10,... | collective-permute-start | bytes 1216520 | tf_op jit(solution)/shard_map/ppermute | solution.py:39
  214.9 1.9 collective-permute-start.13
  218.0 4.4 %collective-permute-done.10.refs_6_ = bf16[144,1408]{1,0:T(8,128)(2,1)S(1)} collective-permute-done((bf16[144,1408]{1,0:T(8,128)(2,1)S(1)}, bf16[144,1408]{1,0:T(8,128)(2,1)S(1)}, u32[]{:S(2)}, u32[]{:S(2)}) %collective-permute-start.10) | collective-permute-done | bytes 405536 | tf_op jit(solution)/shard_map/ppermute | solution.py:39
  223.2 9.8 %collective-permute-done.11.refs_7_ = bf16[144,1408]{1,0:T(8,128)(2,1)S(1)} collective-permute-done((bf16[144,1408]{1,0:T(8,128)(2,1)S(1)}, bf16[144,1408]{1,0:T(8,128)(2,1)S(1)}, u32[]{:S(2)}, u32[]{:S(2)}) %collective-permute-start.11) | collective-permute-done | bytes 405536 | tf_op jit(solution)/shard_map/ppermute | solution.py:39
  234.4 0.9 copy.19
  235.3 0.9 copy.20
  237.0 2.2 all-to-all-done.2
  239.9 0.9 copy-done.7
  240.8 0.9 copy-done.8
  242.5 5.5 %column_sums.1 = (bf16[128,1280]{1,0:T(8,128)(2,1)S(1)}, bf16[128,1280]{1,0:T(8,128)(2,1)}, bf16[128,1280]{1,0:T(8,128)(2,1)}, bf16[128,1280]{1,0:T(8,128)(2,1)S...) custom-call(s32[1]{0:T(128)} %bitcast.1.refs_0_, ...), custom_call_target="tpu_custom_call" | custom-call | flops 3019898880 | bytes 5570560 | tf_op jit(solution)/shard_map/column_sums/pallas_call | solution.py:331
  252.5 1.4 collective-permute-start.14
  254.7 1.0 copy-done.2
  255.7 1.0 copy-done.4
  256.7 5.3 %group_sums.1 = bf16[384,1408]{1,0:T(8,128)(2,1)} custom-call(f32[384,8]{1,0:T(8,128)S(1)} %bitcast.30, f32[384,8]{1,0:T(8,128)S(1)} %bitcast.31, bf16[144,1408]{1,0:T(8,128)(2,1)S(1)} %get-tuple-element.76.refs_2_, bf16[144,1408]{1,0:T(8,128)(2,1)} %collective-permute-done.7.refs_3_, bf16[144,1408]{1,0:T(8,128)(2,1)} %collective-permute-done.8.refs_4_, ...), custom_call_target="tpu_custom_call" | custom-call | flops 1245708288 | bytes 3244032 | tf_op jit(solution)/shard_map/group_sums/pallas_call | solution.py:216
  262.0 5.4 %all-to-all-start.3 = ((bf16[16,24,1408]{2,1,0:T(8,128)(2,1)}), bf16[16,24,1408]{2,1,0:T(8,128)(2,1)S(1)}, u32[]{:S(2)}, u32[]{:S(2)}) async-start(bf16[16,24,1408]{2,1,0:T(8,128)(2,1)} %bitcast.16), calls=%async_computation.3 | async-start | bytes 2162688 | tf_op jit(solution)/shard_map/all_to_all | solution.py:395
  267.5 1.0 collective-permute-start.16
  268.4 1.4 collective-permute-start.17
  269.8 1.7 collective-permute-start.18
  272.1 2.6 collective-permute-start.20
  274.7 3.4 %collective-permute-done.16 = bf16[128,1280]{1,0:T(8,128)(2,1)S(1)} collective-permute-done((bf16[128,1280]{1,0:T(8,128)(2,1)}, bf16[128,1280]{1,0:T(8,128)(2,1)S(1)}, u32[]{:S(2)}, u32[]{:S(2)}) %collective-permute-start.16) | collective-permute-done | bytes 327712 | tf_op jit(solution)/shard_map/ppermute | solution.py:39
  278.1 7.2 %collective-permute-done.17 = bf16[128,1280]{1,0:T(8,128)(2,1)S(1)} collective-permute-done((bf16[128,1280]{1,0:T(8,128)(2,1)}, bf16[128,1280]{1,0:T(8,128)(2,1)S(1)}, u32[]{:S(2)}, u32[]{:S(2)}) %collective-permute-start.17) | collective-permute-done | bytes 327712 | tf_op jit(solution)/shard_map/ppermute | solution.py:39
  285.3 7.0 %collective-permute-done.18 = bf16[128,1280]{1,0:T(8,128)(2,1)S(1)} collective-permute-done((bf16[128,1280]{1,0:T(8,128)(2,1)}, bf16[128,1280]{1,0:T(8,128)(2,1)S(1)}, u32[]{:S(2)}, u32[]{:S(2)}) %collective-permute-start.18) | collective-permute-done | bytes 327712 | tf_op jit(solution)/shard_map/ppermute | solution.py:39
  292.3 3.6 %collective-permute-done.19 = bf16[128,1280]{1,0:T(8,128)(2,1)S(1)} collective-permute-done((bf16[128,1280]{1,0:T(8,128)(2,1)}, bf16[128,1280]{1,0:T(8,128)(2,1)S(1)}, u32[]{:S(2)}, u32[]{:S(2)}) %collective-permute-start.19) | collective-permute-done | bytes 327712 | tf_op jit(solution)/shard_map/ppermute | solution.py:39
  295.9 7.5 %collective-permute-done.20 = bf16[128,1280]{1,0:T(8,128)(2,1)S(1)} collective-permute-done((bf16[128,1280]{1,0:T(8,128)(2,1)}, bf16[128,1280]{1,0:T(8,128)(2,1)S(1)}, u32[]{:S(2)}, u32[]{:S(2)}) %collective-permute-start.20) | collective-permute-done | bytes 327712 | tf_op jit(solution)/shard_map/ppermute | solution.py:39
  303.4 1.4 add_convert_fusion
  305.3 0.9 select_reduce_fusion
  306.2 0.9 pad_maximum_fusion
  (131 shorter events, 22.3 us)
Async XLA Ops:
  7.2 43.8 %all-gather.2.cloned.1.call-start = ((), (), s32[]{:S(2)}) async-start(), calls=%async_computation.4 | async-start | bytes 5898240 | tf_op jit(solution)/shard_map/all_gather | solution.py:362
  10.5 3.4 %copy-start.40 = (f32[16,128]{1,0:T(8,128)}, f32[16,128]{1,0:T(8,128)S(1)}, u32[]{:S(2)}) copy-start(f32[16,128]{1,0:T(8,128)S(1)} %convolution_select_fusion) | copy-start | bytes 24580
  13.9 47.8 %all-to-all-start = ((bf16[16,24,2688]{2,1,0:T(8,128)(2,1)}), bf16[16,24,2688]{2,1,0:T(8,128)(2,1)S(1)}, u32[]{:S(2)}, u32[]{:S(2)}) async-start(bf16[16,24,2688]{2,1,0:T(8,128)(2,1)} %bitcast.37), calls=%async_computation | async-start | bytes 4128768 | tf_op jit(solution)/shard_map/all_to_all | solution.py:372
  39.2 1.4 copy-start.17
  61.6 107.5 %all-to-all-start.1 = ((bf16[16,72,2560]{2,1,0:T(8,128)(2,1)}), bf16[16,72,2560]{2,1,0:T(8,128)(2,1)}, u32[]{:S(2)}, u32[]{:S(2)}) async-start(bf16[16,72,2560]{2,1,0:T(8,128)(2,1)} %bitcast.38), calls=%async_computation.1 | async-start | bytes 11796480 | tf_op jit(solution)/shard_map/all_to_all | solution.py:378
  73.9 0.9 copy-start.37
  74.8 5.5 %collective-permute-start = (bf16[144,2560]{1,0:T(8,128)(2,1)S(1)}, bf16[144,2560]{1,0:T(8,128)(2,1)S(1)}, u32[]{:S(2)}, u32[]{:S(2)}) collective-permute-start(bf16[144,2560]{1,0:T(8,128)(2,1)S(1)} %get-tuple-element.53), channel_id=1, source_target_pairs={{0,1},{1,0},{2,3},{3,2},{4,5},{5,4},{6,7},{7,6},{8,9},{9,8},{10,11... | collective-permute-start | bytes 2211848 | tf_op jit(solution)/shard_map/ppermute | solution.py:39
  75.4 18.2 %collective-permute-start.1 = (bf16[144,2560]{1,0:T(8,128)(2,1)S(1)}, bf16[144,2560]{1,0:T(8,128)(2,1)S(1)}, u32[]{:S(2)}, u32[]{:S(2)}) collective-permute-start(bf16[144,2560]{1,0:T(8,128)(2,1)S(1)} %get-tuple-element.54), channel_id=1, source_target_pairs={{0,2},{1,3},{2,0},{3,1},{4,6},{5,7},{6,4},{7,5},{8,10},{9,11},{10,... | collective-permute-start | bytes 2211848 | tf_op jit(solution)/shard_map/ppermute | solution.py:39
  75.6 34.6 %collective-permute-start.2 = (bf16[144,2560]{1,0:T(8,128)(2,1)}, bf16[144,2560]{1,0:T(8,128)(2,1)S(1)}, u32[]{:S(2)}, u32[]{:S(2)}) collective-permute-start(bf16[144,2560]{1,0:T(8,128)(2,1)} %get-tuple-element.55), channel_id=1, source_target_pairs={{0,3},{1,2},{2,1},{3,0},{4,7},{5,6},{6,5},{7,4},{8,11},{9,10},{10,... | collective-permute-start | bytes 2211848 | tf_op jit(solution)/shard_map/ppermute | solution.py:39
  77.0 48.5 %collective-permute-start.3 = (bf16[144,2560]{1,0:T(8,128)(2,1)}, bf16[144,2560]{1,0:T(8,128)(2,1)S(1)}, u32[]{:S(2)}, u32[]{:S(2)}) collective-permute-start(bf16[144,2560]{1,0:T(8,128)(2,1)} %get-tuple-element.56), channel_id=1, source_target_pairs={{0,4},{1,5},{2,6},{3,7},{4,0},{5,1},{6,2},{7,3},{8,12},{9,13},{10,... | collective-permute-start | bytes 2211848 | tf_op jit(solution)/shard_map/ppermute | solution.py:39
  78.5 63.0 %collective-permute-start.4 = (bf16[144,2560]{1,0:T(8,128)(2,1)}, bf16[144,2560]{1,0:T(8,128)(2,1)}, u32[]{:S(2)}, u32[]{:S(2)}) collective-permute-start(bf16[144,2560]{1,0:T(8,128)(2,1)} %get-tuple-element.57), channel_id=1, source_target_pairs={{0,5},{1,4},{2,7},{3,6},{4,1},{5,0},{6,3},{7,2},{8,13},{9,12},{10,... | collective-permute-start | bytes 2211848 | tf_op jit(solution)/shard_map/ppermute | solution.py:39
  80.4 0.9 copy-start.22
  81.2 60.2 %collective-permute-start.5 = (bf16[144,2560]{1,0:T(8,128)(2,1)}, bf16[144,2560]{1,0:T(8,128)(2,1)}, u32[]{:S(2)}, u32[]{:S(2)}) collective-permute-start(bf16[144,2560]{1,0:T(8,128)(2,1)} %get-tuple-element.58), channel_id=1, source_target_pairs={{0,6},{1,7},{2,4},{3,5},{4,2},{5,3},{6,0},{7,1},{8,14},{9,15},{10,... | collective-permute-start | bytes 2211848 | tf_op jit(solution)/shard_map/ppermute | solution.py:39
  93.6 0.9 copy-start.24
  94.5 53.9 %collective-permute-start.6 = (bf16[144,2560]{1,0:T(8,128)(2,1)S(1)}, bf16[144,2560]{1,0:T(8,128)(2,1)}, u32[]{:S(2)}, u32[]{:S(2)}) collective-permute-start(bf16[144,2560]{1,0:T(8,128)(2,1)S(1)} %get-tuple-element.59), channel_id=1, source_target_pairs={{0,7},{1,6},{2,5},{3,4},{4,3},{5,2},{6,1},{7,0},{8,15},{9,14},{10,... | collective-permute-start | bytes 2211848 | tf_op jit(solution)/shard_map/ppermute | solution.py:39
  110.2 0.9 copy-start.26
  125.5 0.9 copy-start.28
  148.4 1.1 copy-start.23
  149.5 1.1 copy-start.25
  150.6 1.1 copy-start.27
  151.7 1.1 copy-start.29
  152.8 1.1 copy-start.38
  169.1 9.6 %copy-start.16 = (bf16[1,2560,768]{2,1,0:T(8,128)(2,1)S(1)}, bf16[1,2560,768]{2,1,0:T(8,128)(2,1)}, u32[]{:S(2)}) copy-start(bf16[1,2560,768]{2,1,0:T(8,128)(2,1)} %param.11) | copy-start | bytes 11796484
  178.7 7.2 %copy-start.18 = (bf16[1152,768]{1,0:T(8,128)(2,1)}, bf16[1152,768]{1,0:T(8,128)(2,1)S(1)}, u32[]{:S(2)}) copy-start(bf16[1152,768]{1,0:T(8,128)(2,1)S(1)} %get-tuple-element.62.grad_gate.refs_1_) | copy-start | bytes 5308420
  178.7 7.2 %copy-start.20 = (bf16[1152,768]{1,0:T(8,128)(2,1)}, bf16[1152,768]{1,0:T(8,128)(2,1)S(1)}, u32[]{:S(2)}) copy-start(bf16[1152,768]{1,0:T(8,128)(2,1)S(1)} %get-tuple-element.63.grad_up.refs_2_) | copy-start | bytes 5308420
  178.7 7.2 %copy-start.35 = (bf16[1152,128]{1,0:T(8,128)(2,1)}, bf16[1152,128]{1,0:T(8,128)(2,1)S(1)}, u32[]{:S(2)}) copy-start(bf16[1152,128]{1,0:T(8,128)(2,1)S(1)} %get-tuple-element.75.refs_5_) | copy-start | bytes 884740
  185.9 1.7 copy-start
  187.6 51.6 %all-to-all-start.2 = ((bf16[16,72,1280]{2,1,0:T(8,128)(2,1)}), bf16[16,72,1280]{2,1,0:T(8,128)(2,1)S(1)}, u32[]{:S(2)}, u32[]{:S(2)}) async-start(bf16[16,72,1280]{2,1,0:T(8,128)(2,1)} %bitcast.28), calls=%async_computation.2 | async-start | bytes 5898240 | tf_op jit(solution)/shard_map/all_to_all | solution.py:391
  194.8 1.5 copy-start.19
  196.3 1.5 copy-start.21
  197.8 1.0 copy-start.36
  198.7 35.7 %copy-start.12 = (f32[16,1024]{1,0:T(8,128)S(1)}, f32[16,1024]{1,0:T(8,128)}, u32[]{:S(2)}) copy-start(f32[16,1024]{1,0:T(8,128)} %copy-done.11) | copy-start | bytes 196612
  198.7 36.6 %copy-start.10 = (f32[16,1024]{1,0:T(8,128)S(1)}, f32[16,1024]{1,0:T(8,128)}, u32[]{:S(2)}) copy-start(f32[16,1024]{1,0:T(8,128)} %copy-done.9) | copy-start | bytes 196612
  210.6 11.9 %collective-permute-start.10 = (bf16[144,1408]{1,0:T(8,128)(2,1)S(1)}, bf16[144,1408]{1,0:T(8,128)(2,1)S(1)}, u32[]{:S(2)}, u32[]{:S(2)}) collective-permute-start(bf16[144,1408]{1,0:T(8,128)(2,1)S(1)} %get-tuple-element.80), channel_id=1, source_target_pairs={{0,4},{1,5},{2,6},{3,7},{4,0},{5,1},{6,2},{7,3},{8,12},{9,13},{10,... | collective-permute-start | bytes 1216520 | tf_op jit(solution)/shard_map/ppermute | solution.py:39
  211.1 21.9 %collective-permute-start.11 = (bf16[144,1408]{1,0:T(8,128)(2,1)S(1)}, bf16[144,1408]{1,0:T(8,128)(2,1)S(1)}, u32[]{:S(2)}, u32[]{:S(2)}) collective-permute-start(bf16[144,1408]{1,0:T(8,128)(2,1)S(1)} %get-tuple-element.81), channel_id=1, source_target_pairs={{0,5},{1,4},{2,7},{3,6},{4,1},{5,0},{6,3},{7,2},{8,13},{9,12},{10,... | collective-permute-start | bytes 1216520 | tf_op jit(solution)/shard_map/ppermute | solution.py:39
  214.3 38.1 %collective-permute-start.12 = (bf16[144,1408]{1,0:T(8,128)(2,1)}, bf16[144,1408]{1,0:T(8,128)(2,1)}, u32[]{:S(2)}, u32[]{:S(2)}) collective-permute-start(bf16[144,1408]{1,0:T(8,128)(2,1)} %get-tuple-element.82), channel_id=1, source_target_pairs={{0,6},{1,7},{2,4},{3,5},{4,2},{5,3},{6,0},{7,1},{8,14},{9,15},{10,... | collective-permute-start | bytes 1216520 | tf_op jit(solution)/shard_map/ppermute | solution.py:39
  214.9 39.0 %collective-permute-start.13 = (bf16[144,1408]{1,0:T(8,128)(2,1)}, bf16[144,1408]{1,0:T(8,128)(2,1)}, u32[]{:S(2)}, u32[]{:S(2)}) collective-permute-start(bf16[144,1408]{1,0:T(8,128)(2,1)} %get-tuple-element.83), channel_id=1, source_target_pairs={{0,7},{1,6},{2,5},{3,4},{4,3},{5,2},{6,1},{7,0},{8,15},{9,14},{10,... | collective-permute-start | bytes 1216520 | tf_op jit(solution)/shard_map/ppermute | solution.py:39
  217.4 37.3 %collective-permute-start.7 = (bf16[144,1408]{1,0:T(8,128)(2,1)}, bf16[144,1408]{1,0:T(8,128)(2,1)}, u32[]{:S(2)}, u32[]{:S(2)}) collective-permute-start(bf16[144,1408]{1,0:T(8,128)(2,1)} %get-tuple-element.77), channel_id=1, source_target_pairs={{0,1},{1,0},{2,3},{3,2},{4,5},{5,4},{6,7},{7,6},{8,9},{9,8},{10,11... | collective-permute-start | bytes 1216520 | tf_op jit(solution)/shard_map/ppermute | solution.py:39
  222.5 0.8 copy-start.1
  223.2 31.5 %collective-permute-start.8 = (bf16[144,1408]{1,0:T(8,128)(2,1)}, bf16[144,1408]{1,0:T(8,128)(2,1)}, u32[]{:S(2)}, u32[]{:S(2)}) collective-permute-start(bf16[144,1408]{1,0:T(8,128)(2,1)} %get-tuple-element.78), channel_id=1, source_target_pairs={{0,2},{1,3},{2,0},{3,1},{4,6},{5,7},{6,4},{7,5},{8,10},{9,11},{10,... | collective-permute-start | bytes 1216520 | tf_op jit(solution)/shard_map/ppermute | solution.py:39
  233.0 0.8 copy-start.3
  233.8 20.9 %collective-permute-start.9 = (bf16[144,1408]{1,0:T(8,128)(2,1)}, bf16[144,1408]{1,0:T(8,128)(2,1)}, u32[]{:S(2)}, u32[]{:S(2)}) collective-permute-start(bf16[144,1408]{1,0:T(8,128)(2,1)} %get-tuple-element.79), channel_id=1, source_target_pairs={{0,3},{1,2},{2,1},{3,0},{4,7},{5,6},{6,5},{7,4},{8,11},{9,10},{10,... | collective-permute-start | bytes 1216520 | tf_op jit(solution)/shard_map/ppermute | solution.py:39
  239.9 0.9 copy-start.7
  240.8 0.9 copy-start.8
  241.8 0.8 copy-start.13
  248.0 0.7 copy-start.5
  248.8 0.7 copy-start.30
  249.5 0.7 copy-start.31
  250.2 0.7 copy-start.32
  250.9 0.7 copy-start.33
  251.7 0.8 copy-start.34
  252.5 19.0 %collective-permute-start.14 = (bf16[128,1280]{1,0:T(8,128)(2,1)}, bf16[128,1280]{1,0:T(8,128)(2,1)}, u32[]{:S(2)}, u32[]{:S(2)}) collective-permute-start(bf16[128,1280]{1,0:T(8,128)(2,1)} %get-tuple-element.85), channel_id=1, source_target_pairs={{0,1},{1,0},{2,3},{3,2},{4,5},{5,4},{6,7},{7,6},{8,9},{9,8},{10,11... | collective-permute-start | bytes 983048 | tf_op jit(solution)/shard_map/ppermute | solution.py:39
  253.9 18.2 %collective-permute-start.15 = (bf16[128,1280]{1,0:T(8,128)(2,1)}, bf16[128,1280]{1,0:T(8,128)(2,1)}, u32[]{:S(2)}, u32[]{:S(2)}) collective-permute-start(bf16[128,1280]{1,0:T(8,128)(2,1)} %get-tuple-element.86), channel_id=1, source_target_pairs={{0,2},{1,3},{2,0},{3,1},{4,6},{5,7},{6,4},{7,5},{8,10},{9,11},{10,... | collective-permute-start | bytes 983048 | tf_op jit(solution)/shard_map/ppermute | solution.py:39
  254.7 1.0 copy-start.2
  255.7 1.0 copy-start.4
  256.7 46.6 %copy-start.6 = (bf16[128,1280]{1,0:T(8,128)(2,1)S(1)}, bf16[128,1280]{1,0:T(8,128)(2,1)}, u32[]{:S(2)}) copy-start(bf16[128,1280]{1,0:T(8,128)(2,1)} %copy-done.5) | copy-start | bytes 983044
  262.0 42.8 %copy-start.41 = (f32[16,128]{1,0:T(8,128)S(1)}, f32[16,128]{1,0:T(8,128)}, u32[]{:S(2)}) copy-start(f32[16,128]{1,0:T(8,128)} %copy-done.40) | copy-start | bytes 24580
  262.0 42.8 %all-to-all-start.3 = ((bf16[16,24,1408]{2,1,0:T(8,128)(2,1)}), bf16[16,24,1408]{2,1,0:T(8,128)(2,1)S(1)}, u32[]{:S(2)}, u32[]{:S(2)}) async-start(bf16[16,24,1408]{2,1,0:T(8,128)(2,1)} %bitcast.16), calls=%async_computation.3 | async-start | bytes 2162688 | tf_op jit(solution)/shard_map/all_to_all | solution.py:395
  267.4 37.9 %copy-start.39 = (s32[128,6]{0,1:T(8,128)S(1)}, s32[128,6]{0,1:T(8,128)}, u32[]{:S(2)}) copy-start(s32[128,6]{0,1:T(8,128)} %param.9) | copy-start | bytes 9220
  267.5 10.6 %collective-permute-start.16 = (bf16[128,1280]{1,0:T(8,128)(2,1)}, bf16[128,1280]{1,0:T(8,128)(2,1)S(1)}, u32[]{:S(2)}, u32[]{:S(2)}) collective-permute-start(bf16[128,1280]{1,0:T(8,128)(2,1)} %copy-done.34), channel_id=1, source_target_pairs={{0,3},{1,2},{2,1},{3,0},{4,7},{5,6},{6,5},{7,4},{8,11},{9,10},{10,... | collective-permute-start | bytes 983048 | tf_op jit(solution)/shard_map/ppermute | solution.py:39
  268.4 16.8 %collective-permute-start.17 = (bf16[128,1280]{1,0:T(8,128)(2,1)}, bf16[128,1280]{1,0:T(8,128)(2,1)S(1)}, u32[]{:S(2)}, u32[]{:S(2)}) collective-permute-start(bf16[128,1280]{1,0:T(8,128)(2,1)} %copy-done.33), channel_id=1, source_target_pairs={{0,4},{1,5},{2,6},{3,7},{4,0},{5,1},{6,2},{7,3},{8,12},{9,13},{10,... | collective-permute-start | bytes 983048 | tf_op jit(solution)/shard_map/ppermute | solution.py:39
  269.8 22.5 %collective-permute-start.18 = (bf16[128,1280]{1,0:T(8,128)(2,1)}, bf16[128,1280]{1,0:T(8,128)(2,1)S(1)}, u32[]{:S(2)}, u32[]{:S(2)}) collective-permute-start(bf16[128,1280]{1,0:T(8,128)(2,1)} %copy-done.32), channel_id=1, source_target_pairs={{0,5},{1,4},{2,7},{3,6},{4,1},{5,0},{6,3},{7,2},{8,13},{9,12},{10,... | collective-permute-start | bytes 983048 | tf_op jit(solution)/shard_map/ppermute | solution.py:39
  271.5 24.4 %collective-permute-start.19 = (bf16[128,1280]{1,0:T(8,128)(2,1)}, bf16[128,1280]{1,0:T(8,128)(2,1)S(1)}, u32[]{:S(2)}, u32[]{:S(2)}) collective-permute-start(bf16[128,1280]{1,0:T(8,128)(2,1)} %copy-done.31), channel_id=1, source_target_pairs={{0,6},{1,7},{2,4},{3,5},{4,2},{5,3},{6,0},{7,1},{8,14},{9,15},{10,... | collective-permute-start | bytes 983048 | tf_op jit(solution)/shard_map/ppermute | solution.py:39
  272.1 31.3 %collective-permute-start.20 = (bf16[128,1280]{1,0:T(8,128)(2,1)}, bf16[128,1280]{1,0:T(8,128)(2,1)S(1)}, u32[]{:S(2)}, u32[]{:S(2)}) collective-permute-start(bf16[128,1280]{1,0:T(8,128)(2,1)} %copy-done.30), channel_id=1, source_target_pairs={{0,7},{1,6},{2,5},{3,4},{4,3},{5,2},{6,1},{7,0},{8,15},{9,14},{10,... | collective-permute-start | bytes 983048 | tf_op jit(solution)/shard_map/ppermute | solution.py:39
  (4 other events, 2.4 us)
Sparse Core Ops, SparseCore 0:
  9.7 41.2 all-gather.1
where the time goes:
time: 315 us; the launch traced here: 314 us
  waiting for transfers between devices  118 us (37%)
  Pallas kernels  59.5 us (19%)
  starting transfers between devices  50.4 us (16%)
  local copies, waits for them, and re-layouts  37.1 us (12%)
  blocking collectives  14.5 us (5%)
  between operations  14.5 us (5%)
  matrix products  13.2 us (4%)
  other arithmetic  6.32 us (2%)
    ppermute x21, waiting for transfers between devices, exchange(): lax.ppermute(blocks[k], 'exp', [(i, i ^ k) for i in range(n_exp)])  105 us
    unnamed x86, local copies, waits for them, and re-layouts  31.6 us
    ppermute x21, starting transfers between devices, exchange(): lax.ppermute(blocks[k], 'exp', [(i, i ^ k) for i in range(n_exp)])  23 us
    pallas_call x1, Pallas kernels, pre_products(): pl.pallas_call(lambda *refs: pre_kernel(n_exp, pairs, *refs), grid=(units...  15.2 us
    all_gather x1, blocking collectives, per_device(): column_meta = lax.all_gather(meta, 'exp', axis=0, tiled=True)  14.5 us
    dot_general x2, matrix products, dot(): return jnp.dot(a, b, preferred_element_type=F32)  12.7 us
    pallas_call x1, Pallas kernels, returned_a(): pl.pallas_call(lambda *refs: back_a_kernel(n_exp, pairs, *refs), grid=(ha...  11.9 us
    all_gather x1, waiting for transfers between devices, per_device(): column = lax.all_gather(grad_out, 'exp', axis=0, tiled=True)  10.4 us
  transfers between devices with their start and end apart: 26, of which 14 were waited for; matrix products, arithmetic and copies ran while one was open for 8% of the time, Pallas kernels for 14%

commit v1 on v0

v1 whole, which is shorter than its diff:
```python
import jax
import jax.numpy as jnp
from jax import lax
from jax.experimental import pallas as pl
from jax.experimental.pallas import tpu as pltpu
from jax.sharding import PartitionSpec as P

BF = jnp.bfloat16
F32 = jnp.float32
LANES = 128
VMEM_MIB = 60


def dot(a, b):
    return jnp.dot(a, b, preferred_element_type=F32)


def dot_t(a, b):
    return lax.dot_general(a, b, (((0,), (0,)), ((), ())), preferred_element_type=F32)


def dot_nt(a, b):
    return lax.dot_general(a, b, (((1,), (1,)), ((), ())), preferred_element_type=F32)


def earlier_counts(names):
    n = names.shape[-2]
    lower = (jnp.arange(n)[:, None] > jnp.arange(n)[None, :]).astype(BF)
    counts = jnp.einsum("ij,...jm->...im", lower, names.astype(BF), preferred_element_type=F32)
    return jnp.where(names, counts, -1.0)


def barrier(*values):
    return lax.optimization_barrier(values)


def swap(x, k):
    return lax.ppermute(x, "exp", [(i, i ^ k) for i in range(lax.axis_size("exp"))])


def exchange(blocks):
    return [blocks[0]] + [swap(block, 2 * a) for a, block in enumerate(blocks) if a]


def whole(shape, at=(0, 0)):
    return pl.BlockSpec(shape, lambda *_: at, pipeline_mode=pl.Buffered(1))


def params(mib):
    return pltpu.CompilerParams(vmem_limit_bytes=mib * 2**20)


def cost(flops, nbytes):
    return pl.CostEstimate(flops=flops, bytes_accessed=nbytes, transcendentals=0)


def window_tables(n_seq, n_exp, cap):
    pair = 2 * n_exp * cap
    d = jnp.arange(pair)
    source = d % (n_exp * cap) // cap * 32 + d // (n_exp * cap) * cap + d % cap
    i = jnp.arange(n_seq // 2)
    at = source[None, :] + (2 * cap - 16) * i[:, None]
    wide = jnp.arange(32 * n_exp)
    to_b = (at[:, :, None] == wide[None, None, :]).astype(BF)
    to_a = (at[:, None, :] == wide[None, :, None]).astype(BF)
    return to_b, to_a


def pre_kernel(chips, pairs, table, *refs):
    blocks, (gate, up, out_gate, out_up, rows) = refs[:chips], refs[chips:]
    size = table.shape[1]

    @pl.when(pl.program_id(0) == 0)
    def _():
        for i in range(pairs):
            at = [(b, 16 * i + side) for b in blocks for side in (0, b.shape[0] // 2)]
            window = jnp.concatenate([b[start:start + 32, :] for b, start in at], axis=0)
            rows[size * i:size * (i + 1), :] = dot(table[i], window).astype(BF)

    out_gate[...] = dot(rows[...], gate[...])
    out_up[...] = dot(rows[...], up[...])


def pre_products(table, blocks, gate_mat, up_mat):
    chips, pairs = len(blocks), table.shape[0]
    rows, features = blocks[0].shape
    total, units = rows * chips, gate_mat.shape[1]
    wide = 256 if units % 256 == 0 else units
    column = pl.BlockSpec((features, wide), lambda j: (0, j))
    result = pl.BlockSpec((total, wide), lambda j: (0, j))
    return pl.pallas_call(
        lambda *refs: pre_kernel(chips, pairs, *refs),
        grid=(units // wide,),
        in_specs=[whole(table.shape, (0, 0, 0))] + [whole((rows, features))] * chips + [column, column],
        out_specs=[result, result],
        out_shape=[jax.ShapeDtypeStruct((total, units), F32)] * 2,
        scratch_shapes=[pltpu.VMEM((total, features), BF)],
        compiler_params=params(VMEM_MIB),
        cost_estimate=cost(40 * total * features * units, 2 * total * features + 4 * features * units + 8 * total * units),
        name="pre_products",
    )(table, *blocks, gate_mat, up_mat)


def grad_kernel(lane, grad, down, pre_gate, pre_up, out_gate, out_up, out_dot):
    grad_hidden = dot_nt(grad[...], down[...])
    gate, up = pre_gate[...], pre_up[...]
    sigmoid = jax.nn.sigmoid(gate)
    active = gate * sigmoid
    hidden = (active * up).astype(BF).astype(F32)
    gate_dot = jnp.sum(hidden * grad_hidden, axis=1, keepdims=True)
    out_dot[...] = (gate_dot * lane[0:1, :]).astype(BF)
    out_gate[...] = (grad_hidden * up * sigmoid * (1.0 + gate * (1.0 - sigmoid))).astype(BF)
    out_up[...] = (grad_hidden * active).astype(BF)


def hidden_grads(lane, rows_grad, down_mat, pre_gate, pre_up):
    total, features = rows_grad.shape
    units = down_mat.shape[0]
    tall = total // 4
    row = lambda width: pl.BlockSpec((tall, width), lambda i: (i, 0))
    return pl.pallas_call(
        grad_kernel,
        grid=(4,),
        in_specs=[whole(lane.shape), row(features), whole(down_mat.shape), row(units), row(units)],
        out_specs=[row(units), row(units), row(LANES)],
        out_shape=[jax.ShapeDtypeStruct((total, units), BF)] * 2 + [jax.ShapeDtypeStruct((total, LANES), BF)],
        compiler_params=params(VMEM_MIB),
        cost_estimate=cost(2 * total * features * units, 2 * total * features + 2 * features * units + 12 * total * units),
        name="hidden_grads",
    )(lane, rows_grad, down_mat, pre_gate, pre_up)


def back_a_kernel(n_exp, pairs, table, grad_gate, grad_up, gate, up, gate_dot, *outs):
    wide = gate.shape[0]
    rows, half = outs[0].shape[0] // 2, outs[0].shape[1] - LANES
    size = table.shape[2]

    def reorder(values, start, width):
        before = None
        for i in range(pairs):
            moved = dot(table[i], values[size * i:size * (i + 1), :])
            for k in range(n_exp):
                part = moved[32 * k:32 * k + 16, :]
                if before is not None:
                    part = part + before[32 * k + 16:32 * k + 32, :]
                outs[k // 2][k % 2 * rows + 16 * i:k % 2 * rows + 16 * i + 16, pl.ds(start, width)] = part.astype(BF)
            before = moved
        for k in range(n_exp):
            part = before[32 * k + 16:32 * k + 32, :]
            outs[k // 2][k % 2 * rows + 16 * pairs:k % 2 * rows + 16 * pairs + 16, pl.ds(start, width)] = part.astype(BF)

    j = pl.program_id(0)
    values = dot_nt(grad_gate[...], gate[...]) + dot_nt(grad_up[...], up[...])
    reorder(values.astype(BF), pl.multiple_of(j * wide, wide), wide)

    @pl.when(j == 0)
    def _():
        reorder(gate_dot[...], half, LANES)


def returned_a(table, grad_gate, grad_up, gate_mat, up_mat, gate_dot, n_exp):
    total, units = grad_gate.shape
    half = gate_mat.shape[0] // 2
    pairs = table.shape[0]
    wide = 256 if half % 256 == 0 else half
    mat = pl.BlockSpec((wide, units), lambda j: (j, 0))
    block = (2 * total // n_exp, half + LANES)
    return pl.pallas_call(
        lambda *refs: back_a_kernel(n_exp, pairs, *refs),
        grid=(half // wide,),
        in_specs=[whole(table.shape, (0, 0, 0)), whole(grad_gate.shape), whole(grad_up.shape), mat, mat, whole(gate_dot.shape)],
        out_specs=[whole(block)] * (n_exp // 2),
        out_shape=[jax.ShapeDtypeStruct(block, BF)] * (n_exp // 2),
        compiler_params=params(VMEM_MIB),
        cost_estimate=cost(4 * total * half * units, 4 * half * units + 4 * total * units + 2 * total * half),
        name="returned_a",
    )(table, grad_gate, grad_up, gate_mat, up_mat, gate_dot)


def back_b_kernel(grad_gate, grad_up, gate, up, out):
    out[...] = (dot_nt(grad_gate[...], gate[...]) + dot_nt(grad_up[...], up[...])).astype(BF)


def returned_b(grad_gate, grad_up, gate_mat, up_mat):
    total, units = grad_gate.shape
    half = gate_mat.shape[0] // 2
    wide = 256 if half % 256 == 0 else half
    mat = pl.BlockSpec((wide, units), lambda j: (half // wide + j, 0))
    return pl.pallas_call(
        back_b_kernel,
        grid=(half // wide,),
        in_specs=[whole(grad_gate.shape), whole(grad_up.shape), mat, mat],
        out_specs=pl.BlockSpec((total, wide), lambda j: (0, j)),
        out_shape=jax.ShapeDtypeStruct((total, half), BF),
        compiler_params=params(VMEM_MIB),
        cost_estimate=cost(4 * total * half * units, 4 * half * units + 4 * total * units + 2 * total * half),
        name="returned_b",
    )(grad_gate, grad_up, gate_mat, up_mat)


def sum_kernel(chips, slot, weight, *refs):
    blocks, outs = refs[:chips], refs[chips:]
    half = outs[0].shape[1] - LANES
    rows = blocks[0].shape[0] // 2
    place = lax.broadcasted_iota(jnp.int32, (slot.shape[1], rows), 1).astype(F32)
    for side, out in enumerate(outs):
        sums = jnp.zeros((slot.shape[1], half), F32)
        gates = jnp.zeros((slot.shape[1], LANES), F32)
        for a in range(chips):
            hot = slot[side, :, 2 * a:2 * a + 1] == place
            block = blocks[a][rows * side:rows * (side + 1), :]
            sums += dot(jnp.where(hot, weight[side, :, 2 * a:2 * a + 1], 0.0).astype(BF), block[:, :half])
            gates += dot(jnp.where(hot, 1.0, 0.0).astype(BF), block[:, half:])
        out[:, :half] = sums.astype(out.dtype)
        out[:, half:] = gates.astype(out.dtype)


def group_sums(slot, weight, blocks):
    chips = len(blocks)
    shape = (slot.shape[1], blocks[0].shape[1])
    return pl.pallas_call(
        lambda *refs: sum_kernel(chips, *refs),
        grid=(1,),
        in_specs=[whole(slot.shape, (0, 0, 0)), whole(weight.shape, (0, 0, 0))] + [whole(blocks[0].shape)] * chips,
        out_specs=[whole(shape)] * 2,
        out_shape=[jax.ShapeDtypeStruct(shape, F32), jax.ShapeDtypeStruct(shape, BF)],
        compiler_params=params(VMEM_MIB),
        cost_estimate=cost(2 * shape[0] * blocks[0].size * chips, 2 * chips * blocks[0].size),
        name="group_sums",
    )(slot, weight, *blocks)


def named_here(top, eye, meta, local):
    flat = dot_nt(eye[...], meta)
    named = weight = jnp.zeros((local.shape[0], flat.shape[1]), F32)
    for k in range(top):
        hit = flat[k:k + 1, :] == local[:, 0:1]
        named += jnp.where(hit, 1.0, 0.0)
        weight += jnp.where(hit, flat[top + k:top + k + 1, :], 0.0)
    return named, weight


def hub_kernel(top, cap, eye, local, before, block, hub, other, *outs):
    *blocks, out_slot, out_weight = outs
    rows, features = blocks[0].shape[0] // 2, blocks[0].shape[1]
    for side, ref in enumerate((hub, other)):
        named, weight = named_here(top, eye, ref[:, features:], local)
        slot = jnp.where(named > 0.0, block[0:1, :] * cap + dot(named.astype(BF), before[...]), -1.0)
        out_slot[side], out_weight[side] = slot, weight
        place = lax.broadcasted_iota(jnp.int32, (rows, slot.shape[1]), 0).astype(F32)
        for a, out in enumerate(blocks):
            hot = jnp.where(place == slot[2 * a:2 * a + 1, :], 1.0, 0.0).astype(BF)
            out[rows * side:rows * (side + 1), :] = dot(hot, ref[:, :features]).astype(BF)


def lower_counts(total, size):
    at = jnp.arange(total)
    same = at[:, None] // size == at[None, :] // size
    return (same & (at[:, None] < at[None, :])).astype(BF), jnp.broadcast_to((at // size).astype(F32), (8, total))


def hub_blocks(hub, other, local, per_group, top, cap):
    n_rows, width = hub.shape
    n_exp = local.shape[0]
    before, block = lower_counts(n_rows, per_group)
    shape = (2 * (n_rows // per_group) * cap, width - LANES)
    pair = (2, n_exp, n_rows)
    eye = jnp.eye(LANES, dtype=BF)
    *blocks, slot, weight = pl.pallas_call(
        lambda *refs: hub_kernel(top, cap, *refs),
        grid=(1,),
        in_specs=[whole(x.shape) for x in (eye, local, before, block, hub, other)],
        out_specs=[whole(shape)] * (n_exp // 2) + [whole(pair, (0, 0, 0))] * 2,
        out_shape=[jax.ShapeDtypeStruct(shape, BF)] * (n_exp // 2) + [jax.ShapeDtypeStruct(pair, F32)] * 2,
        compiler_params=params(VMEM_MIB),
        cost_estimate=cost(shape[0] * n_exp * n_rows * width, n_exp * shape[0] * shape[1]),
        name="hub_blocks",
    )(eye, local, before, block, hub, other)
    return blocks, slot.transpose(0, 2, 1), weight.transpose(0, 2, 1)


def slots_kernel(top, n_exp, cap, member, eye, theirs, before, start, spread, place, meta, out_hot, out_slot, out_weight):
    n_tok = before.shape[0]
    parts = [meta[pl.ds(pl.multiple_of((member[0] ^ k) * n_tok, n_tok), n_tok), :] for k in range(n_exp)]
    named, out_weight[...] = named_here(top, eye, jnp.concatenate(parts, axis=0), theirs)
    counts = [dot(named[:, at:at + n_tok].astype(BF), before[...]) for at in range(0, named.shape[1], n_tok)]
    rank = jnp.concatenate(counts, axis=1)
    out_slot[...] = jnp.where(named > 0.0, start[0:1, :] + rank, -1.0)
    rank = jnp.where(named > 0.0, rank, -1.0).astype(BF)
    size = spread.shape[0]
    for k in range(n_exp):
        hot = dot(spread[...], rank[:, n_tok * k:n_tok * (k + 1)]) == place[:, 0:1]
        out_hot[size * k:size * (k + 1), :] = jnp.where(hot, 1.0, 0.0).astype(BF)


def column_slots(meta, theirs, member, n_tok, top, cap):
    total = meta.shape[0]
    n_seq, n_exp = theirs.shape[0], total // n_tok
    before, block = lower_counts(n_tok, n_tok)
    start = jnp.broadcast_to((jnp.arange(total) // n_tok * cap).astype(F32), (8, total))
    at = jnp.arange(n_seq * cap)
    spread = (at[:, None] // cap == jnp.arange(n_seq)[None, :]).astype(BF)
    place = jnp.broadcast_to((at % cap).astype(F32)[:, None], (n_seq * cap, LANES))
    eye = jnp.eye(LANES, dtype=BF)
    shapes = (n_seq * n_exp * cap, n_tok), (n_seq, total), (n_seq, total)
    inputs = (eye, theirs, before, start, spread, place, meta)
    hot, slot, weight = pl.pallas_call(
        lambda *refs: slots_kernel(top, n_exp, cap, *refs),
        grid=(1,),
        in_specs=[pl.BlockSpec(memory_space=pltpu.SMEM)] + [whole(x.shape) for x in inputs],
        out_specs=[whole(shape) for shape in shapes],
        out_shape=[jax.ShapeDtypeStruct(shape, kind) for shape, kind in zip(shapes, (BF, F32, F32))],
        compiler_params=params(VMEM_MIB),
        cost_estimate=cost(4 * total * LANES * LANES, 2 * shapes[0][0] * n_tok),
        name="column_slots",
    )(member.reshape(1), *inputs)
    return hot, slot.T, weight.T


def rows_kernel(n_exp, member, table, hot, column, out):
    pairs, size = table.shape[:2]
    n_tok = hot.shape[1]
    blocks = []
    for k in range(n_exp):
        rows = pl.ds(pl.multiple_of((member[0] ^ k) * n_tok, n_tok), n_tok)
        blocks.append(dot(hot[size * k:size * (k + 1), :], column[rows, :]).astype(BF))
    for i in range(pairs):
        window = jnp.concatenate([b[16 * i:16 * i + 32, :] for b in blocks], axis=0)
        out[size * i:size * (i + 1), :] = dot(table[i], window).astype(BF)


def column_rows(member, table, hot, column, n_exp):
    total, features = hot.shape[0], column.shape[1]
    wide = 512 if features % 512 == 0 else features
    return pl.pallas_call(
        lambda *refs: rows_kernel(n_exp, *refs),
        grid=(features // wide,),
        in_specs=[pl.BlockSpec(memory_space=pltpu.SMEM), whole(table.shape, (0, 0, 0)), whole(hot.shape),
                  pl.BlockSpec((column.shape[0], wide), lambda j: (0, j))],
        out_specs=pl.BlockSpec((total, wide), lambda j: (0, j)),
        out_shape=jax.ShapeDtypeStruct((total, features), BF),
        compiler_params=params(VMEM_MIB),
        cost_estimate=cost(2 * total * (hot.shape[1] + table.shape[2]) * features, 2 * column.size + 2 * total * features),
        name="column_rows",
    )(member.reshape(1), table, hot, column)


def column_kernel(n_exp, place, spread, slot, weight, got, out_mine, out_other, mixed):
    n_tok = out_mine.shape[0] // (n_exp // 2)
    mixed[...] = jnp.where(dot(slot[...], spread[...]) == place[0:1, :], dot(weight[...], spread[...]), 0.0).astype(BF)
    half = got.shape[1]
    wide = 256 if half % 256 == 0 else half
    for start in range(0, half, wide):
        sums = dot(mixed[...], got[:, start:start + wide])
        for k in range(0, n_exp, 2):
            at = slice(n_tok * k // 2, n_tok * (k // 2 + 1))
            out_mine[at, start:start + wide] = sums[n_tok * k:n_tok * (k + 1), :]
            out_other[at, start:start + wide] = sums[n_tok * (k + 1):n_tok * (k + 2), :].astype(BF)


def column_sums(slot, weight, got, n_exp):
    n_rows, n_seq = slot.shape
    total, half = got.shape
    at = jnp.arange(total)
    place = jnp.broadcast_to((at % (total // n_seq)).astype(F32), (8, total))
    spread = (jnp.arange(n_seq)[:, None] == at[None, :] // (total // n_seq)).astype(BF)
    shape = (n_rows // 2, half)
    return pl.pallas_call(
        lambda *refs: column_kernel(n_exp, *refs),
        grid=(1,),
        in_specs=[whole(place.shape), whole(spread.shape), whole(slot.shape), whole(weight.shape), whole(got.shape)],
        out_specs=[whole(shape)] * 2,
        out_shape=[jax.ShapeDtypeStruct(shape, F32), jax.ShapeDtypeStruct(shape, BF)],
        scratch_shapes=[pltpu.VMEM((n_rows, total), BF)],
        compiler_params=params(VMEM_MIB),
        cost_estimate=cost(40 * n_rows * total * half, 2 * total * half + 3 * n_rows * half),
        name="column_sums",
    )(place, spread, slot.astype(BF), weight.astype(BF), got)


def per_device(hidden_in, grad_out, expert_ids, gate_weights, w_gate, w_up, w_down):
    n_tok, features = hidden_in.shape
    top = expert_ids.shape[1]
    n_seq, n_exp = lax.axis_size("seq"), lax.axis_size("exp")
    group, member = lax.axis_index("seq"), lax.axis_index("exp")
    experts = n_seq * n_exp
    cap = 3 * top * n_tok // (2 * experts)
    per_group = top // 2 * n_tok // n_seq
    half = features // 2
    gate_mat, up_mat, down_mat = w_gate[0], w_up[0], w_down[0]
    partner = member ^ jnp.arange(n_exp)
    to_b, to_a = window_tables(n_seq, n_exp, cap)

    meta = jnp.concatenate(
        (expert_ids.astype(BF), gate_weights.astype(BF), jnp.zeros((n_tok, LANES - 2 * top), BF)), axis=1)

    column_meta = lax.all_gather(meta, "exp", axis=0, tiled=True)
    column = lax.all_gather(grad_out, "exp", axis=0, tiled=True)
    theirs = jnp.broadcast_to((jnp.arange(n_seq) * n_exp + member).astype(F32)[:, None], (n_seq, LANES))
    put_b, slot_b, weight_b = column_slots(column_meta, theirs, member, n_tok, top, cap)

    group_ids = expert_ids // n_exp
    in_group = jnp.any(group_ids[:, :, None] == jnp.arange(n_seq)[None, None, :], axis=1)
    group_rank = earlier_counts(in_group).T
    pick = (group_rank[:, None, :] == jnp.arange(per_group, dtype=F32)[None, :, None])
    pick = pick.astype(BF).reshape(n_seq * per_group, n_tok)
    send = dot(pick, jnp.concatenate((hidden_in, meta), axis=1)).astype(BF)
    hub = lax.all_to_all(send.reshape(n_seq, per_group, features + LANES), "seq", 0, 0, tiled=True)
    hub = hub.reshape(n_seq * per_group, features + LANES)

    send_b = column_rows(member, to_b, put_b, column, n_exp)
    rows_b = n_exp * cap
    recv_b = lax.all_to_all(send_b.reshape(n_seq, rows_b, features), "seq", 0, 0, tiled=True)
    recv_b = recv_b.reshape(n_seq * rows_b, features)

    local = jnp.broadcast_to((partner + group * n_exp).astype(F32)[:, None], (n_exp, LANES))
    blocks, slot_a, weight_a = hub_blocks(hub, swap(hub, 1), local, per_group, top, cap)
    rows_in = exchange(blocks)

    pre_gate, pre_up = pre_products(to_b, rows_in, gate_mat, up_mat)
    lane = jnp.broadcast_to((jnp.arange(LANES) == group * n_exp + member).astype(F32), (8, LANES))
    grad_gate, grad_up, gate_dot = hidden_grads(lane, recv_b, down_mat, pre_gate, pre_up)

    back_a = returned_a(to_a, grad_gate, grad_up, gate_mat, up_mat, gate_dot, n_exp)
    got_a = exchange(back_a)
    back_b = returned_b(grad_gate, grad_up, gate_mat, up_mat)
    got_b = lax.all_to_all(back_b.reshape(n_seq, rows_b, half), "seq", 0, 0, tiled=True)
    got_b, *_ = barrier(got_b, *back_a)
    mine, other = column_sums(slot_b, weight_b, got_b.reshape(n_seq * rows_b, half), n_exp)
    other, slot_a = barrier(other, slot_a)
    chip = (mine + swap(other, 1).astype(F32)).astype(BF).reshape(n_exp // 2, n_tok, half)
    final_b = sum(p.astype(F32) for p in exchange(list(chip)))
    mine, other = group_sums(slot_a, weight_a, got_a)
    back = (mine + swap(other, 1).astype(F32)).astype(BF)
    back = lax.all_to_all(back.reshape(n_seq, per_group, half + LANES), "seq", 0, 0, tiled=True)
    final_a = dot_t(pick, back.reshape(n_seq * per_group, half + LANES))

    grad_in = jnp.concatenate((final_a[:, :half], final_b), axis=1).astype(BF)
    table = final_a[:, half:]
    chosen = expert_ids[:, :, None] == jnp.arange(experts)[None, None, :]
    grad_gates = jnp.sum(jnp.where(chosen, table[:, None, :experts], 0.0), axis=2).astype(BF)
    return grad_in, grad_gates


def solution(mesh):
    rows, mats = P(("seq", "exp"), None), P(("seq", "exp"), None, None)
    return jax.shard_map(
        per_device, mesh=mesh, in_specs=(rows,) * 4 + (mats,) * 3, out_specs=(rows, rows), check_vma=False
    )
```

time: 315 us -> 322 us (1.022)
  blocking collectives: 14.5 us -> 49.8 us
  Pallas kernels: 59.5 us -> 84.9 us
  local copies, waits for them, and re-layouts: 37.1 us -> 12.2 us
  starting transfers between devices: 50.4 us -> 34.9 us
  matrix products: 13.2 us -> 1.25 us
  waiting for transfers between devices: 118 us -> 110 us
  other arithmetic: 6.32 us -> 13.8 us
    ppermute x21 -> x12, waiting for transfers between devices: 105 us -> 68.8 us  [swap(): lax.ppermute(x, 'exp', [(i, i ^ k) for i in range(lax.axis_size('exp'))])]
    all_to_all x0 -> x1, blocking collectives: none -> 35.4 us  [per_device(): lax.all_to_all(send.reshape(n_seq, per_group, features + LANES), 'seq', 0...]
    unnamed x86 -> x22, local copies, waits for them, and re-layouts: 31.6 us -> 2.77 us
    all_to_all x1, waiting for transfers between devices: 0.01 us -> 24.1 us  [per_device(): lax.all_to_all(send_b.reshape(n_seq, rows_b, features), 'seq', 0, 0, tile...]
    all_to_all x1, waiting for transfers between devices: 2.19 us -> 16.5 us  [per_device(): lax.all_to_all(back_b.reshape(n_seq, rows_b, half), 'seq', 0, 0, tiled=True)]
    pallas_call x3 -> x4, Pallas kernels: 21.3 us -> 33.5 us  [the longest x1 16.7 us: pre_products(): pl.pallas_call(lambda *refs: pre_kernel(chips, pairs, *refs), grid=(units...]
    dot_general x2 -> x1, matrix products: 12.7 us -> 0.69 us  [dot(): return jnp.dot(a, b, preferred_element_type=F32)]
    all_gather x1, waiting for transfers between devices: 10.4 us -> 0.01 us  [per_device(): column = lax.all_gather(grad_out, 'exp', axis=0, tiled=True)]
  transfers between devices with their start and end apart: 26 -> 16, of which waited for: 14 -> 9; matrix products, arithmetic and copies ran while one was open for 8% -> 7% of each run, Pallas kernels for 14% -> 18%
where the time goes in v1:
time: 322 us; the launch traced here: 321 us
  waiting for transfers between devices  110 us (34%)
  Pallas kernels  84.9 us (26%)
  blocking collectives  49.8 us (15%)
  starting transfers between devices  34.9 us (11%)
  between operations  14.3 us (4%)
  other arithmetic  13.8 us (4%)
  local copies, waits for them, and re-layouts  12.2 us (4%)
    ppermute x12, waiting for transfers between devices, swap(): lax.ppermute(x, 'exp', [(i, i ^ k) for i in range(lax.axis_size('exp'))])  68.8 us
    all_to_all x1, blocking collectives, per_device(): lax.all_to_all(send.reshape(n_seq, per_group, features + LANES), 'seq', 0...  35.4 us
    all_to_all x1, waiting for transfers between devices, per_device(): lax.all_to_all(send_b.reshape(n_seq, rows_b, features), 'seq', 0, 0, tile...  24.1 us
    ppermute x12, starting transfers between devices, swap(): lax.ppermute(x, 'exp', [(i, i ^ k) for i in range(lax.axis_size('exp'))])  18 us
    pallas_call x1, Pallas kernels, pre_products(): pl.pallas_call(lambda *refs: pre_kernel(chips, pairs, *refs), grid=(units...  16.7 us
    all_to_all x1, waiting for transfers between devices, per_device(): lax.all_to_all(back_b.reshape(n_seq, rows_b, half), 'seq', 0, 0, tiled=True)  16.5 us
    all_gather x1, blocking collectives, per_device(): column_meta = lax.all_gather(meta, 'exp', axis=0, tiled=True)  14.4 us
    pallas_call x1, Pallas kernels, returned_a(): pl.pallas_call(lambda *refs: back_a_kernel(n_exp, pairs, *refs), grid=(ha...  13.8 us
  transfers between devices with their start and end apart: 16, of which 9 were waited for; matrix products, arithmetic and copies ran while one was open for 7% of the time, Pallas kernels for 18%

profile of v1, /device:TPU:1, one launch (start us, length us, event | category | flops | bytes accessed | tf_op | source)
XLA Modules:
  0.0 321.2 jit_solution(13308517975332742940)
XLA Ops:
  7.2 0.7 all-gather.2.cloned.1.call-update
  7.9 0.8 copy.17
  8.7 0.8 copy.18
  9.6 0.7 add_select_fusion.3
  10.6 1.2 concatenate.12
  11.8 0.7 convolution_convert_fusion
  12.5 35.4 %all_to_all.20 = bf16[16,24,2688]{2,1,0:T(8,128)(2,1)S(1)} all-to-all(bf16[16,24,2688]{2,1,0:T(8,128)(2,1)S(1)} %bitcast.26), channel_id=1, replica_groups=mesh['seq'=16,'exp'=8] {'seq'}, dimensions={0} | all-to-all | bytes 4128768 | tf_op jit(solution)/shard_map/all_to_all | solution.py:408
  47.9 1.8 collective-permute-start
  49.8 0.6 fusion.7.refs_1_.refs_0_
  50.6 14.4 %all_gather.6.refs_7_ = bf16[1024,128]{1,0:T(8,128)(2,1)} all-gather(bf16[128,128]{1,0:T(8,128)(2,1)S(1)} %pad_maximum_fusion.1), channel_id=1, replica_groups=mesh['seq'=16,'exp'=8] {'exp'}, dimensions={0}, use_global_device_ids=true | all-gather | bytes 294912 | tf_op jit(solution)/shard_map/all_gather | solution.py:397
  65.0 0.8 fusion.3.refs_2_
  65.8 0.7 broadcast_in_dim.35.refs_1_
  66.5 0.6 broadcast_in_dim.36.refs_3_
  67.1 7.5 %hub_blocks.1 = (bf16[288,2560]{1,0:T(8,128)(2,1)}, bf16[288,2560]{1,0:T(8,128)(2,1)}, bf16[288,2560]{1,0:T(8,128)(2,1)}, bf16[288,2560]{1,0:T(8,128)(2,1)}, f32[2,8,384]{2,1,0:T(8,128)}, /*index=5*/f32[2,8,384]{2,1,0:T(8,128)}) custom-call(bf16[128,128]{1,0:T(8,128)(2,1)} %fusion.7.refs_1_.refs_0_, f32[8,128]{1,0:T(8,128)} %broadcast_in_dim.35.refs_1_, ...), custom_call_target="tpu_custom_call" | custom-call | flops 2378170368 | bytes 5898240 | tf_op jit(solution)/shard_map/hub_blocks/pallas_call | solution.py:269
  74.6 1.0 collective-permute-start.1
  75.6 2.4 collective-permute-start.2
  78.0 0.4 collective-permute-start.3
  78.4 0.7 fusion.9.refs_3_
  79.1 0.7 fusion.6.refs_5_
  79.8 0.7 broadcast_in_dim.30.refs_2_
  80.5 0.7 broadcast_in_dim.32.refs_6_
  81.2 0.6 broadcast_in_dim.31.refs_4_
  81.8 2.4 column_slots.1
  84.3 1.0 fusion.1.refs_1_.refs_0_
  85.4 8.6 %column_rows.1 = bf16[1152,2560]{1,0:T(8,128)(2,1)} custom-call(s32[1]{0:T(128)} %bitcast.1.refs_0_, bf16[8,144,256]{2,1,0:T(8,128)(2,1)} %fusion.1.refs_1_.refs_0_, bf16[1152,128]{1,0:T(8,128)(2,1)} %get-tuple-element.29.refs_2_, bf16[1024,2560]{1,0:T(8,128)(2,1)} %all-gather.2.cloned.1.call-done.refs_3_), custom_call_target="tpu_custom_call" | custom-call | flops 2264924160 | bytes 11141120 | tf_op jit(solution)/shard_map/column_rows/pallas_call | solution.py:335
  93.9 4.8 %all-to-all-start = ((bf16[16,72,2560]{2,1,0:T(8,128)(2,1)}), bf16[16,72,2560]{2,1,0:T(8,128)(2,1)}, u32[]{:S(2)}, u32[]{:S(2)}) async-start(bf16[16,72,2560]{2,1,0:T(8,128)(2,1)} %bitcast.25), calls=%async_computation | async-start | bytes 11796480 | tf_op jit(solution)/shard_map/all_to_all | solution.py:413
  98.7 9.9 %collective-permute-done.1.refs_2_ = bf16[288,2560]{1,0:T(8,128)(2,1)S(1)} collective-permute-done((bf16[288,2560]{1,0:T(8,128)(2,1)}, bf16[288,2560]{1,0:T(8,128)(2,1)S(1)}, u32[]{:S(2)}, u32[]{:S(2)}) %collective-permute-start.1) | collective-permute-done | bytes 1474592 | tf_op jit(solution)/shard_map/ppermute | solution.py:38
  108.6 33.6 %collective-permute-done.2.refs_3_ = bf16[288,2560]{1,0:T(8,128)(2,1)} collective-permute-done((bf16[288,2560]{1,0:T(8,128)(2,1)}, bf16[288,2560]{1,0:T(8,128)(2,1)}, u32[]{:S(2)}, u32[]{:S(2)}) %collective-permute-start.2) | collective-permute-done | bytes 1474592 | tf_op jit(solution)/shard_map/ppermute | solution.py:38
  142.2 2.0 collective-permute-done.3.refs_4_
  144.2 16.7 %pre_products.1 = (f32[1152,768]{1,0:T(8,128)}, f32[1152,768]{1,0:T(8,128)}) custom-call(bf16[8,144,256]{2,1,0:T(8,128)(2,1)} %fusion.1.refs_1_.refs_0_, bf16[288,2560]{1,0:T(8,128)(2,1)} %get-tuple-element.30.refs_1_, bf16[288,2560]{1,0:T(8,128)(2,1)} %copy-done.9, bf16[288,2560]{1,0:T(8,128)(2,1)} %collective-permute-done.2.refs_3_, ...), custom_call_target="tpu_custom_call" | custom-call | flops 90596966400 | bytes 20840448 | tf_op jit(solution)/shard_map/pre_products/pallas_call | solution.py:91
  160.9 24.1 %all-to-all-done = bf16[16,72,2560]{2,1,0:T(8,128)(2,1)} async-done(((bf16[16,72,2560]{2,1,0:T(8,128)(2,1)}), bf16[16,72,2560]{2,1,0:T(8,128)(2,1)}, u32[]{:S(2)}, u32[]{:S(2)}) %all-to-all-start) | async-done | bytes 5898272 | tf_op jit(solution)/shard_map/all_to_all | solution.py:413
  185.1 0.6 broadcast_in_dim.34.lane
  185.7 11.4 %hidden_grads.1 = (bf16[1152,768]{1,0:T(8,128)(2,1)}, bf16[1152,768]{1,0:T(8,128)(2,1)}, bf16[1152,128]{1,0:T(8,128)(2,1)}) custom-call(f32[8,128]{1,0:T(8,128)} %broadcast_in_dim.34.lane, bf16[1152,2560]{1,0:T(8,128)(2,1)} %bitcast.5.grad, bf16[768,2560]{1,0:T(8,128)(2,1)} %bitcast.27, f32[1152,768]{1,0:T(8,128)} %get-tuple-element.34.pre_gate, ...), custom_call_target="tpu_custom_call" | custom-call | flops 4529848320 | bytes 20447232 | tf_op jit(solution)/shard_map/hidden_grads/pallas_call | solution.py:121
  197.1 9.2 %returned_b.1 = bf16[1152,1280]{1,0:T(8,128)(2,1)} custom-call(bf16[1152,768]{1,0:T(8,128)(2,1)} %get-tuple-element.36.grad_gate.refs_1_, bf16[1152,768]{1,0:T(8,128)(2,1)} %get-tuple-element.37.grad_up.refs_2_, bf16[2560,768]{1,0:T(8,128)(2,1)} %bitcast.37, bf16[2560,768]{1,0:T(8,128)(2,1)} %bitcast.40), custom_call_target="tpu_custom_call" | custom-call | flops 4529848320 | bytes 10420224 | tf_op jit(solution)/shard_map/returned_b/pallas_call | solution.py:189
  206.3 5.4 %all-to-all-start.2 = ((bf16[16,72,1280]{2,1,0:T(8,128)(2,1)}), bf16[16,72,1280]{2,1,0:T(8,128)(2,1)S(1)}, u32[]{:S(2)}, u32[]{:S(2)}) async-start(bf16[16,72,1280]{2,1,0:T(8,128)(2,1)} %bitcast.29), calls=%async_computation.2 | async-start | bytes 5898240 | tf_op jit(solution)/shard_map/all_to_all | solution.py:427
  211.8 0.8 copy.19
  212.6 0.9 copy.20
  213.5 1.3 fusion.refs_0_
  214.8 0.6 fusion.5.refs_1_
  215.4 0.9 copy.21
  216.4 0.9 copy.22
  217.3 13.8 %returned_a.1 = (bf16[288,1408]{1,0:T(8,128)(2,1)}, bf16[288,1408]{1,0:T(8,128)(2,1)}, bf16[288,1408]{1,0:T(8,128)(2,1)}, bf16[288,1408]{1,0:T(8,128)(2,1)}) custom-call(bf16[8,256,144]{2,1,0:T(8,128)(2,1)} %fusion.refs_0_, bf16[1152,768]{1,0:T(8,128)(2,1)} %get-tuple-element.36.grad_gate.refs_1_, bf16[1152,768]{1,0:T(8,128)(2,1)} %get-tuple-element.37.grad_up.refs_2_, ...), custom_call_target="tpu_custom_call" | custom-call | flops 4529848320 | bytes 10420224 | tf_op jit(solution)/shard_map/returned_a/pallas_call | solution.py:168
  231.1 3.4 %collective-permute-start.5 = (bf16[288,1408]{1,0:T(8,128)(2,1)}, bf16[288,1408]{1,0:T(8,128)(2,1)}, u32[]{:S(2)}, u32[]{:S(2)}) collective-permute-start(bf16[288,1408]{1,0:T(8,128)(2,1)} %get-tuple-element.41), channel_id=1, source_target_pairs={{0,4},{1,5},{2,6},{3,7},{4,0},{5,1},{6,2},{7,3},{8,12},{9,13},{10,... | collective-permute-start | bytes 2433032 | tf_op jit(solution)/shard_map/ppermute | solution.py:38
  234.5 0.5 collective-permute-start.6
  235.0 16.5 %all-to-all-done.2 = bf16[16,72,1280]{2,1,0:T(8,128)(2,1)S(1)} async-done(((bf16[16,72,1280]{2,1,0:T(8,128)(2,1)}), bf16[16,72,1280]{2,1,0:T(8,128)(2,1)S(1)}, u32[]{:S(2)}, u32[]{:S(2)}) %all-to-all-start.2) | async-done | bytes 2949152 | tf_op jit(solution)/shard_map/all_to_all | solution.py:427
  251.5 0.6 broadcast_in_dim.29.refs_0_
  252.1 1.0 copy-done
  253.1 9.5 %column_sums.1 = (f32[512,1280]{1,0:T(8,128)}, bf16[512,1280]{1,0:T(8,128)(2,1)}) custom-call(f32[8,1152]{1,0:T(8,128)} %broadcast_in_dim.29.refs_0_, bf16[16,1152]{1,0:T(8,128)(2,1)} %fusion.5.refs_1_, bf16[1024,16]{1,0:T(8,128)(2,1)} %bitcast.34, bf16[1024,16]{1,0:T(8,128)(2,1)} %bitcast.35, bf16[1152,1280]{1,0:T(8,128)(2,1)} %bitcast.28), custom_call_target="tpu_custom_call" | custom-call | flops 60397977600 | bytes 6881280 | tf_op jit(solution)/shard_map/column_sums/pallas_call | solution.py:368
  262.5 5.6 %collective-permute-done.5.refs_4_ = bf16[288,1408]{1,0:T(8,128)(2,1)} collective-permute-done((bf16[288,1408]{1,0:T(8,128)(2,1)}, bf16[288,1408]{1,0:T(8,128)(2,1)}, u32[]{:S(2)}, u32[]{:S(2)}) %collective-permute-start.5) | collective-permute-done | bytes 811040 | tf_op jit(solution)/shard_map/ppermute | solution.py:38
  268.2 5.8 %group_sums.1 = (f32[384,1408]{1,0:T(8,128)}, bf16[384,1408]{1,0:T(8,128)(2,1)}) custom-call(f32[2,384,8]{2,1,0:T(8,128)} %bitcast.32, f32[2,384,8]{2,1,0:T(8,128)} %bitcast.33, bf16[288,1408]{1,0:T(8,128)(2,1)} %get-tuple-element.39.refs_2_, bf16[288,1408]{1,0:T(8,128)(2,1)} %collective-permute-done.4.refs_3_, ...), custom_call_target="tpu_custom_call" | custom-call | flops 1245708288 | bytes 3244032 | tf_op jit(solution)/shard_map/group_sums/pallas_call | solution.py:221
  274.0 5.7 %collective-permute-start.7 = (bf16[384,1408]{1,0:T(8,128)(2,1)}, bf16[384,1408]{1,0:T(8,128)(2,1)S(1)}, u32[]{:S(2)}, u32[]{:S(2)}) collective-permute-start(bf16[384,1408]{1,0:T(8,128)(2,1)} %get-tuple-element.49), channel_id=1, source_target_pairs={{0,1},{1,0},{2,3},{3,2},{4,5},{5,4},{6,7},{7,6},{8,9},{9,8},{10,11... | collective-permute-start | bytes 3244040 | tf_op jit(solution)/shard_map/ppermute | solution.py:38
  279.7 2.5 collective-permute-done.7
  282.3 2.9 add_convert_fusion.1
  285.1 6.7 %all-to-all-start.3 = ((bf16[16,24,1408]{2,1,0:T(8,128)(2,1)}), bf16[16,24,1408]{2,1,0:T(8,128)(2,1)S(1)}, u32[]{:S(2)}, u32[]{:S(2)}) async-start(bf16[16,24,1408]{2,1,0:T(8,128)(2,1)} %bitcast.16), calls=%async_computation.3 | async-start | bytes 2162688 | tf_op jit(solution)/shard_map/all_to_all | solution.py:435
  291.8 2.0 add_convert_fusion
  294.0 0.6 collective-permute-start.11
  294.6 2.0 collective-permute-start.9
  296.6 7.5 %collective-permute-done.10 = bf16[128,1280]{1,0:T(8,128)(2,1)S(1)} collective-permute-done((bf16[128,1280]{1,0:T(8,128)(2,1)S(1)}, bf16[128,1280]{1,0:T(8,128)(2,1)S(1)}, u32[]{:S(2)}, u32[]{:S(2)}) %collective-permute-start.10) | collective-permute-done | bytes 327712 | tf_op jit(solution)/shard_map/ppermute | solution.py:38
  304.2 7.6 %collective-permute-done.11 = bf16[128,1280]{1,0:T(8,128)(2,1)S(1)} collective-permute-done((bf16[128,1280]{1,0:T(8,128)(2,1)S(1)}, bf16[128,1280]{1,0:T(8,128)(2,1)S(1)}, u32[]{:S(2)}, u32[]{:S(2)}) %collective-permute-start.11) | collective-permute-done | bytes 327712 | tf_op jit(solution)/shard_map/ppermute | solution.py:38
  311.7 0.2 add_convert_fusion.2
  311.9 0.4 convolution_bitcast_fusion
  312.4 0.2 copy-done.4
  312.6 0.9 select_reduce_fusion
  313.5 0.9 pad_maximum_fusion
  (56 shorter events, 1.0 us)
Async XLA Ops:
  7.2 78.2 %all-gather.2.cloned.1.call-start = ((), (), s32[]{:S(2)}) async-start(), calls=%async_computation.4 | async-start | bytes 5898240 | tf_op jit(solution)/shard_map/all_gather | solution.py:398
  10.5 2.1 copy-start.5
  47.9 19.2 %copy-start.1 = (bf16[16,24,2688]{2,1,0:T(8,128)(2,1)}, bf16[16,24,2688]{2,1,0:T(8,128)(2,1)S(1)}, u32[]{:S(2)}) copy-start(bf16[16,24,2688]{2,1,0:T(8,128)(2,1)S(1)} %all_to_all.20) | copy-start | bytes 6193156
  47.9 17.9 %collective-permute-start = (bf16[384,2688]{1,0:T(8,128)(2,1)S(1)}, bf16[384,2688]{1,0:T(8,128)(2,1)}, u32[]{:S(2)}, u32[]{:S(2)}) collective-permute-start(bf16[384,2688]{1,0:T(8,128)(2,1)S(1)} %bitcast.30), channel_id=1, source_target_pairs={{0,1},{1,0},{2,3},{3,2},{4,5},{5,4},{6,7},{7,6},{8,9},{9,8},{10,11... | collective-permute-start | bytes 6193160 | tf_op jit(solution)/shard_map/ppermute | solution.py:38
  74.6 34.0 %collective-permute-start.1 = (bf16[288,2560]{1,0:T(8,128)(2,1)}, bf16[288,2560]{1,0:T(8,128)(2,1)S(1)}, u32[]{:S(2)}, u32[]{:S(2)}) collective-permute-start(bf16[288,2560]{1,0:T(8,128)(2,1)} %get-tuple-element.31), channel_id=1, source_target_pairs={{0,2},{1,3},{2,0},{3,1},{4,6},{5,7},{6,4},{7,5},{8,10},{9,11},{10,... | collective-permute-start | bytes 4423688 | tf_op jit(solution)/shard_map/ppermute | solution.py:38
  75.6 66.6 %collective-permute-start.2 = (bf16[288,2560]{1,0:T(8,128)(2,1)}, bf16[288,2560]{1,0:T(8,128)(2,1)}, u32[]{:S(2)}, u32[]{:S(2)}) collective-permute-start(bf16[288,2560]{1,0:T(8,128)(2,1)} %get-tuple-element.32), channel_id=1, source_target_pairs={{0,4},{1,5},{2,6},{3,7},{4,0},{5,1},{6,2},{7,3},{8,12},{9,13},{10,... | collective-permute-start | bytes 4423688 | tf_op jit(solution)/shard_map/ppermute | solution.py:38
  78.0 66.2 %collective-permute-start.3 = (bf16[288,2560]{1,0:T(8,128)(2,1)}, bf16[288,2560]{1,0:T(8,128)(2,1)}, u32[]{:S(2)}, u32[]{:S(2)}) collective-permute-start(bf16[288,2560]{1,0:T(8,128)(2,1)} %get-tuple-element.33), channel_id=1, source_target_pairs={{0,6},{1,7},{2,4},{3,5},{4,2},{5,3},{6,0},{7,1},{8,14},{9,15},{10,... | collective-permute-start | bytes 4423688 | tf_op jit(solution)/shard_map/ppermute | solution.py:38
  93.9 91.2 %all-to-all-start = ((bf16[16,72,2560]{2,1,0:T(8,128)(2,1)}), bf16[16,72,2560]{2,1,0:T(8,128)(2,1)}, u32[]{:S(2)}, u32[]{:S(2)}) async-start(bf16[16,72,2560]{2,1,0:T(8,128)(2,1)} %bitcast.25), calls=%async_computation | async-start | bytes 11796480 | tf_op jit(solution)/shard_map/all_to_all | solution.py:413
  108.6 35.6 %copy-start.9 = (bf16[288,2560]{1,0:T(8,128)(2,1)}, bf16[288,2560]{1,0:T(8,128)(2,1)S(1)}, u32[]{:S(2)}) copy-start(bf16[288,2560]{1,0:T(8,128)(2,1)S(1)} %collective-permute-done.1.refs_2_) | copy-start | bytes 4423684
  206.3 5.4 %copy-start.3 = (f32[16,1024]{1,0:T(8,128)S(1)}, f32[16,1024]{1,0:T(8,128)}, u32[]{:S(2)}) copy-start(f32[16,1024]{1,0:T(8,128)} %get-tuple-element.27) | copy-start | bytes 196612
  206.3 6.3 %copy-start.2 = (f32[16,1024]{1,0:T(8,128)S(1)}, f32[16,1024]{1,0:T(8,128)}, u32[]{:S(2)}) copy-start(f32[16,1024]{1,0:T(8,128)} %get-tuple-element.28) | copy-start | bytes 196612
  206.3 45.1 %all-to-all-start.2 = ((bf16[16,72,1280]{2,1,0:T(8,128)(2,1)}), bf16[16,72,1280]{2,1,0:T(8,128)(2,1)S(1)}, u32[]{:S(2)}, u32[]{:S(2)}) async-start(bf16[16,72,1280]{2,1,0:T(8,128)(2,1)} %bitcast.29), calls=%async_computation.2 | async-start | bytes 5898240 | tf_op jit(solution)/shard_map/all_to_all | solution.py:427
  211.7 3.7 %copy-start.8 = (f32[2,8,384]{2,1,0:T(8,128)S(1)}, f32[2,8,384]{2,1,0:T(8,128)}, u32[]{:S(2)}) copy-start(f32[2,8,384]{2,1,0:T(8,128)} %get-tuple-element.45) | copy-start | bytes 73732
  211.7 4.6 %copy-start.7 = (f32[2,8,384]{2,1,0:T(8,128)S(1)}, f32[2,8,384]{2,1,0:T(8,128)}, u32[]{:S(2)}) copy-start(f32[2,8,384]{2,1,0:T(8,128)} %get-tuple-element.47) | copy-start | bytes 73732
  231.1 31.4 %collective-permute-start.4 = (bf16[288,1408]{1,0:T(8,128)(2,1)}, bf16[288,1408]{1,0:T(8,128)(2,1)}, u32[]{:S(2)}, u32[]{:S(2)}) collective-permute-start(bf16[288,1408]{1,0:T(8,128)(2,1)} %get-tuple-element.40), channel_id=1, source_target_pairs={{0,2},{1,3},{2,0},{3,1},{4,6},{5,7},{6,4},{7,5},{8,10},{9,11},{10,... | collective-permute-start | bytes 2433032 | tf_op jit(solution)/shard_map/ppermute | solution.py:38
  231.1 37.0 %collective-permute-start.5 = (bf16[288,1408]{1,0:T(8,128)(2,1)}, bf16[288,1408]{1,0:T(8,128)(2,1)}, u32[]{:S(2)}, u32[]{:S(2)}) collective-permute-start(bf16[288,1408]{1,0:T(8,128)(2,1)} %get-tuple-element.41), channel_id=1, source_target_pairs={{0,4},{1,5},{2,6},{3,7},{4,0},{5,1},{6,2},{7,3},{8,12},{9,13},{10,... | collective-permute-start | bytes 2433032 | tf_op jit(solution)/shard_map/ppermute | solution.py:38
  234.5 33.7 %collective-permute-start.6 = (bf16[288,1408]{1,0:T(8,128)(2,1)}, bf16[288,1408]{1,0:T(8,128)(2,1)}, u32[]{:S(2)}, u32[]{:S(2)}) collective-permute-start(bf16[288,1408]{1,0:T(8,128)(2,1)} %get-tuple-element.42), channel_id=1, source_target_pairs={{0,6},{1,7},{2,4},{3,5},{4,2},{5,3},{6,0},{7,1},{8,14},{9,15},{10,... | collective-permute-start | bytes 2433032 | tf_op jit(solution)/shard_map/ppermute | solution.py:38
  251.5 1.6 copy-start
  274.0 8.3 %collective-permute-start.7 = (bf16[384,1408]{1,0:T(8,128)(2,1)}, bf16[384,1408]{1,0:T(8,128)(2,1)S(1)}, u32[]{:S(2)}, u32[]{:S(2)}) collective-permute-start(bf16[384,1408]{1,0:T(8,128)(2,1)} %get-tuple-element.49), channel_id=1, source_target_pairs={{0,1},{1,0},{2,3},{3,2},{4,5},{5,4},{6,7},{7,6},{8,9},{9,8},{10,11... | collective-permute-start | bytes 3244040 | tf_op jit(solution)/shard_map/ppermute | solution.py:38
  279.7 12.1 %collective-permute-start.8 = (bf16[512,1280]{1,0:T(8,128)(2,1)}, bf16[512,1280]{1,0:T(8,128)(2,1)S(1)}, u32[]{:S(2)}, u32[]{:S(2)}) collective-permute-start(bf16[512,1280]{1,0:T(8,128)(2,1)} %get-tuple-element.51), channel_id=1, source_target_pairs={{0,1},{1,0},{2,3},{3,2},{4,5},{5,4},{6,7},{7,6},{8,9},{9,8},{10,11... | collective-permute-start | bytes 3932168 | tf_op jit(solution)/shard_map/ppermute | solution.py:38
  285.1 26.8 %all-to-all-start.3 = ((bf16[16,24,1408]{2,1,0:T(8,128)(2,1)}), bf16[16,24,1408]{2,1,0:T(8,128)(2,1)S(1)}, u32[]{:S(2)}, u32[]{:S(2)}) async-start(bf16[16,24,1408]{2,1,0:T(8,128)(2,1)} %bitcast.16), calls=%async_computation.3 | async-start | bytes 2162688 | tf_op jit(solution)/shard_map/all_to_all | solution.py:435
  293.8 18.1 %copy-start.6 = (f32[16,128]{1,0:T(8,128)S(1)}, f32[16,128]{1,0:T(8,128)}, u32[]{:S(2)}) copy-start(f32[16,128]{1,0:T(8,128)} %copy-done.5) | copy-start | bytes 24580
  293.9 10.3 %collective-permute-start.10 = (bf16[128,1280]{1,0:T(8,128)(2,1)S(1)}, bf16[128,1280]{1,0:T(8,128)(2,1)S(1)}, u32[]{:S(2)}, u32[]{:S(2)}) collective-permute-start(bf16[128,1280]{1,0:T(8,128)(2,1)S(1)} %get-tuple-element.54), channel_id=1, source_target_pairs={{0,4},{1,5},{2,6},{3,7},{4,0},{5,1},{6,2},{7,3},{8,12},{9,13},{10,... | collective-permute-start | bytes 983048 | tf_op jit(solution)/shard_map/ppermute | solution.py:38
  294.0 17.7 %collective-permute-start.11 = (bf16[128,1280]{1,0:T(8,128)(2,1)S(1)}, bf16[128,1280]{1,0:T(8,128)(2,1)S(1)}, u32[]{:S(2)}, u32[]{:S(2)}) collective-permute-start(bf16[128,1280]{1,0:T(8,128)(2,1)S(1)} %get-tuple-element.53), channel_id=1, source_target_pairs={{0,6},{1,7},{2,4},{3,5},{4,2},{5,3},{6,0},{7,1},{8,14},{9,15},{10,... | collective-permute-start | bytes 983048 | tf_op jit(solution)/shard_map/ppermute | solution.py:38
  294.6 17.1 %collective-permute-start.9 = (bf16[128,1280]{1,0:T(8,128)(2,1)S(1)}, bf16[128,1280]{1,0:T(8,128)(2,1)S(1)}, u32[]{:S(2)}, u32[]{:S(2)}) collective-permute-start(bf16[128,1280]{1,0:T(8,128)(2,1)S(1)} %get-tuple-element.52), channel_id=1, source_target_pairs={{0,2},{1,3},{2,0},{3,1},{4,6},{5,7},{6,4},{7,5},{8,10},{9,11},{10,... | collective-permute-start | bytes 983048 | tf_op jit(solution)/shard_map/ppermute | solution.py:38
  311.9 0.7 copy-start.4
Sparse Core Ops, SparseCore 0:
  9.7 40.2 all-gather.1

commit v2 on v1

--- a/solution.py
+++ b/solution.py
@@ -198,8 +198,13 @@
     )(grad_gate, grad_up, gate_mat, up_mat)
 
 
-def sum_kernel(chips, slot, weight, *refs):
-    blocks, outs = refs[:chips], refs[chips:]
+def sum_kernel(chips, slot, weight, mine, first, last, *refs):
+    blocks, outs, column = refs[:chips], refs[chips:chips + 2], refs[chips + 2:]
+    n_tok = column[0].shape[0]
+    for a, out in enumerate(column):
+        half, at = (first, a) if 2 * a < chips else (last, a - chips // 2)
+        other = half[n_tok * at:n_tok * (at + 1), :].astype(F32)
+        out[...] = (mine[n_tok * a:n_tok * (a + 1), :] + other).astype(BF)
     half = outs[0].shape[1] - LANES
     rows = blocks[0].shape[0] // 2
     place = lax.broadcasted_iota(jnp.int32, (slot.shape[1], rows), 1).astype(F32)
@@ -215,19 +220,22 @@
         out[:, half:] = gates.astype(out.dtype)
 
 
-def group_sums(slot, weight, blocks):
+def group_sums(slot, weight, mine, first, last, blocks):
     chips = len(blocks)
     shape = (slot.shape[1], blocks[0].shape[1])
+    column = (mine.shape[0] // chips, mine.shape[1])
     return pl.pallas_call(
         lambda *refs: sum_kernel(chips, *refs),
         grid=(1,),
-        in_specs=[whole(slot.shape, (0, 0, 0)), whole(weight.shape, (0, 0, 0))] + [whole(blocks[0].shape)] * chips,
-        out_specs=[whole(shape)] * 2,
-        out_shape=[jax.ShapeDtypeStruct(shape, F32), jax.ShapeDtypeStruct(shape, BF)],
+        in_specs=[whole(slot.shape, (0, 0, 0)), whole(weight.shape, (0, 0, 0))]
+        + [whole(x.shape) for x in (mine, first, last)] + [whole(blocks[0].shape)] * chips,
+        out_specs=[whole(shape)] * 2 + [whole(column)] * chips,
+        out_shape=[jax.ShapeDtypeStruct(shape, F32), jax.ShapeDtypeStruct(shape, BF)]
+        + [jax.ShapeDtypeStruct(column, BF)] * chips,
         compiler_params=params(VMEM_MIB),
         cost_estimate=cost(2 * shape[0] * blocks[0].size * chips, 2 * chips * blocks[0].size),
         name="group_sums",
-    )(slot, weight, *blocks)
+    )(slot, weight, mine, first, last, *blocks)
 
 
 def named_here(top, eye, meta, local):
@@ -240,17 +248,26 @@
     return named, weight
 
 
-def hub_kernel(top, cap, eye, local, before, block, hub, other, *outs):
-    *blocks, out_slot, out_weight = outs
-    rows, features = blocks[0].shape[0] // 2, blocks[0].shape[1]
+def hub_kernel(top, cap, eye, local, before, block, meta, other_meta, hub, other, *outs):
+    *blocks, out_slot, out_weight, puts = outs
+    rows = blocks[0].shape[0] // 2
+    n_rows = hub.shape[0]
+
+    @pl.when(pl.program_id(0) == 0)
+    def _():
+        for side, ref in enumerate((meta, other_meta)):
+            named, weight = named_here(top, eye, ref[...], local)
+            slot = jnp.where(named > 0.0, block[0:1, :] * cap + dot(named.astype(BF), before[...]), -1.0)
+            out_slot[side], out_weight[side] = slot, weight
+            place = lax.broadcasted_iota(jnp.int32, (rows, n_rows), 0).astype(F32)
+            for a in range(len(blocks)):
+                hot = jnp.where(place == slot[2 * a:2 * a + 1, :], 1.0, 0.0).astype(BF)
+                puts[side, rows * a:rows * (a + 1), :] = hot
+
     for side, ref in enumerate((hub, other)):
-        named, weight = named_here(top, eye, ref[:, features:], local)
-        slot = jnp.where(named > 0.0, block[0:1, :] * cap + dot(named.astype(BF), before[...]), -1.0)
-        out_slot[side], out_weight[side] = slot, weight
-        place = lax.broadcasted_iota(jnp.int32, (rows, slot.shape[1]), 0).astype(F32)
+        placed = dot(puts[side], ref[...]).astype(BF)
         for a, out in enumerate(blocks):
-            hot = jnp.where(place == slot[2 * a:2 * a + 1, :], 1.0, 0.0).astype(BF)
-            out[rows * side:rows * (side + 1), :] = dot(hot, ref[:, :features]).astype(BF)
+            out[rows * side:rows * (side + 1), :] = placed[rows * a:rows * (a + 1), :]
 
 
 def lower_counts(total, size):
@@ -266,22 +283,33 @@
     shape = (2 * (n_rows // per_group) * cap, width - LANES)
     pair = (2, n_exp, n_rows)
     eye = jnp.eye(LANES, dtype=BF)
+    features, chips = width - LANES, n_exp // 2
+    wide = 512 if features % 512 == 0 else features
+    lanes = whole((n_rows, LANES), (0, width // LANES - 1))
+    part = pl.BlockSpec((n_rows, wide), lambda j: (0, j))
     *blocks, slot, weight = pl.pallas_call(
         lambda *refs: hub_kernel(top, cap, *refs),
-        grid=(1,),
-        in_specs=[whole(x.shape) for x in (eye, local, before, block, hub, other)],
-        out_specs=[whole(shape)] * (n_exp // 2) + [whole(pair, (0, 0, 0))] * 2,
-        out_shape=[jax.ShapeDtypeStruct(shape, BF)] * (n_exp // 2) + [jax.ShapeDtypeStruct(pair, F32)] * 2,
+        grid=(features // wide,),
+        in_specs=[whole(x.shape) for x in (eye, local, before, block)] + [lanes, lanes, part, part],
+        out_specs=[pl.BlockSpec((shape[0], wide), lambda j: (0, j))] * chips + [whole(pair, (0, 0, 0))] * 2,
+        out_shape=[jax.ShapeDtypeStruct(shape, BF)] * chips + [jax.ShapeDtypeStruct(pair, F32)] * 2,
+        scratch_shapes=[pltpu.VMEM((2, shape[0] // 2 * chips, n_rows), BF)],
         compiler_params=params(VMEM_MIB),
         cost_estimate=cost(shape[0] * n_exp * n_rows * width, n_exp * shape[0] * shape[1]),
         name="hub_blocks",
-    )(eye, local, before, block, hub, other)
+    )(eye, local, before, block, hub, other, hub, other)
     return blocks, slot.transpose(0, 2, 1), weight.transpose(0, 2, 1)
 
 
-def slots_kernel(top, n_exp, cap, member, eye, theirs, before, start, spread, place, meta, out_hot, out_slot, out_weight):
+def column_block(k, member, n_tok, mine, other):
+    rows = pl.ds(pl.multiple_of((member[0] ^ k) // 2 * n_tok, n_tok), n_tok)
+    return other[k // 2][...] if k % 2 else mine[rows, :]
+
+
+def slots_kernel(top, n_exp, cap, member, eye, theirs, before, start, spread, place, meta, *refs):
+    *other, out_hot, out_slot, out_weight = refs
     n_tok = before.shape[0]
-    parts = [meta[pl.ds(pl.multiple_of((member[0] ^ k) * n_tok, n_tok), n_tok), :] for k in range(n_exp)]
+    parts = [column_block(k, member, n_tok, meta, other) for k in range(n_exp)]
     named, out_weight[...] = named_here(top, eye, jnp.concatenate(parts, axis=0), theirs)
     counts = [dot(named[:, at:at + n_tok].astype(BF), before[...]) for at in range(0, named.shape[1], n_tok)]
     rank = jnp.concatenate(counts, axis=1)
@@ -293,9 +321,10 @@
         out_hot[size * k:size * (k + 1), :] = jnp.where(hot, 1.0, 0.0).astype(BF)
 
 
-def column_slots(meta, theirs, member, n_tok, top, cap):
-    total = meta.shape[0]
+def column_slots(mine, other, theirs, member, n_tok, top, cap):
+    total, last = 2 * mine.shape[0], mine.shape[1] // LANES - 1
     n_seq, n_exp = theirs.shape[0], total // n_tok
+    lanes = whole((total // 2, LANES), (0, last))
     before, block = lower_counts(n_tok, n_tok)
     start = jnp.broadcast_to((jnp.arange(total) // n_tok * cap).astype(F32), (8, total))
     at = jnp.arange(n_seq * cap)
@@ -303,59 +332,63 @@
     place = jnp.broadcast_to((at % cap).astype(F32)[:, None], (n_seq * cap, LANES))
     eye = jnp.eye(LANES, dtype=BF)
     shapes = (n_seq * n_exp * cap, n_tok), (n_seq, total), (n_seq, total)
-    inputs = (eye, theirs, before, start, spread, place, meta)
+    inputs = (eye, theirs, before, start, spread, place)
     hot, slot, weight = pl.pallas_call(
         lambda *refs: slots_kernel(top, n_exp, cap, *refs),
         grid=(1,),
-        in_specs=[pl.BlockSpec(memory_space=pltpu.SMEM)] + [whole(x.shape) for x in inputs],
+        in_specs=[pl.BlockSpec(memory_space=pltpu.SMEM)] + [whole(x.shape) for x in inputs] + [lanes] + [whole((n_tok, LANES), (0, last))] * len(other),
         out_specs=[whole(shape) for shape in shapes],
         out_shape=[jax.ShapeDtypeStruct(shape, kind) for shape, kind in zip(shapes, (BF, F32, F32))],
         compiler_params=params(VMEM_MIB),
         cost_estimate=cost(4 * total * LANES * LANES, 2 * shapes[0][0] * n_tok),
         name="column_slots",
-    )(member.reshape(1), *inputs)
+    )(member.reshape(1), *inputs, mine, *other)
     return hot, slot.T, weight.T
 
 
-def rows_kernel(n_exp, member, table, hot, column, out):
+def rows_kernel(n_exp, member, table, hot, mine, *refs):
+    *other, out = refs
     pairs, size = table.shape[:2]
     n_tok = hot.shape[1]
     blocks = []
     for k in range(n_exp):
-        rows = pl.ds(pl.multiple_of((member[0] ^ k) * n_tok, n_tok), n_tok)
-        blocks.append(dot(hot[size * k:size * (k + 1), :], column[rows, :]).astype(BF))
+        blocks.append(dot(hot[size * k:size * (k + 1), :], column_block(k, member, n_tok, mine, other)).astype(BF))
     for i in range(pairs):
         window = jnp.concatenate([b[16 * i:16 * i + 32, :] for b in blocks], axis=0)
         out[size * i:size * (i + 1), :] = dot(table[i], window).astype(BF)
 
 
-def column_rows(member, table, hot, column, n_exp):
-    total, features = hot.shape[0], column.shape[1]
+def column_rows(member, table, hot, mine, other, n_exp):
+    total, features = hot.shape[0], mine.shape[1] - LANES
     wide = 512 if features % 512 == 0 else features
+    part = lambda rows: pl.BlockSpec((rows, wide), lambda j: (0, j))
     return pl.pallas_call(
         lambda *refs: rows_kernel(n_exp, *refs),
         grid=(features // wide,),
         in_specs=[pl.BlockSpec(memory_space=pltpu.SMEM), whole(table.shape, (0, 0, 0)), whole(hot.shape),
-                  pl.BlockSpec((column.shape[0], wide), lambda j: (0, j))],
-        out_specs=pl.BlockSpec((total, wide), lambda j: (0, j)),
+                  part(mine.shape[0])] + [part(hot.shape[1])] * len(other),
+        out_specs=part(total),
         out_shape=jax.ShapeDtypeStruct((total, features), BF),
         compiler_params=params(VMEM_MIB),
-        cost_estimate=cost(2 * total * (hot.shape[1] + table.shape[2]) * features, 2 * column.size + 2 * total * features),
+        cost_estimate=cost(2 * total * hot.shape[1] * LANES, 2 * total * LANES),
         name="column_rows",
-    )(member.reshape(1), table, hot, column)
-
-
-def column_kernel(n_exp, place, spread, slot, weight, got, out_mine, out_other, mixed):
+    )(member.reshape(1), table, hot, mine, *other)
+
+
+def column_kernel(n_exp, place, spread, slot, weight, got, out_mine, out_first, out_last, mixed):
     n_tok = out_mine.shape[0] // (n_exp // 2)
-    mixed[...] = jnp.where(dot(slot[...], spread[...]) == place[0:1, :], dot(weight[...], spread[...]), 0.0).astype(BF)
-    half = got.shape[1]
-    wide = 256 if half % 256 == 0 else half
-    for start in range(0, half, wide):
-        sums = dot(mixed[...], got[:, start:start + wide])
-        for k in range(0, n_exp, 2):
-            at = slice(n_tok * k // 2, n_tok * (k // 2 + 1))
-            out_mine[at, start:start + wide] = sums[n_tok * k:n_tok * (k + 1), :]
-            out_other[at, start:start + wide] = sums[n_tok * (k + 1):n_tok * (k + 2), :].astype(BF)
+
+    @pl.when(pl.program_id(0) == 0)
+    def _():
+        hot = dot(slot[...], spread[...]) == place[0:1, :]
+        mixed[...] = jnp.where(hot, dot(weight[...], spread[...]), 0.0).astype(BF)
+
+    sums = dot(mixed[...], got[...])
+    for k in range(0, n_exp, 2):
+        at = slice(n_tok * k // 2, n_tok * (k // 2 + 1))
+        out_mine[at, :] = sums[n_tok * k:n_tok * (k + 1), :]
+        out, at = (out_first, k) if 2 * k < n_exp else (out_last, k - n_exp // 2)
+        out[n_tok * at // 2:n_tok * (at // 2 + 1), :] = sums[n_tok * (k + 1):n_tok * (k + 2), :].astype(BF)
 
 
 def column_sums(slot, weight, got, n_exp):
@@ -365,15 +398,17 @@
     place = jnp.broadcast_to((at % (total // n_seq)).astype(F32), (8, total))
     spread = (jnp.arange(n_seq)[:, None] == at[None, :] // (total // n_seq)).astype(BF)
     shape = (n_rows // 2, half)
+    wide = 256 if half % 256 == 0 else half
+    part = lambda rows: pl.BlockSpec((rows, wide), lambda j: (0, j))
     return pl.pallas_call(
         lambda *refs: column_kernel(n_exp, *refs),
-        grid=(1,),
-        in_specs=[whole(place.shape), whole(spread.shape), whole(slot.shape), whole(weight.shape), whole(got.shape)],
-        out_specs=[whole(shape)] * 2,
-        out_shape=[jax.ShapeDtypeStruct(shape, F32), jax.ShapeDtypeStruct(shape, BF)],
+        grid=(half // wide,),
+        in_specs=[whole(place.shape), whole(spread.shape), whole(slot.shape), whole(weight.shape), part(total)],
+        out_specs=[part(shape[0])] + [part(shape[0] // 2)] * 2,
+        out_shape=[jax.ShapeDtypeStruct(shape, F32)] + [jax.ShapeDtypeStruct((shape[0] // 2, half), BF)] * 2,
         scratch_shapes=[pltpu.VMEM((n_rows, total), BF)],
         compiler_params=params(VMEM_MIB),
-        cost_estimate=cost(40 * n_rows * total * half, 2 * total * half + 3 * n_rows * half),
+        cost_estimate=cost(400 * n_rows * total * half, 2 * total * half + 3 * n_rows * half),
         name="column_sums",
     )(place, spread, slot.astype(BF), weight.astype(BF), got)
 
@@ -394,10 +429,13 @@
     meta = jnp.concatenate(
         (expert_ids.astype(BF), gate_weights.astype(BF), jnp.zeros((n_tok, LANES - 2 * top), BF)), axis=1)
 
-    column_meta = lax.all_gather(meta, "exp", axis=0, tiled=True)
-    column = lax.all_gather(grad_out, "exp", axis=0, tiled=True)
+    places = [list(range(c, n_exp, 2)) for c in range(2)]
+    column = lax.all_gather(jnp.concatenate((grad_out, meta), axis=1), "exp", axis_index_groups=places, axis=0, tiled=True)
+    other_column = [
+        swap(lax.dynamic_slice_in_dim(column, (member // 2 ^ a) * n_tok, n_tok, 0), 1) for a in range(n_exp // 2)]
     theirs = jnp.broadcast_to((jnp.arange(n_seq) * n_exp + member).astype(F32)[:, None], (n_seq, LANES))
-    put_b, slot_b, weight_b = column_slots(column_meta, theirs, member, n_tok, top, cap)
+    put_b, slot_b, weight_b = column_slots(column, other_column, theirs, member, n_tok, top, cap)
+    send_b = column_rows(member, to_b, put_b, column, other_column, n_exp)
 
     group_ids = expert_ids // n_exp
     in_group = jnp.any(group_ids[:, :, None] == jnp.arange(n_seq)[None, None, :], axis=1)
@@ -407,8 +445,8 @@
     send = dot(pick, jnp.concatenate((hidden_in, meta), axis=1)).astype(BF)
     hub = lax.all_to_all(send.reshape(n_seq, per_group, features + LANES), "seq", 0, 0, tiled=True)
     hub = hub.reshape(n_seq * per_group, features + LANES)
-
-    send_b = column_rows(member, to_b, put_b, column, n_exp)
+    hub, send_b = barrier(hub, send_b)
+
     rows_b = n_exp * cap
     recv_b = lax.all_to_all(send_b.reshape(n_seq, rows_b, features), "seq", 0, 0, tiled=True)
     recv_b = recv_b.reshape(n_seq * rows_b, features)
@@ -426,11 +464,9 @@
     back_b = returned_b(grad_gate, grad_up, gate_mat, up_mat)
     got_b = lax.all_to_all(back_b.reshape(n_seq, rows_b, half), "seq", 0, 0, tiled=True)
     got_b, *_ = barrier(got_b, *back_a)
-    mine, other = column_sums(slot_b, weight_b, got_b.reshape(n_seq * rows_b, half), n_exp)
-    other, slot_a = barrier(other, slot_a)
-    chip = (mine + swap(other, 1).astype(F32)).astype(BF).reshape(n_exp // 2, n_tok, half)
-    final_b = sum(p.astype(F32) for p in exchange(list(chip)))
-    mine, other = group_sums(slot_a, weight_a, got_a)
+    mine, *other = column_sums(slot_b, weight_b, got_b.reshape(n_seq * rows_b, half), n_exp)
+    mine, other, *chip = group_sums(slot_a, weight_a, mine, *(swap(x, 1) for x in other), got_a)
+    final_b = sum(p.astype(F32) for p in exchange(chip))
     back = (mine + swap(other, 1).astype(F32)).astype(BF)
     back = lax.all_to_all(back.reshape(n_seq, per_group, half + LANES), "seq", 0, 0, tiled=True)
     final_a = dot_t(pick, back.reshape(n_seq * per_group, half + LANES))

time: 322 us -> 318 us (0.988)
  blocking collectives: 49.8 us -> 0 us
  waiting for transfers between devices: 110 us -> 137 us
  starting transfers between devices: 34.9 us -> 48.3 us
  local copies, waits for them, and re-layouts: 12.2 us -> 16.7 us
  other arithmetic: 13.8 us -> 10.3 us
    all_to_all x1 -> x0, blocking collectives: 35.4 us -> none  [per_device(): lax.all_to_all(send.reshape(n_seq, per_group, features + LANES), 'seq', 0...]
    all_gather x1, waiting for transfers between devices: 0.01 us -> 26.9 us  [per_device(): lax.all_gather(jnp.concatenate((grad_out, meta), axis=1), 'exp', axis_ind...]
    all_gather x1 -> x0, blocking collectives: 14.4 us -> none  [per_device(): column_meta = lax.all_gather(meta, 'exp', axis=0, tiled=True)]
    ppermute x12 -> x17, waiting for transfers between devices: 68.8 us -> 81.3 us  [swap(): lax.ppermute(x, 'exp', [(i, i ^ k) for i in range(lax.axis_size('exp'))])]
    all_to_all x1, waiting for transfers between devices: 24.1 us -> 12.3 us  [per_device(): lax.all_to_all(send_b.reshape(n_seq, rows_b, features), 'seq', 0, 0, tile...]
    all_to_all x0 -> x1, starting transfers between devices: none -> 8.47 us  [per_device(): lax.all_to_all(send.reshape(n_seq, per_group, features + LANES), 'seq', 0...]
    ppermute x12 -> x17, starting transfers between devices: 18 us -> 21.6 us  [swap(): lax.ppermute(x, 'exp', [(i, i ^ k) for i in range(lax.axis_size('exp'))])]
  transfers between devices with their start and end apart: 16 -> 22, of which waited for: 9 -> 15; matrix products, arithmetic and copies ran while one was open for 7% -> 5% of each run, Pallas kernels for 18% -> 16%
where the time goes in v2:
time: 318 us; the launch traced here: 316 us
  waiting for transfers between devices  137 us (43%)
  Pallas kernels  86.3 us (27%)
  starting transfers between devices  48.3 us (15%)
  local copies, waits for them, and re-layouts  16.7 us (5%)
  between operations  14.4 us (5%)
  other arithmetic  10.3 us (3%)
    ppermute x17, waiting for transfers between devices, swap(): lax.ppermute(x, 'exp', [(i, i ^ k) for i in range(lax.axis_size('exp'))])  81.3 us
    all_gather x1, waiting for transfers between devices, per_device(): lax.all_gather(jnp.concatenate((grad_out, meta), axis=1), 'exp', axis_ind...  26.9 us
    ppermute x17, starting transfers between devices, swap(): lax.ppermute(x, 'exp', [(i, i ^ k) for i in range(lax.axis_size('exp'))])  21.6 us
    all_to_all x1, waiting for transfers between devices, per_device(): lax.all_to_all(back_b.reshape(n_seq, rows_b, half), 'seq', 0, 0, tiled=True)  16.7 us
    pallas_call x1, Pallas kernels, pre_products(): pl.pallas_call(lambda *refs: pre_kernel(chips, pairs, *refs), grid=(units...  16.6 us
    pallas_call x1, Pallas kernels, returned_a(): pl.pallas_call(lambda *refs: back_a_kernel(n_exp, pairs, *refs), grid=(ha...  13.8 us
    all_to_all x1, waiting for transfers between devices, per_device(): lax.all_to_all(send_b.reshape(n_seq, rows_b, features), 'seq', 0, 0, tile...  12.3 us
    pallas_call x1, Pallas kernels, hidden_grads(): pl.pallas_call(grad_kernel, grid=(4,), in_specs=[whole(lane.shape), row(f...  11.4 us
  transfers between devices with their start and end apart: 22, of which 15 were waited for; matrix products, arithmetic and copies ran while one was open for 5% of the time, Pallas kernels for 16%

profile of v2, /device:TPU:1, one launch (start us, length us, event | category | flops | bytes accessed | tf_op | source)
XLA Modules:
  0.0 316.1 jit_solution(17820456310983187482)
XLA Ops:
  7.2 0.9 copy.17
  8.1 0.8 copy.18
  8.9 1.9 concatenate.14
  11.5 0.6 copy-done.13
  12.2 2.1 convolution_convert_fusion
  14.3 8.5 %all-to-all-start = ((bf16[16,24,2688]{2,1,0:T(8,128)(2,1)}), bf16[16,24,2688]{2,1,0:T(8,128)(2,1)}, u32[]{:S(2)}, u32[]{:S(2)}) async-start(bf16[16,24,2688]{2,1,0:T(8,128)(2,1)} %bitcast.2), calls=%async_computation | async-start | bytes 4128768 | tf_op jit(solution)/shard_map/all_to_all | solution.py:446
  22.9 0.7 fusion.5.refs_5_
  23.6 26.9 %all-gather.2.cloned.1.call-done.refs_7_.refs_3_ = bf16[512,2688]{1,0:T(8,128)(2,1)} async-done(((bf16[128,2688]{1,0:T(8,128)(2,1)}), bf16[512,2688]{1,0:T(8,128)(2,1)}) %all-gather.2.cloned.1.call-update) | async-done | bytes 2752528 | tf_op jit(solution)/shard_map/all_gather | solution.py:433
  50.5 1.9 constant_dynamic-slice_fusion
  52.5 0.8 collective-permute-start
  53.9 0.7 fusion.7
  54.6 1.0 fusion.1.refs_1_.refs_0_
  56.0 1.0 collective-permute-done.2.refs_10_.refs_6_
  57.0 1.0 collective-permute-done.3.refs_11_.refs_7_
  57.9 0.8 broadcast_in_dim.32.refs_2_
  58.7 0.7 broadcast_in_dim.34.refs_6_
  59.4 0.6 broadcast_in_dim.33.refs_4_
  60.0 2.4 column_slots.1
  62.4 8.5 %column_rows.1 = bf16[1152,2560]{1,0:T(8,128)(2,1)} custom-call(s32[1]{0:T(128)} %bitcast.4.refs_0_, bf16[8,144,256]{2,1,0:T(8,128)(2,1)} %fusion.1.refs_1_.refs_0_, bf16[1152,128]{1,0:T(8,128)(2,1)} %get-tuple-element.32.refs_2_, bf16[512,2688]{1,0:T(8,128)(2,1)} %all-gather.2.cloned.1.call-done.refs_7_.refs_3_, bf16[128,2688]{1,0:T(8,128)(2,1)} %copy-done.1, ...), custom_call_target="tpu_custom_call" | custom-call | flops 37748736 | bytes 294912 | tf_op jit(solution)/shard_map/column_rows/pallas_call | solution.py:365
  71.4 0.9 fusion.3.refs_2_
  72.3 3.1 collective-permute-done.4.refs_5_.refs_7_
  75.4 0.8 broadcast_in_dim.29.refs_1_
  76.1 0.6 broadcast_in_dim.30.refs_3_
  76.7 8.3 %hub_blocks.1 = (bf16[288,2560]{1,0:T(8,128)(2,1)}, bf16[288,2560]{1,0:T(8,128)(2,1)}, bf16[288,2560]{1,0:T(8,128)(2,1)}, bf16[288,2560]{1,0:T(8,128)(2,1)}, f32[2,8,384]{2,1,0:T(8,128)}, /*index=5*/f32[2,8,384]{2,1,0:T(8,128)}) custom-call(bf16[128,128]{1,0:T(8,128)(2,1)} %get-tuple-element.68.refs_1_.refs_0_, f32[8,128]{1,0:T(8,128)} %broadcast_in_dim.29.refs_1_, ...), custom_call_target="tpu_custom_call" | custom-call | flops 2378170368 | bytes 5898240 | tf_op jit(solution)/shard_map/hub_blocks/pallas_call | solution.py:290
  85.4 1.4 collective-permute-start.6
  86.8 2.1 collective-permute-start.7
  89.0 6.7 %all-to-all-start.1 = ((bf16[16,72,2560]{2,1,0:T(8,128)(2,1)}), bf16[16,72,2560]{2,1,0:T(8,128)(2,1)}, u32[]{:S(2)}, u32[]{:S(2)}) async-start(bf16[16,72,2560]{2,1,0:T(8,128)(2,1)} %bitcast.25), calls=%async_computation.1 | async-start | bytes 11796480 | tf_op jit(solution)/shard_map/all_to_all | solution.py:451
  95.7 23.2 %collective-permute-done.5.refs_2_ = bf16[288,2560]{1,0:T(8,128)(2,1)S(1)} collective-permute-done((bf16[288,2560]{1,0:T(8,128)(2,1)}, bf16[288,2560]{1,0:T(8,128)(2,1)S(1)}, u32[]{:S(2)}, u32[]{:S(2)}) %collective-permute-start.5) | collective-permute-done | bytes 1474592 | tf_op jit(solution)/shard_map/ppermute | solution.py:38
  118.9 31.9 %collective-permute-done.6.refs_3_ = bf16[288,2560]{1,0:T(8,128)(2,1)S(1)} collective-permute-done((bf16[288,2560]{1,0:T(8,128)(2,1)}, bf16[288,2560]{1,0:T(8,128)(2,1)S(1)}, u32[]{:S(2)}, u32[]{:S(2)}) %collective-permute-start.6) | collective-permute-done | bytes 1474592 | tf_op jit(solution)/shard_map/ppermute | solution.py:38
  150.8 2.0 collective-permute-done.7.refs_4_
  152.8 16.6 %pre_products.1 = (f32[1152,768]{1,0:T(8,128)}, f32[1152,768]{1,0:T(8,128)}) custom-call(bf16[8,144,256]{2,1,0:T(8,128)(2,1)} %fusion.1.refs_1_.refs_0_, bf16[288,2560]{1,0:T(8,128)(2,1)} %get-tuple-element.39.refs_1_, bf16[288,2560]{1,0:T(8,128)(2,1)} %copy-done.18, bf16[288,2560]{1,0:T(8,128)(2,1)} %copy-done.19, ...), custom_call_target="tpu_custom_call" | custom-call | flops 90596966400 | bytes 20840448 | tf_op jit(solution)/shard_map/pre_products/pallas_call | solution.py:91
  169.5 12.3 %all-to-all-done.1 = bf16[16,72,2560]{2,1,0:T(8,128)(2,1)} async-done(((bf16[16,72,2560]{2,1,0:T(8,128)(2,1)}), bf16[16,72,2560]{2,1,0:T(8,128)(2,1)}, u32[]{:S(2)}, u32[]{:S(2)}) %all-to-all-start.1) | async-done | bytes 5898272 | tf_op jit(solution)/shard_map/all_to_all | solution.py:451
  181.8 0.6 broadcast_in_dim.36.lane
  182.4 11.4 %hidden_grads.1 = (bf16[1152,768]{1,0:T(8,128)(2,1)}, bf16[1152,768]{1,0:T(8,128)(2,1)}, bf16[1152,128]{1,0:T(8,128)(2,1)}) custom-call(f32[8,128]{1,0:T(8,128)} %broadcast_in_dim.36.lane, bf16[1152,2560]{1,0:T(8,128)(2,1)} %bitcast.10.grad, bf16[768,2560]{1,0:T(8,128)(2,1)} %bitcast.26, f32[1152,768]{1,0:T(8,128)} %get-tuple-element.43.pre_gate, ...), custom_call_target="tpu_custom_call" | custom-call | flops 4529848320 | bytes 20447232 | tf_op jit(solution)/shard_map/hidden_grads/pallas_call | solution.py:121
  193.8 9.2 %returned_b.1 = bf16[1152,1280]{1,0:T(8,128)(2,1)} custom-call(bf16[1152,768]{1,0:T(8,128)(2,1)} %get-tuple-element.45.grad_gate.refs_1_, bf16[1152,768]{1,0:T(8,128)(2,1)} %get-tuple-element.46.grad_up.refs_2_, bf16[2560,768]{1,0:T(8,128)(2,1)} %bitcast.34, bf16[2560,768]{1,0:T(8,128)(2,1)} %bitcast.37), custom_call_target="tpu_custom_call" | custom-call | flops 4529848320 | bytes 10420224 | tf_op jit(solution)/shard_map/returned_b/pallas_call | solution.py:189
  203.0 4.7 %all-to-all-start.2 = ((bf16[16,72,1280]{2,1,0:T(8,128)(2,1)}), bf16[16,72,1280]{2,1,0:T(8,128)(2,1)S(1)}, u32[]{:S(2)}, u32[]{:S(2)}) async-start(bf16[16,72,1280]{2,1,0:T(8,128)(2,1)} %bitcast.28), calls=%async_computation.2 | async-start | bytes 5898240 | tf_op jit(solution)/shard_map/all_to_all | solution.py:465
  207.7 1.3 fusion.refs_0_
  209.1 0.6 fusion.6.refs_1_
  209.7 0.9 copy.21
  210.6 0.8 copy.22
  211.4 13.8 %returned_a.1 = (bf16[288,1408]{1,0:T(8,128)(2,1)}, bf16[288,1408]{1,0:T(8,128)(2,1)}, bf16[288,1408]{1,0:T(8,128)(2,1)}, bf16[288,1408]{1,0:T(8,128)(2,1)}) custom-call(bf16[8,256,144]{2,1,0:T(8,128)(2,1)} %fusion.refs_0_, bf16[1152,768]{1,0:T(8,128)(2,1)} %get-tuple-element.45.grad_gate.refs_1_, bf16[1152,768]{1,0:T(8,128)(2,1)} %get-tuple-element.46.grad_up.refs_2_, ...), custom_call_target="tpu_custom_call" | custom-call | flops 4529848320 | bytes 10420224 | tf_op jit(solution)/shard_map/returned_a/pallas_call | solution.py:168
  225.2 1.8 collective-permute-start.11
  227.0 2.1 collective-permute-start.12
  229.1 16.7 %all-to-all-done.2 = bf16[16,72,1280]{2,1,0:T(8,128)(2,1)S(1)} async-done(((bf16[16,72,1280]{2,1,0:T(8,128)(2,1)}), bf16[16,72,1280]{2,1,0:T(8,128)(2,1)S(1)}, u32[]{:S(2)}, u32[]{:S(2)}) %all-to-all-start.2) | async-done | bytes 2949152 | tf_op jit(solution)/shard_map/all_to_all | solution.py:465
  245.8 0.7 broadcast_in_dim.35.refs_0_
  246.5 0.9 copy-done
  247.4 8.6 %column_sums.1 = (f32[512,1280]{1,0:T(8,128)}, bf16[256,1280]{1,0:T(8,128)(2,1)}, bf16[256,1280]{1,0:T(8,128)(2,1)}) custom-call(f32[8,1152]{1,0:T(8,128)} %broadcast_in_dim.35.refs_0_, bf16[16,1152]{1,0:T(8,128)(2,1)} %fusion.6.refs_1_, bf16[1024,16]{1,0:T(8,128)(2,1)} %bitcast.31, bf16[1024,16]{1,0:T(8,128)(2,1)} %bitcast.32, bf16[1152,1280]{1,0:T(8,128)(2,1)} %bitcast.27), custom_call_target="tpu_custom_call" | custom-call | flops 603979776000 | bytes 6881280 | tf_op jit(solution)/shard_map/column_sums/pallas_call | solution.py:403
  256.0 4.0 %collective-permute-start.8 = (bf16[256,1280]{1,0:T(8,128)(2,1)}, bf16[256,1280]{1,0:T(8,128)(2,1)S(1)}, u32[]{:S(2)}, u32[]{:S(2)}) collective-permute-start(bf16[256,1280]{1,0:T(8,128)(2,1)} %get-tuple-element.54), channel_id=1, source_target_pairs={{0,1},{1,0},{2,3},{3,2},{4,5},{5,4},{6,7},{7,6},{8,9},{9,8},{10,11... | collective-permute-start | bytes 1966088 | tf_op jit(solution)/shard_map/ppermute | solution.py:38
  260.3 1.0 copy.19
  261.2 0.9 copy.20
  262.2 0.6 collective-permute-done.9.refs_4_
  263.0 0.7 copy-done.7
  263.7 7.5 %group_sums.1 = (f32[384,1408]{1,0:T(8,128)}, bf16[384,1408]{1,0:T(8,128)(2,1)}, bf16[128,1280]{1,0:T(8,128)(2,1)}, bf16[128,1280]{1,0:T(8,128)(2,1)}, bf16[128,...) custom-call(f32[2,384,8]{2,1,0:T(8,128)} %bitcast.29, f32[2,384,8]{2,1,0:T(8,128)} %bitcast.30, ...), custom_call_target="tpu_custom_call" | custom-call | flops 1245708288 | bytes 3244032 | tf_op jit(solution)/shard_map/group_sums/pallas_call | solution.py:227
  271.2 3.8 %collective-permute-start.13 = (bf16[384,1408]{1,0:T(8,128)(2,1)}, bf16[384,1408]{1,0:T(8,128)(2,1)S(1)}, u32[]{:S(2)}, u32[]{:S(2)}) collective-permute-start(bf16[384,1408]{1,0:T(8,128)(2,1)} %get-tuple-element.57), channel_id=1, source_target_pairs={{0,1},{1,0},{2,3},{3,2},{4,5},{5,4},{6,7},{7,6},{8,9},{9,8},{10,11... | collective-permute-start | bytes 3244040 | tf_op jit(solution)/shard_map/ppermute | solution.py:38
  275.0 2.5 collective-permute-done.13
  277.5 2.9 add_convert_fusion
  280.4 6.8 %all-to-all-start.3 = ((bf16[16,24,1408]{2,1,0:T(8,128)(2,1)}), bf16[16,24,1408]{2,1,0:T(8,128)(2,1)S(1)}, u32[]{:S(2)}, u32[]{:S(2)}) async-start(bf16[16,24,1408]{2,1,0:T(8,128)(2,1)} %bitcast.16), calls=%async_computation.3 | async-start | bytes 2162688 | tf_op jit(solution)/shard_map/all_to_all | solution.py:471
  287.3 3.2 %collective-permute-start.15 = (bf16[128,1280]{1,0:T(8,128)(2,1)S(1)}, bf16[128,1280]{1,0:T(8,128)(2,1)S(1)}, u32[]{:S(2)}, u32[]{:S(2)}) collective-permute-start(bf16[128,1280]{1,0:T(8,128)(2,1)S(1)} %copy-done.21), channel_id=1, source_target_pairs={{0,4},{1,5},{2,6},{3,7},{4,0},{5,1},{6,2},{7,3},{8,12},{9,13},{10,... | collective-permute-start | bytes 983048 | tf_op jit(solution)/shard_map/ppermute | solution.py:38
  290.5 0.6 collective-permute-start.16
  291.1 4.7 %collective-permute-done.14 = bf16[128,1280]{1,0:T(8,128)(2,1)S(1)} collective-permute-done((bf16[128,1280]{1,0:T(8,128)(2,1)S(1)}, bf16[128,1280]{1,0:T(8,128)(2,1)S(1)}, u32[]{:S(2)}, u32[]{:S(2)}) %collective-permute-start.14) | collective-permute-done | bytes 327712 | tf_op jit(solution)/shard_map/ppermute | solution.py:38
  295.9 8.9 %collective-permute-done.15 = bf16[128,1280]{1,0:T(8,128)(2,1)S(1)} collective-permute-done((bf16[128,1280]{1,0:T(8,128)(2,1)S(1)}, bf16[128,1280]{1,0:T(8,128)(2,1)S(1)}, u32[]{:S(2)}, u32[]{:S(2)}) %collective-permute-start.15) | collective-permute-done | bytes 327712 | tf_op jit(solution)/shard_map/ppermute | solution.py:38
  304.7 2.0 collective-permute-done.16
  307.4 0.9 select_reduce_fusion
  308.3 0.9 pad_maximum_fusion
  (89 shorter events, 4.1 us)
Async XLA Ops:
  7.2 4.1 %copy-start.11 = (s32[128,6]{0,1:T(8,128)S(1)}, s32[128,6]{0,1:T(8,128)}, u32[]{:S(2)}) copy-start(s32[128,6]{0,1:T(8,128)} %param.9) | copy-start | bytes 9220
  7.2 3.7 %copy-start.5 = (bf16[128,2560]{1,0:T(8,128)(2,1)S(1)}, bf16[128,2560]{1,0:T(8,128)(2,1)}, u32[]{:S(2)}) copy-start(bf16[128,2560]{1,0:T(8,128)(2,1)} %param.7) | copy-start | bytes 1966084
  7.2 43.4 %all-gather.2.cloned.1.call-start = ((), (), s32[]{:S(2)}) async-start(), calls=%async_computation.4 | async-start | bytes 3440640 | tf_op jit(solution)/shard_map/all_gather | solution.py:433
  11.5 0.6 copy-start.13
  14.3 56.7 %all-to-all-start = ((bf16[16,24,2688]{2,1,0:T(8,128)(2,1)}), bf16[16,24,2688]{2,1,0:T(8,128)(2,1)}, u32[]{:S(2)}, u32[]{:S(2)}) async-start(bf16[16,24,2688]{2,1,0:T(8,128)(2,1)} %bitcast.2), calls=%async_computation | async-start | bytes 4128768 | tf_op jit(solution)/shard_map/all_to_all | solution.py:446
  52.5 3.2 collective-permute-start
  53.2 2.8 collective-permute-start.1
  53.3 3.6 %collective-permute-start.2 = (bf16[128,2688]{1,0:T(8,128)(2,1)S(1)}, bf16[128,2688]{1,0:T(8,128)(2,1)S(1)}, u32[]{:S(2)}, u32[]{:S(2)}) collective-permute-start(bf16[128,2688]{1,0:T(8,128)(2,1)S(1)} %get-tuple-element.63), channel_id=1, source_target_pairs={{0,1},{1,0},{2,3},{3,2},{4,5},{5,4},{6,7},{7,6},{8,9},{9,8},{10,11... | collective-permute-start | bytes 2064392 | tf_op jit(solution)/shard_map/ppermute | solution.py:38
  53.7 4.2 %collective-permute-start.3 = (bf16[128,2688]{1,0:T(8,128)(2,1)S(1)}, bf16[128,2688]{1,0:T(8,128)(2,1)S(1)}, u32[]{:S(2)}, u32[]{:S(2)}) collective-permute-start(bf16[128,2688]{1,0:T(8,128)(2,1)S(1)} %get-tuple-element.62), channel_id=1, source_target_pairs={{0,1},{1,0},{2,3},{3,2},{4,5},{5,4},{6,7},{7,6},{8,9},{9,8},{10,11... | collective-permute-start | bytes 2064392 | tf_op jit(solution)/shard_map/ppermute | solution.py:38
  55.6 4.4 %copy-start.1 = (bf16[128,2688]{1,0:T(8,128)(2,1)}, bf16[128,2688]{1,0:T(8,128)(2,1)S(1)}, u32[]{:S(2)}) copy-start(bf16[128,2688]{1,0:T(8,128)(2,1)S(1)} %collective-permute-done.refs_8_.refs_4_) | copy-start | bytes 2064388
  56.0 4.1 %copy-start.2 = (bf16[128,2688]{1,0:T(8,128)(2,1)}, bf16[128,2688]{1,0:T(8,128)(2,1)S(1)}, u32[]{:S(2)}) copy-start(bf16[128,2688]{1,0:T(8,128)(2,1)S(1)} %collective-permute-done.1.refs_9_.refs_5_) | copy-start | bytes 2064388
  57.0 3.1 copy-start.3
  57.9 2.1 copy-start.4
  71.0 4.4 %collective-permute-start.4 = (bf16[384,2688]{1,0:T(8,128)(2,1)}, bf16[384,2688]{1,0:T(8,128)(2,1)S(1)}, u32[]{:S(2)}, u32[]{:S(2)}) collective-permute-start(bf16[384,2688]{1,0:T(8,128)(2,1)} %bitcast.3.refs_4_.refs_6_), channel_id=1, source_target_pairs={{0,1},{1,0},{2,3},{3,2},{4,5},{5,4},{6,7},{7,6},{8,9},{9,8},{10,11... | collective-permute-start | bytes 6193160 | tf_op jit(solution)/shard_map/ppermute | solution.py:38
  75.4 1.4 copy-start.17
  85.0 33.9 %collective-permute-start.5 = (bf16[288,2560]{1,0:T(8,128)(2,1)}, bf16[288,2560]{1,0:T(8,128)(2,1)S(1)}, u32[]{:S(2)}, u32[]{:S(2)}) collective-permute-start(bf16[288,2560]{1,0:T(8,128)(2,1)} %get-tuple-element.40), channel_id=1, source_target_pairs={{0,2},{1,3},{2,0},{3,1},{4,6},{5,7},{6,4},{7,5},{8,10},{9,11},{10,... | collective-permute-start | bytes 4423688 | tf_op jit(solution)/shard_map/ppermute | solution.py:38
  85.4 65.4 %collective-permute-start.6 = (bf16[288,2560]{1,0:T(8,128)(2,1)}, bf16[288,2560]{1,0:T(8,128)(2,1)S(1)}, u32[]{:S(2)}, u32[]{:S(2)}) collective-permute-start(bf16[288,2560]{1,0:T(8,128)(2,1)} %get-tuple-element.41), channel_id=1, source_target_pairs={{0,4},{1,5},{2,6},{3,7},{4,0},{5,1},{6,2},{7,3},{8,12},{9,13},{10,... | collective-permute-start | bytes 4423688 | tf_op jit(solution)/shard_map/ppermute | solution.py:38
  86.8 66.0 %collective-permute-start.7 = (bf16[288,2560]{1,0:T(8,128)(2,1)}, bf16[288,2560]{1,0:T(8,128)(2,1)}, u32[]{:S(2)}, u32[]{:S(2)}) collective-permute-start(bf16[288,2560]{1,0:T(8,128)(2,1)} %get-tuple-element.42), channel_id=1, source_target_pairs={{0,6},{1,7},{2,4},{3,5},{4,2},{5,3},{6,0},{7,1},{8,14},{9,15},{10,... | collective-permute-start | bytes 4423688 | tf_op jit(solution)/shard_map/ppermute | solution.py:38
  89.0 92.8 %all-to-all-start.1 = ((bf16[16,72,2560]{2,1,0:T(8,128)(2,1)}), bf16[16,72,2560]{2,1,0:T(8,128)(2,1)}, u32[]{:S(2)}, u32[]{:S(2)}) async-start(bf16[16,72,2560]{2,1,0:T(8,128)(2,1)} %bitcast.25), calls=%async_computation.1 | async-start | bytes 11796480 | tf_op jit(solution)/shard_map/all_to_all | solution.py:451
  118.9 33.9 %copy-start.18 = (bf16[288,2560]{1,0:T(8,128)(2,1)}, bf16[288,2560]{1,0:T(8,128)(2,1)S(1)}, u32[]{:S(2)}) copy-start(bf16[288,2560]{1,0:T(8,128)(2,1)S(1)} %collective-permute-done.5.refs_2_) | copy-start | bytes 4423684
  150.8 2.0 copy-start.19
  203.0 6.7 %copy-start.10 = (f32[16,1024]{1,0:T(8,128)S(1)}, f32[16,1024]{1,0:T(8,128)}, u32[]{:S(2)}) copy-start(f32[16,1024]{1,0:T(8,128)} %get-tuple-element.36) | copy-start | bytes 196612
  203.0 7.5 %copy-start.9 = (f32[16,1024]{1,0:T(8,128)S(1)}, f32[16,1024]{1,0:T(8,128)}, u32[]{:S(2)}) copy-start(f32[16,1024]{1,0:T(8,128)} %get-tuple-element.37) | copy-start | bytes 196612
  203.0 42.8 %all-to-all-start.2 = ((bf16[16,72,1280]{2,1,0:T(8,128)(2,1)}), bf16[16,72,1280]{2,1,0:T(8,128)(2,1)S(1)}, u32[]{:S(2)}, u32[]{:S(2)}) async-start(bf16[16,72,1280]{2,1,0:T(8,128)(2,1)} %bitcast.28), calls=%async_computation.2 | async-start | bytes 5898240 | tf_op jit(solution)/shard_map/all_to_all | solution.py:465
  225.2 36.9 %collective-permute-start.10 = (bf16[288,1408]{1,0:T(8,128)(2,1)}, bf16[288,1408]{1,0:T(8,128)(2,1)}, u32[]{:S(2)}, u32[]{:S(2)}) collective-permute-start(bf16[288,1408]{1,0:T(8,128)(2,1)} %get-tuple-element.49), channel_id=1, source_target_pairs={{0,2},{1,3},{2,0},{3,1},{4,6},{5,7},{6,4},{7,5},{8,10},{9,11},{10,... | collective-permute-start | bytes 2433032 | tf_op jit(solution)/shard_map/ppermute | solution.py:38
  225.2 36.9 %collective-permute-start.11 = (bf16[288,1408]{1,0:T(8,128)(2,1)}, bf16[288,1408]{1,0:T(8,128)(2,1)}, u32[]{:S(2)}, u32[]{:S(2)}) collective-permute-start(bf16[288,1408]{1,0:T(8,128)(2,1)} %get-tuple-element.50), channel_id=1, source_target_pairs={{0,4},{1,5},{2,6},{3,7},{4,0},{5,1},{6,2},{7,3},{8,12},{9,13},{10,... | collective-permute-start | bytes 2433032 | tf_op jit(solution)/shard_map/ppermute | solution.py:38
  227.0 35.2 %collective-permute-start.12 = (bf16[288,1408]{1,0:T(8,128)(2,1)}, bf16[288,1408]{1,0:T(8,128)(2,1)}, u32[]{:S(2)}, u32[]{:S(2)}) collective-permute-start(bf16[288,1408]{1,0:T(8,128)(2,1)} %get-tuple-element.51), channel_id=1, source_target_pairs={{0,6},{1,7},{2,4},{3,5},{4,2},{5,3},{6,0},{7,1},{8,14},{9,15},{10,... | collective-permute-start | bytes 2433032 | tf_op jit(solution)/shard_map/ppermute | solution.py:38
  245.8 1.6 copy-start
  247.4 12.9 %copy-start.16 = (f32[2,8,384]{2,1,0:T(8,128)S(1)}, f32[2,8,384]{2,1,0:T(8,128)}, u32[]{:S(2)}) copy-start(f32[2,8,384]{2,1,0:T(8,128)} %get-tuple-element.34) | copy-start | bytes 73732
  247.4 13.8 %copy-start.15 = (f32[2,8,384]{2,1,0:T(8,128)S(1)}, f32[2,8,384]{2,1,0:T(8,128)}, u32[]{:S(2)}) copy-start(f32[2,8,384]{2,1,0:T(8,128)} %get-tuple-element.35) | copy-start | bytes 73732
  256.0 6.2 %collective-permute-start.8 = (bf16[256,1280]{1,0:T(8,128)(2,1)}, bf16[256,1280]{1,0:T(8,128)(2,1)S(1)}, u32[]{:S(2)}, u32[]{:S(2)}) collective-permute-start(bf16[256,1280]{1,0:T(8,128)(2,1)} %get-tuple-element.54), channel_id=1, source_target_pairs={{0,1},{1,0},{2,3},{3,2},{4,5},{5,4},{6,7},{7,6},{8,9},{9,8},{10,11... | collective-permute-start | bytes 1966088 | tf_op jit(solution)/shard_map/ppermute | solution.py:38
  260.0 2.9 collective-permute-start.9
  262.2 0.8 copy-start.6
  262.8 0.8 copy-start.7
  271.2 6.3 %collective-permute-start.13 = (bf16[384,1408]{1,0:T(8,128)(2,1)}, bf16[384,1408]{1,0:T(8,128)(2,1)S(1)}, u32[]{:S(2)}, u32[]{:S(2)}) collective-permute-start(bf16[384,1408]{1,0:T(8,128)(2,1)} %get-tuple-element.57), channel_id=1, source_target_pairs={{0,1},{1,0},{2,3},{3,2},{4,5},{5,4},{6,7},{7,6},{8,9},{9,8},{10,11... | collective-permute-start | bytes 3244040 | tf_op jit(solution)/shard_map/ppermute | solution.py:38
  280.3 6.8 %copy-start.22 = (bf16[128,1280]{1,0:T(8,128)(2,1)S(1)}, bf16[128,1280]{1,0:T(8,128)(2,1)}, u32[]{:S(2)}) copy-start(bf16[128,1280]{1,0:T(8,128)(2,1)} %get-tuple-element.59) | copy-start | bytes 983044
  280.3 6.9 %copy-start.21 = (bf16[128,1280]{1,0:T(8,128)(2,1)S(1)}, bf16[128,1280]{1,0:T(8,128)(2,1)}, u32[]{:S(2)}) copy-start(bf16[128,1280]{1,0:T(8,128)(2,1)} %get-tuple-element.60) | copy-start | bytes 983044
  280.4 10.2 %copy-start.20 = (bf16[128,1280]{1,0:T(8,128)(2,1)S(1)}, bf16[128,1280]{1,0:T(8,128)(2,1)}, u32[]{:S(2)}) copy-start(bf16[128,1280]{1,0:T(8,128)(2,1)} %get-tuple-element.61) | copy-start | bytes 983044
  280.4 26.4 %copy-start.8 = (bf16[128,1280]{1,0:T(8,128)(2,1)S(1)}, bf16[128,1280]{1,0:T(8,128)(2,1)}, u32[]{:S(2)}) copy-start(bf16[128,1280]{1,0:T(8,128)(2,1)} %get-tuple-element.58) | copy-start | bytes 983044
  280.4 26.6 %copy-start.14 = (f32[16,128]{1,0:T(8,128)S(1)}, f32[16,128]{1,0:T(8,128)}, u32[]{:S(2)}) copy-start(f32[16,128]{1,0:T(8,128)} %copy-done.13) | copy-start | bytes 24580
  280.4 26.6 %all-to-all-start.3 = ((bf16[16,24,1408]{2,1,0:T(8,128)(2,1)}), bf16[16,24,1408]{2,1,0:T(8,128)(2,1)S(1)}, u32[]{:S(2)}, u32[]{:S(2)}) async-start(bf16[16,24,1408]{2,1,0:T(8,128)(2,1)} %bitcast.16), calls=%async_computation.3 | async-start | bytes 2162688 | tf_op jit(solution)/shard_map/all_to_all | solution.py:471
  287.2 8.7 %collective-permute-start.14 = (bf16[128,1280]{1,0:T(8,128)(2,1)S(1)}, bf16[128,1280]{1,0:T(8,128)(2,1)S(1)}, u32[]{:S(2)}, u32[]{:S(2)}) collective-permute-start(bf16[128,1280]{1,0:T(8,128)(2,1)S(1)} %copy-done.22), channel_id=1, source_target_pairs={{0,2},{1,3},{2,0},{3,1},{4,6},{5,7},{6,4},{7,5},{8,10},{9,11},{10,... | collective-permute-start | bytes 983048 | tf_op jit(solution)/shard_map/ppermute | solution.py:38
  287.3 17.4 %collective-permute-start.15 = (bf16[128,1280]{1,0:T(8,128)(2,1)S(1)}, bf16[128,1280]{1,0:T(8,128)(2,1)S(1)}, u32[]{:S(2)}, u32[]{:S(2)}) collective-permute-start(bf16[128,1280]{1,0:T(8,128)(2,1)S(1)} %copy-done.21), channel_id=1, source_target_pairs={{0,4},{1,5},{2,6},{3,7},{4,0},{5,1},{6,2},{7,3},{8,12},{9,13},{10,... | collective-permute-start | bytes 983048 | tf_op jit(solution)/shard_map/ppermute | solution.py:38
  290.5 16.2 %collective-permute-start.16 = (bf16[128,1280]{1,0:T(8,128)(2,1)S(1)}, bf16[128,1280]{1,0:T(8,128)(2,1)S(1)}, u32[]{:S(2)}, u32[]{:S(2)}) collective-permute-start(bf16[128,1280]{1,0:T(8,128)(2,1)S(1)} %copy-done.20), channel_id=1, source_target_pairs={{0,6},{1,7},{2,4},{3,5},{4,2},{5,3},{6,0},{7,1},{8,14},{9,15},{10,... | collective-permute-start | bytes 983048 | tf_op jit(solution)/shard_map/ppermute | solution.py:38
  306.8 0.7 copy-start.12
Sparse Core Ops, SparseCore 0:
  11.0 39.5 all-gather.1

commit v3 on v2

v3 whole, which is shorter than its diff:
```python
import jax
import jax.numpy as jnp
from jax import lax
from jax.experimental import pallas as pl
from jax.experimental.pallas import tpu as pltpu
from jax.sharding import PartitionSpec as P

BF = jnp.bfloat16
F32 = jnp.float32
LANES = 128
VMEM_MIB = 60


def dot(a, b):
    return jnp.dot(a, b, preferred_element_type=F32)


def dot_t(a, b):
    return lax.dot_general(a, b, (((0,), (0,)), ((), ())), preferred_element_type=F32)


def dot_nt(a, b):
    return lax.dot_general(a, b, (((1,), (1,)), ((), ())), preferred_element_type=F32)


def earlier_counts(names):
    n = names.shape[-2]
    lower = (jnp.arange(n)[:, None] > jnp.arange(n)[None, :]).astype(BF)
    counts = jnp.einsum("ij,...jm->...im", lower, names.astype(BF), preferred_element_type=F32)
    return jnp.where(names, counts, -1.0)


def barrier(*values):
    return lax.optimization_barrier(values)


def swap(x, k):
    return lax.ppermute(x, "exp", [(i, i ^ k) for i in range(lax.axis_size("exp"))])


def exchange(blocks, step=1):
    return [blocks[0]] + [swap(block, step * k) for k, block in enumerate(blocks) if k]


def whole(shape, at=(0, 0)):
    return pl.BlockSpec(shape, lambda *_: at, pipeline_mode=pl.Buffered(1))


def params(mib):
    return pltpu.CompilerParams(vmem_limit_bytes=mib * 2**20)


def cost(flops, nbytes):
    return pl.CostEstimate(flops=flops, bytes_accessed=nbytes, transcendentals=0)


def window_tables(n_seq, n_exp, cap):
    pair = 2 * n_exp * cap
    d = jnp.arange(pair)
    source = d % (n_exp * cap) // cap * 32 + d // (n_exp * cap) * cap + d % cap
    i = jnp.arange(n_seq // 2)
    at = source[None, :] + (2 * cap - 16) * i[:, None]
    wide = jnp.arange(32 * n_exp)
    to_b = (at[:, :, None] == wide[None, None, :]).astype(BF)
    to_a = (at[:, None, :] == wide[None, :, None]).astype(BF)
    return to_b, to_a


def pre_kernel(n_exp, pairs, table, *refs):
    blocks, (gate, up, out_gate, out_up, rows) = refs[:n_exp], refs[n_exp:]
    size = table.shape[1]

    @pl.when(pl.program_id(0) == 0)
    def _():
        for i in range(pairs):
            window = jnp.concatenate([b[16 * i:16 * i + 32, :] for b in blocks], axis=0)
            rows[size * i:size * (i + 1), :] = dot(table[i], window).astype(BF)

    out_gate[...] = dot(rows[...], gate[...])
    out_up[...] = dot(rows[...], up[...])


def pre_products(table, blocks, gate_mat, up_mat):
    chips, pairs = len(blocks), table.shape[0]
    rows, features = blocks[0].shape
    total, units = rows * chips, gate_mat.shape[1]
    wide = 256 if units % 256 == 0 else units
    column = pl.BlockSpec((features, wide), lambda j: (0, j))
    result = pl.BlockSpec((total, wide), lambda j: (0, j))
    return pl.pallas_call(
        lambda *refs: pre_kernel(chips, pairs, *refs),
        grid=(units // wide,),
        in_specs=[whole(table.shape, (0, 0, 0))] + [whole((rows, features))] * chips + [column, column],
        out_specs=[result, result],
        out_shape=[jax.ShapeDtypeStruct((total, units), F32)] * 2,
        scratch_shapes=[pltpu.VMEM((total, features), BF)],
        compiler_params=params(VMEM_MIB),
        cost_estimate=cost(4 * total * features * units, 2 * total * features + 4 * features * units + 8 * total * units),
        name="pre_products",
    )(table, *blocks, gate_mat, up_mat)


def grad_kernel(steps, lane, grad, down, pre_gate, pre_up, gate_mat, up_mat, out_gate, out_up, out_dot, out, all_gate, all_up):
    i = pl.program_id(0)
    tall = grad.shape[0]

    @pl.when(i < steps)
    def _():
        grad_hidden = dot_nt(grad[...], down[...])
        gate, up = pre_gate[...], pre_up[...]
        sigmoid = jax.nn.sigmoid(gate)
        active = gate * sigmoid
        hidden = (active * up).astype(BF).astype(F32)
        gate_dot = jnp.sum(hidden * grad_hidden, axis=1, keepdims=True)
        out_dot[...] = (gate_dot * lane[0:1, :]).astype(BF)
        rows = pl.ds(pl.multiple_of(i * tall, tall), tall)
        grad_gate = (grad_hidden * up * sigmoid * (1.0 + gate * (1.0 - sigmoid))).astype(BF)
        grad_up = (grad_hidden * active).astype(BF)
        out_gate[...] = grad_gate
        out_up[...] = grad_up
        all_gate[rows, :] = grad_gate
        all_up[rows, :] = grad_up

    @pl.when(i >= steps)
    def _():
        out[...] = (dot_nt(all_gate[...], gate_mat[...]) + dot_nt(all_up[...], up_mat[...])).astype(BF)


def hidden_grads(lane, rows_grad, down_mat, pre_gate, pre_up, gate_mat, up_mat):
    total, features = rows_grad.shape
    units, half, steps = down_mat.shape[0], features // 2, 4
    tall = total // steps
    wide = 256 if half % 256 == 0 else half
    row = lambda width: pl.BlockSpec((tall, width), lambda i: (jnp.minimum(i, steps - 1), 0))
    mat = pl.BlockSpec((wide, units), lambda i: (half // wide + jnp.maximum(i - steps, 0), 0))
    return pl.pallas_call(
        lambda *refs: grad_kernel(steps, *refs),
        grid=(steps + half // wide,),
        in_specs=[whole(lane.shape), row(features), whole(down_mat.shape), row(units), row(units), mat, mat],
        out_specs=[row(units), row(units), row(LANES),
                   pl.BlockSpec((total, wide), lambda i: (0, jnp.maximum(i - steps, 0)))],
        out_shape=[jax.ShapeDtypeStruct((total, units), BF)] * 2
        + [jax.ShapeDtypeStruct((total, LANES), BF), jax.ShapeDtypeStruct((total, half), BF)],
        scratch_shapes=[pltpu.VMEM((total, units), BF)] * 2,
        compiler_params=params(VMEM_MIB),
        cost_estimate=cost(4 * total * features * units, 4 * total * features + 4 * features * units + 12 * total * units),
        name="hidden_grads",
    )(lane, rows_grad, down_mat, pre_gate, pre_up, gate_mat, up_mat)


def back_a_kernel(n_exp, pairs, table, grad_gate, grad_up, gate, up, gate_dot, *outs):
    wide = gate.shape[0]
    half = outs[0].shape[1] - LANES
    size = table.shape[2]

    def reorder(values, start, width):
        before = None
        for i in range(pairs):
            moved = dot(table[i], values[size * i:size * (i + 1), :])
            for k in range(n_exp):
                part = moved[32 * k:32 * k + 16, :]
                if before is not None:
                    part = part + before[32 * k + 16:32 * k + 32, :]
                outs[k][16 * i:16 * i + 16, pl.ds(start, width)] = part.astype(BF)
            before = moved
        for k in range(n_exp):
            part = before[32 * k + 16:32 * k + 32, :]
            outs[k][16 * pairs:16 * pairs + 16, pl.ds(start, width)] = part.astype(BF)

    j = pl.program_id(0)
    values = dot_nt(grad_gate[...], gate[...]) + dot_nt(grad_up[...], up[...])
    reorder(values.astype(BF), pl.multiple_of(j * wide, wide), wide)

    @pl.when(j == 0)
    def _():
        reorder(gate_dot[...], half, LANES)


def returned_a(table, grad_gate, grad_up, gate_mat, up_mat, gate_dot, n_exp):
    total, units = grad_gate.shape
    half = gate_mat.shape[0] // 2
    pairs = table.shape[0]
    wide = 256 if half % 256 == 0 else half
    mat = pl.BlockSpec((wide, units), lambda j: (j, 0))
    block = (total // n_exp, half + LANES)
    return pl.pallas_call(
        lambda *refs: back_a_kernel(n_exp, pairs, *refs),
        grid=(half // wide,),
        in_specs=[whole(table.shape, (0, 0, 0)), whole(grad_gate.shape), whole(grad_up.shape), mat, mat, whole(gate_dot.shape)],
        out_specs=[whole(block)] * n_exp,
        out_shape=[jax.ShapeDtypeStruct(block, BF)] * n_exp,
        compiler_params=params(VMEM_MIB),
        cost_estimate=cost(4 * total * half * units, 4 * half * units + 4 * total * units + 2 * total * half),
        name="returned_a",
    )(table, grad_gate, grad_up, gate_mat, up_mat, gate_dot)


def sum_kernel(n_exp, slot, weight, mine, first, last, *refs):
    blocks, out, column = refs[:n_exp], refs[n_exp], refs[n_exp + 1:]
    n_tok, chips = column[0].shape[0], len(column)
    for a, total in enumerate(column):
        half, at = (first, a) if 2 * a < chips else (last, a - chips // 2)
        other = half[n_tok * at:n_tok * (at + 1), :].astype(F32)
        total[...] = (mine[n_tok * a:n_tok * (a + 1), :] + other).astype(BF)
    half = out.shape[1] - LANES
    place = lax.broadcasted_iota(jnp.int32, (slot.shape[0], blocks[0].shape[0]), 1).astype(F32)
    sums = jnp.zeros((slot.shape[0], half), F32)
    gates = jnp.zeros((slot.shape[0], LANES), F32)
    for k in range(n_exp):
        hot = slot[:, k:k + 1] == place
        sums += dot(jnp.where(hot, weight[:, k:k + 1], 0.0).astype(BF), blocks[k][:, :half])
        gates += dot(jnp.where(hot, 1.0, 0.0).astype(BF), blocks[k][:, half:])
    out[:, :half] = sums.astype(BF)
    out[:, half:] = gates.astype(BF)


def group_sums(slot, weight, mine, first, last, blocks):
    n_exp = len(blocks)
    shape = (slot.shape[0], blocks[0].shape[1])
    column = (2 * mine.shape[0] // n_exp, mine.shape[1])
    return pl.pallas_call(
        lambda *refs: sum_kernel(n_exp, *refs),
        grid=(1,),
        in_specs=[whole(x.shape) for x in (slot, weight, mine, first, last)] + [whole(blocks[0].shape)] * n_exp,
        out_specs=[whole(shape)] + [whole(column)] * (n_exp // 2),
        out_shape=[jax.ShapeDtypeStruct(shape, BF)] + [jax.ShapeDtypeStruct(column, BF)] * (n_exp // 2),
        compiler_params=params(VMEM_MIB),
        cost_estimate=cost(2 * shape[0] * blocks[0].size * n_exp, 2 * n_exp * blocks[0].size),
        name="group_sums",
    )(slot, weight, mine, first, last, *blocks)


def named_here(top, eye, meta, local):
    flat = dot_nt(eye[...], meta)
    named = weight = jnp.zeros((local.shape[0], flat.shape[1]), F32)
    for k in range(top):
        hit = flat[k:k + 1, :] == local[:, 0:1]
        named += jnp.where(hit, 1.0, 0.0)
        weight += jnp.where(hit, flat[top + k:top + k + 1, :], 0.0)
    return named, weight


def hub_kernel(top, cap, eye, local, before, block, meta, hub, *outs):
    *blocks, out_slot, out_weight, puts = outs
    rows, n_rows = blocks[0].shape[0], hub.shape[0]

    @pl.when(pl.program_id(0) == 0)
    def _():
        named, out_weight[...] = named_here(top, eye, meta[...], local)
        slot = jnp.where(named > 0.0, block[0:1, :] * cap + dot(named.astype(BF), before[...]), -1.0)
        out_slot[...] = slot
        place = lax.broadcasted_iota(jnp.int32, (rows, n_rows), 0).astype(F32)
        for k in range(len(blocks)):
            puts[rows * k:rows * (k + 1), :] = jnp.where(place == slot[k:k + 1, :], 1.0, 0.0).astype(BF)

    placed = dot(puts[...], hub[...]).astype(BF)
    for k, out in enumerate(blocks):
        out[...] = placed[rows * k:rows * (k + 1), :]


def lower_counts(total, size):
    at = jnp.arange(total)
    same = at[:, None] // size == at[None, :] // size
    return (same & (at[:, None] < at[None, :])).astype(BF), jnp.broadcast_to((at // size).astype(F32), (8, total))


def hub_blocks(hub, local, per_group, top, cap):
    n_rows, width = hub.shape
    n_exp = local.shape[0]
    before, block = lower_counts(n_rows, per_group)
    features = width - LANES
    wide = 512 if features % 512 == 0 else features
    shape = (n_rows // per_group * cap, features)
    row = (n_exp, n_rows)
    eye = jnp.eye(LANES, dtype=BF)
    part = lambda rows: pl.BlockSpec((rows, wide), lambda j: (0, j))
    *blocks, slot, weight = pl.pallas_call(
        lambda *refs: hub_kernel(top, cap, *refs),
        grid=(features // wide,),
        in_specs=[whole(x.shape) for x in (eye, local, before, block)]
        + [whole((n_rows, LANES), (0, features // LANES)), part(n_rows)],
        out_specs=[part(shape[0])] * n_exp + [whole(row)] * 2,
        out_shape=[jax.ShapeDtypeStruct(shape, BF)] * n_exp + [jax.ShapeDtypeStruct(row, F32)] * 2,
        scratch_shapes=[pltpu.VMEM((shape[0] * n_exp, n_rows), BF)],
        compiler_params=params(VMEM_MIB),
        cost_estimate=cost(2 * shape[0] * n_exp * n_rows * width, 2 * n_exp * shape[0] * shape[1]),
        name="hub_blocks",
    )(eye, local, before, block, hub, hub)
    return blocks, slot.T, weight.T


def column_block(k, member, n_tok, column):
    return column[pl.ds(pl.multiple_of((member[0] ^ k) * n_tok, n_tok), n_tok), :]


def slots_kernel(top, n_exp, cap, member, eye, theirs, before, start, spread, place, meta, out_hot, out_slot, out_weight):
    n_tok = before.shape[0]
    parts = [column_block(k, member, n_tok, meta) for k in range(n_exp)]
    named, out_weight[...] = named_here(top, eye, jnp.concatenate(parts, axis=0), theirs)
    counts = [dot(named[:, at:at + n_tok].astype(BF), before[...]) for at in range(0, named.shape[1], n_tok)]
    rank = jnp.concatenate(counts, axis=1)
    out_slot[...] = jnp.where(named > 0.0, start[0:1, :] + rank, -1.0)
    rank = jnp.where(named > 0.0, rank, -1.0).astype(BF)
    size = spread.shape[0]
    for k in range(n_exp):
        hot = dot(spread[...], rank[:, n_tok * k:n_tok * (k + 1)]) == place[:, 0:1]
        out_hot[size * k:size * (k + 1), :] = jnp.where(hot, 1.0, 0.0).astype(BF)


def column_slots(meta, theirs, member, n_tok, top, cap):
    total = meta.shape[0]
    n_seq, n_exp = theirs.shape[0], total // n_tok
    before, block = lower_counts(n_tok, n_tok)
    start = jnp.broadcast_to((jnp.arange(total) // n_tok * cap).astype(F32), (8, total))
    at = jnp.arange(n_seq * cap)
    spread = (at[:, None] // cap == jnp.arange(n_seq)[None, :]).astype(BF)
    place = jnp.broadcast_to((at % cap).astype(F32)[:, None], (n_seq * cap, LANES))
    eye = jnp.eye(LANES, dtype=BF)
    shapes = (n_seq * n_exp * cap, n_tok), (n_seq, total), (n_seq, total)
    inputs = (eye, theirs, before, start, spread, place, meta)
    hot, slot, weight = pl.pallas_call(
        lambda *refs: slots_kernel(top, n_exp, cap, *refs),
        grid=(1,),
        in_specs=[pl.BlockSpec(memory_space=pltpu.SMEM)] + [whole(x.shape) for x in inputs],
        out_specs=[whole(shape) for shape in shapes],
        out_shape=[jax.ShapeDtypeStruct(shape, kind) for shape, kind in zip(shapes, (BF, F32, F32))],
        compiler_params=params(VMEM_MIB),
        cost_estimate=cost(4 * total * LANES * LANES, 2 * shapes[0][0] * n_tok),
        name="column_slots",
    )(member.reshape(1), *inputs)
    return hot, slot.T, weight.T


def rows_kernel(n_exp, member, table, hot, column, out):
    pairs, size = table.shape[:2]
    n_tok = hot.shape[1]
    blocks = []
    for k in range(n_exp):
        blocks.append(dot(hot[size * k:size * (k + 1), :], column_block(k, member, n_tok, column)).astype(BF))
    for i in range(pairs):
        window = jnp.concatenate([b[16 * i:16 * i + 32, :] for b in blocks], axis=0)
        out[size * i:size * (i + 1), :] = dot(table[i], window).astype(BF)


def column_rows(member, table, hot, column, n_exp):
    total, features = hot.shape[0], column.shape[1]
    wide = 512 if features % 512 == 0 else features
    part = lambda rows: pl.BlockSpec((rows, wide), lambda j: (0, j))
    return pl.pallas_call(
        lambda *refs: rows_kernel(n_exp, *refs),
        grid=(features // wide,),
        in_specs=[pl.BlockSpec(memory_space=pltpu.SMEM), whole(table.shape, (0, 0, 0)), whole(hot.shape),
                  part(column.shape[0])],
        out_specs=part(total),
        out_shape=jax.ShapeDtypeStruct((total, features), BF),
        compiler_params=params(VMEM_MIB),
        cost_estimate=cost(2 * total * hot.shape[1] * LANES, 2 * total * LANES),
        name="column_rows",
    )(member.reshape(1), table, hot, column)


def column_kernel(n_exp, place, spread, slot, weight, got, out_mine, out_first, out_last, mixed):
    n_tok = out_mine.shape[0] // (n_exp // 2)

    @pl.when(pl.program_id(0) == 0)
    def _():
        hot = dot(slot[...], spread[...]) == place[0:1, :]
        mixed[...] = jnp.where(hot, dot(weight[...], spread[...]), 0.0).astype(BF)

    sums = dot(mixed[...], got[...])
    for k in range(0, n_exp, 2):
        at = slice(n_tok * k // 2, n_tok * (k // 2 + 1))
        out_mine[at, :] = sums[n_tok * k:n_tok * (k + 1), :]
        out, at = (out_first, k) if 2 * k < n_exp else (out_last, k - n_exp // 2)
        out[n_tok * at // 2:n_tok * (at // 2 + 1), :] = sums[n_tok * (k + 1):n_tok * (k + 2), :].astype(BF)


def column_sums(slot, weight, got, n_exp):
    n_rows, n_seq = slot.shape
    total, half = got.shape
    at = jnp.arange(total)
    place = jnp.broadcast_to((at % (total // n_seq)).astype(F32), (8, total))
    spread = (jnp.arange(n_seq)[:, None] == at[None, :] // (total // n_seq)).astype(BF)
    shape = (n_rows // 2, half)
    wide = 256 if half % 256 == 0 else half
    part = lambda rows: pl.BlockSpec((rows, wide), lambda j: (0, j))
    return pl.pallas_call(
        lambda *refs: column_kernel(n_exp, *refs),
        grid=(half // wide,),
        in_specs=[whole(place.shape), whole(spread.shape), whole(slot.shape), whole(weight.shape), part(total)],
        out_specs=[part(shape[0])] + [part(shape[0] // 2)] * 2,
        out_shape=[jax.ShapeDtypeStruct(shape, F32)] + [jax.ShapeDtypeStruct((shape[0] // 2, half), BF)] * 2,
        scratch_shapes=[pltpu.VMEM((n_rows, total), BF)],
        compiler_params=params(VMEM_MIB),
        cost_estimate=cost(400 * n_rows * total * half, 2 * total * half + 3 * n_rows * half),
        name="column_sums",
    )(place, spread, slot.astype(BF), weight.astype(BF), got)


def per_device(hidden_in, grad_out, expert_ids, gate_weights, w_gate, w_up, w_down):
    n_tok, features = hidden_in.shape
    top = expert_ids.shape[1]
    n_seq, n_exp = lax.axis_size("seq"), lax.axis_size("exp")
    group, member = lax.axis_index("seq"), lax.axis_index("exp")
    experts = n_seq * n_exp
    cap = 3 * top * n_tok // (2 * experts)
    per_group = top // 2 * n_tok // n_seq
    half = features // 2
    gate_mat, up_mat, down_mat = w_gate[0], w_up[0], w_down[0]
    partner = member ^ jnp.arange(n_exp)
    to_b, to_a = window_tables(n_seq, n_exp, cap)

    meta = jnp.concatenate(
        (expert_ids.astype(BF), gate_weights.astype(BF), jnp.zeros((n_tok, LANES - 2 * top), BF)), axis=1)

    column_meta = lax.all_gather(meta, "exp", axis=0, tiled=True)
    column = lax.all_gather(grad_out, "exp", axis=0, tiled=True)
    theirs = jnp.broadcast_to((jnp.arange(n_seq) * n_exp + member).astype(F32)[:, None], (n_seq, LANES))
    put_b, slot_b, weight_b = column_slots(column_meta, theirs, member, n_tok, top, cap)
    send_b = column_rows(member, to_b, put_b, column, n_exp)

    group_ids = expert_ids // n_exp
    in_group = jnp.any(group_ids[:, :, None] == jnp.arange(n_seq)[None, None, :], axis=1)
    group_rank = earlier_counts(in_group).T
    pick = (group_rank[:, None, :] == jnp.arange(per_group, dtype=F32)[None, :, None])
    pick = pick.astype(BF).reshape(n_seq * per_group, n_tok)
    send = dot(pick, jnp.concatenate((hidden_in, meta), axis=1)).astype(BF)
    hub = lax.all_to_all(send.reshape(n_seq, per_group, features + LANES), "seq", 0, 0, tiled=True)
    hub = hub.reshape(n_seq * per_group, features + LANES)
    hub, send_b = barrier(hub, send_b)

    rows_b = n_exp * cap
    recv_b = lax.all_to_all(send_b.reshape(n_seq, rows_b, features), "seq", 0, 0, tiled=True)
    recv_b = recv_b.reshape(n_seq * rows_b, features)

    local = jnp.broadcast_to((partner + group * n_exp).astype(F32)[:, None], (n_exp, LANES))
    blocks, slot_a, weight_a = hub_blocks(hub, local, per_group, top, cap)
    rows_in = exchange(blocks)

    pre_gate, pre_up = pre_products(to_b, rows_in, gate_mat, up_mat)
    lane = jnp.broadcast_to((jnp.arange(LANES) == group * n_exp + member).astype(F32), (8, LANES))
    grad_gate, grad_up, gate_dot, back_b = hidden_grads(lane, recv_b, down_mat, pre_gate, pre_up, gate_mat, up_mat)

    back_a = returned_a(to_a, grad_gate, grad_up, gate_mat, up_mat, gate_dot, n_exp)
    got_a = exchange(back_a)
    got_b = lax.all_to_all(back_b.reshape(n_seq, rows_b, half), "seq", 0, 0, tiled=True)
    got_b, *_ = barrier(got_b, *back_a)
    mine, *other = column_sums(slot_b, weight_b, got_b.reshape(n_seq * rows_b, half), n_exp)
    back, *chip = group_sums(slot_a, weight_a, mine, *(swap(x, 1) for x in other), got_a)
    final_b = sum(p.astype(F32) for p in exchange(chip, 2))
    back = lax.all_to_all(back.reshape(n_seq, per_group, half + LANES), "seq", 0, 0, tiled=True)
    final_a = dot_t(pick, back.reshape(n_seq * per_group, half + LANES))

    grad_in = jnp.concatenate((final_a[:, :half], final_b), axis=1).astype(BF)
    table = final_a[:, half:]
    chosen = expert_ids[:, :, None] == jnp.arange(experts)[None, None, :]
    grad_gates = jnp.sum(jnp.where(chosen, table[:, None, :experts], 0.0), axis=2).astype(BF)
    return grad_in, grad_gates


def solution(mesh):
    rows, mats = P(("seq", "exp"), None), P(("seq", "exp"), None, None)
    return jax.shard_map(
        per_device, mesh=mesh, in_specs=(rows,) * 4 + (mats,) * 3, out_specs=(rows, rows), check_vma=False
    )
```

time: 318 us -> 312 us (0.981)
  blocking collectives: 0 us -> 15.6 us
  waiting for transfers between devices: 137 us -> 125 us
  Pallas kernels: 86.3 us -> 83 us
    all_gather x1, waiting for transfers between devices: 26.9 us -> 6 us  [per_device(): column = lax.all_gather(grad_out, 'exp', axis=0, tiled=True)]
    all_gather x0 -> x1, blocking collectives: none -> 15.6 us  [per_device(): column_meta = lax.all_gather(meta, 'exp', axis=0, tiled=True)]
    ppermute x17 -> x19, waiting for transfers between devices: 81.3 us -> 96.2 us  [swap(): lax.ppermute(x, 'exp', [(i, i ^ k) for i in range(lax.axis_size('exp'))])]
    all_to_all x1, waiting for transfers between devices: 12.3 us -> 0.01 us  [per_device(): lax.all_to_all(send_b.reshape(n_seq, rows_b, features), 'seq', 0, 0, tile...]
    all_to_all x1, waiting for transfers between devices: 16.7 us -> 22.3 us  [per_device(): lax.all_to_all(back_b.reshape(n_seq, rows_b, half), 'seq', 0, 0, tiled=True)]
    pallas_call x3 -> x2, Pallas kernels: 28.1 us -> 25.6 us  [the longest x1 18.3 us: hidden_grads(): pl.pallas_call(lambda *refs: grad_kernel(steps, *refs), grid=(steps + hal...]
    ppermute x17 -> x19, starting transfers between devices: 21.6 us -> 21.5 us  [swap(): lax.ppermute(x, 'exp', [(i, i ^ k) for i in range(lax.axis_size('exp'))])]
  transfers between devices with their start and end apart: 22 -> 24, of which waited for: 15 -> 13; matrix products, arithmetic and copies ran while one was open for 5% -> 6% of each run, Pallas kernels for 16% -> 18%
where the time goes in v3:
time: 312 us; the launch traced here: 311 us
  waiting for transfers between devices  125 us (40%)
  Pallas kernels  83 us (27%)
  starting transfers between devices  47.6 us (15%)
  blocking collectives  15.6 us (5%)
  between operations  14.4 us (5%)
  local copies, waits for them, and re-layouts  14.3 us (5%)
  other arithmetic  8.32 us (3%)
    ppermute x19, waiting for transfers between devices, swap(): lax.ppermute(x, 'exp', [(i, i ^ k) for i in range(lax.axis_size('exp'))])  96.2 us
    all_to_all x1, waiting for transfers between devices, per_device(): lax.all_to_all(back_b.reshape(n_seq, rows_b, half), 'seq', 0, 0, tiled=True)  22.3 us
    ppermute x19, starting transfers between devices, swap(): lax.ppermute(x, 'exp', [(i, i ^ k) for i in range(lax.axis_size('exp'))])  21.5 us
    pallas_call x1, Pallas kernels, hidden_grads(): pl.pallas_call(lambda *refs: grad_kernel(steps, *refs), grid=(steps + hal...  18.3 us
    pallas_call x1, Pallas kernels, pre_products(): pl.pallas_call(lambda *refs: pre_kernel(chips, pairs, *refs), grid=(units...  16.6 us
    all_gather x1, blocking collectives, per_device(): column_meta = lax.all_gather(meta, 'exp', axis=0, tiled=True)  15.6 us
    pallas_call x1, Pallas kernels, returned_a(): pl.pallas_call(lambda *refs: back_a_kernel(n_exp, pairs, *refs), grid=(ha...  13.9 us
    pallas_call x1, Pallas kernels, column_sums(): pl.pallas_call(lambda *refs: column_kernel(n_exp, *refs), grid=(half // w...  8.61 us
  transfers between devices with their start and end apart: 24, of which 13 were waited for; matrix products, arithmetic and copies ran while one was open for 6% of the time, Pallas kernels for 18%

profile of v3, /device:TPU:1, one launch (start us, length us, event | category | flops | bytes accessed | tf_op | source)
XLA Modules:
  0.0 311.2 jit_solution(2673150153236236105)
XLA Ops:
  7.2 0.7 all-gather.2.cloned.1.call-update
  7.9 0.8 copy.17
  8.7 0.8 copy.18
  9.6 0.7 add_select_fusion.3
  10.6 1.2 concatenate.11
  11.8 2.0 convolution_convert_fusion
  13.9 8.4 %all-to-all-start = ((bf16[16,24,2688]{2,1,0:T(8,128)(2,1)}), bf16[16,24,2688]{2,1,0:T(8,128)(2,1)S(1)}, u32[]{:S(2)}, u32[]{:S(2)}) async-start(bf16[16,24,2688]{2,1,0:T(8,128)(2,1)} %bitcast.2), calls=%async_computation | async-start | bytes 4128768 | tf_op jit(solution)/shard_map/all_to_all | solution.py:428
  22.5 15.6 %all_gather.6.refs_7_ = bf16[1024,128]{1,0:T(8,128)(2,1)} all-gather(bf16[128,128]{1,0:T(8,128)(2,1)S(1)} %pad_maximum_fusion.1), channel_id=1, replica_groups=mesh['seq'=16,'exp'=8] {'exp'}, dimensions={0}, use_global_device_ids=true | all-gather | bytes 294912 | tf_op jit(solution)/shard_map/all_gather | solution.py:416
  38.1 0.7 fusion.5.refs_5_
  38.8 0.7 fusion.7
  39.5 0.7 broadcast_in_dim.32.refs_2_
  40.1 0.7 broadcast_in_dim.34.refs_6_
  40.9 0.6 broadcast_in_dim.33.refs_4_
  41.5 2.4 column_slots.1
  44.0 1.0 fusion.1.refs_1_.refs_0_
  45.0 6.0 %all-gather.2.cloned.1.call-done.refs_3_ = bf16[1024,2560]{1,0:T(8,128)(2,1)} async-done(((bf16[128,2560]{1,0:T(8,128)(2,1)}), bf16[1024,2560]{1,0:T(8,128)(2,1)}) %all-gather.2.cloned.1.call-update) | async-done | bytes 5242896 | tf_op jit(solution)/shard_map/all_gather | solution.py:417
  51.0 8.5 %column_rows.1 = bf16[1152,2560]{1,0:T(8,128)(2,1)} custom-call(s32[1]{0:T(128)} %bitcast.4.refs_0_, bf16[8,144,256]{2,1,0:T(8,128)(2,1)} %fusion.1.refs_1_.refs_0_, bf16[1152,128]{1,0:T(8,128)(2,1)} %get-tuple-element.40.refs_2_, bf16[1024,2560]{1,0:T(8,128)(2,1)} %all-gather.2.cloned.1.call-done.refs_3_), custom_call_target="tpu_custom_call" | custom-call | flops 37748736 | bytes 294912 | tf_op jit(solution)/shard_map/column_rows/pallas_call | solution.py:349
  59.5 1.3 copy-done.1
  60.9 6.7 %all-to-all-start.1 = ((bf16[16,72,2560]{2,1,0:T(8,128)(2,1)}), bf16[16,72,2560]{2,1,0:T(8,128)(2,1)}, u32[]{:S(2)}, u32[]{:S(2)}) async-start(bf16[16,72,2560]{2,1,0:T(8,128)(2,1)} %bitcast.25), calls=%async_computation.1 | async-start | bytes 11796480 | tf_op jit(solution)/shard_map/all_to_all | solution.py:433
  67.6 0.8 fusion.3.refs_2_
  68.5 0.7 broadcast_in_dim.29.refs_1_
  69.1 0.6 broadcast_in_dim.30.refs_3_
  69.7 7.4 %hub_blocks.1 = (bf16[144,2560]{1,0:T(8,128)(2,1)}, bf16[144,2560]{1,0:T(8,128)(2,1)}, bf16[144,2560]{1,0:T(8,128)(2,1)}, bf16[144,2560]{1,0:T(8,128)(2,1)}, bf1...) custom-call(bf16[128,128]{1,0:T(8,128)(2,1)} %get-tuple-element.78.r, ...), custom_call_target="tpu_custom_call" | custom-call | flops 2378170368 | bytes 5898240 | tf_op jit(solution)/shard_map/hub_blocks/pallas_call | solution.py:277
  77.1 0.6 collective-permute-start
  78.0 1.5 collective-permute-start.2
  79.4 1.4 collective-permute-start.3
  80.9 1.9 collective-permute-start.4
  83.3 12.8 %collective-permute-done.1.refs_3_ = bf16[144,2560]{1,0:T(8,128)(2,1)S(1)} collective-permute-done((bf16[144,2560]{1,0:T(8,128)(2,1)}, bf16[144,2560]{1,0:T(8,128)(2,1)S(1)}, u32[]{:S(2)}, u32[]{:S(2)}) %collective-permute-start.1) | collective-permute-done | bytes 737312 | tf_op jit(solution)/shard_map/ppermute | solution.py:38
  96.1 1.7 collective-permute-start.6
  97.8 15.1 %collective-permute-done.2.refs_4_ = bf16[144,2560]{1,0:T(8,128)(2,1)S(1)} collective-permute-done((bf16[144,2560]{1,0:T(8,128)(2,1)}, bf16[144,2560]{1,0:T(8,128)(2,1)S(1)}, u32[]{:S(2)}, u32[]{:S(2)}) %collective-permute-start.2) | collective-permute-done | bytes 737312 | tf_op jit(solution)/shard_map/ppermute | solution.py:38
  112.8 15.1 %collective-permute-done.3.refs_5_ = bf16[144,2560]{1,0:T(8,128)(2,1)S(1)} collective-permute-done((bf16[144,2560]{1,0:T(8,128)(2,1)}, bf16[144,2560]{1,0:T(8,128)(2,1)S(1)}, u32[]{:S(2)}, u32[]{:S(2)}) %collective-permute-start.3) | collective-permute-done | bytes 737312 | tf_op jit(solution)/shard_map/ppermute | solution.py:38
  128.0 16.0 %collective-permute-done.4.refs_6_ = bf16[144,2560]{1,0:T(8,128)(2,1)} collective-permute-done((bf16[144,2560]{1,0:T(8,128)(2,1)}, bf16[144,2560]{1,0:T(8,128)(2,1)}, u32[]{:S(2)}, u32[]{:S(2)}) %collective-permute-start.4) | collective-permute-done | bytes 737312 | tf_op jit(solution)/shard_map/ppermute | solution.py:38
  144.0 6.2 %collective-permute-done.6.refs_8_ = bf16[144,2560]{1,0:T(8,128)(2,1)} collective-permute-done((bf16[144,2560]{1,0:T(8,128)(2,1)}, bf16[144,2560]{1,0:T(8,128)(2,1)}, u32[]{:S(2)}, u32[]{:S(2)}) %collective-permute-start.6) | collective-permute-done | bytes 737312 | tf_op jit(solution)/shard_map/ppermute | solution.py:38
  150.2 16.6 %pre_products.1 = (f32[1152,768]{1,0:T(8,128)}, f32[1152,768]{1,0:T(8,128)}) custom-call(bf16[8,144,256]{2,1,0:T(8,128)(2,1)} %fusion.1.refs_1_.refs_0_, bf16[144,2560]{1,0:T(8,128)(2,1)} %get-tuple-element.47.refs_1_, bf16[144,2560]{1,0:T(8,128)(2,1)} %copy-done.15, bf16[144,2560]{1,0:T(8,128)(2,1)} %copy-done.16, bf16[144,2560]{1,0:T(8,128)(2,1)} %copy-done.17, ...), custom_call_target="tpu_custom_call" | custom-call | flops 9059696640 | bytes 20840448 | tf_op jit(solution)/shard_map/pre_products/pallas_call | solution.py:90
  166.8 0.6 broadcast_in_dim.36.refs_0_
  167.4 18.3 %hidden_grads.1 = (bf16[1152,768]{1,0:T(8,128)(2,1)}, bf16[1152,768]{1,0:T(8,128)(2,1)}, bf16[1152,128]{1,0:T(8,128)(2,1)}, bf16[1152,1280]{1,0:T(8,128)(2,1)}) custom-call(f32[8,128]{1,0:T(8,128)} %broadcast_in_dim.36.refs_0_, bf16[1152,2560]{1,0:T(8,128)(2,1)} %bitcast.10.refs_1_, bf16[768,2560]{1,0:T(8,128)(2,1)} %bitcast.35, ...), custom_call_target="tpu_custom_call" | custom-call | flops 9059696640 | bytes 30277632 | tf_op jit(solution)/shard_map/hidden_grads/pallas_call | solution.py:136
  185.8 6.7 %all-to-all-start.2 = ((bf16[16,72,1280]{2,1,0:T(8,128)(2,1)}), bf16[16,72,1280]{2,1,0:T(8,128)(2,1)S(1)}, u32[]{:S(2)}, u32[]{:S(2)}) async-start(bf16[16,72,1280]{2,1,0:T(8,128)(2,1)} %bitcast.27), calls=%async_computation.2 | async-start | bytes 5898240 | tf_op jit(solution)/shard_map/all_to_all | solution.py:446
  192.5 0.9 copy.21
  193.4 0.8 copy.22
  194.2 1.3 fusion.refs_0_
  195.6 0.6 fusion.6.refs_1_
  196.2 13.9 %returned_a.1 = (bf16[144,1408]{1,0:T(8,128)(2,1)}, bf16[144,1408]{1,0:T(8,128)(2,1)}, bf16[144,1408]{1,0:T(8,128)(2,1)}, bf16[144,1408]{1,0:T(8,128)(2,1)}, bf1...) custom-call(bf16[8,256,144]{2,1,0:T(8,128)(2,1)} %fusion.refs_0_, ...), custom_call_target="tpu_custom_call" | custom-call | flops 4529848320 | bytes 10420224 | tf_op jit(solution)/shard_map/returned_a/pallas_call | solution.py:186
  210.1 2.1 collective-permute-start.11
  212.5 2.6 collective-permute-start.13
  215.1 22.3 %all-to-all-done.2 = bf16[16,72,1280]{2,1,0:T(8,128)(2,1)S(1)} async-done(((bf16[16,72,1280]{2,1,0:T(8,128)(2,1)}), bf16[16,72,1280]{2,1,0:T(8,128)(2,1)S(1)}, u32[]{:S(2)}, u32[]{:S(2)}) %all-to-all-start.2) | async-done | bytes 2949152 | tf_op jit(solution)/shard_map/all_to_all | solution.py:446
  237.4 0.7 broadcast_in_dim.35.refs_0_
  238.1 0.9 copy-done
  239.0 8.6 %column_sums.1 = (f32[512,1280]{1,0:T(8,128)}, bf16[256,1280]{1,0:T(8,128)(2,1)}, bf16[256,1280]{1,0:T(8,128)(2,1)}) custom-call(f32[8,1152]{1,0:T(8,128)} %broadcast_in_dim.35.refs_0_, bf16[16,1152]{1,0:T(8,128)(2,1)} %fusion.6.refs_1_, bf16[1024,16]{1,0:T(8,128)(2,1)} %bitcast.33, bf16[1024,16]{1,0:T(8,128)(2,1)} %bitcast.34, bf16[1152,1280]{1,0:T(8,128)(2,1)} %bitcast.26), custom_call_target="tpu_custom_call" | custom-call | flops 603979776000 | bytes 6881280 | tf_op jit(solution)/shard_map/column_sums/pallas_call | solution.py:387
  247.6 1.4 collective-permute-start.7
  249.6 2.7 collective-permute-start.15
  252.3 0.8 copy.19
  253.2 0.8 copy.20
  254.0 7.1 %collective-permute-done.14.refs_11_ = bf16[144,1408]{1,0:T(8,128)(2,1)S(1)} collective-permute-done((bf16[144,1408]{1,0:T(8,128)(2,1)}, bf16[144,1408]{1,0:T(8,128)(2,1)S(1)}, u32[]{:S(2)}, u32[]{:S(2)}) %collective-permute-start.14) | collective-permute-done | bytes 405536 | tf_op jit(solution)/shard_map/ppermute | solution.py:38
  261.0 9.2 %collective-permute-done.15.refs_12_ = bf16[144,1408]{1,0:T(8,128)(2,1)S(1)} collective-permute-done((bf16[144,1408]{1,0:T(8,128)(2,1)}, bf16[144,1408]{1,0:T(8,128)(2,1)S(1)}, u32[]{:S(2)}, u32[]{:S(2)}) %collective-permute-start.15) | collective-permute-done | bytes 405536 | tf_op jit(solution)/shard_map/ppermute | solution.py:38
  270.3 0.7 copy-done.5
  271.6 7.2 %group_sums.1 = (bf16[384,1408]{1,0:T(8,128)(2,1)}, bf16[128,1280]{1,0:T(8,128)(2,1)}, bf16[128,1280]{1,0:T(8,128)(2,1)}, bf16[128,1280]{1,0:T(8,128)(2,1)}, bf16[128,1280]{1,0:T(8,128)(2,1)}) custom-call(f32[384,8]{1,0:T(8,128)} %bitcast.31, f32[384,8]{1,0:T(8,128)} %bitcast.32, f32[512,1280]{1,0:T(8,128)} %get-tuple-element.70.refs_2_, ...), custom_call_target="tpu_custom_call" | custom-call | flops 1245708288 | bytes 3244032 | tf_op jit(solution)/shard_map/group_sums/pallas_call | solution.py:221
  278.9 4.2 %all-to-all-start.3 = ((bf16[16,24,1408]{2,1,0:T(8,128)(2,1)}), bf16[16,24,1408]{2,1,0:T(8,128)(2,1)S(1)}, u32[]{:S(2)}, u32[]{:S(2)}) async-start(bf16[16,24,1408]{2,1,0:T(8,128)(2,1)} %bitcast.30), calls=%async_computation.3 | async-start | bytes 2162688 | tf_op jit(solution)/shard_map/all_to_all | solution.py:451
  283.2 1.7 collective-permute-start.17
  284.9 2.1 collective-permute-start.18
  287.1 5.3 %collective-permute-done.16 = bf16[128,1280]{1,0:T(8,128)(2,1)S(1)} collective-permute-done((bf16[128,1280]{1,0:T(8,128)(2,1)S(1)}, bf16[128,1280]{1,0:T(8,128)(2,1)S(1)}, u32[]{:S(2)}, u32[]{:S(2)}) %collective-permute-start.16) | collective-permute-done | bytes 327712 | tf_op jit(solution)/shard_map/ppermute | solution.py:38
  292.4 7.3 %collective-permute-done.17 = bf16[128,1280]{1,0:T(8,128)(2,1)S(1)} collective-permute-done((bf16[128,1280]{1,0:T(8,128)(2,1)S(1)}, bf16[128,1280]{1,0:T(8,128)(2,1)S(1)}, u32[]{:S(2)}, u32[]{:S(2)}) %collective-permute-start.17) | collective-permute-done | bytes 327712 | tf_op jit(solution)/shard_map/ppermute | solution.py:38
  299.7 2.0 collective-permute-done.18
  302.6 0.9 select_reduce_fusion
  303.5 0.9 pad_maximum_fusion
  (92 shorter events, 4.0 us)
Async XLA Ops:
  7.2 43.8 %all-gather.2.cloned.1.call-start = ((), (), s32[]{:S(2)}) async-start(), calls=%async_computation.4 | async-start | bytes 5898240 | tf_op jit(solution)/shard_map/all_gather | solution.py:417
  10.5 3.4 %copy-start.11 = (f32[16,128]{1,0:T(8,128)}, f32[16,128]{1,0:T(8,128)S(1)}, u32[]{:S(2)}) copy-start(f32[16,128]{1,0:T(8,128)S(1)} %convolution_select_fusion) | copy-start | bytes 24580
  13.9 45.7 %all-to-all-start = ((bf16[16,24,2688]{2,1,0:T(8,128)(2,1)}), bf16[16,24,2688]{2,1,0:T(8,128)(2,1)S(1)}, u32[]{:S(2)}, u32[]{:S(2)}) async-start(bf16[16,24,2688]{2,1,0:T(8,128)(2,1)} %bitcast.2), calls=%async_computation | async-start | bytes 4128768 | tf_op jit(solution)/shard_map/all_to_all | solution.py:428
  59.5 1.3 copy-start.1
  60.9 106.0 %all-to-all-start.1 = ((bf16[16,72,2560]{2,1,0:T(8,128)(2,1)}), bf16[16,72,2560]{2,1,0:T(8,128)(2,1)}, u32[]{:S(2)}, u32[]{:S(2)}) async-start(bf16[16,72,2560]{2,1,0:T(8,128)(2,1)} %bitcast.25), calls=%async_computation.1 | async-start | bytes 11796480 | tf_op jit(solution)/shard_map/all_to_all | solution.py:433
  77.1 5.7 %collective-permute-start = (bf16[144,2560]{1,0:T(8,128)(2,1)}, bf16[144,2560]{1,0:T(8,128)(2,1)S(1)}, u32[]{:S(2)}, u32[]{:S(2)}) collective-permute-start(bf16[144,2560]{1,0:T(8,128)(2,1)} %get-tuple-element.48), channel_id=1, source_target_pairs={{0,1},{1,0},{2,3},{3,2},{4,5},{5,4},{6,7},{7,6},{8,9},{9,8},{10,11... | collective-permute-start | bytes 2211848 | tf_op jit(solution)/shard_map/ppermute | solution.py:38
  77.7 18.4 %collective-permute-start.1 = (bf16[144,2560]{1,0:T(8,128)(2,1)}, bf16[144,2560]{1,0:T(8,128)(2,1)S(1)}, u32[]{:S(2)}, u32[]{:S(2)}) collective-permute-start(bf16[144,2560]{1,0:T(8,128)(2,1)} %get-tuple-element.49), channel_id=1, source_target_pairs={{0,2},{1,3},{2,0},{3,1},{4,6},{5,7},{6,4},{7,5},{8,10},{9,11},{10,... | collective-permute-start | bytes 2211848 | tf_op jit(solution)/shard_map/ppermute | solution.py:38
  78.0 34.9 %collective-permute-start.2 = (bf16[144,2560]{1,0:T(8,128)(2,1)}, bf16[144,2560]{1,0:T(8,128)(2,1)S(1)}, u32[]{:S(2)}, u32[]{:S(2)}) collective-permute-start(bf16[144,2560]{1,0:T(8,128)(2,1)} %get-tuple-element.50), channel_id=1, source_target_pairs={{0,3},{1,2},{2,1},{3,0},{4,7},{5,6},{6,5},{7,4},{8,11},{9,10},{10,... | collective-permute-start | bytes 2211848 | tf_op jit(solution)/shard_map/ppermute | solution.py:38
  79.4 48.5 %collective-permute-start.3 = (bf16[144,2560]{1,0:T(8,128)(2,1)}, bf16[144,2560]{1,0:T(8,128)(2,1)S(1)}, u32[]{:S(2)}, u32[]{:S(2)}) collective-permute-start(bf16[144,2560]{1,0:T(8,128)(2,1)} %get-tuple-element.51), channel_id=1, source_target_pairs={{0,4},{1,5},{2,6},{3,7},{4,0},{5,1},{6,2},{7,3},{8,12},{9,13},{10,... | collective-permute-start | bytes 2211848 | tf_op jit(solution)/shard_map/ppermute | solution.py:38
  80.9 63.1 %collective-permute-start.4 = (bf16[144,2560]{1,0:T(8,128)(2,1)}, bf16[144,2560]{1,0:T(8,128)(2,1)}, u32[]{:S(2)}, u32[]{:S(2)}) collective-permute-start(bf16[144,2560]{1,0:T(8,128)(2,1)} %get-tuple-element.52), channel_id=1, source_target_pairs={{0,5},{1,4},{2,7},{3,6},{4,1},{5,0},{6,3},{7,2},{8,13},{9,12},{10,... | collective-permute-start | bytes 2211848 | tf_op jit(solution)/shard_map/ppermute | solution.py:38
  82.8 67.4 %copy-start.15 = (bf16[144,2560]{1,0:T(8,128)(2,1)}, bf16[144,2560]{1,0:T(8,128)(2,1)S(1)}, u32[]{:S(2)}) copy-start(bf16[144,2560]{1,0:T(8,128)(2,1)S(1)} %collective-permute-done.refs_2_) | copy-start | bytes 2211844
  82.8 61.3 %collective-permute-start.5 = (bf16[144,2560]{1,0:T(8,128)(2,1)}, bf16[144,2560]{1,0:T(8,128)(2,1)}, u32[]{:S(2)}, u32[]{:S(2)}) collective-permute-start(bf16[144,2560]{1,0:T(8,128)(2,1)} %get-tuple-element.53), channel_id=1, source_target_pairs={{0,6},{1,7},{2,4},{3,5},{4,2},{5,3},{6,0},{7,1},{8,14},{9,15},{10,... | collective-permute-start | bytes 2211848 | tf_op jit(solution)/shard_map/ppermute | solution.py:38
  96.1 54.1 %copy-start.16 = (bf16[144,2560]{1,0:T(8,128)(2,1)}, bf16[144,2560]{1,0:T(8,128)(2,1)S(1)}, u32[]{:S(2)}) copy-start(bf16[144,2560]{1,0:T(8,128)(2,1)S(1)} %collective-permute-done.1.refs_3_) | copy-start | bytes 2211844
  96.1 54.1 %collective-permute-start.6 = (bf16[144,2560]{1,0:T(8,128)(2,1)}, bf16[144,2560]{1,0:T(8,128)(2,1)}, u32[]{:S(2)}, u32[]{:S(2)}) collective-permute-start(bf16[144,2560]{1,0:T(8,128)(2,1)} %get-tuple-element.54), channel_id=1, source_target_pairs={{0,7},{1,6},{2,5},{3,4},{4,3},{5,2},{6,1},{7,0},{8,15},{9,14},{10,... | collective-permute-start | bytes 2211848 | tf_op jit(solution)/shard_map/ppermute | solution.py:38
  112.8 37.4 %copy-start.17 = (bf16[144,2560]{1,0:T(8,128)(2,1)}, bf16[144,2560]{1,0:T(8,128)(2,1)S(1)}, u32[]{:S(2)}) copy-start(bf16[144,2560]{1,0:T(8,128)(2,1)S(1)} %collective-permute-done.2.refs_4_) | copy-start | bytes 2211844
  128.0 22.2 %copy-start.18 = (bf16[144,2560]{1,0:T(8,128)(2,1)}, bf16[144,2560]{1,0:T(8,128)(2,1)S(1)}, u32[]{:S(2)}) copy-start(bf16[144,2560]{1,0:T(8,128)(2,1)S(1)} %collective-permute-done.3.refs_5_) | copy-start | bytes 2211844
  185.7 6.7 %copy-start.9 = (f32[16,1024]{1,0:T(8,128)S(1)}, f32[16,1024]{1,0:T(8,128)}, u32[]{:S(2)}) copy-start(f32[16,1024]{1,0:T(8,128)} %get-tuple-element.44) | copy-start | bytes 196612
  185.8 7.6 %copy-start.8 = (f32[16,1024]{1,0:T(8,128)S(1)}, f32[16,1024]{1,0:T(8,128)}, u32[]{:S(2)}) copy-start(f32[16,1024]{1,0:T(8,128)} %get-tuple-element.45) | copy-start | bytes 196612
  185.8 51.6 %all-to-all-start.2 = ((bf16[16,72,1280]{2,1,0:T(8,128)(2,1)}), bf16[16,72,1280]{2,1,0:T(8,128)(2,1)S(1)}, u32[]{:S(2)}, u32[]{:S(2)}) async-start(bf16[16,72,1280]{2,1,0:T(8,128)(2,1)} %bitcast.27), calls=%async_computation.2 | async-start | bytes 5898240 | tf_op jit(solution)/shard_map/all_to_all | solution.py:446
  210.1 38.8 %collective-permute-start.10 = (bf16[144,1408]{1,0:T(8,128)(2,1)}, bf16[144,1408]{1,0:T(8,128)(2,1)}, u32[]{:S(2)}, u32[]{:S(2)}) collective-permute-start(bf16[144,1408]{1,0:T(8,128)(2,1)} %get-tuple-element.63), channel_id=1, source_target_pairs={{0,2},{1,3},{2,0},{3,1},{4,6},{5,7},{6,4},{7,5},{8,10},{9,11},{10,... | collective-permute-start | bytes 1216520 | tf_op jit(solution)/shard_map/ppermute | solution.py:38
  210.1 38.9 %collective-permute-start.11 = (bf16[144,1408]{1,0:T(8,128)(2,1)}, bf16[144,1408]{1,0:T(8,128)(2,1)}, u32[]{:S(2)}, u32[]{:S(2)}) collective-permute-start(bf16[144,1408]{1,0:T(8,128)(2,1)} %get-tuple-element.64), channel_id=1, source_target_pairs={{0,3},{1,2},{2,1},{3,0},{4,7},{5,6},{6,5},{7,4},{8,11},{9,10},{10,... | collective-permute-start | bytes 1216520 | tf_op jit(solution)/shard_map/ppermute | solution.py:38
  212.3 37.3 %collective-permute-start.12 = (bf16[144,1408]{1,0:T(8,128)(2,1)}, bf16[144,1408]{1,0:T(8,128)(2,1)}, u32[]{:S(2)}, u32[]{:S(2)}) collective-permute-start(bf16[144,1408]{1,0:T(8,128)(2,1)} %get-tuple-element.65), channel_id=1, source_target_pairs={{0,4},{1,5},{2,6},{3,7},{4,0},{5,1},{6,2},{7,3},{8,12},{9,13},{10,... | collective-permute-start | bytes 1216520 | tf_op jit(solution)/shard_map/ppermute | solution.py:38
  212.5 39.8 %collective-permute-start.13 = (bf16[144,1408]{1,0:T(8,128)(2,1)}, bf16[144,1408]{1,0:T(8,128)(2,1)}, u32[]{:S(2)}, u32[]{:S(2)}) collective-permute-start(bf16[144,1408]{1,0:T(8,128)(2,1)} %get-tuple-element.66), channel_id=1, source_target_pairs={{0,5},{1,4},{2,7},{3,6},{4,1},{5,0},{6,3},{7,2},{8,13},{9,12},{10,... | collective-permute-start | bytes 1216520 | tf_op jit(solution)/shard_map/ppermute | solution.py:38
  237.4 1.6 copy-start
  239.0 13.3 %copy-start.19 = (bf16[144,1408]{1,0:T(8,128)(2,1)S(1)}, bf16[144,1408]{1,0:T(8,128)(2,1)}, u32[]{:S(2)}) copy-start(bf16[144,1408]{1,0:T(8,128)(2,1)} %get-tuple-element.62) | copy-start | bytes 1216516
  239.0 13.3 %copy-start.14 = (f32[8,384]{1,0:T(8,128)S(1)}, f32[8,384]{1,0:T(8,128)}, u32[]{:S(2)}) copy-start(f32[8,384]{1,0:T(8,128)} %get-tuple-element.42) | copy-start | bytes 36868
  239.0 14.2 %copy-start.13 = (f32[8,384]{1,0:T(8,128)S(1)}, f32[8,384]{1,0:T(8,128)}, u32[]{:S(2)}) copy-start(f32[8,384]{1,0:T(8,128)} %get-tuple-element.43) | copy-start | bytes 36868
  247.6 22.7 %collective-permute-start.7 = (bf16[256,1280]{1,0:T(8,128)(2,1)}, bf16[256,1280]{1,0:T(8,128)(2,1)S(1)}, u32[]{:S(2)}, u32[]{:S(2)}) collective-permute-start(bf16[256,1280]{1,0:T(8,128)(2,1)} %get-tuple-element.71), channel_id=1, source_target_pairs={{0,1},{1,0},{2,3},{3,2},{4,5},{5,4},{6,7},{7,6},{8,9},{9,8},{10,11... | collective-permute-start | bytes 1966088 | tf_op jit(solution)/shard_map/ppermute | solution.py:38
  249.0 21.3 %collective-permute-start.8 = (bf16[256,1280]{1,0:T(8,128)(2,1)}, bf16[256,1280]{1,0:T(8,128)(2,1)S(1)}, u32[]{:S(2)}, u32[]{:S(2)}) collective-permute-start(bf16[256,1280]{1,0:T(8,128)(2,1)} %get-tuple-element.72), channel_id=1, source_target_pairs={{0,1},{1,0},{2,3},{3,2},{4,5},{5,4},{6,7},{7,6},{8,9},{9,8},{10,11... | collective-permute-start | bytes 1966088 | tf_op jit(solution)/shard_map/ppermute | solution.py:38
  249.1 12.0 %collective-permute-start.14 = (bf16[144,1408]{1,0:T(8,128)(2,1)}, bf16[144,1408]{1,0:T(8,128)(2,1)S(1)}, u32[]{:S(2)}, u32[]{:S(2)}) collective-permute-start(bf16[144,1408]{1,0:T(8,128)(2,1)} %get-tuple-element.67), channel_id=1, source_target_pairs={{0,6},{1,7},{2,4},{3,5},{4,2},{5,3},{6,0},{7,1},{8,14},{9,15},{10,... | collective-permute-start | bytes 1216520 | tf_op jit(solution)/shard_map/ppermute | solution.py:38
  249.6 20.7 %collective-permute-start.15 = (bf16[144,1408]{1,0:T(8,128)(2,1)}, bf16[144,1408]{1,0:T(8,128)(2,1)S(1)}, u32[]{:S(2)}, u32[]{:S(2)}) collective-permute-start(bf16[144,1408]{1,0:T(8,128)(2,1)} %get-tuple-element.68), channel_id=1, source_target_pairs={{0,7},{1,6},{2,5},{3,4},{4,3},{5,2},{6,1},{7,0},{8,15},{9,14},{10,... | collective-permute-start | bytes 1216520 | tf_op jit(solution)/shard_map/ppermute | solution.py:38
  252.3 17.9 %collective-permute-start.9 = (bf16[144,1408]{1,0:T(8,128)(2,1)S(1)}, bf16[144,1408]{1,0:T(8,128)(2,1)S(1)}, u32[]{:S(2)}, u32[]{:S(2)}) collective-permute-start(bf16[144,1408]{1,0:T(8,128)(2,1)S(1)} %copy-done.19), channel_id=1, source_target_pairs={{0,1},{1,0},{2,3},{3,2},{4,5},{5,4},{6,7},{7,6},{8,9},{9,8},{10,11... | collective-permute-start | bytes 1216520 | tf_op jit(solution)/shard_map/ppermute | solution.py:38
  261.0 9.3 %copy-start.4 = (bf16[144,1408]{1,0:T(8,128)(2,1)}, bf16[144,1408]{1,0:T(8,128)(2,1)S(1)}, u32[]{:S(2)}) copy-start(bf16[144,1408]{1,0:T(8,128)(2,1)S(1)} %collective-permute-done.14.refs_11_) | copy-start | bytes 1216516
  270.3 0.8 copy-start.5
  270.3 0.9 copy-start.6
  270.3 1.1 copy-start.2
  270.3 1.3 copy-start.3
  278.8 4.3 %copy-start.22 = (bf16[128,1280]{1,0:T(8,128)(2,1)S(1)}, bf16[128,1280]{1,0:T(8,128)(2,1)}, u32[]{:S(2)}) copy-start(bf16[128,1280]{1,0:T(8,128)(2,1)} %get-tuple-element.75) | copy-start | bytes 983044
  278.8 4.4 %copy-start.21 = (bf16[128,1280]{1,0:T(8,128)(2,1)S(1)}, bf16[128,1280]{1,0:T(8,128)(2,1)}, u32[]{:S(2)}) copy-start(bf16[128,1280]{1,0:T(8,128)(2,1)} %get-tuple-element.76) | copy-start | bytes 983044
  278.8 6.1 %copy-start.20 = (bf16[128,1280]{1,0:T(8,128)(2,1)S(1)}, bf16[128,1280]{1,0:T(8,128)(2,1)}, u32[]{:S(2)}) copy-start(bf16[128,1280]{1,0:T(8,128)(2,1)} %get-tuple-element.77) | copy-start | bytes 983044
  278.9 22.9 %copy-start.7 = (bf16[128,1280]{1,0:T(8,128)(2,1)S(1)}, bf16[128,1280]{1,0:T(8,128)(2,1)}, u32[]{:S(2)}) copy-start(bf16[128,1280]{1,0:T(8,128)(2,1)} %get-tuple-element.74) | copy-start | bytes 983044
  278.9 23.3 %copy-start.12 = (f32[16,128]{1,0:T(8,128)S(1)}, f32[16,128]{1,0:T(8,128)}, u32[]{:S(2)}) copy-start(f32[16,128]{1,0:T(8,128)} %copy-done.11) | copy-start | bytes 24580
  278.9 23.2 %all-to-all-start.3 = ((bf16[16,24,1408]{2,1,0:T(8,128)(2,1)}), bf16[16,24,1408]{2,1,0:T(8,128)(2,1)S(1)}, u32[]{:S(2)}, u32[]{:S(2)}) async-start(bf16[16,24,1408]{2,1,0:T(8,128)(2,1)} %bitcast.30), calls=%async_computation.3 | async-start | bytes 2162688 | tf_op jit(solution)/shard_map/all_to_all | solution.py:451
  283.1 9.3 %collective-permute-start.16 = (bf16[128,1280]{1,0:T(8,128)(2,1)S(1)}, bf16[128,1280]{1,0:T(8,128)(2,1)S(1)}, u32[]{:S(2)}, u32[]{:S(2)}) collective-permute-start(bf16[128,1280]{1,0:T(8,128)(2,1)S(1)} %copy-done.22), channel_id=1, source_target_pairs={{0,2},{1,3},{2,0},{3,1},{4,6},{5,7},{6,4},{7,5},{8,10},{9,11},{10,... | collective-permute-start | bytes 983048 | tf_op jit(solution)/shard_map/ppermute | solution.py:38
  283.2 16.5 %collective-permute-start.17 = (bf16[128,1280]{1,0:T(8,128)(2,1)S(1)}, bf16[128,1280]{1,0:T(8,128)(2,1)S(1)}, u32[]{:S(2)}, u32[]{:S(2)}) collective-permute-start(bf16[128,1280]{1,0:T(8,128)(2,1)S(1)} %copy-done.21), channel_id=1, source_target_pairs={{0,4},{1,5},{2,6},{3,7},{4,0},{5,1},{6,2},{7,3},{8,12},{9,13},{10,... | collective-permute-start | bytes 983048 | tf_op jit(solution)/shard_map/ppermute | solution.py:38
  284.9 16.8 %collective-permute-start.18 = (bf16[128,1280]{1,0:T(8,128)(2,1)S(1)}, bf16[128,1280]{1,0:T(8,128)(2,1)S(1)}, u32[]{:S(2)}, u32[]{:S(2)}) collective-permute-start(bf16[128,1280]{1,0:T(8,128)(2,1)S(1)} %copy-done.20), channel_id=1, source_target_pairs={{0,6},{1,7},{2,4},{3,5},{4,2},{5,3},{6,0},{7,1},{8,14},{9,15},{10,... | collective-permute-start | bytes 983048 | tf_op jit(solution)/shard_map/ppermute | solution.py:38
  301.7 0.9 copy-start.10
Sparse Core Ops, SparseCore 0:
  9.7 41.2 all-gather.1

commit v4 on v3

--- a/solution.py
+++ b/solution.py
@@ -264,20 +264,18 @@
     return (same & (at[:, None] < at[None, :])).astype(BF), jnp.broadcast_to((at // size).astype(F32), (8, total))
 
 
-def hub_blocks(hub, local, per_group, top, cap):
+def hub_blocks(hub, tables, per_group, top, cap):
     n_rows, width = hub.shape
-    n_exp = local.shape[0]
-    before, block = lower_counts(n_rows, per_group)
+    n_exp = tables[1].shape[0]
     features = width - LANES
     wide = 512 if features % 512 == 0 else features
     shape = (n_rows // per_group * cap, features)
     row = (n_exp, n_rows)
-    eye = jnp.eye(LANES, dtype=BF)
     part = lambda rows: pl.BlockSpec((rows, wide), lambda j: (0, j))
     *blocks, slot, weight = pl.pallas_call(
         lambda *refs: hub_kernel(top, cap, *refs),
         grid=(features // wide,),
-        in_specs=[whole(x.shape) for x in (eye, local, before, block)]
+        in_specs=[whole(x.shape) for x in tables]
         + [whole((n_rows, LANES), (0, features // LANES)), part(n_rows)],
         out_specs=[part(shape[0])] * n_exp + [whole(row)] * 2,
         out_shape=[jax.ShapeDtypeStruct(shape, BF)] * n_exp + [jax.ShapeDtypeStruct(row, F32)] * 2,
@@ -285,7 +283,7 @@
         compiler_params=params(VMEM_MIB),
         cost_estimate=cost(2 * shape[0] * n_exp * n_rows * width, 2 * n_exp * shape[0] * shape[1]),
         name="hub_blocks",
-    )(eye, local, before, block, hub, hub)
+    )(*tables, hub, hub)
     return blocks, slot.T, weight.T
 
 
@@ -394,7 +392,7 @@
         compiler_params=params(VMEM_MIB),
         cost_estimate=cost(400 * n_rows * total * half, 2 * total * half + 3 * n_rows * half),
         name="column_sums",
-    )(place, spread, slot.astype(BF), weight.astype(BF), got)
+    )(place, spread, slot, weight, got)
 
 
 def per_device(hidden_in, grad_out, expert_ids, gate_weights, w_gate, w_up, w_down):
@@ -417,6 +415,10 @@
     column = lax.all_gather(grad_out, "exp", axis=0, tiled=True)
     theirs = jnp.broadcast_to((jnp.arange(n_seq) * n_exp + member).astype(F32)[:, None], (n_seq, LANES))
     put_b, slot_b, weight_b = column_slots(column_meta, theirs, member, n_tok, top, cap)
+    slot_b, weight_b = slot_b.astype(BF), weight_b.astype(BF)
+    local = jnp.broadcast_to((partner + group * n_exp).astype(F32)[:, None], (n_exp, LANES))
+    tables = (jnp.eye(LANES, dtype=BF), local) + lower_counts(n_seq * per_group, per_group)
+    put_b, to_b, to_a, slot_b, weight_b, *tables = barrier(put_b, to_b, to_a, slot_b, weight_b, *tables)
     send_b = column_rows(member, to_b, put_b, column, n_exp)
 
     group_ids = expert_ids // n_exp
@@ -433,8 +435,7 @@
     recv_b = lax.all_to_all(send_b.reshape(n_seq, rows_b, features), "seq", 0, 0, tiled=True)
     recv_b = recv_b.reshape(n_seq * rows_b, features)
 
-    local = jnp.broadcast_to((partner + group * n_exp).astype(F32)[:, None], (n_exp, LANES))
-    blocks, slot_a, weight_a = hub_blocks(hub, local, per_group, top, cap)
+    blocks, slot_a, weight_a = hub_blocks(hub, tables, per_group, top, cap)
     rows_in = exchange(blocks)
 
     pre_gate, pre_up = pre_products(to_b, rows_in, gate_mat, up_mat)
@@ -444,7 +445,7 @@
     back_a = returned_a(to_a, grad_gate, grad_up, gate_mat, up_mat, gate_dot, n_exp)
     got_a = exchange(back_a)
     got_b = lax.all_to_all(back_b.reshape(n_seq, rows_b, half), "seq", 0, 0, tiled=True)
-    got_b, *_ = barrier(got_b, *back_a)
+    got_b, *got_a = barrier(got_b, *got_a)
     mine, *other = column_sums(slot_b, weight_b, got_b.reshape(n_seq * rows_b, half), n_exp)
     back, *chip = group_sums(slot_a, weight_a, mine, *(swap(x, 1) for x in other), got_a)
     final_b = sum(p.astype(F32) for p in exchange(chip, 2))

time: 312 us -> 306 us (0.981)
  waiting for transfers between devices: 125 us -> 110 us
  starting transfers between devices: 47.6 us -> 52.1 us
    all_to_all x1, waiting for transfers between devices: 22.3 us -> 0.01 us  [per_device(): lax.all_to_all(back_b.reshape(n_seq, rows_b, half), 'seq', 0, 0, tiled=True)]
    ppermute x19, waiting for transfers between devices: 96.2 us -> 110 us  [swap(): lax.ppermute(x, 'exp', [(i, i ^ k) for i in range(lax.axis_size('exp'))])]
    all_gather x1, waiting for transfers between devices: 6 us -> 0.01 us  [per_device(): column = lax.all_gather(grad_out, 'exp', axis=0, tiled=True)]
  transfers between devices with their start and end apart: 24 -> 24, of which waited for: 13 -> 13; matrix products, arithmetic and copies ran while one was open for 6% -> 7% of each run, Pallas kernels for 18% -> 16%
where the time goes in v4:
time: 306 us; the launch traced here: 304 us
  waiting for transfers between devices  110 us (36%)
  Pallas kernels  82.9 us (27%)
  starting transfers between devices  52.1 us (17%)
  local copies, waits for them, and re-layouts  15.8 us (5%)
  blocking collectives  15.6 us (5%)
  between operations  14.3 us (5%)
  other arithmetic  10 us (3%)
    ppermute x19, waiting for transfers between devices, swap(): lax.ppermute(x, 'exp', [(i, i ^ k) for i in range(lax.axis_size('exp'))])  110 us
    ppermute x19, starting transfers between devices, swap(): lax.ppermute(x, 'exp', [(i, i ^ k) for i in range(lax.axis_size('exp'))])  22.8 us
    pallas_call x1, Pallas kernels, hidden_grads(): pl.pallas_call(lambda *refs: grad_kernel(steps, *refs), grid=(steps + hal...  18.3 us
    pallas_call x1, Pallas kernels, pre_products(): pl.pallas_call(lambda *refs: pre_kernel(chips, pairs, *refs), grid=(units...  16.6 us
    all_gather x1, blocking collectives, per_device(): column_meta = lax.all_gather(meta, 'exp', axis=0, tiled=True)  15.6 us
    pallas_call x1, Pallas kernels, returned_a(): pl.pallas_call(lambda *refs: back_a_kernel(n_exp, pairs, *refs), grid=(ha...  13.9 us
    pallas_call x1, Pallas kernels, column_sums(): pl.pallas_call(lambda *refs: column_kernel(n_exp, *refs), grid=(half // w...  8.55 us
    pallas_call x1, Pallas kernels, column_rows(): pl.pallas_call(lambda *refs: rows_kernel(n_exp, *refs), grid=(features //...  8.5 us
  transfers between devices with their start and end apart: 24, of which 13 were waited for; matrix products, arithmetic and copies ran while one was open for 7% of the time, Pallas kernels for 16%

profile of v4, /device:TPU:1, one launch (start us, length us, event | category | flops | bytes accessed | tf_op | source)
XLA Modules:
  0.0 303.6 jit_solution(2305494547790908897)
XLA Ops:
  7.2 0.7 all-gather.2.cloned.1.call-update
  7.9 0.8 copy.17
  8.7 0.8 copy.18
  9.6 0.7 add_select_fusion.3
  10.6 1.2 concatenate.12
  11.8 2.0 convolution_convert_fusion
  13.8 8.4 %all-to-all-start = ((bf16[16,24,2688]{2,1,0:T(8,128)(2,1)}), bf16[16,24,2688]{2,1,0:T(8,128)(2,1)S(1)}, u32[]{:S(2)}, u32[]{:S(2)}) async-start(bf16[16,24,2688]{2,1,0:T(8,128)(2,1)} %bitcast.5), calls=%async_computation | async-start | bytes 4128768 | tf_op jit(solution)/shard_map/all_to_all | solution.py:430
  22.4 15.6 %all_gather.6.refs_7_ = bf16[1024,128]{1,0:T(8,128)(2,1)} all-gather(bf16[128,128]{1,0:T(8,128)(2,1)S(1)} %pad_maximum_fusion.1), channel_id=1, replica_groups=mesh['seq'=16,'exp'=8] {'exp'}, dimensions={0}, use_global_device_ids=true | all-gather | bytes 294912 | tf_op jit(solution)/shard_map/all_gather | solution.py:414
  38.1 0.7 fusion.5.refs_5_
  38.8 0.7 fusion.7
  39.4 0.7 broadcast_in_dim.28.refs_2_
  40.1 0.7 broadcast_in_dim.30.refs_6_
  41.4 2.4 column_slots.1
  43.8 0.8 convert_element_type.107
  44.7 0.8 copy.19
  45.5 0.8 convert_element_type.109
  46.4 0.9 copy.20
  47.3 0.8 fusion.3.refs_2_
  48.2 1.0 fusion.1.refs_1_.refs_0_
  49.2 1.3 fusion.refs_0_
  50.5 0.7 broadcast_in_dim.32.refs_1_
  51.8 8.5 %column_rows.1 = bf16[1152,2560]{1,0:T(8,128)(2,1)} custom-call(s32[1]{0:T(128)} %bitcast.1.refs_0_, bf16[8,144,256]{2,1,0:T(8,128)(2,1)} %fusion.1.refs_1_.refs_0_, bf16[1152,128]{1,0:T(8,128)(2,1)} %get-tuple-element.65.refs_2_, bf16[1024,2560]{1,0:T(8,128)(2,1)} %all-gather.2.cloned.1.call-done.refs_3_), custom_call_target="tpu_custom_call" | custom-call | flops 37748736 | bytes 294912 | tf_op jit(solution)/shard_map/column_rows/pallas_call | solution.py:347
  60.3 1.4 copy-done.1
  61.7 7.0 %all-to-all-start.1 = ((bf16[16,72,2560]{2,1,0:T(8,128)(2,1)}), bf16[16,72,2560]{2,1,0:T(8,128)(2,1)}, u32[]{:S(2)}, u32[]{:S(2)}) async-start(bf16[16,72,2560]{2,1,0:T(8,128)(2,1)} %bitcast.25), calls=%async_computation.1 | async-start | bytes 11796480 | tf_op jit(solution)/shard_map/all_to_all | solution.py:435
  68.7 7.4 %hub_blocks.1 = (bf16[144,2560]{1,0:T(8,128)(2,1)}, bf16[144,2560]{1,0:T(8,128)(2,1)}, bf16[144,2560]{1,0:T(8,128)(2,1)}, bf16[144,2560]{1,0:T(8,128)(2,1)}, bf1...) custom-call(bf16[128,128]{1,0:T(8,128)(2,1)} %get-tuple-element.60.r, ...), custom_call_target="tpu_custom_call" | custom-call | flops 2378170368 | bytes 5898240 | tf_op jit(solution)/shard_map/hub_blocks/pallas_call | solution.py:275
  76.6 1.0 collective-permute-start.1
  77.6 0.7 collective-permute-start.2
  78.4 1.7 collective-permute-start.3
  80.1 1.6 collective-permute-start.4
  81.7 2.2 collective-permute-start.5
  83.9 11.1 %collective-permute-done.1.refs_3_ = bf16[144,2560]{1,0:T(8,128)(2,1)S(1)} collective-permute-done((bf16[144,2560]{1,0:T(8,128)(2,1)}, bf16[144,2560]{1,0:T(8,128)(2,1)S(1)}, u32[]{:S(2)}, u32[]{:S(2)}) %collective-permute-start.1) | collective-permute-done | bytes 737312 | tf_op jit(solution)/shard_map/ppermute | solution.py:38
  95.0 3.3 %collective-permute-start.6 = (bf16[144,2560]{1,0:T(8,128)(2,1)}, bf16[144,2560]{1,0:T(8,128)(2,1)}, u32[]{:S(2)}, u32[]{:S(2)}) collective-permute-start(bf16[144,2560]{1,0:T(8,128)(2,1)} %get-tuple-element.79), channel_id=1, source_target_pairs={{0,7},{1,6},{2,5},{3,4},{4,3},{5,2},{6,1},{7,0},{8,15},{9,14},{10,... | collective-permute-start | bytes 2211848 | tf_op jit(solution)/shard_map/ppermute | solution.py:38
  98.3 13.4 %collective-permute-done.2.refs_4_ = bf16[144,2560]{1,0:T(8,128)(2,1)S(1)} collective-permute-done((bf16[144,2560]{1,0:T(8,128)(2,1)}, bf16[144,2560]{1,0:T(8,128)(2,1)S(1)}, u32[]{:S(2)}, u32[]{:S(2)}) %collective-permute-start.2) | collective-permute-done | bytes 737312 | tf_op jit(solution)/shard_map/ppermute | solution.py:38
  111.7 16.8 %collective-permute-done.3.refs_5_ = bf16[144,2560]{1,0:T(8,128)(2,1)S(1)} collective-permute-done((bf16[144,2560]{1,0:T(8,128)(2,1)}, bf16[144,2560]{1,0:T(8,128)(2,1)S(1)}, u32[]{:S(2)}, u32[]{:S(2)}) %collective-permute-start.3) | collective-permute-done | bytes 737312 | tf_op jit(solution)/shard_map/ppermute | solution.py:38
  128.6 16.0 %collective-permute-done.4.refs_6_ = bf16[144,2560]{1,0:T(8,128)(2,1)} collective-permute-done((bf16[144,2560]{1,0:T(8,128)(2,1)}, bf16[144,2560]{1,0:T(8,128)(2,1)}, u32[]{:S(2)}, u32[]{:S(2)}) %collective-permute-start.4) | collective-permute-done | bytes 737312 | tf_op jit(solution)/shard_map/ppermute | solution.py:38
  144.6 4.2 %collective-permute-done.6.refs_8_ = bf16[144,2560]{1,0:T(8,128)(2,1)} collective-permute-done((bf16[144,2560]{1,0:T(8,128)(2,1)}, bf16[144,2560]{1,0:T(8,128)(2,1)}, u32[]{:S(2)}, u32[]{:S(2)}) %collective-permute-start.6) | collective-permute-done | bytes 737312 | tf_op jit(solution)/shard_map/ppermute | solution.py:38
  148.8 16.6 %pre_products.1 = (f32[1152,768]{1,0:T(8,128)}, f32[1152,768]{1,0:T(8,128)}) custom-call(bf16[8,144,256]{2,1,0:T(8,128)(2,1)} %fusion.1.refs_1_.refs_0_, bf16[144,2560]{1,0:T(8,128)(2,1)} %get-tuple-element.72.refs_1_, bf16[144,2560]{1,0:T(8,128)(2,1)} %copy-done.16, bf16[144,2560]{1,0:T(8,128)(2,1)} %copy-done.17, bf16[144,2560]{1,0:T(8,128)(2,1)} %copy-done.18, ...), custom_call_target="tpu_custom_call" | custom-call | flops 9059696640 | bytes 20840448 | tf_op jit(solution)/shard_map/pre_products/pallas_call | solution.py:90
  166.0 18.3 %hidden_grads.1 = (bf16[1152,768]{1,0:T(8,128)(2,1)}, bf16[1152,768]{1,0:T(8,128)(2,1)}, bf16[1152,128]{1,0:T(8,128)(2,1)}, bf16[1152,1280]{1,0:T(8,128)(2,1)}) custom-call(f32[8,128]{1,0:T(8,128)} %broadcast_in_dim.35.refs_0_, bf16[1152,2560]{1,0:T(8,128)(2,1)} %bitcast.10.refs_1_, bf16[768,2560]{1,0:T(8,128)(2,1)} %bitcast.35, ...), custom_call_target="tpu_custom_call" | custom-call | flops 9059696640 | bytes 30277632 | tf_op jit(solution)/shard_map/hidden_grads/pallas_call | solution.py:136
  184.4 6.9 %all-to-all-start.2 = ((bf16[16,72,1280]{2,1,0:T(8,128)(2,1)}), bf16[16,72,1280]{2,1,0:T(8,128)(2,1)S(1)}, u32[]{:S(2)}, u32[]{:S(2)}) async-start(bf16[16,72,1280]{2,1,0:T(8,128)(2,1)} %bitcast.27), calls=%async_computation.2 | async-start | bytes 5898240 | tf_op jit(solution)/shard_map/all_to_all | solution.py:447
  191.2 13.9 %returned_a.1 = (bf16[144,1408]{1,0:T(8,128)(2,1)}, bf16[144,1408]{1,0:T(8,128)(2,1)}, bf16[144,1408]{1,0:T(8,128)(2,1)}, bf16[144,1408]{1,0:T(8,128)(2,1)}, bf1...) custom-call(bf16[8,256,144]{2,1,0:T(8,128)(2,1)} %fusion.refs_0_, ...), custom_call_target="tpu_custom_call" | custom-call | flops 4529848320 | bytes 10420224 | tf_op jit(solution)/shard_map/returned_a/pallas_call | solution.py:186
  205.1 0.7 collective-permute-start.10
  205.8 2.9 collective-permute-start.11
  208.8 2.3 collective-permute-start.12
  212.0 5.3 %collective-permute-done.10.refs_9_ = bf16[144,1408]{1,0:T(8,128)(2,1)S(1)} collective-permute-done((bf16[144,1408]{1,0:T(8,128)(2,1)}, bf16[144,1408]{1,0:T(8,128)(2,1)S(1)}, u32[]{:S(2)}, u32[]{:S(2)}) %collective-permute-start.10) | collective-permute-done | bytes 405536 | tf_op jit(solution)/shard_map/ppermute | solution.py:38
  217.6 10.1 %collective-permute-done.11.refs_10_ = bf16[144,1408]{1,0:T(8,128)(2,1)S(1)} collective-permute-done((bf16[144,1408]{1,0:T(8,128)(2,1)}, bf16[144,1408]{1,0:T(8,128)(2,1)S(1)}, u32[]{:S(2)}, u32[]{:S(2)}) %collective-permute-start.11) | collective-permute-done | bytes 405536 | tf_op jit(solution)/shard_map/ppermute | solution.py:38
  227.7 0.7 fusion.6.refs_1_
  228.3 7.3 %collective-permute-done.12.refs_11_ = bf16[144,1408]{1,0:T(8,128)(2,1)S(1)} collective-permute-done((bf16[144,1408]{1,0:T(8,128)(2,1)}, bf16[144,1408]{1,0:T(8,128)(2,1)S(1)}, u32[]{:S(2)}, u32[]{:S(2)}) %collective-permute-start.12) | collective-permute-done | bytes 405536 | tf_op jit(solution)/shard_map/ppermute | solution.py:38
  235.6 8.7 %collective-permute-done.13.refs_12_ = bf16[144,1408]{1,0:T(8,128)(2,1)S(1)} collective-permute-done((bf16[144,1408]{1,0:T(8,128)(2,1)}, bf16[144,1408]{1,0:T(8,128)(2,1)S(1)}, u32[]{:S(2)}, u32[]{:S(2)}) %collective-permute-start.13) | collective-permute-done | bytes 405536 | tf_op jit(solution)/shard_map/ppermute | solution.py:38
  244.3 0.7 copy-done.7
  245.2 0.8 copy-done.9
  246.6 1.1 copy-done
  247.7 8.6 %column_sums.1 = (f32[512,1280]{1,0:T(8,128)}, bf16[256,1280]{1,0:T(8,128)(2,1)}, bf16[256,1280]{1,0:T(8,128)(2,1)}) custom-call(f32[8,1152]{1,0:T(8,128)} %broadcast_in_dim.34.refs_0_, bf16[16,1152]{1,0:T(8,128)(2,1)} %fusion.6.refs_1_, bf16[1024,16]{1,0:T(8,128)(2,1)} %bitcast.33, bf16[1024,16]{1,0:T(8,128)(2,1)} %bitcast.34, bf16[1152,1280]{1,0:T(8,128)(2,1)} %bitcast.26), custom_call_target="tpu_custom_call" | custom-call | flops 603979776000 | bytes 6881280 | tf_op jit(solution)/shard_map/column_sums/pallas_call | solution.py:385
  257.0 0.8 copy.21
  257.8 0.8 copy.22
  258.6 0.9 collective-permute-done.15.refs_4_
  259.5 0.9 copy-done.3
  260.4 7.3 %group_sums.1 = (bf16[384,1408]{1,0:T(8,128)(2,1)}, bf16[128,1280]{1,0:T(8,128)(2,1)}, bf16[128,1280]{1,0:T(8,128)(2,1)}, bf16[128,1280]{1,0:T(8,128)(2,1)}, bf16[128,1280]{1,0:T(8,128)(2,1)}) custom-call(f32[384,8]{1,0:T(8,128)} %bitcast.31, f32[384,8]{1,0:T(8,128)} %bitcast.32, f32[512,1280]{1,0:T(8,128)} %get-tuple-element.96.refs_2_, ...), custom_call_target="tpu_custom_call" | custom-call | flops 1245708288 | bytes 3244032 | tf_op jit(solution)/shard_map/group_sums/pallas_call | solution.py:221
  267.7 6.8 %all-to-all-start.3 = ((bf16[16,24,1408]{2,1,0:T(8,128)(2,1)}), bf16[16,24,1408]{2,1,0:T(8,128)(2,1)S(1)}, u32[]{:S(2)}, u32[]{:S(2)}) async-start(bf16[16,24,1408]{2,1,0:T(8,128)(2,1)} %bitcast.30), calls=%async_computation.3 | async-start | bytes 2162688 | tf_op jit(solution)/shard_map/all_to_all | solution.py:452
  274.7 3.4 %collective-permute-start.17 = (bf16[128,1280]{1,0:T(8,128)(2,1)S(1)}, bf16[128,1280]{1,0:T(8,128)(2,1)S(1)}, u32[]{:S(2)}, u32[]{:S(2)}) collective-permute-start(bf16[128,1280]{1,0:T(8,128)(2,1)S(1)} %copy-done.21), channel_id=1, source_target_pairs={{0,4},{1,5},{2,6},{3,7},{4,0},{5,1},{6,2},{7,3},{8,12},{9,13},{10,... | collective-permute-start | bytes 983048 | tf_op jit(solution)/shard_map/ppermute | solution.py:38
  278.5 4.7 %collective-permute-done.16 = bf16[128,1280]{1,0:T(8,128)(2,1)S(1)} collective-permute-done((bf16[128,1280]{1,0:T(8,128)(2,1)S(1)}, bf16[128,1280]{1,0:T(8,128)(2,1)S(1)}, u32[]{:S(2)}, u32[]{:S(2)}) %collective-permute-start.16) | collective-permute-done | bytes 327712 | tf_op jit(solution)/shard_map/ppermute | solution.py:38
  283.2 9.0 %collective-permute-done.17 = bf16[128,1280]{1,0:T(8,128)(2,1)S(1)} collective-permute-done((bf16[128,1280]{1,0:T(8,128)(2,1)S(1)}, bf16[128,1280]{1,0:T(8,128)(2,1)S(1)}, u32[]{:S(2)}, u32[]{:S(2)}) %collective-permute-start.17) | collective-permute-done | bytes 327712 | tf_op jit(solution)/shard_map/ppermute | solution.py:38
  292.2 2.0 collective-permute-done.18
  295.0 0.9 select_reduce_fusion
  295.9 0.9 pad_maximum_fusion
  (92 shorter events, 7.0 us)
Async XLA Ops:
  7.2 44.6 %all-gather.2.cloned.1.call-start = ((), (), s32[]{:S(2)}) async-start(), calls=%async_computation.4 | async-start | bytes 5898240 | tf_op jit(solution)/shard_map/all_gather | solution.py:415
  10.5 3.4 %copy-start.12 = (f32[16,128]{1,0:T(8,128)}, f32[16,128]{1,0:T(8,128)S(1)}, u32[]{:S(2)}) copy-start(f32[16,128]{1,0:T(8,128)S(1)} %convolution_select_fusion) | copy-start | bytes 24580
  13.8 46.5 %all-to-all-start = ((bf16[16,24,2688]{2,1,0:T(8,128)(2,1)}), bf16[16,24,2688]{2,1,0:T(8,128)(2,1)S(1)}, u32[]{:S(2)}, u32[]{:S(2)}) async-start(bf16[16,24,2688]{2,1,0:T(8,128)(2,1)} %bitcast.5), calls=%async_computation | async-start | bytes 4128768 | tf_op jit(solution)/shard_map/all_to_all | solution.py:430
  60.3 1.4 copy-start.1
  61.7 103.8 %all-to-all-start.1 = ((bf16[16,72,2560]{2,1,0:T(8,128)(2,1)}), bf16[16,72,2560]{2,1,0:T(8,128)(2,1)}, u32[]{:S(2)}, u32[]{:S(2)}) async-start(bf16[16,72,2560]{2,1,0:T(8,128)(2,1)} %bitcast.25), calls=%async_computation.1 | async-start | bytes 11796480 | tf_op jit(solution)/shard_map/all_to_all | solution.py:435
  76.1 5.5 %collective-permute-start = (bf16[144,2560]{1,0:T(8,128)(2,1)}, bf16[144,2560]{1,0:T(8,128)(2,1)S(1)}, u32[]{:S(2)}, u32[]{:S(2)}) collective-permute-start(bf16[144,2560]{1,0:T(8,128)(2,1)} %get-tuple-element.73), channel_id=1, source_target_pairs={{0,1},{1,0},{2,3},{3,2},{4,5},{5,4},{6,7},{7,6},{8,9},{9,8},{10,11... | collective-permute-start | bytes 2211848 | tf_op jit(solution)/shard_map/ppermute | solution.py:38
  76.6 18.4 %collective-permute-start.1 = (bf16[144,2560]{1,0:T(8,128)(2,1)}, bf16[144,2560]{1,0:T(8,128)(2,1)S(1)}, u32[]{:S(2)}, u32[]{:S(2)}) collective-permute-start(bf16[144,2560]{1,0:T(8,128)(2,1)} %get-tuple-element.74), channel_id=1, source_target_pairs={{0,2},{1,3},{2,0},{3,1},{4,6},{5,7},{6,4},{7,5},{8,10},{9,11},{10,... | collective-permute-start | bytes 2211848 | tf_op jit(solution)/shard_map/ppermute | solution.py:38
  77.6 34.1 %collective-permute-start.2 = (bf16[144,2560]{1,0:T(8,128)(2,1)}, bf16[144,2560]{1,0:T(8,128)(2,1)S(1)}, u32[]{:S(2)}, u32[]{:S(2)}) collective-permute-start(bf16[144,2560]{1,0:T(8,128)(2,1)} %get-tuple-element.75), channel_id=1, source_target_pairs={{0,3},{1,2},{2,1},{3,0},{4,7},{5,6},{6,5},{7,4},{8,11},{9,10},{10,... | collective-permute-start | bytes 2211848 | tf_op jit(solution)/shard_map/ppermute | solution.py:38
  78.4 50.2 %collective-permute-start.3 = (bf16[144,2560]{1,0:T(8,128)(2,1)}, bf16[144,2560]{1,0:T(8,128)(2,1)S(1)}, u32[]{:S(2)}, u32[]{:S(2)}) collective-permute-start(bf16[144,2560]{1,0:T(8,128)(2,1)} %get-tuple-element.76), channel_id=1, source_target_pairs={{0,4},{1,5},{2,6},{3,7},{4,0},{5,1},{6,2},{7,3},{8,12},{9,13},{10,... | collective-permute-start | bytes 2211848 | tf_op jit(solution)/shard_map/ppermute | solution.py:38
  80.1 64.5 %collective-permute-start.4 = (bf16[144,2560]{1,0:T(8,128)(2,1)}, bf16[144,2560]{1,0:T(8,128)(2,1)}, u32[]{:S(2)}, u32[]{:S(2)}) collective-permute-start(bf16[144,2560]{1,0:T(8,128)(2,1)} %get-tuple-element.77), channel_id=1, source_target_pairs={{0,5},{1,4},{2,7},{3,6},{4,1},{5,0},{6,3},{7,2},{8,13},{9,12},{10,... | collective-permute-start | bytes 2211848 | tf_op jit(solution)/shard_map/ppermute | solution.py:38
  81.7 67.1 %copy-start.16 = (bf16[144,2560]{1,0:T(8,128)(2,1)}, bf16[144,2560]{1,0:T(8,128)(2,1)S(1)}, u32[]{:S(2)}) copy-start(bf16[144,2560]{1,0:T(8,128)(2,1)S(1)} %collective-permute-done.refs_2_) | copy-start | bytes 2211844
  81.7 63.0 %collective-permute-start.5 = (bf16[144,2560]{1,0:T(8,128)(2,1)}, bf16[144,2560]{1,0:T(8,128)(2,1)}, u32[]{:S(2)}, u32[]{:S(2)}) collective-permute-start(bf16[144,2560]{1,0:T(8,128)(2,1)} %get-tuple-element.78), channel_id=1, source_target_pairs={{0,6},{1,7},{2,4},{3,5},{4,2},{5,3},{6,0},{7,1},{8,14},{9,15},{10,... | collective-permute-start | bytes 2211848 | tf_op jit(solution)/shard_map/ppermute | solution.py:38
  95.0 53.8 %copy-start.17 = (bf16[144,2560]{1,0:T(8,128)(2,1)}, bf16[144,2560]{1,0:T(8,128)(2,1)S(1)}, u32[]{:S(2)}) copy-start(bf16[144,2560]{1,0:T(8,128)(2,1)S(1)} %collective-permute-done.1.refs_3_) | copy-start | bytes 2211844
  95.0 53.8 %collective-permute-start.6 = (bf16[144,2560]{1,0:T(8,128)(2,1)}, bf16[144,2560]{1,0:T(8,128)(2,1)}, u32[]{:S(2)}, u32[]{:S(2)}) collective-permute-start(bf16[144,2560]{1,0:T(8,128)(2,1)} %get-tuple-element.79), channel_id=1, source_target_pairs={{0,7},{1,6},{2,5},{3,4},{4,3},{5,2},{6,1},{7,0},{8,15},{9,14},{10,... | collective-permute-start | bytes 2211848 | tf_op jit(solution)/shard_map/ppermute | solution.py:38
  111.7 37.1 %copy-start.18 = (bf16[144,2560]{1,0:T(8,128)(2,1)}, bf16[144,2560]{1,0:T(8,128)(2,1)S(1)}, u32[]{:S(2)}) copy-start(bf16[144,2560]{1,0:T(8,128)(2,1)S(1)} %collective-permute-done.2.refs_4_) | copy-start | bytes 2211844
  128.6 20.2 %copy-start.19 = (bf16[144,2560]{1,0:T(8,128)(2,1)}, bf16[144,2560]{1,0:T(8,128)(2,1)S(1)}, u32[]{:S(2)}) copy-start(bf16[144,2560]{1,0:T(8,128)(2,1)S(1)} %collective-permute-done.3.refs_5_) | copy-start | bytes 2211844
  184.4 61.6 %all-to-all-start.2 = ((bf16[16,72,1280]{2,1,0:T(8,128)(2,1)}), bf16[16,72,1280]{2,1,0:T(8,128)(2,1)S(1)}, u32[]{:S(2)}, u32[]{:S(2)}) async-start(bf16[16,72,1280]{2,1,0:T(8,128)(2,1)} %bitcast.27), calls=%async_computation.2 | async-start | bytes 5898240 | tf_op jit(solution)/shard_map/all_to_all | solution.py:447
  205.1 12.2 %collective-permute-start.10 = (bf16[144,1408]{1,0:T(8,128)(2,1)}, bf16[144,1408]{1,0:T(8,128)(2,1)S(1)}, u32[]{:S(2)}, u32[]{:S(2)}) collective-permute-start(bf16[144,1408]{1,0:T(8,128)(2,1)} %get-tuple-element.91), channel_id=1, source_target_pairs={{0,4},{1,5},{2,6},{3,7},{4,0},{5,1},{6,2},{7,3},{8,12},{9,13},{10,... | collective-permute-start | bytes 1216520 | tf_op jit(solution)/shard_map/ppermute | solution.py:38
  205.8 21.8 %collective-permute-start.11 = (bf16[144,1408]{1,0:T(8,128)(2,1)}, bf16[144,1408]{1,0:T(8,128)(2,1)S(1)}, u32[]{:S(2)}, u32[]{:S(2)}) collective-permute-start(bf16[144,1408]{1,0:T(8,128)(2,1)} %get-tuple-element.92), channel_id=1, source_target_pairs={{0,5},{1,4},{2,7},{3,6},{4,1},{5,0},{6,3},{7,2},{8,13},{9,12},{10,... | collective-permute-start | bytes 1216520 | tf_op jit(solution)/shard_map/ppermute | solution.py:38
  208.8 26.8 %collective-permute-start.12 = (bf16[144,1408]{1,0:T(8,128)(2,1)}, bf16[144,1408]{1,0:T(8,128)(2,1)S(1)}, u32[]{:S(2)}, u32[]{:S(2)}) collective-permute-start(bf16[144,1408]{1,0:T(8,128)(2,1)} %get-tuple-element.93), channel_id=1, source_target_pairs={{0,6},{1,7},{2,4},{3,5},{4,2},{5,3},{6,0},{7,1},{8,14},{9,15},{10,... | collective-permute-start | bytes 1216520 | tf_op jit(solution)/shard_map/ppermute | solution.py:38
  211.1 33.2 %collective-permute-start.13 = (bf16[144,1408]{1,0:T(8,128)(2,1)}, bf16[144,1408]{1,0:T(8,128)(2,1)S(1)}, u32[]{:S(2)}, u32[]{:S(2)}) collective-permute-start(bf16[144,1408]{1,0:T(8,128)(2,1)} %get-tuple-element.94), channel_id=1, source_target_pairs={{0,7},{1,6},{2,5},{3,4},{4,3},{5,2},{6,1},{7,0},{8,15},{9,14},{10,... | collective-permute-start | bytes 1216520 | tf_op jit(solution)/shard_map/ppermute | solution.py:38
  211.4 32.9 %collective-permute-start.7 = (bf16[144,1408]{1,0:T(8,128)(2,1)}, bf16[144,1408]{1,0:T(8,128)(2,1)S(1)}, u32[]{:S(2)}, u32[]{:S(2)}) collective-permute-start(bf16[144,1408]{1,0:T(8,128)(2,1)} %get-tuple-element.88), channel_id=1, source_target_pairs={{0,1},{1,0},{2,3},{3,2},{4,5},{5,4},{6,7},{7,6},{8,9},{9,8},{10,11... | collective-permute-start | bytes 1216520 | tf_op jit(solution)/shard_map/ppermute | solution.py:38
  217.3 27.0 %copy-start.4 = (bf16[144,1408]{1,0:T(8,128)(2,1)}, bf16[144,1408]{1,0:T(8,128)(2,1)S(1)}, u32[]{:S(2)}) copy-start(bf16[144,1408]{1,0:T(8,128)(2,1)S(1)} %collective-permute-done.10.refs_9_) | copy-start | bytes 1216516
  217.3 27.0 %collective-permute-start.8 = (bf16[144,1408]{1,0:T(8,128)(2,1)}, bf16[144,1408]{1,0:T(8,128)(2,1)S(1)}, u32[]{:S(2)}, u32[]{:S(2)}) collective-permute-start(bf16[144,1408]{1,0:T(8,128)(2,1)} %get-tuple-element.89), channel_id=1, source_target_pairs={{0,2},{1,3},{2,0},{3,1},{4,6},{5,7},{6,4},{7,5},{8,10},{9,11},{10,... | collective-permute-start | bytes 1216520 | tf_op jit(solution)/shard_map/ppermute | solution.py:38
  227.7 16.7 %copy-start.5 = (bf16[144,1408]{1,0:T(8,128)(2,1)}, bf16[144,1408]{1,0:T(8,128)(2,1)S(1)}, u32[]{:S(2)}) copy-start(bf16[144,1408]{1,0:T(8,128)(2,1)S(1)} %collective-permute-done.11.refs_10_) | copy-start | bytes 1216516
  227.7 18.3 %collective-permute-start.9 = (bf16[144,1408]{1,0:T(8,128)(2,1)}, bf16[144,1408]{1,0:T(8,128)(2,1)}, u32[]{:S(2)}, u32[]{:S(2)}) collective-permute-start(bf16[144,1408]{1,0:T(8,128)(2,1)} %get-tuple-element.90), channel_id=1, source_target_pairs={{0,3},{1,2},{2,1},{3,0},{4,7},{5,6},{6,5},{7,4},{8,11},{9,10},{10,... | collective-permute-start | bytes 1216520 | tf_op jit(solution)/shard_map/ppermute | solution.py:38
  235.6 8.7 %copy-start.6 = (bf16[144,1408]{1,0:T(8,128)(2,1)}, bf16[144,1408]{1,0:T(8,128)(2,1)S(1)}, u32[]{:S(2)}) copy-start(bf16[144,1408]{1,0:T(8,128)(2,1)S(1)} %collective-permute-done.12.refs_11_) | copy-start | bytes 1216516
  244.3 0.8 copy-start.7
  244.3 0.9 copy-start.8
  245.2 0.8 copy-start.9
  246.0 1.7 copy-start
  247.7 9.3 %copy-start.15 = (f32[8,384]{1,0:T(8,128)S(1)}, f32[8,384]{1,0:T(8,128)}, u32[]{:S(2)}) copy-start(f32[8,384]{1,0:T(8,128)} %get-tuple-element.67) | copy-start | bytes 36868
  247.7 10.1 %copy-start.14 = (f32[8,384]{1,0:T(8,128)S(1)}, f32[8,384]{1,0:T(8,128)}, u32[]{:S(2)}) copy-start(f32[8,384]{1,0:T(8,128)} %get-tuple-element.68) | copy-start | bytes 36868
  256.2 2.3 collective-permute-start.14
  256.6 2.9 collective-permute-start.15
  258.6 0.9 copy-start.2
  259.5 0.9 copy-start.3
  267.7 6.9 %copy-start.22 = (bf16[128,1280]{1,0:T(8,128)(2,1)S(1)}, bf16[128,1280]{1,0:T(8,128)(2,1)}, u32[]{:S(2)}) copy-start(bf16[128,1280]{1,0:T(8,128)(2,1)} %get-tuple-element.109) | copy-start | bytes 983044
  267.7 7.0 %copy-start.21 = (bf16[128,1280]{1,0:T(8,128)(2,1)S(1)}, bf16[128,1280]{1,0:T(8,128)(2,1)}, u32[]{:S(2)}) copy-start(bf16[128,1280]{1,0:T(8,128)(2,1)} %get-tuple-element.110) | copy-start | bytes 983044
  267.7 10.4 %copy-start.20 = (bf16[128,1280]{1,0:T(8,128)(2,1)S(1)}, bf16[128,1280]{1,0:T(8,128)(2,1)}, u32[]{:S(2)}) copy-start(bf16[128,1280]{1,0:T(8,128)(2,1)} %get-tuple-element.111) | copy-start | bytes 983044
  267.7 26.6 %copy-start.10 = (bf16[128,1280]{1,0:T(8,128)(2,1)S(1)}, bf16[128,1280]{1,0:T(8,128)(2,1)}, u32[]{:S(2)}) copy-start(bf16[128,1280]{1,0:T(8,128)(2,1)} %get-tuple-element.108) | copy-start | bytes 983044
  267.7 26.7 %copy-start.13 = (f32[16,128]{1,0:T(8,128)S(1)}, f32[16,128]{1,0:T(8,128)}, u32[]{:S(2)}) copy-start(f32[16,128]{1,0:T(8,128)} %copy-done.12) | copy-start | bytes 24580
  267.7 26.7 %all-to-all-start.3 = ((bf16[16,24,1408]{2,1,0:T(8,128)(2,1)}), bf16[16,24,1408]{2,1,0:T(8,128)(2,1)S(1)}, u32[]{:S(2)}, u32[]{:S(2)}) async-start(bf16[16,24,1408]{2,1,0:T(8,128)(2,1)} %bitcast.30), calls=%async_computation.3 | async-start | bytes 2162688 | tf_op jit(solution)/shard_map/all_to_all | solution.py:452
  274.6 8.7 %collective-permute-start.16 = (bf16[128,1280]{1,0:T(8,128)(2,1)S(1)}, bf16[128,1280]{1,0:T(8,128)(2,1)S(1)}, u32[]{:S(2)}, u32[]{:S(2)}) collective-permute-start(bf16[128,1280]{1,0:T(8,128)(2,1)S(1)} %copy-done.22), channel_id=1, source_target_pairs={{0,2},{1,3},{2,0},{3,1},{4,6},{5,7},{6,4},{7,5},{8,10},{9,11},{10,... | collective-permute-start | bytes 983048 | tf_op jit(solution)/shard_map/ppermute | solution.py:38
  274.7 17.6 %collective-permute-start.17 = (bf16[128,1280]{1,0:T(8,128)(2,1)S(1)}, bf16[128,1280]{1,0:T(8,128)(2,1)S(1)}, u32[]{:S(2)}, u32[]{:S(2)}) collective-permute-start(bf16[128,1280]{1,0:T(8,128)(2,1)S(1)} %copy-done.21), channel_id=1, source_target_pairs={{0,4},{1,5},{2,6},{3,7},{4,0},{5,1},{6,2},{7,3},{8,12},{9,13},{10,... | collective-permute-start | bytes 983048 | tf_op jit(solution)/shard_map/ppermute | solution.py:38
  278.0 16.2 %collective-permute-start.18 = (bf16[128,1280]{1,0:T(8,128)(2,1)S(1)}, bf16[128,1280]{1,0:T(8,128)(2,1)S(1)}, u32[]{:S(2)}, u32[]{:S(2)}) collective-permute-start(bf16[128,1280]{1,0:T(8,128)(2,1)S(1)} %copy-done.20), channel_id=1, source_target_pairs={{0,6},{1,7},{2,4},{3,5},{4,2},{5,3},{6,0},{7,1},{8,14},{9,15},{10,... | collective-permute-start | bytes 983048 | tf_op jit(solution)/shard_map/ppermute | solution.py:38
  294.3 0.7 copy-start.11
Sparse Core Ops, SparseCore 0:
  9.7 41.2 all-gather.1

commit v5 on v4

--- a/solution.py
+++ b/solution.py
@@ -28,6 +28,10 @@
     lower = (jnp.arange(n)[:, None] > jnp.arange(n)[None, :]).astype(BF)
     counts = jnp.einsum("ij,...jm->...im", lower, names.astype(BF), preferred_element_type=F32)
     return jnp.where(names, counts, -1.0)
+
+
+def first_columns(features):
+    return max(2 * features // 5 // 256 * 256, 256)
 
 
 def barrier(*values):
@@ -128,11 +132,12 @@
 
 def hidden_grads(lane, rows_grad, down_mat, pre_gate, pre_up, gate_mat, up_mat):
     total, features = rows_grad.shape
-    units, half, steps = down_mat.shape[0], features // 2, 4
+    units, first, steps = down_mat.shape[0], first_columns(features), 4
+    half = features - first
     tall = total // steps
-    wide = 256 if half % 256 == 0 else half
+    wide = 512 if half % 512 == 0 else half
     row = lambda width: pl.BlockSpec((tall, width), lambda i: (jnp.minimum(i, steps - 1), 0))
-    mat = pl.BlockSpec((wide, units), lambda i: (half // wide + jnp.maximum(i - steps, 0), 0))
+    mat = pl.BlockSpec((wide, units), lambda i: (first // wide + jnp.maximum(i - steps, 0), 0))
     return pl.pallas_call(
         lambda *refs: grad_kernel(steps, *refs),
         grid=(steps + half // wide,),
@@ -178,9 +183,9 @@
 
 def returned_a(table, grad_gate, grad_up, gate_mat, up_mat, gate_dot, n_exp):
     total, units = grad_gate.shape
-    half = gate_mat.shape[0] // 2
+    half = first_columns(gate_mat.shape[0])
     pairs = table.shape[0]
-    wide = 256 if half % 256 == 0 else half
+    wide = 512 if half % 512 == 0 else half
     mat = pl.BlockSpec((wide, units), lambda j: (j, 0))
     block = (total // n_exp, half + LANES)
     return pl.pallas_call(
@@ -268,7 +273,7 @@
     n_rows, width = hub.shape
     n_exp = tables[1].shape[0]
     features = width - LANES
-    wide = 512 if features % 512 == 0 else features
+    wide = 1280 if features % 1280 == 0 else features
     shape = (n_rows // per_group * cap, features)
     row = (n_exp, n_rows)
     part = lambda rows: pl.BlockSpec((rows, wide), lambda j: (0, j))
@@ -342,7 +347,7 @@
 
 def column_rows(member, table, hot, column, n_exp):
     total, features = hot.shape[0], column.shape[1]
-    wide = 512 if features % 512 == 0 else features
+    wide = 1280 if features % 1280 == 0 else features
     part = lambda rows: pl.BlockSpec((rows, wide), lambda j: (0, j))
     return pl.pallas_call(
         lambda *refs: rows_kernel(n_exp, *refs),
@@ -380,7 +385,7 @@
     place = jnp.broadcast_to((at % (total // n_seq)).astype(F32), (8, total))
     spread = (jnp.arange(n_seq)[:, None] == at[None, :] // (total // n_seq)).astype(BF)
     shape = (n_rows // 2, half)
-    wide = 256 if half % 256 == 0 else half
+    wide = 512 if half % 512 == 0 else half
     part = lambda rows: pl.BlockSpec((rows, wide), lambda j: (0, j))
     return pl.pallas_call(
         lambda *refs: column_kernel(n_exp, *refs),
@@ -403,7 +408,8 @@
     experts = n_seq * n_exp
     cap = 3 * top * n_tok // (2 * experts)
     per_group = top // 2 * n_tok // n_seq
-    half = features // 2
+    first = first_columns(features)
+    rest = features - first
     gate_mat, up_mat, down_mat = w_gate[0], w_up[0], w_down[0]
     partner = member ^ jnp.arange(n_exp)
     to_b, to_a = window_tables(n_seq, n_exp, cap)
@@ -444,16 +450,16 @@
 
     back_a = returned_a(to_a, grad_gate, grad_up, gate_mat, up_mat, gate_dot, n_exp)
     got_a = exchange(back_a)
-    got_b = lax.all_to_all(back_b.reshape(n_seq, rows_b, half), "seq", 0, 0, tiled=True)
+    got_b = lax.all_to_all(back_b.reshape(n_seq, rows_b, rest), "seq", 0, 0, tiled=True)
     got_b, *got_a = barrier(got_b, *got_a)
-    mine, *other = column_sums(slot_b, weight_b, got_b.reshape(n_seq * rows_b, half), n_exp)
+    mine, *other = column_sums(slot_b, weight_b, got_b.reshape(n_seq * rows_b, rest), n_exp)
     back, *chip = group_sums(slot_a, weight_a, mine, *(swap(x, 1) for x in other), got_a)
     final_b = sum(p.astype(F32) for p in exchange(chip, 2))
-    back = lax.all_to_all(back.reshape(n_seq, per_group, half + LANES), "seq", 0, 0, tiled=True)
-    final_a = dot_t(pick, back.reshape(n_seq * per_group, half + LANES))
-
-    grad_in = jnp.concatenate((final_a[:, :half], final_b), axis=1).astype(BF)
-    table = final_a[:, half:]
+    back = lax.all_to_all(back.reshape(n_seq, per_group, first + LANES), "seq", 0, 0, tiled=True)
+    final_a = dot_t(pick, back.reshape(n_seq * per_group, first + LANES))
+
+    grad_in = jnp.concatenate((final_a[:, :first], final_b), axis=1).astype(BF)
+    table = final_a[:, first:]
     chosen = expert_ids[:, :, None] == jnp.arange(experts)[None, None, :]
     grad_gates = jnp.sum(jnp.where(chosen, table[:, None, :experts], 0.0), axis=2).astype(BF)
     return grad_in, grad_gates

time: 306 us -> 301 us (0.984)
  Pallas kernels: 82.9 us -> 77.4 us
    all_to_all x2, waiting for transfers between devices: 0.01 us -> 9.18 us  [the longest x1 9.17 us: per_device(): lax.all_to_all(back_b.reshape(n_seq, rows_b, rest), 'seq', 0, 0, tiled=True)]
    ppermute x19, waiting for transfers between devices: 110 us -> 102 us  [swap(): lax.ppermute(x, 'exp', [(i, i ^ k) for i in range(lax.axis_size('exp'))])]
    pallas_call x1, Pallas kernels: 13.9 us -> 10 us  [returned_a(): pl.pallas_call(lambda *refs: back_a_kernel(n_exp, pairs, *refs), grid=(ha...]
    unnamed x48 -> x38, local copies, waits for them, and re-layouts: 6.62 us -> 6.62 us
  transfers between devices with their start and end apart: 24 -> 24, of which waited for: 13 -> 14; matrix products, arithmetic and copies ran while one was open for 7% -> 7% of each run, Pallas kernels for 16% -> 14%
where the time goes in v5:
time: 301 us; the launch traced here: 300 us
  waiting for transfers between devices  112 us (37%)
  Pallas kernels  77.4 us (26%)
  starting transfers between devices  50.3 us (17%)
  local copies, waits for them, and re-layouts  16.5 us (5%)
  blocking collectives  15.6 us (5%)
  between operations  14.3 us (5%)
  other arithmetic  11 us (4%)
    ppermute x19, waiting for transfers between devices, swap(): lax.ppermute(x, 'exp', [(i, i ^ k) for i in range(lax.axis_size('exp'))])  102 us
    ppermute x19, starting transfers between devices, swap(): lax.ppermute(x, 'exp', [(i, i ^ k) for i in range(lax.axis_size('exp'))])  23.6 us
    pallas_call x1, Pallas kernels, hidden_grads(): pl.pallas_call(lambda *refs: grad_kernel(steps, *refs), grid=(steps + hal...  18.9 us
    pallas_call x1, Pallas kernels, pre_products(): pl.pallas_call(lambda *refs: pre_kernel(chips, pairs, *refs), grid=(units...  16.6 us
    all_gather x1, blocking collectives, per_device(): column_meta = lax.all_gather(meta, 'exp', axis=0, tiled=True)  15.6 us
    pallas_call x1, Pallas kernels, returned_a(): pl.pallas_call(lambda *refs: back_a_kernel(n_exp, pairs, *refs), grid=(ha...  10 us
    all_to_all x1, waiting for transfers between devices, per_device(): lax.all_to_all(back_b.reshape(n_seq, rows_b, rest), 'seq', 0, 0, tiled=True)  9.17 us
    pallas_call x1, Pallas kernels, column_sums(): pl.pallas_call(lambda *refs: column_kernel(n_exp, *refs), grid=(half // w...  8.64 us
  transfers between devices with their start and end apart: 24, of which 14 were waited for; matrix products, arithmetic and copies ran while one was open for 7% of the time, Pallas kernels for 14%

profile of v5, /device:TPU:1, one launch (start us, length us, event | category | flops | bytes accessed | tf_op | source)
XLA Modules:
  0.0 299.7 jit_solution(16682861367082841507)
XLA Ops:
  7.2 0.7 all-gather.2.cloned.1.call-update
  7.9 0.8 copy.17
  8.7 0.8 copy.18
  9.6 0.7 add_select_fusion.3
  10.6 1.2 concatenate.12
  11.8 2.0 convolution_convert_fusion
  13.8 8.4 %all-to-all-start = ((bf16[16,24,2688]{2,1,0:T(8,128)(2,1)}), bf16[16,24,2688]{2,1,0:T(8,128)(2,1)S(1)}, u32[]{:S(2)}, u32[]{:S(2)}) async-start(bf16[16,24,2688]{2,1,0:T(8,128)(2,1)} %bitcast.5), calls=%async_computation | async-start | bytes 4128768 | tf_op jit(solution)/shard_map/all_to_all | solution.py:436
  22.4 15.6 %all_gather.6.refs_7_ = bf16[1024,128]{1,0:T(8,128)(2,1)} all-gather(bf16[128,128]{1,0:T(8,128)(2,1)S(1)} %pad_maximum_fusion.1), channel_id=1, replica_groups=mesh['seq'=16,'exp'=8] {'exp'}, dimensions={0}, use_global_device_ids=true | all-gather | bytes 294912 | tf_op jit(solution)/shard_map/all_gather | solution.py:420
  38.1 0.7 fusion.5.refs_5_
  38.8 0.7 fusion.7
  40.1 0.7 broadcast_in_dim.30.refs_6_
  41.5 2.4 column_slots.1
  43.8 0.8 convert_element_type.107
  44.7 0.8 copy.19
  45.5 0.8 convert_element_type.109
  46.4 0.8 copy.20
  47.3 0.8 fusion.3.refs_2_
  48.2 1.0 fusion.1.refs_1_.refs_0_
  49.2 1.3 fusion.refs_0_
  51.8 7.1 %column_rows.1 = bf16[1152,2560]{1,0:T(8,128)(2,1)} custom-call(s32[1]{0:T(128)} %bitcast.1.refs_0_, bf16[8,144,256]{2,1,0:T(8,128)(2,1)} %fusion.1.refs_1_.refs_0_, bf16[1152,128]{1,0:T(8,128)(2,1)} %get-tuple-element.65.refs_2_, bf16[1024,2560]{1,0:T(8,128)(2,1)} %all-gather.2.cloned.1.call-done.refs_3_), custom_call_target="tpu_custom_call" | custom-call | flops 37748736 | bytes 294912 | tf_op jit(solution)/shard_map/column_rows/pallas_call | solution.py:352
  58.9 1.3 copy-done.1
  60.3 7.0 %all-to-all-start.1 = ((bf16[16,72,2560]{2,1,0:T(8,128)(2,1)}), bf16[16,72,2560]{2,1,0:T(8,128)(2,1)}, u32[]{:S(2)}, u32[]{:S(2)}) async-start(bf16[16,72,2560]{2,1,0:T(8,128)(2,1)} %bitcast.25), calls=%async_computation.1 | async-start | bytes 11796480 | tf_op jit(solution)/shard_map/all_to_all | solution.py:441
  67.3 6.7 %hub_blocks.1 = (bf16[144,2560]{1,0:T(8,128)(2,1)}, bf16[144,2560]{1,0:T(8,128)(2,1)}, bf16[144,2560]{1,0:T(8,128)(2,1)}, bf16[144,2560]{1,0:T(8,128)(2,1)}, bf1...) custom-call(bf16[128,128]{1,0:T(8,128)(2,1)} %get-tuple-element.60.r, ...), custom_call_target="tpu_custom_call" | custom-call | flops 2378170368 | bytes 5898240 | tf_op jit(solution)/shard_map/hub_blocks/pallas_call | solution.py:280
  74.6 1.0 collective-permute-start.1
  75.6 0.7 collective-permute-start.2
  76.3 1.7 collective-permute-start.3
  78.0 1.6 collective-permute-start.4
  79.6 2.2 collective-permute-start.5
  81.8 11.1 %collective-permute-done.1.refs_3_ = bf16[144,2560]{1,0:T(8,128)(2,1)S(1)} collective-permute-done((bf16[144,2560]{1,0:T(8,128)(2,1)}, bf16[144,2560]{1,0:T(8,128)(2,1)S(1)}, u32[]{:S(2)}, u32[]{:S(2)}) %collective-permute-start.1) | collective-permute-done | bytes 737312 | tf_op jit(solution)/shard_map/ppermute | solution.py:42
  92.9 3.3 %collective-permute-start.6 = (bf16[144,2560]{1,0:T(8,128)(2,1)}, bf16[144,2560]{1,0:T(8,128)(2,1)}, u32[]{:S(2)}, u32[]{:S(2)}) collective-permute-start(bf16[144,2560]{1,0:T(8,128)(2,1)} %get-tuple-element.79), channel_id=1, source_target_pairs={{0,7},{1,6},{2,5},{3,4},{4,3},{5,2},{6,1},{7,0},{8,15},{9,14},{10,... | collective-permute-start | bytes 2211848 | tf_op jit(solution)/shard_map/ppermute | solution.py:42
  96.3 13.4 %collective-permute-done.2.refs_4_ = bf16[144,2560]{1,0:T(8,128)(2,1)S(1)} collective-permute-done((bf16[144,2560]{1,0:T(8,128)(2,1)}, bf16[144,2560]{1,0:T(8,128)(2,1)S(1)}, u32[]{:S(2)}, u32[]{:S(2)}) %collective-permute-start.2) | collective-permute-done | bytes 737312 | tf_op jit(solution)/shard_map/ppermute | solution.py:42
  109.7 16.8 %collective-permute-done.3.refs_5_ = bf16[144,2560]{1,0:T(8,128)(2,1)S(1)} collective-permute-done((bf16[144,2560]{1,0:T(8,128)(2,1)}, bf16[144,2560]{1,0:T(8,128)(2,1)S(1)}, u32[]{:S(2)}, u32[]{:S(2)}) %collective-permute-start.3) | collective-permute-done | bytes 737312 | tf_op jit(solution)/shard_map/ppermute | solution.py:42
  126.5 16.0 %collective-permute-done.4.refs_6_ = bf16[144,2560]{1,0:T(8,128)(2,1)} collective-permute-done((bf16[144,2560]{1,0:T(8,128)(2,1)}, bf16[144,2560]{1,0:T(8,128)(2,1)}, u32[]{:S(2)}, u32[]{:S(2)}) %collective-permute-start.4) | collective-permute-done | bytes 737312 | tf_op jit(solution)/shard_map/ppermute | solution.py:42
  142.5 4.2 %collective-permute-done.6.refs_8_ = bf16[144,2560]{1,0:T(8,128)(2,1)} collective-permute-done((bf16[144,2560]{1,0:T(8,128)(2,1)}, bf16[144,2560]{1,0:T(8,128)(2,1)}, u32[]{:S(2)}, u32[]{:S(2)}) %collective-permute-start.6) | collective-permute-done | bytes 737312 | tf_op jit(solution)/shard_map/ppermute | solution.py:42
  146.8 16.6 %pre_products.1 = (f32[1152,768]{1,0:T(8,128)}, f32[1152,768]{1,0:T(8,128)}) custom-call(bf16[8,144,256]{2,1,0:T(8,128)(2,1)} %fusion.1.refs_1_.refs_0_, bf16[144,2560]{1,0:T(8,128)(2,1)} %get-tuple-element.72.refs_1_, bf16[144,2560]{1,0:T(8,128)(2,1)} %copy-done.14, bf16[144,2560]{1,0:T(8,128)(2,1)} %copy-done.15, bf16[144,2560]{1,0:T(8,128)(2,1)} %copy-done.16, ...), custom_call_target="tpu_custom_call" | custom-call | flops 9059696640 | bytes 20840448 | tf_op jit(solution)/shard_map/pre_products/pallas_call | solution.py:94
  163.9 18.9 %hidden_grads.1 = (bf16[1152,768]{1,0:T(8,128)(2,1)}, bf16[1152,768]{1,0:T(8,128)(2,1)}, bf16[1152,128]{1,0:T(8,128)(2,1)}, bf16[1152,1536]{1,0:T(8,128)(2,1)}) custom-call(f32[8,128]{1,0:T(8,128)} %broadcast_in_dim.35.refs_0_, bf16[1152,2560]{1,0:T(8,128)(2,1)} %bitcast.10.refs_1_, bf16[768,2560]{1,0:T(8,128)(2,1)} %bitcast.35, ...), custom_call_target="tpu_custom_call" | custom-call | flops 9059696640 | bytes 30277632 | tf_op jit(solution)/shard_map/hidden_grads/pallas_call | solution.py:141
  182.9 6.9 %all-to-all-start.2 = ((bf16[16,72,1536]{2,1,0:T(8,128)(2,1)}), bf16[16,72,1536]{2,1,0:T(8,128)(2,1)S(1)}, u32[]{:S(2)}, u32[]{:S(2)}) async-start(bf16[16,72,1536]{2,1,0:T(8,128)(2,1)} %bitcast.27), calls=%async_computation.2 | async-start | bytes 7077888 | tf_op jit(solution)/shard_map/all_to_all | solution.py:453
  189.8 10.0 %returned_a.1 = (bf16[144,1152]{1,0:T(8,128)(2,1)}, bf16[144,1152]{1,0:T(8,128)(2,1)}, bf16[144,1152]{1,0:T(8,128)(2,1)}, bf16[144,1152]{1,0:T(8,128)(2,1)}, bf1...) custom-call(bf16[8,256,144]{2,1,0:T(8,128)(2,1)} %fusion.refs_0_, ...), custom_call_target="tpu_custom_call" | custom-call | flops 3623878656 | bytes 9043968 | tf_op jit(solution)/shard_map/returned_a/pallas_call | solution.py:191
  199.8 0.9 collective-permute-start.10
  200.7 2.8 collective-permute-start.11
  203.5 2.3 collective-permute-start.12
  206.6 3.8 %collective-permute-done.10.refs_9_ = bf16[144,1152]{1,0:T(8,128)(2,1)S(1)} collective-permute-done((bf16[144,1152]{1,0:T(8,128)(2,1)}, bf16[144,1152]{1,0:T(8,128)(2,1)S(1)}, u32[]{:S(2)}, u32[]{:S(2)}) %collective-permute-start.10) | collective-permute-done | bytes 331808 | tf_op jit(solution)/shard_map/ppermute | solution.py:42
  210.9 8.6 %collective-permute-done.11.refs_10_ = bf16[144,1152]{1,0:T(8,128)(2,1)S(1)} collective-permute-done((bf16[144,1152]{1,0:T(8,128)(2,1)}, bf16[144,1152]{1,0:T(8,128)(2,1)S(1)}, u32[]{:S(2)}, u32[]{:S(2)}) %collective-permute-start.11) | collective-permute-done | bytes 331808 | tf_op jit(solution)/shard_map/ppermute | solution.py:42
  220.1 5.4 %collective-permute-done.12.refs_11_ = bf16[144,1152]{1,0:T(8,128)(2,1)S(1)} collective-permute-done((bf16[144,1152]{1,0:T(8,128)(2,1)}, bf16[144,1152]{1,0:T(8,128)(2,1)S(1)}, u32[]{:S(2)}, u32[]{:S(2)}) %collective-permute-start.12) | collective-permute-done | bytes 331808 | tf_op jit(solution)/shard_map/ppermute | solution.py:42
  225.6 7.1 %collective-permute-done.13.refs_12_ = bf16[144,1152]{1,0:T(8,128)(2,1)S(1)} collective-permute-done((bf16[144,1152]{1,0:T(8,128)(2,1)}, bf16[144,1152]{1,0:T(8,128)(2,1)S(1)}, u32[]{:S(2)}, u32[]{:S(2)}) %collective-permute-start.13) | collective-permute-done | bytes 331808 | tf_op jit(solution)/shard_map/ppermute | solution.py:42
  232.7 0.7 copy-done.7
  233.5 0.7 copy-done.9
  234.3 9.2 %all-to-all-done.2 = bf16[16,72,1536]{2,1,0:T(8,128)(2,1)S(1)} async-done(((bf16[16,72,1536]{2,1,0:T(8,128)(2,1)}), bf16[16,72,1536]{2,1,0:T(8,128)(2,1)S(1)}, u32[]{:S(2)}, u32[]{:S(2)}) %all-to-all-start.2) | async-done | bytes 3538976 | tf_op jit(solution)/shard_map/all_to_all | solution.py:453
  244.1 1.1 copy-done
  245.3 8.6 %column_sums.1 = (f32[512,1536]{1,0:T(8,128)}, bf16[256,1536]{1,0:T(8,128)(2,1)}, bf16[256,1536]{1,0:T(8,128)(2,1)}) custom-call(f32[8,1152]{1,0:T(8,128)} %broadcast_in_dim.34.refs_0_, bf16[16,1152]{1,0:T(8,128)(2,1)} %fusion.6.refs_1_, bf16[1024,16]{1,0:T(8,128)(2,1)} %bitcast.33, bf16[1024,16]{1,0:T(8,128)(2,1)} %bitcast.34, bf16[1152,1536]{1,0:T(8,128)(2,1)} %bitcast.26), custom_call_target="tpu_custom_call" | custom-call | flops 724775731200 | bytes 8257536 | tf_op jit(solution)/shard_map/column_sums/pallas_call | solution.py:390
  253.9 1.4 collective-permute-start.14
  255.3 1.5 copy.21
  256.8 0.8 copy.22
  257.7 0.8 collective-permute-done.15.refs_4_
  258.5 0.9 copy-done.3
  259.5 6.9 %group_sums.1 = (bf16[384,1152]{1,0:T(8,128)(2,1)}, bf16[128,1536]{1,0:T(8,128)(2,1)}, bf16[128,1536]{1,0:T(8,128)(2,1)}, bf16[128,1536]{1,0:T(8,128)(2,1)}, bf16[128,1536]{1,0:T(8,128)(2,1)}) custom-call(f32[384,8]{1,0:T(8,128)} %bitcast.31, f32[384,8]{1,0:T(8,128)} %bitcast.32, f32[512,1536]{1,0:T(8,128)} %get-tuple-element.96.refs_2_, ...), custom_call_target="tpu_custom_call" | custom-call | flops 1019215872 | bytes 2654208 | tf_op jit(solution)/shard_map/group_sums/pallas_call | solution.py:226
  266.9 2.9 collective-permute-start.17
  270.3 4.3 %all-to-all-start.3 = ((bf16[16,24,1152]{2,1,0:T(8,128)(2,1)}), bf16[16,24,1152]{2,1,0:T(8,128)(2,1)S(1)}, u32[]{:S(2)}, u32[]{:S(2)}) async-start(bf16[16,24,1152]{2,1,0:T(8,128)(2,1)} %bitcast.30), calls=%async_computation.3 | async-start | bytes 1769472 | tf_op jit(solution)/shard_map/all_to_all | solution.py:458
  274.6 2.4 collective-permute-done.16
  277.0 10.4 %collective-permute-done.17 = bf16[128,1536]{1,0:T(8,128)(2,1)S(1)} collective-permute-done((bf16[128,1536]{1,0:T(8,128)(2,1)}, bf16[128,1536]{1,0:T(8,128)(2,1)S(1)}, u32[]{:S(2)}, u32[]{:S(2)}) %collective-permute-start.17) | collective-permute-done | bytes 393248 | tf_op jit(solution)/shard_map/ppermute | solution.py:42
  287.4 2.0 collective-permute-done.18
  289.4 1.2 add_convert_fusion
  291.1 0.9 select_reduce_fusion
  292.0 0.9 pad_maximum_fusion
  (82 shorter events, 8.7 us)
Async XLA Ops:
  7.2 44.6 %all-gather.2.cloned.1.call-start = ((), (), s32[]{:S(2)}) async-start(), calls=%async_computation.4 | async-start | bytes 5898240 | tf_op jit(solution)/shard_map/all_gather | solution.py:421
  10.5 3.4 %copy-start.11 = (f32[16,128]{1,0:T(8,128)}, f32[16,128]{1,0:T(8,128)S(1)}, u32[]{:S(2)}) copy-start(f32[16,128]{1,0:T(8,128)S(1)} %convolution_select_fusion) | copy-start | bytes 24580
  13.8 45.1 %all-to-all-start = ((bf16[16,24,2688]{2,1,0:T(8,128)(2,1)}), bf16[16,24,2688]{2,1,0:T(8,128)(2,1)S(1)}, u32[]{:S(2)}, u32[]{:S(2)}) async-start(bf16[16,24,2688]{2,1,0:T(8,128)(2,1)} %bitcast.5), calls=%async_computation | async-start | bytes 4128768 | tf_op jit(solution)/shard_map/all_to_all | solution.py:436
  58.9 1.3 copy-start.1
  60.3 103.1 %all-to-all-start.1 = ((bf16[16,72,2560]{2,1,0:T(8,128)(2,1)}), bf16[16,72,2560]{2,1,0:T(8,128)(2,1)}, u32[]{:S(2)}, u32[]{:S(2)}) async-start(bf16[16,72,2560]{2,1,0:T(8,128)(2,1)} %bitcast.25), calls=%async_computation.1 | async-start | bytes 11796480 | tf_op jit(solution)/shard_map/all_to_all | solution.py:441
  74.0 5.5 %collective-permute-start = (bf16[144,2560]{1,0:T(8,128)(2,1)}, bf16[144,2560]{1,0:T(8,128)(2,1)S(1)}, u32[]{:S(2)}, u32[]{:S(2)}) collective-permute-start(bf16[144,2560]{1,0:T(8,128)(2,1)} %get-tuple-element.73), channel_id=1, source_target_pairs={{0,1},{1,0},{2,3},{3,2},{4,5},{5,4},{6,7},{7,6},{8,9},{9,8},{10,11... | collective-permute-start | bytes 2211848 | tf_op jit(solution)/shard_map/ppermute | solution.py:42
  74.6 18.4 %collective-permute-start.1 = (bf16[144,2560]{1,0:T(8,128)(2,1)}, bf16[144,2560]{1,0:T(8,128)(2,1)S(1)}, u32[]{:S(2)}, u32[]{:S(2)}) collective-permute-start(bf16[144,2560]{1,0:T(8,128)(2,1)} %get-tuple-element.74), channel_id=1, source_target_pairs={{0,2},{1,3},{2,0},{3,1},{4,6},{5,7},{6,4},{7,5},{8,10},{9,11},{10,... | collective-permute-start | bytes 2211848 | tf_op jit(solution)/shard_map/ppermute | solution.py:42
  75.6 34.1 %collective-permute-start.2 = (bf16[144,2560]{1,0:T(8,128)(2,1)}, bf16[144,2560]{1,0:T(8,128)(2,1)S(1)}, u32[]{:S(2)}, u32[]{:S(2)}) collective-permute-start(bf16[144,2560]{1,0:T(8,128)(2,1)} %get-tuple-element.75), channel_id=1, source_target_pairs={{0,3},{1,2},{2,1},{3,0},{4,7},{5,6},{6,5},{7,4},{8,11},{9,10},{10,... | collective-permute-start | bytes 2211848 | tf_op jit(solution)/shard_map/ppermute | solution.py:42
  76.3 50.2 %collective-permute-start.3 = (bf16[144,2560]{1,0:T(8,128)(2,1)}, bf16[144,2560]{1,0:T(8,128)(2,1)S(1)}, u32[]{:S(2)}, u32[]{:S(2)}) collective-permute-start(bf16[144,2560]{1,0:T(8,128)(2,1)} %get-tuple-element.76), channel_id=1, source_target_pairs={{0,4},{1,5},{2,6},{3,7},{4,0},{5,1},{6,2},{7,3},{8,12},{9,13},{10,... | collective-permute-start | bytes 2211848 | tf_op jit(solution)/shard_map/ppermute | solution.py:42
  78.0 64.5 %collective-permute-start.4 = (bf16[144,2560]{1,0:T(8,128)(2,1)}, bf16[144,2560]{1,0:T(8,128)(2,1)}, u32[]{:S(2)}, u32[]{:S(2)}) collective-permute-start(bf16[144,2560]{1,0:T(8,128)(2,1)} %get-tuple-element.77), channel_id=1, source_target_pairs={{0,5},{1,4},{2,7},{3,6},{4,1},{5,0},{6,3},{7,2},{8,13},{9,12},{10,... | collective-permute-start | bytes 2211848 | tf_op jit(solution)/shard_map/ppermute | solution.py:42
  79.6 67.1 %copy-start.14 = (bf16[144,2560]{1,0:T(8,128)(2,1)}, bf16[144,2560]{1,0:T(8,128)(2,1)S(1)}, u32[]{:S(2)}) copy-start(bf16[144,2560]{1,0:T(8,128)(2,1)S(1)} %collective-permute-done.refs_2_) | copy-start | bytes 2211844
  79.6 62.9 %collective-permute-start.5 = (bf16[144,2560]{1,0:T(8,128)(2,1)}, bf16[144,2560]{1,0:T(8,128)(2,1)}, u32[]{:S(2)}, u32[]{:S(2)}) collective-permute-start(bf16[144,2560]{1,0:T(8,128)(2,1)} %get-tuple-element.78), channel_id=1, source_target_pairs={{0,6},{1,7},{2,4},{3,5},{4,2},{5,3},{6,0},{7,1},{8,14},{9,15},{10,... | collective-permute-start | bytes 2211848 | tf_op jit(solution)/shard_map/ppermute | solution.py:42
  92.9 53.8 %copy-start.15 = (bf16[144,2560]{1,0:T(8,128)(2,1)}, bf16[144,2560]{1,0:T(8,128)(2,1)S(1)}, u32[]{:S(2)}) copy-start(bf16[144,2560]{1,0:T(8,128)(2,1)S(1)} %collective-permute-done.1.refs_3_) | copy-start | bytes 2211844
  92.9 53.8 %collective-permute-start.6 = (bf16[144,2560]{1,0:T(8,128)(2,1)}, bf16[144,2560]{1,0:T(8,128)(2,1)}, u32[]{:S(2)}, u32[]{:S(2)}) collective-permute-start(bf16[144,2560]{1,0:T(8,128)(2,1)} %get-tuple-element.79), channel_id=1, source_target_pairs={{0,7},{1,6},{2,5},{3,4},{4,3},{5,2},{6,1},{7,0},{8,15},{9,14},{10,... | collective-permute-start | bytes 2211848 | tf_op jit(solution)/shard_map/ppermute | solution.py:42
  109.7 37.1 %copy-start.16 = (bf16[144,2560]{1,0:T(8,128)(2,1)}, bf16[144,2560]{1,0:T(8,128)(2,1)S(1)}, u32[]{:S(2)}) copy-start(bf16[144,2560]{1,0:T(8,128)(2,1)S(1)} %collective-permute-done.2.refs_4_) | copy-start | bytes 2211844
  126.5 20.3 %copy-start.17 = (bf16[144,2560]{1,0:T(8,128)(2,1)}, bf16[144,2560]{1,0:T(8,128)(2,1)S(1)}, u32[]{:S(2)}) copy-start(bf16[144,2560]{1,0:T(8,128)(2,1)S(1)} %collective-permute-done.3.refs_5_) | copy-start | bytes 2211844
  182.9 60.6 %all-to-all-start.2 = ((bf16[16,72,1536]{2,1,0:T(8,128)(2,1)}), bf16[16,72,1536]{2,1,0:T(8,128)(2,1)S(1)}, u32[]{:S(2)}, u32[]{:S(2)}) async-start(bf16[16,72,1536]{2,1,0:T(8,128)(2,1)} %bitcast.27), calls=%async_computation.2 | async-start | bytes 7077888 | tf_op jit(solution)/shard_map/all_to_all | solution.py:453
  199.8 10.6 %collective-permute-start.10 = (bf16[144,1152]{1,0:T(8,128)(2,1)}, bf16[144,1152]{1,0:T(8,128)(2,1)S(1)}, u32[]{:S(2)}, u32[]{:S(2)}) collective-permute-start(bf16[144,1152]{1,0:T(8,128)(2,1)} %get-tuple-element.91), channel_id=1, source_target_pairs={{0,4},{1,5},{2,6},{3,7},{4,0},{5,1},{6,2},{7,3},{8,12},{9,13},{10,... | collective-permute-start | bytes 995336 | tf_op jit(solution)/shard_map/ppermute | solution.py:42
  200.7 18.8 %collective-permute-start.11 = (bf16[144,1152]{1,0:T(8,128)(2,1)}, bf16[144,1152]{1,0:T(8,128)(2,1)S(1)}, u32[]{:S(2)}, u32[]{:S(2)}) collective-permute-start(bf16[144,1152]{1,0:T(8,128)(2,1)} %get-tuple-element.92), channel_id=1, source_target_pairs={{0,5},{1,4},{2,7},{3,6},{4,1},{5,0},{6,3},{7,2},{8,13},{9,12},{10,... | collective-permute-start | bytes 995336 | tf_op jit(solution)/shard_map/ppermute | solution.py:42
  203.5 22.1 %collective-permute-start.12 = (bf16[144,1152]{1,0:T(8,128)(2,1)}, bf16[144,1152]{1,0:T(8,128)(2,1)S(1)}, u32[]{:S(2)}, u32[]{:S(2)}) collective-permute-start(bf16[144,1152]{1,0:T(8,128)(2,1)} %get-tuple-element.93), channel_id=1, source_target_pairs={{0,6},{1,7},{2,4},{3,5},{4,2},{5,3},{6,0},{7,1},{8,14},{9,15},{10,... | collective-permute-start | bytes 995336 | tf_op jit(solution)/shard_map/ppermute | solution.py:42
  205.7 26.9 %collective-permute-start.13 = (bf16[144,1152]{1,0:T(8,128)(2,1)}, bf16[144,1152]{1,0:T(8,128)(2,1)S(1)}, u32[]{:S(2)}, u32[]{:S(2)}) collective-permute-start(bf16[144,1152]{1,0:T(8,128)(2,1)} %get-tuple-element.94), channel_id=1, source_target_pairs={{0,7},{1,6},{2,5},{3,4},{4,3},{5,2},{6,1},{7,0},{8,15},{9,14},{10,... | collective-permute-start | bytes 995336 | tf_op jit(solution)/shard_map/ppermute | solution.py:42
  206.1 26.5 %collective-permute-start.7 = (bf16[144,1152]{1,0:T(8,128)(2,1)}, bf16[144,1152]{1,0:T(8,128)(2,1)S(1)}, u32[]{:S(2)}, u32[]{:S(2)}) collective-permute-start(bf16[144,1152]{1,0:T(8,128)(2,1)} %get-tuple-element.88), channel_id=1, source_target_pairs={{0,1},{1,0},{2,3},{3,2},{4,5},{5,4},{6,7},{7,6},{8,9},{9,8},{10,11... | collective-permute-start | bytes 995336 | tf_op jit(solution)/shard_map/ppermute | solution.py:42
  210.4 22.2 %copy-start.4 = (bf16[144,1152]{1,0:T(8,128)(2,1)}, bf16[144,1152]{1,0:T(8,128)(2,1)S(1)}, u32[]{:S(2)}) copy-start(bf16[144,1152]{1,0:T(8,128)(2,1)S(1)} %collective-permute-done.10.refs_9_) | copy-start | bytes 995332
  210.4 22.2 %collective-permute-start.8 = (bf16[144,1152]{1,0:T(8,128)(2,1)}, bf16[144,1152]{1,0:T(8,128)(2,1)S(1)}, u32[]{:S(2)}, u32[]{:S(2)}) collective-permute-start(bf16[144,1152]{1,0:T(8,128)(2,1)} %get-tuple-element.89), channel_id=1, source_target_pairs={{0,2},{1,3},{2,0},{3,1},{4,6},{5,7},{6,4},{7,5},{8,10},{9,11},{10,... | collective-permute-start | bytes 995336 | tf_op jit(solution)/shard_map/ppermute | solution.py:42
  219.5 13.2 %copy-start.5 = (bf16[144,1152]{1,0:T(8,128)(2,1)}, bf16[144,1152]{1,0:T(8,128)(2,1)S(1)}, u32[]{:S(2)}) copy-start(bf16[144,1152]{1,0:T(8,128)(2,1)S(1)} %collective-permute-done.11.refs_10_) | copy-start | bytes 995332
  219.5 14.8 %collective-permute-start.9 = (bf16[144,1152]{1,0:T(8,128)(2,1)}, bf16[144,1152]{1,0:T(8,128)(2,1)}, u32[]{:S(2)}, u32[]{:S(2)}) collective-permute-start(bf16[144,1152]{1,0:T(8,128)(2,1)} %get-tuple-element.90), channel_id=1, source_target_pairs={{0,3},{1,2},{2,1},{3,0},{4,7},{5,6},{6,5},{7,4},{8,11},{9,10},{10,... | collective-permute-start | bytes 995336 | tf_op jit(solution)/shard_map/ppermute | solution.py:42
  225.6 7.1 %copy-start.6 = (bf16[144,1152]{1,0:T(8,128)(2,1)}, bf16[144,1152]{1,0:T(8,128)(2,1)S(1)}, u32[]{:S(2)}) copy-start(bf16[144,1152]{1,0:T(8,128)(2,1)S(1)} %collective-permute-done.12.refs_11_) | copy-start | bytes 995332
  232.7 0.7 copy-start.7
  232.7 0.9 copy-start.8
  233.5 0.7 copy-start.9
  243.4 1.8 copy-start
  245.3 11.6 %copy-start.13 = (f32[8,384]{1,0:T(8,128)S(1)}, f32[8,384]{1,0:T(8,128)}, u32[]{:S(2)}) copy-start(f32[8,384]{1,0:T(8,128)} %get-tuple-element.68) | copy-start | bytes 36868
  253.9 3.8 %collective-permute-start.14 = (bf16[256,1536]{1,0:T(8,128)(2,1)}, bf16[256,1536]{1,0:T(8,128)(2,1)S(1)}, u32[]{:S(2)}, u32[]{:S(2)}) collective-permute-start(bf16[256,1536]{1,0:T(8,128)(2,1)} %get-tuple-element.97), channel_id=1, source_target_pairs={{0,1},{1,0},{2,3},{3,2},{4,5},{5,4},{6,7},{7,6},{8,9},{9,8},{10,11... | collective-permute-start | bytes 2359304 | tf_op jit(solution)/shard_map/ppermute | solution.py:42
  255.3 3.2 %collective-permute-start.15 = (bf16[256,1536]{1,0:T(8,128)(2,1)}, bf16[256,1536]{1,0:T(8,128)(2,1)S(1)}, u32[]{:S(2)}, u32[]{:S(2)}) collective-permute-start(bf16[256,1536]{1,0:T(8,128)(2,1)} %get-tuple-element.98), channel_id=1, source_target_pairs={{0,1},{1,0},{2,3},{3,2},{4,5},{5,4},{6,7},{7,6},{8,9},{9,8},{10,11... | collective-permute-start | bytes 2359304 | tf_op jit(solution)/shard_map/ppermute | solution.py:42
  257.7 0.9 copy-start.2
  258.5 0.9 copy-start.3
  266.4 24.2 %copy-start.12 = (f32[16,128]{1,0:T(8,128)S(1)}, f32[16,128]{1,0:T(8,128)}, u32[]{:S(2)}) copy-start(f32[16,128]{1,0:T(8,128)} %copy-done.11) | copy-start | bytes 24580
  266.4 24.7 %copy-start.10 = (s32[128,6]{0,1:T(8,128)S(1)}, s32[128,6]{0,1:T(8,128)}, u32[]{:S(2)}) copy-start(s32[128,6]{0,1:T(8,128)} %param.9) | copy-start | bytes 9220
  266.4 10.6 %collective-permute-start.16 = (bf16[128,1536]{1,0:T(8,128)(2,1)}, bf16[128,1536]{1,0:T(8,128)(2,1)S(1)}, u32[]{:S(2)}, u32[]{:S(2)}) collective-permute-start(bf16[128,1536]{1,0:T(8,128)(2,1)} %get-tuple-element.109), channel_id=1, source_target_pairs={{0,2},{1,3},{2,0},{3,1},{4,6},{5,7},{6,4},{7,5},{8,10},{9,11},{10,... | collective-permute-start | bytes 1179656 | tf_op jit(solution)/shard_map/ppermute | solution.py:42
  266.9 20.5 %collective-permute-start.17 = (bf16[128,1536]{1,0:T(8,128)(2,1)}, bf16[128,1536]{1,0:T(8,128)(2,1)S(1)}, u32[]{:S(2)}, u32[]{:S(2)}) collective-permute-start(bf16[128,1536]{1,0:T(8,128)(2,1)} %get-tuple-element.110), channel_id=1, source_target_pairs={{0,4},{1,5},{2,6},{3,7},{4,0},{5,1},{6,2},{7,3},{8,12},{9,13},{10,... | collective-permute-start | bytes 1179656 | tf_op jit(solution)/shard_map/ppermute | solution.py:42
  269.9 19.5 %collective-permute-start.18 = (bf16[128,1536]{1,0:T(8,128)(2,1)}, bf16[128,1536]{1,0:T(8,128)(2,1)S(1)}, u32[]{:S(2)}, u32[]{:S(2)}) collective-permute-start(bf16[128,1536]{1,0:T(8,128)(2,1)} %get-tuple-element.111), channel_id=1, source_target_pairs={{0,6},{1,7},{2,4},{3,5},{4,2},{5,3},{6,0},{7,1},{8,14},{9,15},{10,... | collective-permute-start | bytes 1179656 | tf_op jit(solution)/shard_map/ppermute | solution.py:42
  270.3 20.3 %all-to-all-start.3 = ((bf16[16,24,1152]{2,1,0:T(8,128)(2,1)}), bf16[16,24,1152]{2,1,0:T(8,128)(2,1)S(1)}, u32[]{:S(2)}, u32[]{:S(2)}) async-start(bf16[16,24,1152]{2,1,0:T(8,128)(2,1)} %bitcast.30), calls=%async_computation.3 | async-start | bytes 1769472 | tf_op jit(solution)/shard_map/all_to_all | solution.py:458
Sparse Core Ops, SparseCore 0:
  9.7 41.2 all-gather.1

commit v6 on v5

--- a/solution.py
+++ b/solution.py
@@ -200,13 +200,8 @@
     )(table, grad_gate, grad_up, gate_mat, up_mat, gate_dot)
 
 
-def sum_kernel(n_exp, slot, weight, mine, first, last, *refs):
-    blocks, out, column = refs[:n_exp], refs[n_exp], refs[n_exp + 1:]
-    n_tok, chips = column[0].shape[0], len(column)
-    for a, total in enumerate(column):
-        half, at = (first, a) if 2 * a < chips else (last, a - chips // 2)
-        other = half[n_tok * at:n_tok * (at + 1), :].astype(F32)
-        total[...] = (mine[n_tok * a:n_tok * (a + 1), :] + other).astype(BF)
+def sum_kernel(n_exp, slot, weight, *refs):
+    blocks, out = refs[:n_exp], refs[n_exp]
     half = out.shape[1] - LANES
     place = lax.broadcasted_iota(jnp.int32, (slot.shape[0], blocks[0].shape[0]), 1).astype(F32)
     sums = jnp.zeros((slot.shape[0], half), F32)
@@ -219,20 +214,19 @@
     out[:, half:] = gates.astype(BF)
 
 
-def group_sums(slot, weight, mine, first, last, blocks):
+def group_sums(slot, weight, blocks):
     n_exp = len(blocks)
     shape = (slot.shape[0], blocks[0].shape[1])
-    column = (2 * mine.shape[0] // n_exp, mine.shape[1])
     return pl.pallas_call(
         lambda *refs: sum_kernel(n_exp, *refs),
         grid=(1,),
-        in_specs=[whole(x.shape) for x in (slot, weight, mine, first, last)] + [whole(blocks[0].shape)] * n_exp,
-        out_specs=[whole(shape)] + [whole(column)] * (n_exp // 2),
-        out_shape=[jax.ShapeDtypeStruct(shape, BF)] + [jax.ShapeDtypeStruct(column, BF)] * (n_exp // 2),
+        in_specs=[whole(slot.shape), whole(weight.shape)] + [whole(blocks[0].shape)] * n_exp,
+        out_specs=whole(shape),
+        out_shape=jax.ShapeDtypeStruct(shape, BF),
         compiler_params=params(VMEM_MIB),
         cost_estimate=cost(2 * shape[0] * blocks[0].size * n_exp, 2 * n_exp * blocks[0].size),
         name="group_sums",
-    )(slot, weight, mine, first, last, *blocks)
+    )(slot, weight, *blocks)
 
 
 def named_here(top, eye, meta, local):
@@ -451,9 +445,12 @@
     back_a = returned_a(to_a, grad_gate, grad_up, gate_mat, up_mat, gate_dot, n_exp)
     got_a = exchange(back_a)
     got_b = lax.all_to_all(back_b.reshape(n_seq, rows_b, rest), "seq", 0, 0, tiled=True)
-    got_b, *got_a = barrier(got_b, *got_a)
+    back = group_sums(slot_a, weight_a, got_a)
+    got_b, back = barrier(got_b, back)
     mine, *other = column_sums(slot_b, weight_b, got_b.reshape(n_seq * rows_b, rest), n_exp)
-    back, *chip = group_sums(slot_a, weight_a, mine, *(swap(x, 1) for x in other), got_a)
+    back, *other = barrier(back, *other)
+    other = jnp.split(jnp.concatenate([swap(x, 1) for x in other], axis=0), n_exp // 2)
+    chip = [(x + y.astype(F32)).astype(BF) for x, y in zip(jnp.split(mine, n_exp // 2), other)]
     final_b = sum(p.astype(F32) for p in exchange(chip, 2))
     back = lax.all_to_all(back.reshape(n_seq, per_group, first + LANES), "seq", 0, 0, tiled=True)
     final_a = dot_t(pick, back.reshape(n_seq * per_group, first + LANES))

time: 301 us -> 296 us (0.983)
  waiting for transfers between devices: 112 us -> 107 us
    ppermute x19, waiting for transfers between devices: 102 us -> 93 us  [swap(): lax.ppermute(x, 'exp', [(i, i ^ k) for i in range(lax.axis_size('exp'))])]
    all_to_all x1, waiting for transfers between devices: 0.01 us -> 7.91 us  [per_device(): lax.all_to_all(back.reshape(n_seq, per_group, first + LANES), 'seq', 0, 0...]
    all_to_all x1, waiting for transfers between devices: 9.17 us -> 5.62 us  [per_device(): lax.all_to_all(back_b.reshape(n_seq, rows_b, rest), 'seq', 0, 0, tiled=True)]
    unnamed x38 -> x20, local copies, waits for them, and re-layouts: 6.62 us -> 4.12 us
  transfers between devices with their start and end apart: 24 -> 24, of which waited for: 14 -> 13; matrix products, arithmetic and copies ran while one was open for 7% -> 9% of each run, Pallas kernels for 14% -> 16%
where the time goes in v6:
time: 296 us; the launch traced here: 294 us
  waiting for transfers between devices  107 us (36%)
  Pallas kernels  75.5 us (26%)
  starting transfers between devices  50.4 us (17%)
  blocking collectives  15.6 us (5%)
  local copies, waits for them, and re-layouts  14.6 us (5%)
  between operations  14.3 us (5%)
  other arithmetic  14 us (5%)
    ppermute x19, waiting for transfers between devices, swap(): lax.ppermute(x, 'exp', [(i, i ^ k) for i in range(lax.axis_size('exp'))])  93 us
    ppermute x19, starting transfers between devices, swap(): lax.ppermute(x, 'exp', [(i, i ^ k) for i in range(lax.axis_size('exp'))])  23.6 us
    pallas_call x1, Pallas kernels, hidden_grads(): pl.pallas_call(lambda *refs: grad_kernel(steps, *refs), grid=(steps + hal...  18.9 us
    pallas_call x1, Pallas kernels, pre_products(): pl.pallas_call(lambda *refs: pre_kernel(chips, pairs, *refs), grid=(units...  16.6 us
    all_gather x1, blocking collectives, per_device(): column_meta = lax.all_gather(meta, 'exp', axis=0, tiled=True)  15.6 us
    pallas_call x1, Pallas kernels, returned_a(): pl.pallas_call(lambda *refs: back_a_kernel(n_exp, pairs, *refs), grid=(ha...  10 us
    pallas_call x1, Pallas kernels, column_sums(): pl.pallas_call(lambda *refs: column_kernel(n_exp, *refs), grid=(half // w...  8.66 us
    all_to_all x1, starting transfers between devices, per_device(): lax.all_to_all(send.reshape(n_seq, per_group, features + LANES), 'seq', 0...  8.43 us
  transfers between devices with their start and end apart: 24, of which 13 were waited for; matrix products, arithmetic and copies ran while one was open for 9% of the time, Pallas kernels for 16%

profile of v6, /device:TPU:1, one launch (start us, length us, event | category | flops | bytes accessed | tf_op | source)
XLA Modules:
  0.0 294.2 jit_solution(8082359258020627320)
XLA Ops:
  7.2 0.7 all-gather.2.cloned.1.call-update
  7.9 0.8 copy.17
  8.7 0.8 copy.18
  9.6 0.7 add_select_fusion.3
  10.6 1.2 concatenate.11
  11.8 2.0 convolution_convert_fusion
  13.8 8.4 %all-to-all-start = ((bf16[16,24,2688]{2,1,0:T(8,128)(2,1)}), bf16[16,24,2688]{2,1,0:T(8,128)(2,1)S(1)}, u32[]{:S(2)}, u32[]{:S(2)}) async-start(bf16[16,24,2688]{2,1,0:T(8,128)(2,1)} %bitcast.2), calls=%async_computation | async-start | bytes 4128768 | tf_op jit(solution)/shard_map/all_to_all | solution.py:430
  22.4 15.6 %all_gather.6.refs_7_ = bf16[1024,128]{1,0:T(8,128)(2,1)} all-gather(bf16[128,128]{1,0:T(8,128)(2,1)S(1)} %pad_maximum_fusion.1), channel_id=1, replica_groups=mesh['seq'=16,'exp'=8] {'exp'}, dimensions={0}, use_global_device_ids=true | all-gather | bytes 294912 | tf_op jit(solution)/shard_map/all_gather | solution.py:414
  38.1 0.7 fusion.5.refs_5_
  38.8 0.7 fusion.7
  39.5 0.7 broadcast_in_dim.30.refs_2_
  40.1 0.7 broadcast_in_dim.32.refs_6_
  41.4 2.4 column_slots.1
  43.8 0.8 convert_element_type.133
  44.7 0.8 copy.19
  45.5 0.8 convert_element_type.135
  46.4 0.8 copy.20
  47.3 0.9 fusion.3.refs_2_
  48.2 1.0 fusion.1.refs_1_.refs_0_
  49.2 1.4 fusion.refs_0_
  50.6 0.7 broadcast_in_dim.33.refs_1_
  51.8 7.1 %column_rows.1 = bf16[1152,2560]{1,0:T(8,128)(2,1)} custom-call(s32[1]{0:T(128)} %bitcast.4.refs_0_, bf16[8,144,256]{2,1,0:T(8,128)(2,1)} %fusion.1.refs_1_.refs_0_, bf16[1152,128]{1,0:T(8,128)(2,1)} %get-tuple-element.52.refs_2_, bf16[1024,2560]{1,0:T(8,128)(2,1)} %all-gather.2.cloned.1.call-done.refs_3_), custom_call_target="tpu_custom_call" | custom-call | flops 37748736 | bytes 294912 | tf_op jit(solution)/shard_map/column_rows/pallas_call | solution.py:346
  59.0 1.3 copy-done.1
  60.3 7.0 %all-to-all-start.1 = ((bf16[16,72,2560]{2,1,0:T(8,128)(2,1)}), bf16[16,72,2560]{2,1,0:T(8,128)(2,1)}, u32[]{:S(2)}, u32[]{:S(2)}) async-start(bf16[16,72,2560]{2,1,0:T(8,128)(2,1)} %bitcast.25), calls=%async_computation.1 | async-start | bytes 11796480 | tf_op jit(solution)/shard_map/all_to_all | solution.py:435
  67.3 6.7 %hub_blocks.1 = (bf16[144,2560]{1,0:T(8,128)(2,1)}, bf16[144,2560]{1,0:T(8,128)(2,1)}, bf16[144,2560]{1,0:T(8,128)(2,1)}, bf16[144,2560]{1,0:T(8,128)(2,1)}, bf1...) custom-call(bf16[128,128]{1,0:T(8,128)(2,1)} %get-tuple-element.54.r, ...), custom_call_target="tpu_custom_call" | custom-call | flops 2378170368 | bytes 5898240 | tf_op jit(solution)/shard_map/hub_blocks/pallas_call | solution.py:274
  74.5 1.0 collective-permute-start.1
  75.6 0.7 collective-permute-start.2
  76.3 1.7 collective-permute-start.3
  78.0 1.6 collective-permute-start.4
  79.6 2.2 collective-permute-start.5
  81.8 11.1 %collective-permute-done.1.refs_3_ = bf16[144,2560]{1,0:T(8,128)(2,1)S(1)} collective-permute-done((bf16[144,2560]{1,0:T(8,128)(2,1)}, bf16[144,2560]{1,0:T(8,128)(2,1)S(1)}, u32[]{:S(2)}, u32[]{:S(2)}) %collective-permute-start.1) | collective-permute-done | bytes 737312 | tf_op jit(solution)/shard_map/ppermute | solution.py:42
  92.9 3.3 %collective-permute-start.6 = (bf16[144,2560]{1,0:T(8,128)(2,1)}, bf16[144,2560]{1,0:T(8,128)(2,1)}, u32[]{:S(2)}, u32[]{:S(2)}) collective-permute-start(bf16[144,2560]{1,0:T(8,128)(2,1)} %get-tuple-element.66), channel_id=1, source_target_pairs={{0,7},{1,6},{2,5},{3,4},{4,3},{5,2},{6,1},{7,0},{8,15},{9,14},{10,... | collective-permute-start | bytes 2211848 | tf_op jit(solution)/shard_map/ppermute | solution.py:42
  96.2 13.4 %collective-permute-done.2.refs_4_ = bf16[144,2560]{1,0:T(8,128)(2,1)S(1)} collective-permute-done((bf16[144,2560]{1,0:T(8,128)(2,1)}, bf16[144,2560]{1,0:T(8,128)(2,1)S(1)}, u32[]{:S(2)}, u32[]{:S(2)}) %collective-permute-start.2) | collective-permute-done | bytes 737312 | tf_op jit(solution)/shard_map/ppermute | solution.py:42
  109.6 16.8 %collective-permute-done.3.refs_5_ = bf16[144,2560]{1,0:T(8,128)(2,1)S(1)} collective-permute-done((bf16[144,2560]{1,0:T(8,128)(2,1)}, bf16[144,2560]{1,0:T(8,128)(2,1)S(1)}, u32[]{:S(2)}, u32[]{:S(2)}) %collective-permute-start.3) | collective-permute-done | bytes 737312 | tf_op jit(solution)/shard_map/ppermute | solution.py:42
  126.5 16.0 %collective-permute-done.4.refs_6_ = bf16[144,2560]{1,0:T(8,128)(2,1)} collective-permute-done((bf16[144,2560]{1,0:T(8,128)(2,1)}, bf16[144,2560]{1,0:T(8,128)(2,1)}, u32[]{:S(2)}, u32[]{:S(2)}) %collective-permute-start.4) | collective-permute-done | bytes 737312 | tf_op jit(solution)/shard_map/ppermute | solution.py:42
  142.5 4.2 %collective-permute-done.6.refs_8_ = bf16[144,2560]{1,0:T(8,128)(2,1)} collective-permute-done((bf16[144,2560]{1,0:T(8,128)(2,1)}, bf16[144,2560]{1,0:T(8,128)(2,1)}, u32[]{:S(2)}, u32[]{:S(2)}) %collective-permute-start.6) | collective-permute-done | bytes 737312 | tf_op jit(solution)/shard_map/ppermute | solution.py:42
  146.7 16.6 %pre_products.1 = (f32[1152,768]{1,0:T(8,128)}, f32[1152,768]{1,0:T(8,128)}) custom-call(bf16[8,144,256]{2,1,0:T(8,128)(2,1)} %fusion.1.refs_1_.refs_0_, bf16[144,2560]{1,0:T(8,128)(2,1)} %get-tuple-element.59.refs_1_, bf16[144,2560]{1,0:T(8,128)(2,1)} %copy-done.5, bf16[144,2560]{1,0:T(8,128)(2,1)} %copy-done.6, bf16[144,2560]{1,0:T(8,128)(2,1)} %copy-done.7, ...), custom_call_target="tpu_custom_call" | custom-call | flops 9059696640 | bytes 20840448 | tf_op jit(solution)/shard_map/pre_products/pallas_call | solution.py:94
  163.9 18.9 %hidden_grads.1 = (bf16[1152,768]{1,0:T(8,128)(2,1)}, bf16[1152,768]{1,0:T(8,128)(2,1)}, bf16[1152,128]{1,0:T(8,128)(2,1)}, bf16[1152,1536]{1,0:T(8,128)(2,1)}) custom-call(f32[8,128]{1,0:T(8,128)} %broadcast_in_dim.28.refs_0_, bf16[1152,2560]{1,0:T(8,128)(2,1)} %bitcast.8.refs_1_, bf16[768,2560]{1,0:T(8,128)(2,1)} %bitcast.35, ...), custom_call_target="tpu_custom_call" | custom-call | flops 9059696640 | bytes 30277632 | tf_op jit(solution)/shard_map/hidden_grads/pallas_call | solution.py:141
  182.9 6.9 %all-to-all-start.2 = ((bf16[16,72,1536]{2,1,0:T(8,128)(2,1)}), bf16[16,72,1536]{2,1,0:T(8,128)(2,1)S(1)}, u32[]{:S(2)}, u32[]{:S(2)}) async-start(bf16[16,72,1536]{2,1,0:T(8,128)(2,1)} %bitcast.27), calls=%async_computation.2 | async-start | bytes 7077888 | tf_op jit(solution)/shard_map/all_to_all | solution.py:447
  189.8 10.0 %returned_a.1 = (bf16[144,1152]{1,0:T(8,128)(2,1)}, bf16[144,1152]{1,0:T(8,128)(2,1)}, bf16[144,1152]{1,0:T(8,128)(2,1)}, bf16[144,1152]{1,0:T(8,128)(2,1)}, bf1...) custom-call(bf16[8,256,144]{2,1,0:T(8,128)(2,1)} %fusion.refs_0_, ...), custom_call_target="tpu_custom_call" | custom-call | flops 3623878656 | bytes 9043968 | tf_op jit(solution)/shard_map/returned_a/pallas_call | solution.py:191
  199.8 0.9 collective-permute-start.10
  200.7 2.7 collective-permute-start.11
  203.5 2.3 collective-permute-start.12
  206.6 3.9 %collective-permute-done.10.refs_6_ = bf16[144,1152]{1,0:T(8,128)(2,1)} collective-permute-done((bf16[144,1152]{1,0:T(8,128)(2,1)}, bf16[144,1152]{1,0:T(8,128)(2,1)}, u32[]{:S(2)}, u32[]{:S(2)}) %collective-permute-start.10) | collective-permute-done | bytes 331808 | tf_op jit(solution)/shard_map/ppermute | solution.py:42
  210.9 8.5 %collective-permute-done.11.refs_7_ = bf16[144,1152]{1,0:T(8,128)(2,1)} collective-permute-done((bf16[144,1152]{1,0:T(8,128)(2,1)}, bf16[144,1152]{1,0:T(8,128)(2,1)}, u32[]{:S(2)}, u32[]{:S(2)}) %collective-permute-start.11) | collective-permute-done | bytes 331808 | tf_op jit(solution)/shard_map/ppermute | solution.py:42
  220.1 1.5 copy.21
  221.6 1.5 copy.22
  223.1 2.5 collective-permute-done.12.refs_8_
  225.6 7.1 %collective-permute-done.13.refs_9_ = bf16[144,1152]{1,0:T(8,128)(2,1)} collective-permute-done((bf16[144,1152]{1,0:T(8,128)(2,1)}, bf16[144,1152]{1,0:T(8,128)(2,1)}, u32[]{:S(2)}, u32[]{:S(2)}) %collective-permute-start.13) | collective-permute-done | bytes 331808 | tf_op jit(solution)/shard_map/ppermute | solution.py:42
  232.7 5.1 %group_sums.1 = bf16[384,1152]{1,0:T(8,128)(2,1)} custom-call(f32[384,8]{1,0:T(8,128)} %bitcast.31, f32[384,8]{1,0:T(8,128)} %bitcast.32, bf16[144,1152]{1,0:T(8,128)(2,1)} %get-tuple-element.76.refs_2_, bf16[144,1152]{1,0:T(8,128)(2,1)} %collective-permute-done.7.refs_3_, bf16[144,1152]{1,0:T(8,128)(2,1)} %collective-permute-done.8.refs_4_, ...), custom_call_target="tpu_custom_call" | custom-call | flops 1019215872 | bytes 2654208 | tf_op jit(solution)/shard_map/group_sums/pallas_call | solution.py:220
  237.8 5.6 %all-to-all-done.2 = bf16[16,72,1536]{2,1,0:T(8,128)(2,1)S(1)} async-done(((bf16[16,72,1536]{2,1,0:T(8,128)(2,1)}), bf16[16,72,1536]{2,1,0:T(8,128)(2,1)S(1)}, u32[]{:S(2)}, u32[]{:S(2)}) %all-to-all-start.2) | async-done | bytes 3538976 | tf_op jit(solution)/shard_map/all_to_all | solution.py:447
  243.4 0.7 broadcast_in_dim.35.refs_0_
  244.1 1.2 copy-done
  245.3 8.7 %column_sums.1 = (f32[512,1536]{1,0:T(8,128)}, bf16[256,1536]{1,0:T(8,128)(2,1)}, bf16[256,1536]{1,0:T(8,128)(2,1)}) custom-call(f32[8,1152]{1,0:T(8,128)} %broadcast_in_dim.35.refs_0_, bf16[16,1152]{1,0:T(8,128)(2,1)} %fusion.6.refs_1_, bf16[1024,16]{1,0:T(8,128)(2,1)} %bitcast.33, bf16[1024,16]{1,0:T(8,128)(2,1)} %bitcast.34, bf16[1152,1536]{1,0:T(8,128)(2,1)} %bitcast.26), custom_call_target="tpu_custom_call" | custom-call | flops 724775731200 | bytes 8257536 | tf_op jit(solution)/shard_map/column_sums/pallas_call | solution.py:384
  253.9 1.4 collective-permute-start.14
  255.4 4.4 %all-to-all-start.3 = ((bf16[16,24,1152]{2,1,0:T(8,128)(2,1)}), bf16[16,24,1152]{2,1,0:T(8,128)(2,1)S(1)}, u32[]{:S(2)}, u32[]{:S(2)}) async-start(bf16[16,24,1152]{2,1,0:T(8,128)(2,1)} %bitcast.28), calls=%async_computation.3 | async-start | bytes 1769472 | tf_op jit(solution)/shard_map/all_to_all | solution.py:455
  259.8 2.7 add_convert_fusion.2
  262.9 3.0 %collective-permute-start.17 = (bf16[128,1536]{1,0:T(8,128)(2,1)S(1)}, bf16[128,1536]{1,0:T(8,128)(2,1)S(1)}, u32[]{:S(2)}, u32[]{:S(2)}) collective-permute-start(bf16[128,1536]{1,0:T(8,128)(2,1)S(1)} %get-tuple-element.94), channel_id=1, source_target_pairs={{0,4},{1,5},{2,6},{3,7},{4,0},{5,1},{6,2},{7,3},{8,12},{9,13},{10,... | collective-permute-start | bytes 1179656 | tf_op jit(solution)/shard_map/ppermute | solution.py:42
  266.4 7.9 %all-to-all-done.3 = bf16[16,24,1152]{2,1,0:T(8,128)(2,1)S(1)} async-done(((bf16[16,24,1152]{2,1,0:T(8,128)(2,1)}), bf16[16,24,1152]{2,1,0:T(8,128)(2,1)S(1)}, u32[]{:S(2)}, u32[]{:S(2)}) %all-to-all-start.3) | async-done | bytes 884768 | tf_op jit(solution)/shard_map/all_to_all | solution.py:455
  274.8 0.9 select_reduce_fusion
  275.7 7.4 %collective-permute-done.17 = bf16[128,1536]{1,0:T(8,128)(2,1)S(1)} collective-permute-done((bf16[128,1536]{1,0:T(8,128)(2,1)S(1)}, bf16[128,1536]{1,0:T(8,128)(2,1)S(1)}, u32[]{:S(2)}, u32[]{:S(2)}) %collective-permute-start.17) | collective-permute-done | bytes 393248 | tf_op jit(solution)/shard_map/ppermute | solution.py:42
  283.1 1.9 collective-permute-done.18
  285.0 1.5 add_convert_fusion
  286.5 0.9 pad_maximum_fusion
  (65 shorter events, 6.4 us)
Async XLA Ops:
  7.2 44.7 %all-gather.2.cloned.1.call-start = ((), (), s32[]{:S(2)}) async-start(), calls=%async_computation.4 | async-start | bytes 5898240 | tf_op jit(solution)/shard_map/all_gather | solution.py:415
  10.5 3.4 %copy-start.3 = (f32[16,128]{1,0:T(8,128)}, f32[16,128]{1,0:T(8,128)S(1)}, u32[]{:S(2)}) copy-start(f32[16,128]{1,0:T(8,128)S(1)} %convolution_select_fusion) | copy-start | bytes 24580
  13.8 45.1 %all-to-all-start = ((bf16[16,24,2688]{2,1,0:T(8,128)(2,1)}), bf16[16,24,2688]{2,1,0:T(8,128)(2,1)S(1)}, u32[]{:S(2)}, u32[]{:S(2)}) async-start(bf16[16,24,2688]{2,1,0:T(8,128)(2,1)} %bitcast.2), calls=%async_computation | async-start | bytes 4128768 | tf_op jit(solution)/shard_map/all_to_all | solution.py:430
  59.0 1.3 copy-start.1
  60.3 103.1 %all-to-all-start.1 = ((bf16[16,72,2560]{2,1,0:T(8,128)(2,1)}), bf16[16,72,2560]{2,1,0:T(8,128)(2,1)}, u32[]{:S(2)}, u32[]{:S(2)}) async-start(bf16[16,72,2560]{2,1,0:T(8,128)(2,1)} %bitcast.25), calls=%async_computation.1 | async-start | bytes 11796480 | tf_op jit(solution)/shard_map/all_to_all | solution.py:435
  74.0 5.6 %collective-permute-start = (bf16[144,2560]{1,0:T(8,128)(2,1)}, bf16[144,2560]{1,0:T(8,128)(2,1)S(1)}, u32[]{:S(2)}, u32[]{:S(2)}) collective-permute-start(bf16[144,2560]{1,0:T(8,128)(2,1)} %get-tuple-element.60), channel_id=1, source_target_pairs={{0,1},{1,0},{2,3},{3,2},{4,5},{5,4},{6,7},{7,6},{8,9},{9,8},{10,11... | collective-permute-start | bytes 2211848 | tf_op jit(solution)/shard_map/ppermute | solution.py:42
  74.5 18.4 %collective-permute-start.1 = (bf16[144,2560]{1,0:T(8,128)(2,1)}, bf16[144,2560]{1,0:T(8,128)(2,1)S(1)}, u32[]{:S(2)}, u32[]{:S(2)}) collective-permute-start(bf16[144,2560]{1,0:T(8,128)(2,1)} %get-tuple-element.61), channel_id=1, source_target_pairs={{0,2},{1,3},{2,0},{3,1},{4,6},{5,7},{6,4},{7,5},{8,10},{9,11},{10,... | collective-permute-start | bytes 2211848 | tf_op jit(solution)/shard_map/ppermute | solution.py:42
  75.6 34.1 %collective-permute-start.2 = (bf16[144,2560]{1,0:T(8,128)(2,1)}, bf16[144,2560]{1,0:T(8,128)(2,1)S(1)}, u32[]{:S(2)}, u32[]{:S(2)}) collective-permute-start(bf16[144,2560]{1,0:T(8,128)(2,1)} %get-tuple-element.62), channel_id=1, source_target_pairs={{0,3},{1,2},{2,1},{3,0},{4,7},{5,6},{6,5},{7,4},{8,11},{9,10},{10,... | collective-permute-start | bytes 2211848 | tf_op jit(solution)/shard_map/ppermute | solution.py:42
  76.3 50.2 %collective-permute-start.3 = (bf16[144,2560]{1,0:T(8,128)(2,1)}, bf16[144,2560]{1,0:T(8,128)(2,1)S(1)}, u32[]{:S(2)}, u32[]{:S(2)}) collective-permute-start(bf16[144,2560]{1,0:T(8,128)(2,1)} %get-tuple-element.63), channel_id=1, source_target_pairs={{0,4},{1,5},{2,6},{3,7},{4,0},{5,1},{6,2},{7,3},{8,12},{9,13},{10,... | collective-permute-start | bytes 2211848 | tf_op jit(solution)/shard_map/ppermute | solution.py:42
  78.0 64.5 %collective-permute-start.4 = (bf16[144,2560]{1,0:T(8,128)(2,1)}, bf16[144,2560]{1,0:T(8,128)(2,1)}, u32[]{:S(2)}, u32[]{:S(2)}) collective-permute-start(bf16[144,2560]{1,0:T(8,128)(2,1)} %get-tuple-element.64), channel_id=1, source_target_pairs={{0,5},{1,4},{2,7},{3,6},{4,1},{5,0},{6,3},{7,2},{8,13},{9,12},{10,... | collective-permute-start | bytes 2211848 | tf_op jit(solution)/shard_map/ppermute | solution.py:42
  79.6 67.1 %copy-start.5 = (bf16[144,2560]{1,0:T(8,128)(2,1)}, bf16[144,2560]{1,0:T(8,128)(2,1)S(1)}, u32[]{:S(2)}) copy-start(bf16[144,2560]{1,0:T(8,128)(2,1)S(1)} %collective-permute-done.refs_2_) | copy-start | bytes 2211844
  79.6 62.9 %collective-permute-start.5 = (bf16[144,2560]{1,0:T(8,128)(2,1)}, bf16[144,2560]{1,0:T(8,128)(2,1)}, u32[]{:S(2)}, u32[]{:S(2)}) collective-permute-start(bf16[144,2560]{1,0:T(8,128)(2,1)} %get-tuple-element.65), channel_id=1, source_target_pairs={{0,6},{1,7},{2,4},{3,5},{4,2},{5,3},{6,0},{7,1},{8,14},{9,15},{10,... | collective-permute-start | bytes 2211848 | tf_op jit(solution)/shard_map/ppermute | solution.py:42
  92.9 53.8 %copy-start.6 = (bf16[144,2560]{1,0:T(8,128)(2,1)}, bf16[144,2560]{1,0:T(8,128)(2,1)S(1)}, u32[]{:S(2)}) copy-start(bf16[144,2560]{1,0:T(8,128)(2,1)S(1)} %collective-permute-done.1.refs_3_) | copy-start | bytes 2211844
  92.9 53.8 %collective-permute-start.6 = (bf16[144,2560]{1,0:T(8,128)(2,1)}, bf16[144,2560]{1,0:T(8,128)(2,1)}, u32[]{:S(2)}, u32[]{:S(2)}) collective-permute-start(bf16[144,2560]{1,0:T(8,128)(2,1)} %get-tuple-element.66), channel_id=1, source_target_pairs={{0,7},{1,6},{2,5},{3,4},{4,3},{5,2},{6,1},{7,0},{8,15},{9,14},{10,... | collective-permute-start | bytes 2211848 | tf_op jit(solution)/shard_map/ppermute | solution.py:42
  109.6 37.1 %copy-start.7 = (bf16[144,2560]{1,0:T(8,128)(2,1)}, bf16[144,2560]{1,0:T(8,128)(2,1)S(1)}, u32[]{:S(2)}) copy-start(bf16[144,2560]{1,0:T(8,128)(2,1)S(1)} %collective-permute-done.2.refs_4_) | copy-start | bytes 2211844
  126.5 20.3 %copy-start.8 = (bf16[144,2560]{1,0:T(8,128)(2,1)}, bf16[144,2560]{1,0:T(8,128)(2,1)S(1)}, u32[]{:S(2)}) copy-start(bf16[144,2560]{1,0:T(8,128)(2,1)S(1)} %collective-permute-done.3.refs_5_) | copy-start | bytes 2211844
  182.9 60.5 %all-to-all-start.2 = ((bf16[16,72,1536]{2,1,0:T(8,128)(2,1)}), bf16[16,72,1536]{2,1,0:T(8,128)(2,1)S(1)}, u32[]{:S(2)}, u32[]{:S(2)}) async-start(bf16[16,72,1536]{2,1,0:T(8,128)(2,1)} %bitcast.27), calls=%async_computation.2 | async-start | bytes 7077888 | tf_op jit(solution)/shard_map/all_to_all | solution.py:447
  199.8 10.7 %collective-permute-start.10 = (bf16[144,1152]{1,0:T(8,128)(2,1)}, bf16[144,1152]{1,0:T(8,128)(2,1)}, u32[]{:S(2)}, u32[]{:S(2)}) collective-permute-start(bf16[144,1152]{1,0:T(8,128)(2,1)} %get-tuple-element.80), channel_id=1, source_target_pairs={{0,4},{1,5},{2,6},{3,7},{4,0},{5,1},{6,2},{7,3},{8,12},{9,13},{10,... | collective-permute-start | bytes 995336 | tf_op jit(solution)/shard_map/ppermute | solution.py:42
  200.7 18.7 %collective-permute-start.11 = (bf16[144,1152]{1,0:T(8,128)(2,1)}, bf16[144,1152]{1,0:T(8,128)(2,1)}, u32[]{:S(2)}, u32[]{:S(2)}) collective-permute-start(bf16[144,1152]{1,0:T(8,128)(2,1)} %get-tuple-element.81), channel_id=1, source_target_pairs={{0,5},{1,4},{2,7},{3,6},{4,1},{5,0},{6,3},{7,2},{8,13},{9,12},{10,... | collective-permute-start | bytes 995336 | tf_op jit(solution)/shard_map/ppermute | solution.py:42
  203.5 22.2 %collective-permute-start.12 = (bf16[144,1152]{1,0:T(8,128)(2,1)}, bf16[144,1152]{1,0:T(8,128)(2,1)}, u32[]{:S(2)}, u32[]{:S(2)}) collective-permute-start(bf16[144,1152]{1,0:T(8,128)(2,1)} %get-tuple-element.82), channel_id=1, source_target_pairs={{0,6},{1,7},{2,4},{3,5},{4,2},{5,3},{6,0},{7,1},{8,14},{9,15},{10,... | collective-permute-start | bytes 995336 | tf_op jit(solution)/shard_map/ppermute | solution.py:42
  205.7 27.0 %collective-permute-start.13 = (bf16[144,1152]{1,0:T(8,128)(2,1)}, bf16[144,1152]{1,0:T(8,128)(2,1)}, u32[]{:S(2)}, u32[]{:S(2)}) collective-permute-start(bf16[144,1152]{1,0:T(8,128)(2,1)} %get-tuple-element.83), channel_id=1, source_target_pairs={{0,7},{1,6},{2,5},{3,4},{4,3},{5,2},{6,1},{7,0},{8,15},{9,14},{10,... | collective-permute-start | bytes 995336 | tf_op jit(solution)/shard_map/ppermute | solution.py:42
  206.1 26.6 %collective-permute-start.7 = (bf16[144,1152]{1,0:T(8,128)(2,1)}, bf16[144,1152]{1,0:T(8,128)(2,1)}, u32[]{:S(2)}, u32[]{:S(2)}) collective-permute-start(bf16[144,1152]{1,0:T(8,128)(2,1)} %get-tuple-element.77), channel_id=1, source_target_pairs={{0,1},{1,0},{2,3},{3,2},{4,5},{5,4},{6,7},{7,6},{8,9},{9,8},{10,11... | collective-permute-start | bytes 995336 | tf_op jit(solution)/shard_map/ppermute | solution.py:42
  210.5 22.3 %collective-permute-start.8 = (bf16[144,1152]{1,0:T(8,128)(2,1)}, bf16[144,1152]{1,0:T(8,128)(2,1)}, u32[]{:S(2)}, u32[]{:S(2)}) collective-permute-start(bf16[144,1152]{1,0:T(8,128)(2,1)} %get-tuple-element.78), channel_id=1, source_target_pairs={{0,2},{1,3},{2,0},{3,1},{4,6},{5,7},{6,4},{7,5},{8,10},{9,11},{10,... | collective-permute-start | bytes 995336 | tf_op jit(solution)/shard_map/ppermute | solution.py:42
  219.4 13.3 %collective-permute-start.9 = (bf16[144,1152]{1,0:T(8,128)(2,1)}, bf16[144,1152]{1,0:T(8,128)(2,1)}, u32[]{:S(2)}, u32[]{:S(2)}) collective-permute-start(bf16[144,1152]{1,0:T(8,128)(2,1)} %get-tuple-element.79), channel_id=1, source_target_pairs={{0,3},{1,2},{2,1},{3,0},{4,7},{5,6},{6,5},{7,4},{8,11},{9,10},{10,... | collective-permute-start | bytes 995336 | tf_op jit(solution)/shard_map/ppermute | solution.py:42
  243.4 1.8 copy-start
  253.9 5.9 %collective-permute-start.14 = (bf16[256,1536]{1,0:T(8,128)(2,1)}, bf16[256,1536]{1,0:T(8,128)(2,1)S(1)}, u32[]{:S(2)}, u32[]{:S(2)}) collective-permute-start(bf16[256,1536]{1,0:T(8,128)(2,1)} %get-tuple-element.92), channel_id=1, source_target_pairs={{0,1},{1,0},{2,3},{3,2},{4,5},{5,4},{6,7},{7,6},{8,9},{9,8},{10,11... | collective-permute-start | bytes 2359304 | tf_op jit(solution)/shard_map/ppermute | solution.py:42
  255.3 4.5 %collective-permute-start.16 = (bf16[256,1536]{1,0:T(8,128)(2,1)}, bf16[256,1536]{1,0:T(8,128)(2,1)S(1)}, u32[]{:S(2)}, u32[]{:S(2)}) collective-permute-start(bf16[256,1536]{1,0:T(8,128)(2,1)} %get-tuple-element.93), channel_id=1, source_target_pairs={{0,1},{1,0},{2,3},{3,2},{4,5},{5,4},{6,7},{7,6},{8,9},{9,8},{10,11... | collective-permute-start | bytes 2359304 | tf_op jit(solution)/shard_map/ppermute | solution.py:42
  255.4 19.0 %copy-start.4 = (f32[16,128]{1,0:T(8,128)S(1)}, f32[16,128]{1,0:T(8,128)}, u32[]{:S(2)}) copy-start(f32[16,128]{1,0:T(8,128)} %copy-done.3) | copy-start | bytes 24580
  255.4 18.9 %all-to-all-start.3 = ((bf16[16,24,1152]{2,1,0:T(8,128)(2,1)}), bf16[16,24,1152]{2,1,0:T(8,128)(2,1)S(1)}, u32[]{:S(2)}, u32[]{:S(2)}) async-start(bf16[16,24,1152]{2,1,0:T(8,128)(2,1)} %bitcast.28), calls=%async_computation.3 | async-start | bytes 1769472 | tf_op jit(solution)/shard_map/all_to_all | solution.py:455
  259.8 14.9 %copy-start.2 = (s32[128,6]{0,1:T(8,128)S(1)}, s32[128,6]{0,1:T(8,128)}, u32[]{:S(2)}) copy-start(s32[128,6]{0,1:T(8,128)} %param.9) | copy-start | bytes 9220
  262.5 13.1 %collective-permute-start.15 = (bf16[128,1536]{1,0:T(8,128)(2,1)}, bf16[128,1536]{1,0:T(8,128)(2,1)S(1)}, u32[]{:S(2)}, u32[]{:S(2)}) collective-permute-start(bf16[128,1536]{1,0:T(8,128)(2,1)} %get-tuple-element.96), channel_id=1, source_target_pairs={{0,2},{1,3},{2,0},{3,1},{4,6},{5,7},{6,4},{7,5},{8,10},{9,11},{10,... | collective-permute-start | bytes 1179656 | tf_op jit(solution)/shard_map/ppermute | solution.py:42
  262.9 20.2 %collective-permute-start.17 = (bf16[128,1536]{1,0:T(8,128)(2,1)S(1)}, bf16[128,1536]{1,0:T(8,128)(2,1)S(1)}, u32[]{:S(2)}, u32[]{:S(2)}) collective-permute-start(bf16[128,1536]{1,0:T(8,128)(2,1)S(1)} %get-tuple-element.94), channel_id=1, source_target_pairs={{0,4},{1,5},{2,6},{3,7},{4,0},{5,1},{6,2},{7,3},{8,12},{9,13},{10,... | collective-permute-start | bytes 1179656 | tf_op jit(solution)/shard_map/ppermute | solution.py:42
  265.9 19.1 %collective-permute-start.18 = (bf16[128,1536]{1,0:T(8,128)(2,1)S(1)}, bf16[128,1536]{1,0:T(8,128)(2,1)}, u32[]{:S(2)}, u32[]{:S(2)}) collective-permute-start(bf16[128,1536]{1,0:T(8,128)(2,1)S(1)} %get-tuple-element.95), channel_id=1, source_target_pairs={{0,6},{1,7},{2,4},{3,5},{4,2},{5,3},{6,0},{7,1},{8,14},{9,15},{10,... | collective-permute-start | bytes 1179656 | tf_op jit(solution)/shard_map/ppermute | solution.py:42
Sparse Core Ops, SparseCore 0:
  9.7 41.2 all-gather.1

commit v7 on v6

--- a/solution.py
+++ b/solution.py
@@ -31,7 +31,7 @@
 
 
 def first_columns(features):
-    return max(2 * features // 5 // 256 * 256, 256)
+    return features // 2
 
 
 def barrier(*values):
@@ -135,7 +135,7 @@
     units, first, steps = down_mat.shape[0], first_columns(features), 4
     half = features - first
     tall = total // steps
-    wide = 512 if half % 512 == 0 else half
+    wide = 640 if half % 640 == 0 else half
     row = lambda width: pl.BlockSpec((tall, width), lambda i: (jnp.minimum(i, steps - 1), 0))
     mat = pl.BlockSpec((wide, units), lambda i: (first // wide + jnp.maximum(i - steps, 0), 0))
     return pl.pallas_call(
@@ -185,7 +185,7 @@
     total, units = grad_gate.shape
     half = first_columns(gate_mat.shape[0])
     pairs = table.shape[0]
-    wide = 512 if half % 512 == 0 else half
+    wide = 640 if half % 640 == 0 else half
     mat = pl.BlockSpec((wide, units), lambda j: (j, 0))
     block = (total // n_exp, half + LANES)
     return pl.pallas_call(
@@ -367,7 +367,7 @@
     sums = dot(mixed[...], got[...])
     for k in range(0, n_exp, 2):
         at = slice(n_tok * k // 2, n_tok * (k // 2 + 1))
-        out_mine[at, :] = sums[n_tok * k:n_tok * (k + 1), :]
+        out_mine[at, :] = sums[n_tok * k:n_tok * (k + 1), :].astype(BF)
         out, at = (out_first, k) if 2 * k < n_exp else (out_last, k - n_exp // 2)
         out[n_tok * at // 2:n_tok * (at // 2 + 1), :] = sums[n_tok * (k + 1):n_tok * (k + 2), :].astype(BF)
 
@@ -379,14 +379,14 @@
     place = jnp.broadcast_to((at % (total // n_seq)).astype(F32), (8, total))
     spread = (jnp.arange(n_seq)[:, None] == at[None, :] // (total // n_seq)).astype(BF)
     shape = (n_rows // 2, half)
-    wide = 512 if half % 512 == 0 else half
+    wide = 640 if half % 640 == 0 else half
     part = lambda rows: pl.BlockSpec((rows, wide), lambda j: (0, j))
     return pl.pallas_call(
         lambda *refs: column_kernel(n_exp, *refs),
         grid=(half // wide,),
         in_specs=[whole(place.shape), whole(spread.shape), whole(slot.shape), whole(weight.shape), part(total)],
         out_specs=[part(shape[0])] + [part(shape[0] // 2)] * 2,
-        out_shape=[jax.ShapeDtypeStruct(shape, F32)] + [jax.ShapeDtypeStruct((shape[0] // 2, half), BF)] * 2,
+        out_shape=[jax.ShapeDtypeStruct(shape, BF)] + [jax.ShapeDtypeStruct((shape[0] // 2, half), BF)] * 2,
         scratch_shapes=[pltpu.VMEM((n_rows, total), BF)],
         compiler_params=params(VMEM_MIB),
         cost_estimate=cost(400 * n_rows * total * half, 2 * total * half + 3 * n_rows * half),
@@ -450,7 +450,7 @@
     mine, *other = column_sums(slot_b, weight_b, got_b.reshape(n_seq * rows_b, rest), n_exp)
     back, *other = barrier(back, *other)
     other = jnp.split(jnp.concatenate([swap(x, 1) for x in other], axis=0), n_exp // 2)
-    chip = [(x + y.astype(F32)).astype(BF) for x, y in zip(jnp.split(mine, n_exp // 2), other)]
+    chip = [(x.astype(F32) + y.astype(F32)).astype(BF) for x, y in zip(jnp.split(mine, n_exp // 2), other)]
     final_b = sum(p.astype(F32) for p in exchange(chip, 2))
     back = lax.all_to_all(back.reshape(n_seq, per_group, first + LANES), "seq", 0, 0, tiled=True)
     final_a = dot_t(pick, back.reshape(n_seq * per_group, first + LANES))

time: 296 us -> 300 us (1.014)
  Pallas kernels: 75.5 us -> 81 us
    ppermute x19, waiting for transfers between devices: 93 us -> 107 us  [swap(): lax.ppermute(x, 'exp', [(i, i ^ k) for i in range(lax.axis_size('exp'))])]
    all_to_all x1, waiting for transfers between devices: 7.91 us -> 0.01 us  [per_device(): lax.all_to_all(back.reshape(n_seq, per_group, first + LANES), 'seq', 0, 0...]
    all_to_all x1, waiting for transfers between devices: 5.62 us -> 0.01 us  [per_device(): lax.all_to_all(back_b.reshape(n_seq, rows_b, rest), 'seq', 0, 0, tiled=True)]
    pallas_call x1, Pallas kernels: 10 us -> 15.4 us  [returned_a(): pl.pallas_call(lambda *refs: back_a_kernel(n_exp, pairs, *refs), grid=(ha...]
  transfers between devices with their start and end apart: 24 -> 24, of which waited for: 13 -> 12; matrix products, arithmetic and copies ran while one was open for 9% -> 7% of each run, Pallas kernels for 16% -> 18%
where the time goes in v7:
time: 300 us; the launch traced here: 298 us
  waiting for transfers between devices  108 us (36%)
  Pallas kernels  81 us (27%)
  starting transfers between devices  52 us (17%)
  blocking collectives  15.6 us (5%)
  between operations  14.3 us (5%)
  local copies, waits for them, and re-layouts  13.1 us (4%)
  other arithmetic  12.2 us (4%)
    ppermute x19, waiting for transfers between devices, swap(): lax.ppermute(x, 'exp', [(i, i ^ k) for i in range(lax.axis_size('exp'))])  107 us
    ppermute x19, starting transfers between devices, swap(): lax.ppermute(x, 'exp', [(i, i ^ k) for i in range(lax.axis_size('exp'))])  23 us
    pallas_call x1, Pallas kernels, hidden_grads(): pl.pallas_call(lambda *refs: grad_kernel(steps, *refs), grid=(steps + hal...  18.9 us
    pallas_call x1, Pallas kernels, pre_products(): pl.pallas_call(lambda *refs: pre_kernel(chips, pairs, *refs), grid=(units...  16.6 us
    all_gather x1, blocking collectives, per_device(): column_meta = lax.all_gather(meta, 'exp', axis=0, tiled=True)  15.6 us
    pallas_call x1, Pallas kernels, returned_a(): pl.pallas_call(lambda *refs: back_a_kernel(n_exp, pairs, *refs), grid=(ha...  15.4 us
    all_to_all x1, starting transfers between devices, per_device(): lax.all_to_all(send.reshape(n_seq, per_group, features + LANES), 'seq', 0...  8.43 us
    pallas_call x1, Pallas kernels, column_sums(): pl.pallas_call(lambda *refs: column_kernel(n_exp, *refs), grid=(half // w...  8.18 us
  transfers between devices with their start and end apart: 24, of which 12 were waited for; matrix products, arithmetic and copies ran while one was open for 7% of the time, Pallas kernels for 18%

profile of v7, /device:TPU:1, one launch (start us, length us, event | category | flops | bytes accessed | tf_op | source)
XLA Modules:
  0.0 298.5 jit_solution(4094516876906650485)
XLA Ops:
  7.2 0.7 all-gather.2.cloned.1.call-update
  7.9 0.8 copy.17
  8.7 0.8 copy.18
  9.6 0.7 add_select_fusion.3
  10.6 1.2 concatenate.11
  11.8 2.0 convolution_convert_fusion
  13.8 8.4 %all-to-all-start = ((bf16[16,24,2688]{2,1,0:T(8,128)(2,1)}), bf16[16,24,2688]{2,1,0:T(8,128)(2,1)S(1)}, u32[]{:S(2)}, u32[]{:S(2)}) async-start(bf16[16,24,2688]{2,1,0:T(8,128)(2,1)} %bitcast.2), calls=%async_computation | async-start | bytes 4128768 | tf_op jit(solution)/shard_map/all_to_all | solution.py:430
  22.4 15.6 %all_gather.6.refs_7_ = bf16[1024,128]{1,0:T(8,128)(2,1)} all-gather(bf16[128,128]{1,0:T(8,128)(2,1)S(1)} %pad_maximum_fusion.1), channel_id=1, replica_groups=mesh['seq'=16,'exp'=8] {'exp'}, dimensions={0}, use_global_device_ids=true | all-gather | bytes 294912 | tf_op jit(solution)/shard_map/all_gather | solution.py:414
  38.1 0.7 fusion.5.refs_5_
  38.8 0.7 fusion.7
  39.5 0.7 broadcast_in_dim.30.refs_2_
  40.1 0.7 broadcast_in_dim.32.refs_6_
  41.5 2.4 column_slots.1
  43.8 0.8 convert_element_type.145
  44.7 0.9 copy.19
  45.5 0.8 convert_element_type.147
  46.4 0.9 copy.20
  47.4 0.8 fusion.3.refs_2_
  48.2 1.0 fusion.1.refs_1_.refs_0_
  49.2 1.3 fusion.refs_0_
  50.6 0.7 broadcast_in_dim.33.refs_1_
  51.2 0.6 broadcast_in_dim.34.refs_3_
  51.8 7.1 %column_rows.1 = bf16[1152,2560]{1,0:T(8,128)(2,1)} custom-call(s32[1]{0:T(128)} %bitcast.4.refs_0_, bf16[8,144,256]{2,1,0:T(8,128)(2,1)} %fusion.1.refs_1_.refs_0_, bf16[1152,128]{1,0:T(8,128)(2,1)} %get-tuple-element.52.refs_2_, bf16[1024,2560]{1,0:T(8,128)(2,1)} %all-gather.2.cloned.1.call-done.refs_3_), custom_call_target="tpu_custom_call" | custom-call | flops 37748736 | bytes 294912 | tf_op jit(solution)/shard_map/column_rows/pallas_call | solution.py:346
  59.0 1.3 copy-done.1
  60.3 7.0 %all-to-all-start.1 = ((bf16[16,72,2560]{2,1,0:T(8,128)(2,1)}), bf16[16,72,2560]{2,1,0:T(8,128)(2,1)}, u32[]{:S(2)}, u32[]{:S(2)}) async-start(bf16[16,72,2560]{2,1,0:T(8,128)(2,1)} %bitcast.25), calls=%async_computation.1 | async-start | bytes 11796480 | tf_op jit(solution)/shard_map/all_to_all | solution.py:435
  67.3 6.7 %hub_blocks.1 = (bf16[144,2560]{1,0:T(8,128)(2,1)}, bf16[144,2560]{1,0:T(8,128)(2,1)}, bf16[144,2560]{1,0:T(8,128)(2,1)}, bf16[144,2560]{1,0:T(8,128)(2,1)}, bf1...) custom-call(bf16[128,128]{1,0:T(8,128)(2,1)} %get-tuple-element.54.r, ...), custom_call_target="tpu_custom_call" | custom-call | flops 2378170368 | bytes 5898240 | tf_op jit(solution)/shard_map/hub_blocks/pallas_call | solution.py:274
  74.6 1.0 collective-permute-start.1
  75.6 0.7 collective-permute-start.2
  76.3 1.7 collective-permute-start.3
  78.1 1.6 collective-permute-start.4
  79.6 2.2 collective-permute-start.5
  81.8 11.1 %collective-permute-done.1.refs_3_ = bf16[144,2560]{1,0:T(8,128)(2,1)S(1)} collective-permute-done((bf16[144,2560]{1,0:T(8,128)(2,1)}, bf16[144,2560]{1,0:T(8,128)(2,1)S(1)}, u32[]{:S(2)}, u32[]{:S(2)}) %collective-permute-start.1) | collective-permute-done | bytes 737312 | tf_op jit(solution)/shard_map/ppermute | solution.py:42
  93.0 3.3 %collective-permute-start.6 = (bf16[144,2560]{1,0:T(8,128)(2,1)}, bf16[144,2560]{1,0:T(8,128)(2,1)}, u32[]{:S(2)}, u32[]{:S(2)}) collective-permute-start(bf16[144,2560]{1,0:T(8,128)(2,1)} %get-tuple-element.66), channel_id=1, source_target_pairs={{0,7},{1,6},{2,5},{3,4},{4,3},{5,2},{6,1},{7,0},{8,15},{9,14},{10,... | collective-permute-start | bytes 2211848 | tf_op jit(solution)/shard_map/ppermute | solution.py:42
  96.3 13.4 %collective-permute-done.2.refs_4_ = bf16[144,2560]{1,0:T(8,128)(2,1)S(1)} collective-permute-done((bf16[144,2560]{1,0:T(8,128)(2,1)}, bf16[144,2560]{1,0:T(8,128)(2,1)S(1)}, u32[]{:S(2)}, u32[]{:S(2)}) %collective-permute-start.2) | collective-permute-done | bytes 737312 | tf_op jit(solution)/shard_map/ppermute | solution.py:42
  109.7 16.8 %collective-permute-done.3.refs_5_ = bf16[144,2560]{1,0:T(8,128)(2,1)S(1)} collective-permute-done((bf16[144,2560]{1,0:T(8,128)(2,1)}, bf16[144,2560]{1,0:T(8,128)(2,1)S(1)}, u32[]{:S(2)}, u32[]{:S(2)}) %collective-permute-start.3) | collective-permute-done | bytes 737312 | tf_op jit(solution)/shard_map/ppermute | solution.py:42
  126.5 16.0 %collective-permute-done.4.refs_6_ = bf16[144,2560]{1,0:T(8,128)(2,1)} collective-permute-done((bf16[144,2560]{1,0:T(8,128)(2,1)}, bf16[144,2560]{1,0:T(8,128)(2,1)}, u32[]{:S(2)}, u32[]{:S(2)}) %collective-permute-start.4) | collective-permute-done | bytes 737312 | tf_op jit(solution)/shard_map/ppermute | solution.py:42
  142.6 4.2 %collective-permute-done.6.refs_8_ = bf16[144,2560]{1,0:T(8,128)(2,1)} collective-permute-done((bf16[144,2560]{1,0:T(8,128)(2,1)}, bf16[144,2560]{1,0:T(8,128)(2,1)}, u32[]{:S(2)}, u32[]{:S(2)}) %collective-permute-start.6) | collective-permute-done | bytes 737312 | tf_op jit(solution)/shard_map/ppermute | solution.py:42
  146.8 16.6 %pre_products.1 = (f32[1152,768]{1,0:T(8,128)}, f32[1152,768]{1,0:T(8,128)}) custom-call(bf16[8,144,256]{2,1,0:T(8,128)(2,1)} %fusion.1.refs_1_.refs_0_, bf16[144,2560]{1,0:T(8,128)(2,1)} %get-tuple-element.59.refs_1_, bf16[144,2560]{1,0:T(8,128)(2,1)} %copy-done.9, bf16[144,2560]{1,0:T(8,128)(2,1)} %copy-done.10, bf16[144,2560]{1,0:T(8,128)(2,1)} %copy-done.11, ...), custom_call_target="tpu_custom_call" | custom-call | flops 9059696640 | bytes 20840448 | tf_op jit(solution)/shard_map/pre_products/pallas_call | solution.py:94
  164.0 18.9 %hidden_grads.1 = (bf16[1152,768]{1,0:T(8,128)(2,1)}, bf16[1152,768]{1,0:T(8,128)(2,1)}, bf16[1152,128]{1,0:T(8,128)(2,1)}, bf16[1152,1280]{1,0:T(8,128)(2,1)}) custom-call(f32[8,128]{1,0:T(8,128)} %broadcast_in_dim.28.refs_0_, bf16[1152,2560]{1,0:T(8,128)(2,1)} %bitcast.8.refs_1_, bf16[768,2560]{1,0:T(8,128)(2,1)} %bitcast.34, ...), custom_call_target="tpu_custom_call" | custom-call | flops 9059696640 | bytes 30277632 | tf_op jit(solution)/shard_map/hidden_grads/pallas_call | solution.py:141
  182.9 6.9 %all-to-all-start.2 = ((bf16[16,72,1280]{2,1,0:T(8,128)(2,1)}), bf16[16,72,1280]{2,1,0:T(8,128)(2,1)S(1)}, u32[]{:S(2)}, u32[]{:S(2)}) async-start(bf16[16,72,1280]{2,1,0:T(8,128)(2,1)} %bitcast.27), calls=%async_computation.2 | async-start | bytes 5898240 | tf_op jit(solution)/shard_map/all_to_all | solution.py:447
  189.8 15.4 %returned_a.1 = (bf16[144,1408]{1,0:T(8,128)(2,1)}, bf16[144,1408]{1,0:T(8,128)(2,1)}, bf16[144,1408]{1,0:T(8,128)(2,1)}, bf16[144,1408]{1,0:T(8,128)(2,1)}, bf1...) custom-call(bf16[8,256,144]{2,1,0:T(8,128)(2,1)} %fusion.refs_0_, ...), custom_call_target="tpu_custom_call" | custom-call | flops 4529848320 | bytes 10420224 | tf_op jit(solution)/shard_map/returned_a/pallas_call | solution.py:191
  205.2 0.9 collective-permute-start.10
  206.1 2.8 collective-permute-start.11
  208.9 2.5 collective-permute-start.12
  212.2 5.1 %collective-permute-done.10.refs_6_ = bf16[144,1408]{1,0:T(8,128)(2,1)S(1)} collective-permute-done((bf16[144,1408]{1,0:T(8,128)(2,1)}, bf16[144,1408]{1,0:T(8,128)(2,1)S(1)}, u32[]{:S(2)}, u32[]{:S(2)}) %collective-permute-start.10) | collective-permute-done | bytes 405536 | tf_op jit(solution)/shard_map/ppermute | solution.py:42
  217.7 10.1 %collective-permute-done.11.refs_7_ = bf16[144,1408]{1,0:T(8,128)(2,1)} collective-permute-done((bf16[144,1408]{1,0:T(8,128)(2,1)}, bf16[144,1408]{1,0:T(8,128)(2,1)}, u32[]{:S(2)}, u32[]{:S(2)}) %collective-permute-start.11) | collective-permute-done | bytes 405536 | tf_op jit(solution)/shard_map/ppermute | solution.py:42
  227.8 0.6 fusion.6.refs_1_
  228.4 0.8 copy.21
  229.3 0.8 copy.22
  230.1 5.7 %collective-permute-done.12.refs_8_ = bf16[144,1408]{1,0:T(8,128)(2,1)} collective-permute-done((bf16[144,1408]{1,0:T(8,128)(2,1)}, bf16[144,1408]{1,0:T(8,128)(2,1)}, u32[]{:S(2)}, u32[]{:S(2)}) %collective-permute-start.12) | collective-permute-done | bytes 405536 | tf_op jit(solution)/shard_map/ppermute | solution.py:42
  235.8 8.7 %collective-permute-done.13.refs_9_ = bf16[144,1408]{1,0:T(8,128)(2,1)} collective-permute-done((bf16[144,1408]{1,0:T(8,128)(2,1)}, bf16[144,1408]{1,0:T(8,128)(2,1)}, u32[]{:S(2)}, u32[]{:S(2)}) %collective-permute-start.13) | collective-permute-done | bytes 405536 | tf_op jit(solution)/shard_map/ppermute | solution.py:42
  244.5 5.7 %group_sums.1 = bf16[384,1408]{1,0:T(8,128)(2,1)} custom-call(f32[384,8]{1,0:T(8,128)} %bitcast.30, f32[384,8]{1,0:T(8,128)} %bitcast.31, bf16[144,1408]{1,0:T(8,128)(2,1)} %get-tuple-element.76.refs_2_, bf16[144,1408]{1,0:T(8,128)(2,1)} %collective-permute-done.7.refs_3_, bf16[144,1408]{1,0:T(8,128)(2,1)} %collective-permute-done.8.refs_4_, ...), custom_call_target="tpu_custom_call" | custom-call | flops 1245708288 | bytes 3244032 | tf_op jit(solution)/shard_map/group_sums/pallas_call | solution.py:220
  250.2 0.6 broadcast_in_dim.35.refs_0_
  250.8 1.0 copy-done
  251.8 8.2 %column_sums.1 = (bf16[512,1280]{1,0:T(8,128)(2,1)}, bf16[256,1280]{1,0:T(8,128)(2,1)}, bf16[256,1280]{1,0:T(8,128)(2,1)}) custom-call(f32[8,1152]{1,0:T(8,128)} %broadcast_in_dim.35.refs_0_, bf16[16,1152]{1,0:T(8,128)(2,1)} %fusion.6.refs_1_, bf16[1024,16]{1,0:T(8,128)(2,1)} %bitcast.32, bf16[1024,16]{1,0:T(8,128)(2,1)} %bitcast.33, bf16[1152,1280]{1,0:T(8,128)(2,1)} %bitcast.26), custom_call_target="tpu_custom_call" | custom-call | flops 603979776000 | bytes 6881280 | tf_op jit(solution)/shard_map/column_sums/pallas_call | solution.py:384
  260.5 6.7 %all-to-all-start.3 = ((bf16[16,24,1408]{2,1,0:T(8,128)(2,1)}), bf16[16,24,1408]{2,1,0:T(8,128)(2,1)S(1)}, u32[]{:S(2)}, u32[]{:S(2)}) async-start(bf16[16,24,1408]{2,1,0:T(8,128)(2,1)} %bitcast.16), calls=%async_computation.3 | async-start | bytes 2162688 | tf_op jit(solution)/shard_map/all_to_all | solution.py:455
  267.3 1.2 add_convert_fusion.2
  268.6 3.4 %collective-permute-start.17 = (bf16[128,1280]{1,0:T(8,128)(2,1)S(1)}, bf16[128,1280]{1,0:T(8,128)(2,1)S(1)}, u32[]{:S(2)}, u32[]{:S(2)}) collective-permute-start(bf16[128,1280]{1,0:T(8,128)(2,1)S(1)} %get-tuple-element.94), channel_id=1, source_target_pairs={{0,4},{1,5},{2,6},{3,7},{4,0},{5,1},{6,2},{7,3},{8,12},{9,13},{10,... | collective-permute-start | bytes 983048 | tf_op jit(solution)/shard_map/ppermute | solution.py:42
  272.4 4.7 %collective-permute-done.15 = bf16[128,1280]{1,0:T(8,128)(2,1)S(1)} collective-permute-done((bf16[128,1280]{1,0:T(8,128)(2,1)S(1)}, bf16[128,1280]{1,0:T(8,128)(2,1)S(1)}, u32[]{:S(2)}, u32[]{:S(2)}) %collective-permute-start.15) | collective-permute-done | bytes 327712 | tf_op jit(solution)/shard_map/ppermute | solution.py:42
  277.1 9.0 %collective-permute-done.17 = bf16[128,1280]{1,0:T(8,128)(2,1)S(1)} collective-permute-done((bf16[128,1280]{1,0:T(8,128)(2,1)S(1)}, bf16[128,1280]{1,0:T(8,128)(2,1)S(1)}, u32[]{:S(2)}, u32[]{:S(2)}) %collective-permute-start.17) | collective-permute-done | bytes 327712 | tf_op jit(solution)/shard_map/ppermute | solution.py:42
  286.2 2.0 collective-permute-done.18
  288.2 1.2 add_convert_fusion
  289.9 0.9 select_reduce_fusion
  290.8 0.9 pad_maximum_fusion
  (73 shorter events, 5.3 us)
Async XLA Ops:
  7.2 44.7 %all-gather.2.cloned.1.call-start = ((), (), s32[]{:S(2)}) async-start(), calls=%async_computation.4 | async-start | bytes 5898240 | tf_op jit(solution)/shard_map/all_gather | solution.py:415
  10.5 3.4 %copy-start.5 = (f32[16,128]{1,0:T(8,128)}, f32[16,128]{1,0:T(8,128)S(1)}, u32[]{:S(2)}) copy-start(f32[16,128]{1,0:T(8,128)S(1)} %convolution_select_fusion) | copy-start | bytes 24580
  13.8 45.1 %all-to-all-start = ((bf16[16,24,2688]{2,1,0:T(8,128)(2,1)}), bf16[16,24,2688]{2,1,0:T(8,128)(2,1)S(1)}, u32[]{:S(2)}, u32[]{:S(2)}) async-start(bf16[16,24,2688]{2,1,0:T(8,128)(2,1)} %bitcast.2), calls=%async_computation | async-start | bytes 4128768 | tf_op jit(solution)/shard_map/all_to_all | solution.py:430
  59.0 1.3 copy-start.1
  60.3 103.1 %all-to-all-start.1 = ((bf16[16,72,2560]{2,1,0:T(8,128)(2,1)}), bf16[16,72,2560]{2,1,0:T(8,128)(2,1)}, u32[]{:S(2)}, u32[]{:S(2)}) async-start(bf16[16,72,2560]{2,1,0:T(8,128)(2,1)} %bitcast.25), calls=%async_computation.1 | async-start | bytes 11796480 | tf_op jit(solution)/shard_map/all_to_all | solution.py:435
  74.1 5.6 %collective-permute-start = (bf16[144,2560]{1,0:T(8,128)(2,1)}, bf16[144,2560]{1,0:T(8,128)(2,1)S(1)}, u32[]{:S(2)}, u32[]{:S(2)}) collective-permute-start(bf16[144,2560]{1,0:T(8,128)(2,1)} %get-tuple-element.60), channel_id=1, source_target_pairs={{0,1},{1,0},{2,3},{3,2},{4,5},{5,4},{6,7},{7,6},{8,9},{9,8},{10,11... | collective-permute-start | bytes 2211848 | tf_op jit(solution)/shard_map/ppermute | solution.py:42
  74.6 18.4 %collective-permute-start.1 = (bf16[144,2560]{1,0:T(8,128)(2,1)}, bf16[144,2560]{1,0:T(8,128)(2,1)S(1)}, u32[]{:S(2)}, u32[]{:S(2)}) collective-permute-start(bf16[144,2560]{1,0:T(8,128)(2,1)} %get-tuple-element.61), channel_id=1, source_target_pairs={{0,2},{1,3},{2,0},{3,1},{4,6},{5,7},{6,4},{7,5},{8,10},{9,11},{10,... | collective-permute-start | bytes 2211848 | tf_op jit(solution)/shard_map/ppermute | solution.py:42
  75.6 34.1 %collective-permute-start.2 = (bf16[144,2560]{1,0:T(8,128)(2,1)}, bf16[144,2560]{1,0:T(8,128)(2,1)S(1)}, u32[]{:S(2)}, u32[]{:S(2)}) collective-permute-start(bf16[144,2560]{1,0:T(8,128)(2,1)} %get-tuple-element.62), channel_id=1, source_target_pairs={{0,3},{1,2},{2,1},{3,0},{4,7},{5,6},{6,5},{7,4},{8,11},{9,10},{10,... | collective-permute-start | bytes 2211848 | tf_op jit(solution)/shard_map/ppermute | solution.py:42
  76.3 50.2 %collective-permute-start.3 = (bf16[144,2560]{1,0:T(8,128)(2,1)}, bf16[144,2560]{1,0:T(8,128)(2,1)S(1)}, u32[]{:S(2)}, u32[]{:S(2)}) collective-permute-start(bf16[144,2560]{1,0:T(8,128)(2,1)} %get-tuple-element.63), channel_id=1, source_target_pairs={{0,4},{1,5},{2,6},{3,7},{4,0},{5,1},{6,2},{7,3},{8,12},{9,13},{10,... | collective-permute-start | bytes 2211848 | tf_op jit(solution)/shard_map/ppermute | solution.py:42
  78.1 64.5 %collective-permute-start.4 = (bf16[144,2560]{1,0:T(8,128)(2,1)}, bf16[144,2560]{1,0:T(8,128)(2,1)}, u32[]{:S(2)}, u32[]{:S(2)}) collective-permute-start(bf16[144,2560]{1,0:T(8,128)(2,1)} %get-tuple-element.64), channel_id=1, source_target_pairs={{0,5},{1,4},{2,7},{3,6},{4,1},{5,0},{6,3},{7,2},{8,13},{9,12},{10,... | collective-permute-start | bytes 2211848 | tf_op jit(solution)/shard_map/ppermute | solution.py:42
  79.6 67.1 %copy-start.9 = (bf16[144,2560]{1,0:T(8,128)(2,1)}, bf16[144,2560]{1,0:T(8,128)(2,1)S(1)}, u32[]{:S(2)}) copy-start(bf16[144,2560]{1,0:T(8,128)(2,1)S(1)} %collective-permute-done.refs_2_) | copy-start | bytes 2211844
  79.6 62.9 %collective-permute-start.5 = (bf16[144,2560]{1,0:T(8,128)(2,1)}, bf16[144,2560]{1,0:T(8,128)(2,1)}, u32[]{:S(2)}, u32[]{:S(2)}) collective-permute-start(bf16[144,2560]{1,0:T(8,128)(2,1)} %get-tuple-element.65), channel_id=1, source_target_pairs={{0,6},{1,7},{2,4},{3,5},{4,2},{5,3},{6,0},{7,1},{8,14},{9,15},{10,... | collective-permute-start | bytes 2211848 | tf_op jit(solution)/shard_map/ppermute | solution.py:42
  93.0 53.8 %copy-start.10 = (bf16[144,2560]{1,0:T(8,128)(2,1)}, bf16[144,2560]{1,0:T(8,128)(2,1)S(1)}, u32[]{:S(2)}) copy-start(bf16[144,2560]{1,0:T(8,128)(2,1)S(1)} %collective-permute-done.1.refs_3_) | copy-start | bytes 2211844
  93.0 53.8 %collective-permute-start.6 = (bf16[144,2560]{1,0:T(8,128)(2,1)}, bf16[144,2560]{1,0:T(8,128)(2,1)}, u32[]{:S(2)}, u32[]{:S(2)}) collective-permute-start(bf16[144,2560]{1,0:T(8,128)(2,1)} %get-tuple-element.66), channel_id=1, source_target_pairs={{0,7},{1,6},{2,5},{3,4},{4,3},{5,2},{6,1},{7,0},{8,15},{9,14},{10,... | collective-permute-start | bytes 2211848 | tf_op jit(solution)/shard_map/ppermute | solution.py:42
  109.7 37.1 %copy-start.11 = (bf16[144,2560]{1,0:T(8,128)(2,1)}, bf16[144,2560]{1,0:T(8,128)(2,1)S(1)}, u32[]{:S(2)}) copy-start(bf16[144,2560]{1,0:T(8,128)(2,1)S(1)} %collective-permute-done.2.refs_4_) | copy-start | bytes 2211844
  126.5 20.3 %copy-start.12 = (bf16[144,2560]{1,0:T(8,128)(2,1)}, bf16[144,2560]{1,0:T(8,128)(2,1)S(1)}, u32[]{:S(2)}) copy-start(bf16[144,2560]{1,0:T(8,128)(2,1)S(1)} %collective-permute-done.3.refs_5_) | copy-start | bytes 2211844
  182.9 67.3 %all-to-all-start.2 = ((bf16[16,72,1280]{2,1,0:T(8,128)(2,1)}), bf16[16,72,1280]{2,1,0:T(8,128)(2,1)S(1)}, u32[]{:S(2)}, u32[]{:S(2)}) async-start(bf16[16,72,1280]{2,1,0:T(8,128)(2,1)} %bitcast.27), calls=%async_computation.2 | async-start | bytes 5898240 | tf_op jit(solution)/shard_map/all_to_all | solution.py:447
  189.8 38.7 %copy-start.8 = (f32[8,384]{1,0:T(8,128)S(1)}, f32[8,384]{1,0:T(8,128)}, u32[]{:S(2)}) copy-start(f32[8,384]{1,0:T(8,128)} %get-tuple-element.70) | copy-start | bytes 36868
  189.8 39.5 %copy-start.7 = (f32[8,384]{1,0:T(8,128)S(1)}, f32[8,384]{1,0:T(8,128)}, u32[]{:S(2)}) copy-start(f32[8,384]{1,0:T(8,128)} %get-tuple-element.71) | copy-start | bytes 36868
  205.2 12.2 %collective-permute-start.10 = (bf16[144,1408]{1,0:T(8,128)(2,1)}, bf16[144,1408]{1,0:T(8,128)(2,1)S(1)}, u32[]{:S(2)}, u32[]{:S(2)}) collective-permute-start(bf16[144,1408]{1,0:T(8,128)(2,1)} %get-tuple-element.80), channel_id=1, source_target_pairs={{0,4},{1,5},{2,6},{3,7},{4,0},{5,1},{6,2},{7,3},{8,12},{9,13},{10,... | collective-permute-start | bytes 1216520 | tf_op jit(solution)/shard_map/ppermute | solution.py:42
  206.1 21.8 %collective-permute-start.11 = (bf16[144,1408]{1,0:T(8,128)(2,1)}, bf16[144,1408]{1,0:T(8,128)(2,1)}, u32[]{:S(2)}, u32[]{:S(2)}) collective-permute-start(bf16[144,1408]{1,0:T(8,128)(2,1)} %get-tuple-element.81), channel_id=1, source_target_pairs={{0,5},{1,4},{2,7},{3,6},{4,1},{5,0},{6,3},{7,2},{8,13},{9,12},{10,... | collective-permute-start | bytes 1216520 | tf_op jit(solution)/shard_map/ppermute | solution.py:42
  208.9 26.9 %collective-permute-start.12 = (bf16[144,1408]{1,0:T(8,128)(2,1)}, bf16[144,1408]{1,0:T(8,128)(2,1)}, u32[]{:S(2)}, u32[]{:S(2)}) collective-permute-start(bf16[144,1408]{1,0:T(8,128)(2,1)} %get-tuple-element.82), channel_id=1, source_target_pairs={{0,6},{1,7},{2,4},{3,5},{4,2},{5,3},{6,0},{7,1},{8,14},{9,15},{10,... | collective-permute-start | bytes 1216520 | tf_op jit(solution)/shard_map/ppermute | solution.py:42
  211.4 33.1 %collective-permute-start.13 = (bf16[144,1408]{1,0:T(8,128)(2,1)}, bf16[144,1408]{1,0:T(8,128)(2,1)}, u32[]{:S(2)}, u32[]{:S(2)}) collective-permute-start(bf16[144,1408]{1,0:T(8,128)(2,1)} %get-tuple-element.83), channel_id=1, source_target_pairs={{0,7},{1,6},{2,5},{3,4},{4,3},{5,2},{6,1},{7,0},{8,15},{9,14},{10,... | collective-permute-start | bytes 1216520 | tf_op jit(solution)/shard_map/ppermute | solution.py:42
  211.7 32.8 %collective-permute-start.7 = (bf16[144,1408]{1,0:T(8,128)(2,1)}, bf16[144,1408]{1,0:T(8,128)(2,1)}, u32[]{:S(2)}, u32[]{:S(2)}) collective-permute-start(bf16[144,1408]{1,0:T(8,128)(2,1)} %get-tuple-element.77), channel_id=1, source_target_pairs={{0,1},{1,0},{2,3},{3,2},{4,5},{5,4},{6,7},{7,6},{8,9},{9,8},{10,11... | collective-permute-start | bytes 1216520 | tf_op jit(solution)/shard_map/ppermute | solution.py:42
  217.4 27.1 %copy-start.3 = (bf16[144,1408]{1,0:T(8,128)(2,1)}, bf16[144,1408]{1,0:T(8,128)(2,1)S(1)}, u32[]{:S(2)}) copy-start(bf16[144,1408]{1,0:T(8,128)(2,1)S(1)} %collective-permute-done.10.refs_6_) | copy-start | bytes 1216516
  217.4 27.1 %collective-permute-start.8 = (bf16[144,1408]{1,0:T(8,128)(2,1)}, bf16[144,1408]{1,0:T(8,128)(2,1)}, u32[]{:S(2)}, u32[]{:S(2)}) collective-permute-start(bf16[144,1408]{1,0:T(8,128)(2,1)} %get-tuple-element.78), channel_id=1, source_target_pairs={{0,2},{1,3},{2,0},{3,1},{4,6},{5,7},{6,4},{7,5},{8,10},{9,11},{10,... | collective-permute-start | bytes 1216520 | tf_op jit(solution)/shard_map/ppermute | solution.py:42
  227.8 16.7 %collective-permute-start.9 = (bf16[144,1408]{1,0:T(8,128)(2,1)}, bf16[144,1408]{1,0:T(8,128)(2,1)}, u32[]{:S(2)}, u32[]{:S(2)}) collective-permute-start(bf16[144,1408]{1,0:T(8,128)(2,1)} %get-tuple-element.79), channel_id=1, source_target_pairs={{0,3},{1,2},{2,1},{3,0},{4,7},{5,6},{6,5},{7,4},{8,11},{9,10},{10,... | collective-permute-start | bytes 1216520 | tf_op jit(solution)/shard_map/ppermute | solution.py:42
  250.2 1.6 copy-start
  260.0 7.2 %copy-start.2 = (bf16[512,1280]{1,0:T(8,128)(2,1)S(1)}, bf16[512,1280]{1,0:T(8,128)(2,1)}, u32[]{:S(2)}) copy-start(bf16[512,1280]{1,0:T(8,128)(2,1)} %get-tuple-element.91) | copy-start | bytes 3932164
  260.0 7.2 %collective-permute-start.14 = (bf16[256,1280]{1,0:T(8,128)(2,1)}, bf16[256,1280]{1,0:T(8,128)(2,1)}, u32[]{:S(2)}, u32[]{:S(2)}) collective-permute-start(bf16[256,1280]{1,0:T(8,128)(2,1)} %get-tuple-element.92), channel_id=1, source_target_pairs={{0,1},{1,0},{2,3},{3,2},{4,5},{5,4},{6,7},{7,6},{8,9},{9,8},{10,11... | collective-permute-start | bytes 1966088 | tf_op jit(solution)/shard_map/ppermute | solution.py:42
  260.4 6.8 %collective-permute-start.16 = (bf16[256,1280]{1,0:T(8,128)(2,1)}, bf16[256,1280]{1,0:T(8,128)(2,1)S(1)}, u32[]{:S(2)}, u32[]{:S(2)}) collective-permute-start(bf16[256,1280]{1,0:T(8,128)(2,1)} %get-tuple-element.93), channel_id=1, source_target_pairs={{0,1},{1,0},{2,3},{3,2},{4,5},{5,4},{6,7},{7,6},{8,9},{9,8},{10,11... | collective-permute-start | bytes 1966088 | tf_op jit(solution)/shard_map/ppermute | solution.py:42
  260.5 28.8 %all-to-all-start.3 = ((bf16[16,24,1408]{2,1,0:T(8,128)(2,1)}), bf16[16,24,1408]{2,1,0:T(8,128)(2,1)S(1)}, u32[]{:S(2)}, u32[]{:S(2)}) async-start(bf16[16,24,1408]{2,1,0:T(8,128)(2,1)} %bitcast.16), calls=%async_computation.3 | async-start | bytes 2162688 | tf_op jit(solution)/shard_map/all_to_all | solution.py:455
  267.3 22.1 %copy-start.6 = (f32[16,128]{1,0:T(8,128)S(1)}, f32[16,128]{1,0:T(8,128)}, u32[]{:S(2)}) copy-start(f32[16,128]{1,0:T(8,128)} %copy-done.5) | copy-start | bytes 24580
  268.5 8.6 %collective-permute-start.15 = (bf16[128,1280]{1,0:T(8,128)(2,1)S(1)}, bf16[128,1280]{1,0:T(8,128)(2,1)S(1)}, u32[]{:S(2)}, u32[]{:S(2)}) collective-permute-start(bf16[128,1280]{1,0:T(8,128)(2,1)S(1)} %get-tuple-element.96), channel_id=1, source_target_pairs={{0,2},{1,3},{2,0},{3,1},{4,6},{5,7},{6,4},{7,5},{8,10},{9,11},{10,... | collective-permute-start | bytes 983048 | tf_op jit(solution)/shard_map/ppermute | solution.py:42
  268.6 17.6 %collective-permute-start.17 = (bf16[128,1280]{1,0:T(8,128)(2,1)S(1)}, bf16[128,1280]{1,0:T(8,128)(2,1)S(1)}, u32[]{:S(2)}, u32[]{:S(2)}) collective-permute-start(bf16[128,1280]{1,0:T(8,128)(2,1)S(1)} %get-tuple-element.94), channel_id=1, source_target_pairs={{0,4},{1,5},{2,6},{3,7},{4,0},{5,1},{6,2},{7,3},{8,12},{9,13},{10,... | collective-permute-start | bytes 983048 | tf_op jit(solution)/shard_map/ppermute | solution.py:42
  272.0 17.9 %copy-start.4 = (s32[128,6]{0,1:T(8,128)S(1)}, s32[128,6]{0,1:T(8,128)}, u32[]{:S(2)}) copy-start(s32[128,6]{0,1:T(8,128)} %param.9) | copy-start | bytes 9220
  272.0 16.2 %collective-permute-start.18 = (bf16[128,1280]{1,0:T(8,128)(2,1)S(1)}, bf16[128,1280]{1,0:T(8,128)(2,1)S(1)}, u32[]{:S(2)}, u32[]{:S(2)}) collective-permute-start(bf16[128,1280]{1,0:T(8,128)(2,1)S(1)} %get-tuple-element.95), channel_id=1, source_target_pairs={{0,6},{1,7},{2,4},{3,5},{4,2},{5,3},{6,0},{7,1},{8,14},{9,15},{10,... | collective-permute-start | bytes 983048 | tf_op jit(solution)/shard_map/ppermute | solution.py:42
Sparse Core Ops, SparseCore 0:
  9.7 41.2 all-gather.1

commit v8 on v6

--- a/solution.py
+++ b/solution.py
@@ -367,7 +367,7 @@
     sums = dot(mixed[...], got[...])
     for k in range(0, n_exp, 2):
         at = slice(n_tok * k // 2, n_tok * (k // 2 + 1))
-        out_mine[at, :] = sums[n_tok * k:n_tok * (k + 1), :]
+        out_mine[at, :] = sums[n_tok * k:n_tok * (k + 1), :].astype(BF)
         out, at = (out_first, k) if 2 * k < n_exp else (out_last, k - n_exp // 2)
         out[n_tok * at // 2:n_tok * (at // 2 + 1), :] = sums[n_tok * (k + 1):n_tok * (k + 2), :].astype(BF)
 
@@ -386,7 +386,7 @@
         grid=(half // wide,),
         in_specs=[whole(place.shape), whole(spread.shape), whole(slot.shape), whole(weight.shape), part(total)],
         out_specs=[part(shape[0])] + [part(shape[0] // 2)] * 2,
-        out_shape=[jax.ShapeDtypeStruct(shape, F32)] + [jax.ShapeDtypeStruct((shape[0] // 2, half), BF)] * 2,
+        out_shape=[jax.ShapeDtypeStruct(shape, BF)] + [jax.ShapeDtypeStruct((shape[0] // 2, half), BF)] * 2,
         scratch_shapes=[pltpu.VMEM((n_rows, total), BF)],
         compiler_params=params(VMEM_MIB),
         cost_estimate=cost(400 * n_rows * total * half, 2 * total * half + 3 * n_rows * half),
@@ -450,7 +450,7 @@
     mine, *other = column_sums(slot_b, weight_b, got_b.reshape(n_seq * rows_b, rest), n_exp)
     back, *other = barrier(back, *other)
     other = jnp.split(jnp.concatenate([swap(x, 1) for x in other], axis=0), n_exp // 2)
-    chip = [(x + y.astype(F32)).astype(BF) for x, y in zip(jnp.split(mine, n_exp // 2), other)]
+    chip = [(x.astype(F32) + y.astype(F32)).astype(BF) for x, y in zip(jnp.split(mine, n_exp // 2), other)]
     final_b = sum(p.astype(F32) for p in exchange(chip, 2))
     back = lax.all_to_all(back.reshape(n_seq, per_group, first + LANES), "seq", 0, 0, tiled=True)
     final_a = dot_t(pick, back.reshape(n_seq * per_group, first + LANES))

time: 296 us -> 295 us (level)
  transfers between devices with their start and end apart: 24 -> 24, of which waited for: 13 -> 13; matrix products, arithmetic and copies ran while one was open for 9% -> 8% of each run, Pallas kernels for 16% -> 16%
where the time goes in v8:
time: 295 us; the launch traced here: 294 us
  waiting for transfers between devices  108 us (37%)
  Pallas kernels  75.3 us (26%)
  starting transfers between devices  50.2 us (17%)
  blocking collectives  15.6 us (5%)
  local copies, waits for them, and re-layouts  14.7 us (5%)
  between operations  14.3 us (5%)
  other arithmetic  13.6 us (5%)
    ppermute x19, waiting for transfers between devices, swap(): lax.ppermute(x, 'exp', [(i, i ^ k) for i in range(lax.axis_size('exp'))])  92.9 us
    ppermute x19, starting transfers between devices, swap(): lax.ppermute(x, 'exp', [(i, i ^ k) for i in range(lax.axis_size('exp'))])  23.5 us
    pallas_call x1, Pallas kernels, hidden_grads(): pl.pallas_call(lambda *refs: grad_kernel(steps, *refs), grid=(steps + hal...  19 us
    pallas_call x1, Pallas kernels, pre_products(): pl.pallas_call(lambda *refs: pre_kernel(chips, pairs, *refs), grid=(units...  16.6 us
    all_gather x1, blocking collectives, per_device(): column_meta = lax.all_gather(meta, 'exp', axis=0, tiled=True)  15.6 us
    pallas_call x1, Pallas kernels, returned_a(): pl.pallas_call(lambda *refs: back_a_kernel(n_exp, pairs, *refs), grid=(ha...  10 us
    all_to_all x1, starting transfers between devices, per_device(): lax.all_to_all(send.reshape(n_seq, per_group, features + LANES), 'seq', 0...  8.43 us
    all_to_all x1, waiting for transfers between devices, per_device(): lax.all_to_all(back.reshape(n_seq, per_group, first + LANES), 'seq', 0, 0...  8.34 us
  transfers between devices with their start and end apart: 24, of which 13 were waited for; matrix products, arithmetic and copies ran while one was open for 8% of the time, Pallas kernels for 16%

profile of v8, /device:TPU:1, one launch (start us, length us, event | category | flops | bytes accessed | tf_op | source)
XLA Modules:
  0.0 293.7 jit_solution(13216328454396824873)
XLA Ops:
  7.2 0.7 all-gather.2.cloned.1.call-update
  7.9 0.8 copy.17
  8.7 0.8 copy.18
  9.6 0.7 add_select_fusion.3
  10.6 1.2 concatenate.11
  11.8 2.0 convolution_convert_fusion
  13.8 8.4 %all-to-all-start = ((bf16[16,24,2688]{2,1,0:T(8,128)(2,1)}), bf16[16,24,2688]{2,1,0:T(8,128)(2,1)S(1)}, u32[]{:S(2)}, u32[]{:S(2)}) async-start(bf16[16,24,2688]{2,1,0:T(8,128)(2,1)} %bitcast.2), calls=%async_computation | async-start | bytes 4128768 | tf_op jit(solution)/shard_map/all_to_all | solution.py:430
  22.4 15.6 %all_gather.6.refs_7_ = bf16[1024,128]{1,0:T(8,128)(2,1)} all-gather(bf16[128,128]{1,0:T(8,128)(2,1)S(1)} %pad_maximum_fusion.1), channel_id=1, replica_groups=mesh['seq'=16,'exp'=8] {'exp'}, dimensions={0}, use_global_device_ids=true | all-gather | bytes 294912 | tf_op jit(solution)/shard_map/all_gather | solution.py:414
  38.1 0.7 fusion.5.refs_5_
  38.8 0.7 fusion.7
  39.5 0.7 broadcast_in_dim.30.refs_2_
  40.1 0.7 broadcast_in_dim.32.refs_6_
  41.5 2.4 column_slots.1
  43.8 0.8 convert_element_type.145
  44.7 0.8 copy.19
  45.5 0.8 convert_element_type.147
  46.4 0.8 copy.20
  47.4 0.8 fusion.3.refs_2_
  48.2 1.0 fusion.1.refs_1_.refs_0_
  49.2 1.3 fusion.refs_0_
  50.6 0.7 broadcast_in_dim.33.refs_1_
  51.8 7.2 %column_rows.1 = bf16[1152,2560]{1,0:T(8,128)(2,1)} custom-call(s32[1]{0:T(128)} %bitcast.4.refs_0_, bf16[8,144,256]{2,1,0:T(8,128)(2,1)} %fusion.1.refs_1_.refs_0_, bf16[1152,128]{1,0:T(8,128)(2,1)} %get-tuple-element.52.refs_2_, bf16[1024,2560]{1,0:T(8,128)(2,1)} %all-gather.2.cloned.1.call-done.refs_3_), custom_call_target="tpu_custom_call" | custom-call | flops 37748736 | bytes 294912 | tf_op jit(solution)/shard_map/column_rows/pallas_call | solution.py:346
  59.0 1.3 copy-done.1
  60.3 7.0 %all-to-all-start.1 = ((bf16[16,72,2560]{2,1,0:T(8,128)(2,1)}), bf16[16,72,2560]{2,1,0:T(8,128)(2,1)}, u32[]{:S(2)}, u32[]{:S(2)}) async-start(bf16[16,72,2560]{2,1,0:T(8,128)(2,1)} %bitcast.25), calls=%async_computation.1 | async-start | bytes 11796480 | tf_op jit(solution)/shard_map/all_to_all | solution.py:435
  67.4 6.7 %hub_blocks.1 = (bf16[144,2560]{1,0:T(8,128)(2,1)}, bf16[144,2560]{1,0:T(8,128)(2,1)}, bf16[144,2560]{1,0:T(8,128)(2,1)}, bf16[144,2560]{1,0:T(8,128)(2,1)}, bf1...) custom-call(bf16[128,128]{1,0:T(8,128)(2,1)} %get-tuple-element.54.r, ...), custom_call_target="tpu_custom_call" | custom-call | flops 2378170368 | bytes 5898240 | tf_op jit(solution)/shard_map/hub_blocks/pallas_call | solution.py:274
  74.6 1.0 collective-permute-start.1
  75.6 0.7 collective-permute-start.2
  76.3 1.7 collective-permute-start.3
  78.1 1.6 collective-permute-start.4
  79.6 2.2 collective-permute-start.5
  81.8 11.1 %collective-permute-done.1.refs_3_ = bf16[144,2560]{1,0:T(8,128)(2,1)S(1)} collective-permute-done((bf16[144,2560]{1,0:T(8,128)(2,1)}, bf16[144,2560]{1,0:T(8,128)(2,1)S(1)}, u32[]{:S(2)}, u32[]{:S(2)}) %collective-permute-start.1) | collective-permute-done | bytes 737312 | tf_op jit(solution)/shard_map/ppermute | solution.py:42
  93.0 3.3 %collective-permute-start.6 = (bf16[144,2560]{1,0:T(8,128)(2,1)}, bf16[144,2560]{1,0:T(8,128)(2,1)}, u32[]{:S(2)}, u32[]{:S(2)}) collective-permute-start(bf16[144,2560]{1,0:T(8,128)(2,1)} %get-tuple-element.66), channel_id=1, source_target_pairs={{0,7},{1,6},{2,5},{3,4},{4,3},{5,2},{6,1},{7,0},{8,15},{9,14},{10,... | collective-permute-start | bytes 2211848 | tf_op jit(solution)/shard_map/ppermute | solution.py:42
  96.3 13.4 %collective-permute-done.2.refs_4_ = bf16[144,2560]{1,0:T(8,128)(2,1)S(1)} collective-permute-done((bf16[144,2560]{1,0:T(8,128)(2,1)}, bf16[144,2560]{1,0:T(8,128)(2,1)S(1)}, u32[]{:S(2)}, u32[]{:S(2)}) %collective-permute-start.2) | collective-permute-done | bytes 737312 | tf_op jit(solution)/shard_map/ppermute | solution.py:42
  109.7 16.8 %collective-permute-done.3.refs_5_ = bf16[144,2560]{1,0:T(8,128)(2,1)S(1)} collective-permute-done((bf16[144,2560]{1,0:T(8,128)(2,1)}, bf16[144,2560]{1,0:T(8,128)(2,1)S(1)}, u32[]{:S(2)}, u32[]{:S(2)}) %collective-permute-start.3) | collective-permute-done | bytes 737312 | tf_op jit(solution)/shard_map/ppermute | solution.py:42
  126.5 16.0 %collective-permute-done.4.refs_6_ = bf16[144,2560]{1,0:T(8,128)(2,1)} collective-permute-done((bf16[144,2560]{1,0:T(8,128)(2,1)}, bf16[144,2560]{1,0:T(8,128)(2,1)}, u32[]{:S(2)}, u32[]{:S(2)}) %collective-permute-start.4) | collective-permute-done | bytes 737312 | tf_op jit(solution)/shard_map/ppermute | solution.py:42
  142.6 4.2 %collective-permute-done.6.refs_8_ = bf16[144,2560]{1,0:T(8,128)(2,1)} collective-permute-done((bf16[144,2560]{1,0:T(8,128)(2,1)}, bf16[144,2560]{1,0:T(8,128)(2,1)}, u32[]{:S(2)}, u32[]{:S(2)}) %collective-permute-start.6) | collective-permute-done | bytes 737312 | tf_op jit(solution)/shard_map/ppermute | solution.py:42
  146.8 16.6 %pre_products.1 = (f32[1152,768]{1,0:T(8,128)}, f32[1152,768]{1,0:T(8,128)}) custom-call(bf16[8,144,256]{2,1,0:T(8,128)(2,1)} %fusion.1.refs_1_.refs_0_, bf16[144,2560]{1,0:T(8,128)(2,1)} %get-tuple-element.59.refs_1_, bf16[144,2560]{1,0:T(8,128)(2,1)} %copy-done.6, bf16[144,2560]{1,0:T(8,128)(2,1)} %copy-done.7, bf16[144,2560]{1,0:T(8,128)(2,1)} %copy-done.8, ...), custom_call_target="tpu_custom_call" | custom-call | flops 9059696640 | bytes 20840448 | tf_op jit(solution)/shard_map/pre_products/pallas_call | solution.py:94
  164.0 19.0 %hidden_grads.1 = (bf16[1152,768]{1,0:T(8,128)(2,1)}, bf16[1152,768]{1,0:T(8,128)(2,1)}, bf16[1152,128]{1,0:T(8,128)(2,1)}, bf16[1152,1536]{1,0:T(8,128)(2,1)}) custom-call(f32[8,128]{1,0:T(8,128)} %broadcast_in_dim.28.refs_0_, bf16[1152,2560]{1,0:T(8,128)(2,1)} %bitcast.8.refs_1_, bf16[768,2560]{1,0:T(8,128)(2,1)} %bitcast.35, ...), custom_call_target="tpu_custom_call" | custom-call | flops 9059696640 | bytes 30277632 | tf_op jit(solution)/shard_map/hidden_grads/pallas_call | solution.py:141
  183.0 6.9 %all-to-all-start.2 = ((bf16[16,72,1536]{2,1,0:T(8,128)(2,1)}), bf16[16,72,1536]{2,1,0:T(8,128)(2,1)S(1)}, u32[]{:S(2)}, u32[]{:S(2)}) async-start(bf16[16,72,1536]{2,1,0:T(8,128)(2,1)} %bitcast.27), calls=%async_computation.2 | async-start | bytes 7077888 | tf_op jit(solution)/shard_map/all_to_all | solution.py:447
  189.9 10.0 %returned_a.1 = (bf16[144,1152]{1,0:T(8,128)(2,1)}, bf16[144,1152]{1,0:T(8,128)(2,1)}, bf16[144,1152]{1,0:T(8,128)(2,1)}, bf16[144,1152]{1,0:T(8,128)(2,1)}, bf1...) custom-call(bf16[8,256,144]{2,1,0:T(8,128)(2,1)} %fusion.refs_0_, ...), custom_call_target="tpu_custom_call" | custom-call | flops 3623878656 | bytes 9043968 | tf_op jit(solution)/shard_map/returned_a/pallas_call | solution.py:191
  200.0 0.9 collective-permute-start.10
  200.9 2.7 collective-permute-start.11
  203.6 2.3 collective-permute-start.12
  206.8 3.9 %collective-permute-done.10.refs_6_ = bf16[144,1152]{1,0:T(8,128)(2,1)} collective-permute-done((bf16[144,1152]{1,0:T(8,128)(2,1)}, bf16[144,1152]{1,0:T(8,128)(2,1)}, u32[]{:S(2)}, u32[]{:S(2)}) %collective-permute-start.10) | collective-permute-done | bytes 331808 | tf_op jit(solution)/shard_map/ppermute | solution.py:42
  211.0 8.5 %collective-permute-done.11.refs_7_ = bf16[144,1152]{1,0:T(8,128)(2,1)} collective-permute-done((bf16[144,1152]{1,0:T(8,128)(2,1)}, bf16[144,1152]{1,0:T(8,128)(2,1)}, u32[]{:S(2)}, u32[]{:S(2)}) %collective-permute-start.11) | collective-permute-done | bytes 331808 | tf_op jit(solution)/shard_map/ppermute | solution.py:42
  220.2 1.5 copy.21
  221.7 1.5 copy.22
  223.2 2.6 collective-permute-done.12.refs_8_
  225.8 7.1 %collective-permute-done.13.refs_9_ = bf16[144,1152]{1,0:T(8,128)(2,1)} collective-permute-done((bf16[144,1152]{1,0:T(8,128)(2,1)}, bf16[144,1152]{1,0:T(8,128)(2,1)}, u32[]{:S(2)}, u32[]{:S(2)}) %collective-permute-start.13) | collective-permute-done | bytes 331808 | tf_op jit(solution)/shard_map/ppermute | solution.py:42
  232.9 5.1 %group_sums.1 = bf16[384,1152]{1,0:T(8,128)(2,1)} custom-call(f32[384,8]{1,0:T(8,128)} %bitcast.31, f32[384,8]{1,0:T(8,128)} %bitcast.32, bf16[144,1152]{1,0:T(8,128)(2,1)} %get-tuple-element.76.refs_2_, bf16[144,1152]{1,0:T(8,128)(2,1)} %collective-permute-done.7.refs_3_, bf16[144,1152]{1,0:T(8,128)(2,1)} %collective-permute-done.8.refs_4_, ...), custom_call_target="tpu_custom_call" | custom-call | flops 1019215872 | bytes 2654208 | tf_op jit(solution)/shard_map/group_sums/pallas_call | solution.py:220
  238.0 5.7 %all-to-all-done.2 = bf16[16,72,1536]{2,1,0:T(8,128)(2,1)S(1)} async-done(((bf16[16,72,1536]{2,1,0:T(8,128)(2,1)}), bf16[16,72,1536]{2,1,0:T(8,128)(2,1)S(1)}, u32[]{:S(2)}, u32[]{:S(2)}) %all-to-all-start.2) | async-done | bytes 3538976 | tf_op jit(solution)/shard_map/all_to_all | solution.py:447
  243.6 0.7 broadcast_in_dim.35.refs_0_
  244.3 1.2 copy-done
  245.5 8.3 %column_sums.1 = (bf16[512,1536]{1,0:T(8,128)(2,1)}, bf16[256,1536]{1,0:T(8,128)(2,1)}, bf16[256,1536]{1,0:T(8,128)(2,1)}) custom-call(f32[8,1152]{1,0:T(8,128)} %broadcast_in_dim.35.refs_0_, bf16[16,1152]{1,0:T(8,128)(2,1)} %fusion.6.refs_1_, bf16[1024,16]{1,0:T(8,128)(2,1)} %bitcast.33, bf16[1024,16]{1,0:T(8,128)(2,1)} %bitcast.34, bf16[1152,1536]{1,0:T(8,128)(2,1)} %bitcast.26), custom_call_target="tpu_custom_call" | custom-call | flops 724775731200 | bytes 8257536 | tf_op jit(solution)/shard_map/column_sums/pallas_call | solution.py:384
  253.8 1.3 collective-permute-start.14
  255.2 4.3 %all-to-all-start.3 = ((bf16[16,24,1152]{2,1,0:T(8,128)(2,1)}), bf16[16,24,1152]{2,1,0:T(8,128)(2,1)S(1)}, u32[]{:S(2)}, u32[]{:S(2)}) async-start(bf16[16,24,1152]{2,1,0:T(8,128)(2,1)} %bitcast.28), calls=%async_computation.3 | async-start | bytes 1769472 | tf_op jit(solution)/shard_map/all_to_all | solution.py:455
  259.6 2.3 add_convert_fusion.2
  262.2 3.0 %collective-permute-start.17 = (bf16[128,1536]{1,0:T(8,128)(2,1)}, bf16[128,1536]{1,0:T(8,128)(2,1)}, u32[]{:S(2)}, u32[]{:S(2)}) collective-permute-start(bf16[128,1536]{1,0:T(8,128)(2,1)} %get-tuple-element.94), channel_id=1, source_target_pairs={{0,4},{1,5},{2,6},{3,7},{4,0},{5,1},{6,2},{7,3},{8,12},{9,13},{10,... | collective-permute-start | bytes 1179656 | tf_op jit(solution)/shard_map/ppermute | solution.py:42
  265.7 8.3 %all-to-all-done.3 = bf16[16,24,1152]{2,1,0:T(8,128)(2,1)S(1)} async-done(((bf16[16,24,1152]{2,1,0:T(8,128)(2,1)}), bf16[16,24,1152]{2,1,0:T(8,128)(2,1)S(1)}, u32[]{:S(2)}, u32[]{:S(2)}) %all-to-all-start.3) | async-done | bytes 884768 | tf_op jit(solution)/shard_map/all_to_all | solution.py:455
  274.5 0.9 select_reduce_fusion
  275.4 7.1 %collective-permute-done.17 = bf16[128,1536]{1,0:T(8,128)(2,1)} collective-permute-done((bf16[128,1536]{1,0:T(8,128)(2,1)}, bf16[128,1536]{1,0:T(8,128)(2,1)}, u32[]{:S(2)}, u32[]{:S(2)}) %collective-permute-start.17) | collective-permute-done | bytes 393248 | tf_op jit(solution)/shard_map/ppermute | solution.py:42
  282.5 2.0 collective-permute-done.18
  284.5 1.5 add_convert_fusion
  286.0 0.9 pad_maximum_fusion
  (67 shorter events, 6.3 us)
Async XLA Ops:
  7.2 44.7 %all-gather.2.cloned.1.call-start = ((), (), s32[]{:S(2)}) async-start(), calls=%async_computation.4 | async-start | bytes 5898240 | tf_op jit(solution)/shard_map/all_gather | solution.py:415
  10.5 3.4 %copy-start.4 = (f32[16,128]{1,0:T(8,128)}, f32[16,128]{1,0:T(8,128)S(1)}, u32[]{:S(2)}) copy-start(f32[16,128]{1,0:T(8,128)S(1)} %convolution_select_fusion) | copy-start | bytes 24580
  13.8 45.2 %all-to-all-start = ((bf16[16,24,2688]{2,1,0:T(8,128)(2,1)}), bf16[16,24,2688]{2,1,0:T(8,128)(2,1)S(1)}, u32[]{:S(2)}, u32[]{:S(2)}) async-start(bf16[16,24,2688]{2,1,0:T(8,128)(2,1)} %bitcast.2), calls=%async_computation | async-start | bytes 4128768 | tf_op jit(solution)/shard_map/all_to_all | solution.py:430
  59.0 1.3 copy-start.1
  60.3 103.1 %all-to-all-start.1 = ((bf16[16,72,2560]{2,1,0:T(8,128)(2,1)}), bf16[16,72,2560]{2,1,0:T(8,128)(2,1)}, u32[]{:S(2)}, u32[]{:S(2)}) async-start(bf16[16,72,2560]{2,1,0:T(8,128)(2,1)} %bitcast.25), calls=%async_computation.1 | async-start | bytes 11796480 | tf_op jit(solution)/shard_map/all_to_all | solution.py:435
  74.1 5.6 %collective-permute-start = (bf16[144,2560]{1,0:T(8,128)(2,1)}, bf16[144,2560]{1,0:T(8,128)(2,1)S(1)}, u32[]{:S(2)}, u32[]{:S(2)}) collective-permute-start(bf16[144,2560]{1,0:T(8,128)(2,1)} %get-tuple-element.60), channel_id=1, source_target_pairs={{0,1},{1,0},{2,3},{3,2},{4,5},{5,4},{6,7},{7,6},{8,9},{9,8},{10,11... | collective-permute-start | bytes 2211848 | tf_op jit(solution)/shard_map/ppermute | solution.py:42
  74.6 18.4 %collective-permute-start.1 = (bf16[144,2560]{1,0:T(8,128)(2,1)}, bf16[144,2560]{1,0:T(8,128)(2,1)S(1)}, u32[]{:S(2)}, u32[]{:S(2)}) collective-permute-start(bf16[144,2560]{1,0:T(8,128)(2,1)} %get-tuple-element.61), channel_id=1, source_target_pairs={{0,2},{1,3},{2,0},{3,1},{4,6},{5,7},{6,4},{7,5},{8,10},{9,11},{10,... | collective-permute-start | bytes 2211848 | tf_op jit(solution)/shard_map/ppermute | solution.py:42
  75.6 34.1 %collective-permute-start.2 = (bf16[144,2560]{1,0:T(8,128)(2,1)}, bf16[144,2560]{1,0:T(8,128)(2,1)S(1)}, u32[]{:S(2)}, u32[]{:S(2)}) collective-permute-start(bf16[144,2560]{1,0:T(8,128)(2,1)} %get-tuple-element.62), channel_id=1, source_target_pairs={{0,3},{1,2},{2,1},{3,0},{4,7},{5,6},{6,5},{7,4},{8,11},{9,10},{10,... | collective-permute-start | bytes 2211848 | tf_op jit(solution)/shard_map/ppermute | solution.py:42
  76.3 50.2 %collective-permute-start.3 = (bf16[144,2560]{1,0:T(8,128)(2,1)}, bf16[144,2560]{1,0:T(8,128)(2,1)S(1)}, u32[]{:S(2)}, u32[]{:S(2)}) collective-permute-start(bf16[144,2560]{1,0:T(8,128)(2,1)} %get-tuple-element.63), channel_id=1, source_target_pairs={{0,4},{1,5},{2,6},{3,7},{4,0},{5,1},{6,2},{7,3},{8,12},{9,13},{10,... | collective-permute-start | bytes 2211848 | tf_op jit(solution)/shard_map/ppermute | solution.py:42
  78.1 64.5 %collective-permute-start.4 = (bf16[144,2560]{1,0:T(8,128)(2,1)}, bf16[144,2560]{1,0:T(8,128)(2,1)}, u32[]{:S(2)}, u32[]{:S(2)}) collective-permute-start(bf16[144,2560]{1,0:T(8,128)(2,1)} %get-tuple-element.64), channel_id=1, source_target_pairs={{0,5},{1,4},{2,7},{3,6},{4,1},{5,0},{6,3},{7,2},{8,13},{9,12},{10,... | collective-permute-start | bytes 2211848 | tf_op jit(solution)/shard_map/ppermute | solution.py:42
  79.6 67.1 %copy-start.6 = (bf16[144,2560]{1,0:T(8,128)(2,1)}, bf16[144,2560]{1,0:T(8,128)(2,1)S(1)}, u32[]{:S(2)}) copy-start(bf16[144,2560]{1,0:T(8,128)(2,1)S(1)} %collective-permute-done.refs_2_) | copy-start | bytes 2211844
  79.6 62.9 %collective-permute-start.5 = (bf16[144,2560]{1,0:T(8,128)(2,1)}, bf16[144,2560]{1,0:T(8,128)(2,1)}, u32[]{:S(2)}, u32[]{:S(2)}) collective-permute-start(bf16[144,2560]{1,0:T(8,128)(2,1)} %get-tuple-element.65), channel_id=1, source_target_pairs={{0,6},{1,7},{2,4},{3,5},{4,2},{5,3},{6,0},{7,1},{8,14},{9,15},{10,... | collective-permute-start | bytes 2211848 | tf_op jit(solution)/shard_map/ppermute | solution.py:42
  93.0 53.8 %copy-start.7 = (bf16[144,2560]{1,0:T(8,128)(2,1)}, bf16[144,2560]{1,0:T(8,128)(2,1)S(1)}, u32[]{:S(2)}) copy-start(bf16[144,2560]{1,0:T(8,128)(2,1)S(1)} %collective-permute-done.1.refs_3_) | copy-start | bytes 2211844
  93.0 53.8 %collective-permute-start.6 = (bf16[144,2560]{1,0:T(8,128)(2,1)}, bf16[144,2560]{1,0:T(8,128)(2,1)}, u32[]{:S(2)}, u32[]{:S(2)}) collective-permute-start(bf16[144,2560]{1,0:T(8,128)(2,1)} %get-tuple-element.66), channel_id=1, source_target_pairs={{0,7},{1,6},{2,5},{3,4},{4,3},{5,2},{6,1},{7,0},{8,15},{9,14},{10,... | collective-permute-start | bytes 2211848 | tf_op jit(solution)/shard_map/ppermute | solution.py:42
  109.7 37.1 %copy-start.8 = (bf16[144,2560]{1,0:T(8,128)(2,1)}, bf16[144,2560]{1,0:T(8,128)(2,1)S(1)}, u32[]{:S(2)}) copy-start(bf16[144,2560]{1,0:T(8,128)(2,1)S(1)} %collective-permute-done.2.refs_4_) | copy-start | bytes 2211844
  126.5 20.3 %copy-start.9 = (bf16[144,2560]{1,0:T(8,128)(2,1)}, bf16[144,2560]{1,0:T(8,128)(2,1)S(1)}, u32[]{:S(2)}) copy-start(bf16[144,2560]{1,0:T(8,128)(2,1)S(1)} %collective-permute-done.3.refs_5_) | copy-start | bytes 2211844
  183.0 60.6 %all-to-all-start.2 = ((bf16[16,72,1536]{2,1,0:T(8,128)(2,1)}), bf16[16,72,1536]{2,1,0:T(8,128)(2,1)S(1)}, u32[]{:S(2)}, u32[]{:S(2)}) async-start(bf16[16,72,1536]{2,1,0:T(8,128)(2,1)} %bitcast.27), calls=%async_computation.2 | async-start | bytes 7077888 | tf_op jit(solution)/shard_map/all_to_all | solution.py:447
  200.0 10.7 %collective-permute-start.10 = (bf16[144,1152]{1,0:T(8,128)(2,1)}, bf16[144,1152]{1,0:T(8,128)(2,1)}, u32[]{:S(2)}, u32[]{:S(2)}) collective-permute-start(bf16[144,1152]{1,0:T(8,128)(2,1)} %get-tuple-element.80), channel_id=1, source_target_pairs={{0,4},{1,5},{2,6},{3,7},{4,0},{5,1},{6,2},{7,3},{8,12},{9,13},{10,... | collective-permute-start | bytes 995336 | tf_op jit(solution)/shard_map/ppermute | solution.py:42
  200.9 18.7 %collective-permute-start.11 = (bf16[144,1152]{1,0:T(8,128)(2,1)}, bf16[144,1152]{1,0:T(8,128)(2,1)}, u32[]{:S(2)}, u32[]{:S(2)}) collective-permute-start(bf16[144,1152]{1,0:T(8,128)(2,1)} %get-tuple-element.81), channel_id=1, source_target_pairs={{0,5},{1,4},{2,7},{3,6},{4,1},{5,0},{6,3},{7,2},{8,13},{9,12},{10,... | collective-permute-start | bytes 995336 | tf_op jit(solution)/shard_map/ppermute | solution.py:42
  203.6 22.2 %collective-permute-start.12 = (bf16[144,1152]{1,0:T(8,128)(2,1)}, bf16[144,1152]{1,0:T(8,128)(2,1)}, u32[]{:S(2)}, u32[]{:S(2)}) collective-permute-start(bf16[144,1152]{1,0:T(8,128)(2,1)} %get-tuple-element.82), channel_id=1, source_target_pairs={{0,6},{1,7},{2,4},{3,5},{4,2},{5,3},{6,0},{7,1},{8,14},{9,15},{10,... | collective-permute-start | bytes 995336 | tf_op jit(solution)/shard_map/ppermute | solution.py:42
  205.9 27.0 %collective-permute-start.13 = (bf16[144,1152]{1,0:T(8,128)(2,1)}, bf16[144,1152]{1,0:T(8,128)(2,1)}, u32[]{:S(2)}, u32[]{:S(2)}) collective-permute-start(bf16[144,1152]{1,0:T(8,128)(2,1)} %get-tuple-element.83), channel_id=1, source_target_pairs={{0,7},{1,6},{2,5},{3,4},{4,3},{5,2},{6,1},{7,0},{8,15},{9,14},{10,... | collective-permute-start | bytes 995336 | tf_op jit(solution)/shard_map/ppermute | solution.py:42
  206.3 26.6 %collective-permute-start.7 = (bf16[144,1152]{1,0:T(8,128)(2,1)}, bf16[144,1152]{1,0:T(8,128)(2,1)}, u32[]{:S(2)}, u32[]{:S(2)}) collective-permute-start(bf16[144,1152]{1,0:T(8,128)(2,1)} %get-tuple-element.77), channel_id=1, source_target_pairs={{0,1},{1,0},{2,3},{3,2},{4,5},{5,4},{6,7},{7,6},{8,9},{9,8},{10,11... | collective-permute-start | bytes 995336 | tf_op jit(solution)/shard_map/ppermute | solution.py:42
  210.7 22.2 %collective-permute-start.8 = (bf16[144,1152]{1,0:T(8,128)(2,1)}, bf16[144,1152]{1,0:T(8,128)(2,1)}, u32[]{:S(2)}, u32[]{:S(2)}) collective-permute-start(bf16[144,1152]{1,0:T(8,128)(2,1)} %get-tuple-element.78), channel_id=1, source_target_pairs={{0,2},{1,3},{2,0},{3,1},{4,6},{5,7},{6,4},{7,5},{8,10},{9,11},{10,... | collective-permute-start | bytes 995336 | tf_op jit(solution)/shard_map/ppermute | solution.py:42
  219.6 13.3 %collective-permute-start.9 = (bf16[144,1152]{1,0:T(8,128)(2,1)}, bf16[144,1152]{1,0:T(8,128)(2,1)}, u32[]{:S(2)}, u32[]{:S(2)}) collective-permute-start(bf16[144,1152]{1,0:T(8,128)(2,1)} %get-tuple-element.79), channel_id=1, source_target_pairs={{0,3},{1,2},{2,1},{3,0},{4,7},{5,6},{6,5},{7,4},{8,11},{9,10},{10,... | collective-permute-start | bytes 995336 | tf_op jit(solution)/shard_map/ppermute | solution.py:42
  243.6 1.8 copy-start
  253.8 5.8 %copy-start.2 = (bf16[512,1536]{1,0:T(8,128)(2,1)S(1)}, bf16[512,1536]{1,0:T(8,128)(2,1)}, u32[]{:S(2)}) copy-start(bf16[512,1536]{1,0:T(8,128)(2,1)} %get-tuple-element.91) | copy-start | bytes 4718596
  253.8 5.7 %collective-permute-start.14 = (bf16[256,1536]{1,0:T(8,128)(2,1)}, bf16[256,1536]{1,0:T(8,128)(2,1)S(1)}, u32[]{:S(2)}, u32[]{:S(2)}) collective-permute-start(bf16[256,1536]{1,0:T(8,128)(2,1)} %get-tuple-element.92), channel_id=1, source_target_pairs={{0,1},{1,0},{2,3},{3,2},{4,5},{5,4},{6,7},{7,6},{8,9},{9,8},{10,11... | collective-permute-start | bytes 2359304 | tf_op jit(solution)/shard_map/ppermute | solution.py:42
  255.1 4.4 %collective-permute-start.16 = (bf16[256,1536]{1,0:T(8,128)(2,1)}, bf16[256,1536]{1,0:T(8,128)(2,1)}, u32[]{:S(2)}, u32[]{:S(2)}) collective-permute-start(bf16[256,1536]{1,0:T(8,128)(2,1)} %get-tuple-element.93), channel_id=1, source_target_pairs={{0,1},{1,0},{2,3},{3,2},{4,5},{5,4},{6,7},{7,6},{8,9},{9,8},{10,11... | collective-permute-start | bytes 2359304 | tf_op jit(solution)/shard_map/ppermute | solution.py:42
  255.2 18.8 %all-to-all-start.3 = ((bf16[16,24,1152]{2,1,0:T(8,128)(2,1)}), bf16[16,24,1152]{2,1,0:T(8,128)(2,1)S(1)}, u32[]{:S(2)}, u32[]{:S(2)}) async-start(bf16[16,24,1152]{2,1,0:T(8,128)(2,1)} %bitcast.28), calls=%async_computation.3 | async-start | bytes 1769472 | tf_op jit(solution)/shard_map/all_to_all | solution.py:455
  259.5 14.5 %copy-start.5 = (f32[16,128]{1,0:T(8,128)S(1)}, f32[16,128]{1,0:T(8,128)}, u32[]{:S(2)}) copy-start(f32[16,128]{1,0:T(8,128)} %copy-done.4) | copy-start | bytes 24580
  259.6 14.9 %copy-start.3 = (s32[128,6]{0,1:T(8,128)S(1)}, s32[128,6]{0,1:T(8,128)}, u32[]{:S(2)}) copy-start(s32[128,6]{0,1:T(8,128)} %param.9) | copy-start | bytes 9220
  261.9 13.5 %collective-permute-start.15 = (bf16[128,1536]{1,0:T(8,128)(2,1)}, bf16[128,1536]{1,0:T(8,128)(2,1)}, u32[]{:S(2)}, u32[]{:S(2)}) collective-permute-start(bf16[128,1536]{1,0:T(8,128)(2,1)} %get-tuple-element.96), channel_id=1, source_target_pairs={{0,2},{1,3},{2,0},{3,1},{4,6},{5,7},{6,4},{7,5},{8,10},{9,11},{10,... | collective-permute-start | bytes 1179656 | tf_op jit(solution)/shard_map/ppermute | solution.py:42
  262.2 20.3 %collective-permute-start.17 = (bf16[128,1536]{1,0:T(8,128)(2,1)}, bf16[128,1536]{1,0:T(8,128)(2,1)}, u32[]{:S(2)}, u32[]{:S(2)}) collective-permute-start(bf16[128,1536]{1,0:T(8,128)(2,1)} %get-tuple-element.94), channel_id=1, source_target_pairs={{0,4},{1,5},{2,6},{3,7},{4,0},{5,1},{6,2},{7,3},{8,12},{9,13},{10,... | collective-permute-start | bytes 1179656 | tf_op jit(solution)/shard_map/ppermute | solution.py:42
  265.2 19.3 %collective-permute-start.18 = (bf16[128,1536]{1,0:T(8,128)(2,1)}, bf16[128,1536]{1,0:T(8,128)(2,1)}, u32[]{:S(2)}, u32[]{:S(2)}) collective-permute-start(bf16[128,1536]{1,0:T(8,128)(2,1)} %get-tuple-element.95), channel_id=1, source_target_pairs={{0,6},{1,7},{2,4},{3,5},{4,2},{5,3},{6,0},{7,1},{8,14},{9,15},{10,... | collective-permute-start | bytes 1179656 | tf_op jit(solution)/shard_map/ppermute | solution.py:42
Sparse Core Ops, SparseCore 0:
  9.7 41.2 all-gather.1
